TPU v7x, 32 devices: a whole 2x2x4 slice. The times are simulated.
32 devices in a mesh: seq: 8 (over y, x, core), tp: 4 (over z).
Axes of the slice: x: 2, y: 2, z: 4, core: 2. Of those that a mesh axis runs over, the one named last changes fastest.
Arguments:
- tokens: bfloat16 [4096, 1024], P('seq', 'tp'), may hold values from -6 to 6
- variate: int32 [4096], P('seq'), may hold values from 0 to 3
- positions: int32 [4096], P('seq'), may hold values from 0 to 511
- lengths: int32 [4], replicated, may hold values from 1 to 2048, 4096 in all
- page_table: int32 [72], replicated, may hold values from 0 to 71, each once
- gain_attn: bfloat16 [1024], replicated, may hold values from 0.099609375 to 1.8984375
- w_query: bfloat16 [1024, 512], P(None, 'tp'), may hold values from -1 to 1
- w_key: bfloat16 [1024, 512], P(None, 'tp'), may hold values from -1 to 1
- w_value: bfloat16 [1024, 512], P(None, 'tp'), may hold values from -0.1875 to 0.1875
- var_bias: float32 [2, 8], P(None, 'tp'), may hold values from -2 to 2
- w_out: bfloat16 [512, 1024], P('tp'), may hold values from -0.25 to 0.25
- gain_ffn: bfloat16 [1024], replicated, may hold values from 0.099609375 to 1.8984375
- w_gate: bfloat16 [1024, 4096], P(None, 'tp'), may hold values from -0.1875 to 0.1875
- w_up: bfloat16 [1024, 4096], P(None, 'tp'), may hold values from -0.1875 to 0.1875
- w_down: bfloat16 [4096, 1024], P('tp'), may hold values from -0.09375 to 0.09375
Outputs:
- mixed: bfloat16 [4096, 1024], P('seq', 'tp')
- cache: bfloat16 [4608, 2, 512], P('seq', None, 'tp')
Inputs may be any that keep to these rules, and one draw needn't show every extreme that they name: The lengths fill all 4096 token positions in order; some request has exactly 2048 tokens. `page_table`: each physical page appears once.
All inputs are finite; a program needn't handle non-finite values.
Results may differ from a plain program's by a relative error of at most 0.018.
Values may be sent and summed in bfloat16 or wider, within the bound.
No kernel may reach another device: no remote copies, remote signals or barrier semaphores. Data moves between devices by JAX's collectives and lax.ppermute only.
A program may use at most 64 MiB of HBM per device.

v0:
```python
import jax
import jax.numpy as jnp
from jax import lax
from jax.sharding import PartitionSpec as P

HD = 64
PAGE = 64


def passed_along(value, axis, steps):
    count = lax.axis_size(axis)
    initial, last = (max(0, -steps), min(count, count - steps))
    return lax.ppermute(value, axis, [(source, source + steps) for source in range(initial, last)])


def root_mean_norm(values, gain):
    values = values.astype(jnp.float32)
    scale = lax.rsqrt(jnp.mean(values * values, axis=-1, keepdims=True) + 1e-06)
    return values * scale * gain.astype(jnp.float32)


def rotate(vectors, positions):
    half_dim = vectors.shape[-1] // 2
    frequency = 10000.0 ** (-jnp.arange(half_dim, dtype=jnp.float32) / half_dim)
    angles = positions.astype(jnp.float32)[:, None] * frequency[None, :]
    cosine = jnp.cos(angles)[:, None, :]
    sine_part = jnp.sin(angles)[:, None, :]
    first_half = vectors[..., :half_dim]
    second_half = vectors[..., half_dim:]
    return jnp.concatenate(
        [
            first_half * cosine - second_half * sine_part,
            second_half * cosine + first_half * sine_part,
        ],
        axis=-1,
    )


def segment_of(index, request_ends):
    return jnp.sum((index[:, None] >= request_ends[None, :]).astype(jnp.int32), axis=1)


def cache_slots(lengths, page_table, index):
    request_ends = jnp.cumsum(lengths)
    request_starts = request_ends - lengths
    page_counts = (lengths + PAGE - 1) // PAGE
    page_bases = jnp.cumsum(page_counts) - page_counts
    segment = segment_of(index, request_ends)
    chosen = segment[:, None] == jnp.arange(lengths.shape[0], dtype=jnp.int32)[None, :]
    offset_in = index - jnp.sum(jnp.where(chosen, request_starts[None, :], 0), axis=1)
    logical = jnp.sum(jnp.where(chosen, page_bases[None, :], 0), axis=1) + offset_in // PAGE
    page_ids = jnp.arange(page_table.shape[0], dtype=jnp.int32)
    physical = jnp.sum(
        jnp.where(logical[:, None] == page_ids[None, :], page_table[None, :], 0), axis=1
    )
    return physical * PAGE + offset_in % PAGE


def per_device(
    tokens,
    variate,
    positions,
    lengths,
    page_table,
    gain_attn,
    w_query,
    w_key,
    w_value,
    var_bias,
    w_out,
    gain_ffn,
    w_gate,
    w_up,
    w_down,
):
    token_rows = lax.all_gather(tokens, "tp", axis=1, tiled=True)
    tok_rows = token_rows.shape[0]
    row_first = lax.axis_index("seq") * tok_rows
    index = row_first + jnp.arange(tok_rows, dtype=jnp.int32)
    normed = root_mean_norm(token_rows, gain_attn).astype(jnp.bfloat16)
    local_heads = w_query.shape[1] // HD
    query_rows = rotate(
        jnp.dot(normed, w_query, preferred_element_type=jnp.float32).reshape(
            tok_rows, local_heads, HD
        ),
        positions,
    ).astype(jnp.bfloat16)
    key_rows = (
        rotate(
            jnp.dot(normed, w_key, preferred_element_type=jnp.float32).reshape(
                tok_rows, local_heads, HD
            ),
            positions,
        )
        .astype(jnp.bfloat16)
        .reshape(tok_rows, local_heads * HD)
    )
    value_rows = jnp.dot(normed, w_value, preferred_element_type=jnp.float32).astype(jnp.bfloat16)
    request_ends = jnp.cumsum(lengths)
    query_segment = segment_of(index, request_ends)
    bias_same = var_bias[0]
    bias_diff = var_bias[1]

    def attend(state, key_piece, offset):
        running_peak, running_total, weighted = state
        piece_keys, piece_values, piece_variate = key_piece
        piece_rows = piece_keys.shape[0]
        key_index = offset + jnp.arange(piece_rows, dtype=jnp.int32)
        key_segment = segment_of(key_index, request_ends)
        scores = jnp.einsum(
            "qhd,khd->hqk",
            query_rows,
            piece_keys.reshape(piece_rows, local_heads, HD),
            preferred_element_type=jnp.float32,
        ) * HD ** (-0.5)
        same = variate[:, None] == piece_variate[None, :]
        scores = scores + jnp.where(same[None], bias_same[:, None, None], bias_diff[:, None, None])
        visible = (
            (query_segment[:, None] == key_segment[None, :])
            & (index[:, None] >= key_index[None, :])
            & (key_index >= 0)[None, :]
        )
        scores = jnp.where(visible[None], scores, -1e30)
        new_peak = jnp.maximum(running_peak, jnp.max(scores, axis=-1))
        weights = jnp.where(visible[None], jnp.exp(scores - new_peak[..., None]), 0.0)
        rescale = jnp.exp(running_peak - new_peak)
        new_total = running_total * rescale + jnp.sum(weights, axis=-1)
        product = jnp.einsum(
            "hqk,khd->hqd",
            weights.astype(jnp.bfloat16),
            piece_values.reshape(piece_rows, local_heads, HD),
            preferred_element_type=jnp.float32,
        )
        return (new_peak, new_total, weighted * rescale[..., None] + product)

    state = (
        jnp.full((local_heads, tok_rows), -1e30, jnp.float32),
        jnp.zeros((local_heads, tok_rows), jnp.float32),
        jnp.zeros((local_heads, tok_rows, HD), jnp.float32),
    )
    state = attend(state, (key_rows, value_rows, variate), row_first)
    reach = lax.axis_size("seq") // 2
    for distance in range(1, reach + 1):
        moved = passed_along((key_rows, value_rows, variate), "seq", distance)
        state = attend(state, moved, row_first - distance * tok_rows)
    attended = (
        (state[2] / state[1][..., None])
        .transpose(1, 0, 2)
        .reshape(tok_rows, local_heads * HD)
        .astype(jnp.bfloat16)
    )
    projected = jnp.dot(attended, w_out, preferred_element_type=jnp.float32)
    shares = lax.psum_scatter(
        projected.astype(jnp.bfloat16), "tp", scatter_dimension=1, tiled=True
    ).astype(jnp.float32)
    residual_local = (tokens.astype(jnp.float32) + shares).astype(jnp.bfloat16)
    residual_full = lax.all_gather(residual_local, "tp", axis=1, tiled=True)
    normed_mid = root_mean_norm(residual_full, gain_ffn).astype(jnp.bfloat16)
    gate_part = jnp.dot(normed_mid, w_gate, preferred_element_type=jnp.float32)
    up_part = jnp.dot(normed_mid, w_up, preferred_element_type=jnp.float32)
    hidden = (jax.nn.silu(gate_part) * up_part).astype(jnp.bfloat16)
    down_part = jnp.dot(hidden, w_down, preferred_element_type=jnp.float32)
    ffn_share = lax.psum_scatter(
        down_part.astype(jnp.bfloat16), "tp", scatter_dimension=1, tiled=True
    ).astype(jnp.float32)
    mixed = (residual_local.astype(jnp.float32) + ffn_share).astype(jnp.bfloat16)
    pair_rows = jnp.concatenate([key_rows, value_rows], axis=1)
    cache_slot = cache_slots(lengths, page_table, index)
    cache_width = (tok_rows // PAGE + 1) * PAGE
    targets = jnp.arange(cache_width * lax.axis_size("seq"), dtype=jnp.int32)
    selector = (targets[:, None] == cache_slot[None, :]).astype(jnp.bfloat16)
    placed = lax.psum_scatter(
        jnp.dot(selector, pair_rows, preferred_element_type=jnp.float32).astype(jnp.bfloat16),
        "seq",
        scatter_dimension=0,
        tiled=True,
    )
    cache = placed.reshape(cache_width, 2, local_heads * HD)
    return (mixed, cache)


def solution(mesh):
    placed = (
        P("seq", "tp"),
        P("seq"),
        P("seq"),
        P(),
        P(),
        P(),
        P(None, "tp"),
        P(None, "tp"),
        P(None, "tp"),
        P(None, "tp"),
        P("tp", None),
        P(),
        P(None, "tp"),
        P(None, "tp"),
        P("tp", None),
    )
    return jax.shard_map(
        per_device,
        mesh=mesh,
        in_specs=placed,
        out_specs=(P("seq", "tp"), P("seq", None, "tp")),
        check_vma=False,
    )
```

profile of v0, /device:TPU:2, one launch (start us, length us, event | category | flops | bytes accessed | tf_op | source)
XLA Modules:
  0.0 242.4 jit_solution(17048040946947991294)
XLA Ops:
  7.2 2.1 collective-permute-start.1
  9.3 3.4 %collective-permute-start.4 = (s32[512]{0:T(512)}, s32[512]{0:T(512)S(1)}, u32[]{:S(2)}, u32[]{:S(2)}) collective-permute-start(s32[512]{0:T(512)} %param.16), channel_id=1, source_target_pairs={{0,8},{4,12},{8,16},{12,20},{16,24},{20,28},{1,9},{5,13},{9,17},{1... | collective-permute-start | bytes 6152 | tf_op jit(solution)/shard_map/ppermute | solution.py:13
  12.7 1.3 collective-permute-start.10
  14.0 3.7 %collective-permute-start.7 = (s32[512]{0:T(512)}, s32[512]{0:T(512)}, u32[]{:S(2)}, u32[]{:S(2)}) collective-permute-start(s32[512]{0:T(512)} %param.16), channel_id=1, source_target_pairs={{0,12},{4,16},{8,20},{12,24},{16,28},{1,13},{5,17},{9,21},{13,25},... | collective-permute-start | bytes 6152 | tf_op jit(solution)/shard_map/ppermute | solution.py:13
  17.9 0.7 convert_element_type.107
  18.5 0.8 reduce-window.17
  19.8 2.4 and_and_fusion
  22.2 1.3 slice_bitcast_fusion.1
  23.6 0.7 convert_element_type.105
  24.8 2.4 broadcast_compare_fusion
  27.2 20.4 %all-gather.3.cloned.1.call-done = bf16[512,1024]{1,0:T(8,128)(2,1)} async-done(((bf16[512,256]{1,0:T(8,128)(2,1)}), bf16[512,1024]{1,0:T(8,128)(2,1)}) %all-gather.3.cloned.1.call-update) | async-done | bytes 1048592 | tf_op jit(solution)/shard_map/all_gather | solution.py:76
  47.6 1.6 fusion.3
  49.2 1.9 convolution_convert_fusion.2
  51.2 3.4 %collective-permute-start.11 = (bf16[512,128]{0,1:T(8,128)(2,1)S(1)}, bf16[512,128]{0,1:T(8,128)(2,1)S(1)}, u32[]{:S(2)}, u32[]{:S(2)}) collective-permute-start(bf16[512,128]{0,1:T(8,128)(2,1)S(1)} %convolution_convert_fusion.2), channel_id=1, source_target_pairs={{0,16},{4,20},{8,24},{12,28},{1,17},{5,21},{9,25},{13,29},{2,18},{... | collective-permute-start | bytes 393224 | tf_op jit(solution)/shard_map/ppermute | solution.py:13
  54.5 1.3 collective-permute-start.8
  55.8 3.0 %collective-permute-start.5 = (bf16[512,128]{0,1:T(8,128)(2,1)S(1)}, bf16[512,128]{0,1:T(8,128)(2,1)S(1)}, u32[]{:S(2)}, u32[]{:S(2)}) collective-permute-start(bf16[512,128]{0,1:T(8,128)(2,1)S(1)} %convolution_convert_fusion.2), channel_id=1, source_target_pairs={{0,8},{4,12},{8,16},{12,20},{16,24},{20,28},{1,9},{5,13},{9,17},{1... | collective-permute-start | bytes 393224 | tf_op jit(solution)/shard_map/ppermute | solution.py:13
  58.9 1.9 collective-permute-start.2
  61.5 0.6 fusion.92
  62.2 1.3 collective-permute-start.6
  63.5 0.9 fusion.98
  64.5 1.5 collective-permute-done.6
  66.0 4.4 %collective-permute-start.9 = (bf16[512,128]{0,1:T(8,128)(2,1)S(1)}, bf16[512,128]{0,1:T(8,128)(2,1)S(1)}, u32[]{:S(2)}, u32[]{:S(2)}) collective-permute-start(bf16[512,128]{0,1:T(8,128)(2,1)S(1)} %bitcast.173), channel_id=1, source_target_pairs={{0,16},{4,20},{8,24},{12,28},{1,17},{5,21},{9,25},{13,29},{2,18},{... | collective-permute-start | bytes 393224 | tf_op jit(solution)/shard_map/ppermute | solution.py:13
  70.9 2.2 collective-permute-done.9
  73.0 1.9 collective-permute-start
  75.4 3.9 %collective-permute-done = bf16[512,128]{0,1:T(8,128)(2,1)S(1)} collective-permute-done((bf16[512,128]{0,1:T(8,128)(2,1)S(1)}, bf16[512,128]{0,1:T(8,128)(2,1)S(1)}, u32[]{:S(2)}, u32[]{:S(2)}) %collective-permute-start) | collective-permute-done | bytes 131104 | tf_op jit(solution)/shard_map/ppermute | solution.py:13
  79.3 7.5 %collective-permute-start.3 = (bf16[512,128]{0,1:T(8,128)(2,1)S(1)}, bf16[512,128]{0,1:T(8,128)(2,1)S(1)}, u32[]{:S(2)}, u32[]{:S(2)}) collective-permute-start(bf16[512,128]{0,1:T(8,128)(2,1)S(1)} %bitcast.175), channel_id=1, source_target_pairs={{0,8},{4,12},{8,16},{12,20},{16,24},{20,28},{1,9},{5,13},{9,17},{1... | collective-permute-start | bytes 393224 | tf_op jit(solution)/shard_map/ppermute | solution.py:13
  86.9 1.0 fusion.30
  87.9 1.3 collective-permute-done.3
  89.1 3.5 %fusion.11 = (f32[2,512]{1,0:T(2,128)S(1)}, f32[2,512]{1,0:T(2,128)S(1)}, f32[2,512]{1,0:T(2,128)S(1)}, f32[2,512]{1,0:T(2,128)S(1)}, f32[2,512,512]{1,2,0:T(8,128)S(1)}) fusion(f32[2,512,512]{1,2,0:T(8,128)S(1)} %get-tuple-element.50, f32[2,512]{1,0:T(2,128)S(1)} %get-tuple-element.30, f32[2]{0:T(128)S(1)} %copy-done.13, f32[2]{0:T(128)S(1)} %copy-done.12, ...), kind=kOutput, calls=%fused_computation.27 | convolution fusion | flops 78901248 | bytes 10768400 | tf_op jit(solution)/shard_map/qhd,khd->hqk/dot_general | solution.py:110
  92.6 2.4 %fusion.13 = (f32[2,512]{1,0:T(2,128)S(1)}, f32[2,512]{1,0:T(2,128)S(1)}, f32[2,512]{1,0:T(2,128)S(1)}) fusion(f32[2,512,512]{1,2,0:T(8,128)S(1)} %get-tuple-element.51, f32[2,512]{1,0:T(2,128)S(1)} %get-tuple-element.22, f32[2]{0:T(128)S(1)} %copy-done.13, f32[2]{0:T(128)S(1)} %copy-done.12, pred[512,512]{0,1:T(8,128)(4,1)S(1)} %get-tuple-element.39, ...), kind=kLoop, calls=%fused_computation.29 | loop fusion | flops 11006976 | bytes 7888912 | tf_op jit(solution)/shard_map/reduce_sum | solution.py:127
  95.1 1.1 convolution_bitcast_fusion.1
  96.2 1.1 convolution_bitcast_fusion
  97.3 1.1 convolution_bitcast_fusion.2
  98.9 0.6 fusion.20
  99.5 1.1 fusion.29
  100.7 1.4 convolution_convert_fusion
  102.2 27.1 %reduce-scatter.4.cloned.1.call-done = bf16[512,256]{1,0:T(8,128)(2,1)} async-done(((bf16[512,1024]{1,0:T(8,128)(2,1)}), bf16[512,256]{1,0:T(8,128)(2,1)}) %reduce-scatter.4.cloned.1.call-update) | async-done | bytes 262160 | tf_op jit(solution)/shard_map/reduce_scatter | solution.py:153
  129.4 1.7 add_convert_fusion.1
  131.8 3.1 %fusion.1 = bf16[4608,256]{1,0:T(8,128)(2,1)} fusion(s32[512]{0:T(512)S(1)} %fusion.67, bf16[512,128]{0,1:T(8,128)(2,1)S(1)} %copy-done.22, bf16[512,128]{0,1:T(8,128)(2,1)S(1)} %bitcast.176), kind=kOutput, calls=%fused_computation.2 | convolution fusion | flops 1212022784 | bytes 2623488 | tf_op jit(solution)/shard_map/dot_general | solution.py:173
  135.0 0.6 copy-done.14
  135.6 23.8 %all-gather.5.cloned.1.call-done = bf16[512,1024]{1,0:T(8,128)(2,1)} async-done(((bf16[512,256]{1,0:T(8,128)(2,1)}), bf16[512,1024]{1,0:T(8,128)(2,1)}) %all-gather.5.cloned.1.call-update) | async-done | bytes 1048592 | tf_op jit(solution)/shard_map/all_gather | solution.py:157
  159.5 1.5 fusion.6
  161.0 3.9 %fusion.53 = f32[512,1024]{1,0:T(8,128)} fusion(bf16[1024,1024]{1,0:T(8,128)(2,1)S(1)} %copy-done, bf16[512,1024]{1,0:T(8,128)(2,1)} %all-gather.5.cloned.1.call-done, f32[1024]{0:T(1024)S(1)} %convert_element_type.127, f32[512]{0:T(512)S(1)} %add_rsqrt_fusion), kind=kOutput, calls=%fused_computation.82 | convolution fusion | flops 1075838976 | bytes 5249024 | tf_op jit(solution)/shard_map/dot_general | solution.py:159
  164.9 6.3 %convolution_convert_fusion.1 = bf16[512,1024]{1,0:T(8,128)(2,1)} fusion(bf16[1024,1024]{1,0:T(8,128)(2,1)} %param.29, f32[512,1024]{1,0:T(8,128)} %fusion.53, bf16[1024,1024]{1,0:T(8,128)(2,1)} %param.28, bf16[512,1024]{1,0:T(8,128)(2,1)S(1)} %copy-done.6, f32[1024]{0:T(1024)S(1)} %convert_element_type.127, f32[512]{0:T(512)S(1)} %add_rsqrt_fusion), kind=kOutput, calls=%fused_computation.36 | convolution fusion | flops 2153250816 | bytes 8394752 | tf_op jit(solution)/shard_map/dot_general | solution.py:162
  171.2 33.6 %reduce-scatter.8.cloned.1.call-done = bf16[576,256]{1,0:T(8,128)(2,1)} async-done(((bf16[4608,256]{1,0:T(8,128)(2,1)}), bf16[576,256]{1,0:T(8,128)(2,1)}) %reduce-scatter.8.cloned.1.call-update) | async-done | bytes 294928 | tf_op jit(solution)/shard_map/reduce_scatter | solution.py:172
  204.8 1.7 reshape.855
  206.6 27.6 %reduce-scatter.6.cloned.1.call-done = bf16[512,256]{1,0:T(8,128)(2,1)} async-done(((bf16[512,1024]{1,0:T(8,128)(2,1)}), bf16[512,256]{1,0:T(8,128)(2,1)}) %reduce-scatter.6.cloned.1.call-update) | async-done | bytes 262160 | tf_op jit(solution)/shard_map/reduce_scatter | solution.py:163
  234.2 1.7 add_convert_fusion
  (92 shorter events, 4.2 us)
Async XLA Ops:
  7.2 153.8 %copy-start = (bf16[1024,1024]{1,0:T(8,128)(2,1)S(1)}, bf16[1024,1024]{1,0:T(8,128)(2,1)}, u32[]{:S(2)}) copy-start(bf16[1024,1024]{1,0:T(8,128)(2,1)} %param.27) | copy-start | bytes 6291460
  7.2 40.4 %all-gather.3.cloned.1.call-start = ((), (), s32[]{:S(2)}) async-start(), calls=%async_computation.3 | async-start | bytes 1310720 | tf_op jit(solution)/shard_map/all_gather | solution.py:76
  7.2 17.0 %collective-permute-start.1 = (s32[512]{0:T(512)}, s32[512]{0:T(512)S(1)}, u32[]{:S(2)}, u32[]{:S(2)}) collective-permute-start(s32[512]{0:T(512)} %param.16), channel_id=1, source_target_pairs={{0,4},{4,8},{8,12},{12,16},{16,20},{20,24},{24,28},{1,5},{5,9},{9,... | collective-permute-start | bytes 6152 | tf_op jit(solution)/shard_map/ppermute | solution.py:13
  9.3 15.0 %collective-permute-start.4 = (s32[512]{0:T(512)}, s32[512]{0:T(512)S(1)}, u32[]{:S(2)}, u32[]{:S(2)}) collective-permute-start(s32[512]{0:T(512)} %param.16), channel_id=1, source_target_pairs={{0,8},{4,12},{8,16},{12,20},{16,24},{20,28},{1,9},{5,13},{9,17},{1... | collective-permute-start | bytes 6152 | tf_op jit(solution)/shard_map/ppermute | solution.py:13
  12.7 11.6 %collective-permute-start.10 = (s32[512]{0:T(512)}, s32[512]{0:T(512)S(1)}, u32[]{:S(2)}, u32[]{:S(2)}) collective-permute-start(s32[512]{0:T(512)} %param.16), channel_id=1, source_target_pairs={{0,16},{4,20},{8,24},{12,28},{1,17},{5,21},{9,25},{13,29},{2,18},{... | collective-permute-start | bytes 6152 | tf_op jit(solution)/shard_map/ppermute | solution.py:13
  14.0 10.8 %collective-permute-start.7 = (s32[512]{0:T(512)}, s32[512]{0:T(512)}, u32[]{:S(2)}, u32[]{:S(2)}) collective-permute-start(s32[512]{0:T(512)} %param.16), channel_id=1, source_target_pairs={{0,12},{4,16},{8,20},{12,24},{16,28},{1,13},{5,17},{9,21},{13,25},... | collective-permute-start | bytes 6152 | tf_op jit(solution)/shard_map/ppermute | solution.py:13
  17.7 111.6 %reduce-scatter.4.cloned.1.call-start = ((), (), s32[]{:S(2)}) async-start(), calls=%async_computation.4 | async-start | bytes 1310720 | tf_op jit(solution)/shard_map/reduce_scatter | solution.py:153
  19.4 2.9 %copy-start.15 = (s32[4,1]{0,1:T(1,128)}, s32[4,1]{0,1:T(1,128)S(1)}, u32[]{:S(2)}) copy-start(s32[4,1]{0,1:T(1,128)S(1)} %reduce-window.17) | copy-start | bytes 52
  24.3 0.6 copy-start.11
  47.6 13.2 %copy-start.5 = (bf16[512,1024]{1,0:T(8,128)(2,1)S(1)}, bf16[512,1024]{1,0:T(8,128)(2,1)}, u32[]{:S(2)}) copy-start(bf16[512,1024]{1,0:T(8,128)(2,1)} %all-gather.3.cloned.1.call-done) | copy-start | bytes 3145732
  47.6 13.2 %copy-start.19 = (bf16[1024,128]{1,0:T(8,128)(2,1)S(1)}, bf16[1024,128]{1,0:T(8,128)(2,1)}, u32[]{:S(2)}) copy-start(bf16[1024,128]{1,0:T(8,128)(2,1)} %param.21) | copy-start | bytes 786436
  49.2 12.3 %copy-start.20 = (bf16[1024,128]{1,0:T(8,128)(2,1)S(1)}, bf16[1024,128]{1,0:T(8,128)(2,1)}, u32[]{:S(2)}) copy-start(bf16[1024,128]{1,0:T(8,128)(2,1)} %param.22) | copy-start | bytes 786436
  51.1 47.7 %copy-start.21 = (bf16[512,128]{0,1:T(8,128)(2,1)}, bf16[512,128]{0,1:T(8,128)(2,1)S(1)}, u32[]{:S(2)}) copy-start(bf16[512,128]{0,1:T(8,128)(2,1)S(1)} %convolution_convert_fusion.2) | copy-start | bytes 393220
  51.2 45.0 %collective-permute-start.11 = (bf16[512,128]{0,1:T(8,128)(2,1)S(1)}, bf16[512,128]{0,1:T(8,128)(2,1)S(1)}, u32[]{:S(2)}, u32[]{:S(2)}) collective-permute-start(bf16[512,128]{0,1:T(8,128)(2,1)S(1)} %convolution_convert_fusion.2), channel_id=1, source_target_pairs={{0,16},{4,20},{8,24},{12,28},{1,17},{5,21},{9,25},{13,29},{2,18},{... | collective-permute-start | bytes 393224 | tf_op jit(solution)/shard_map/ppermute | solution.py:13
  54.5 40.5 %collective-permute-start.8 = (bf16[512,128]{0,1:T(8,128)(2,1)S(1)}, bf16[512,128]{0,1:T(8,128)(2,1)S(1)}, u32[]{:S(2)}, u32[]{:S(2)}) collective-permute-start(bf16[512,128]{0,1:T(8,128)(2,1)S(1)} %convolution_convert_fusion.2), channel_id=1, source_target_pairs={{0,12},{4,16},{8,20},{12,24},{16,28},{1,13},{5,17},{9,21},{13,25},... | collective-permute-start | bytes 393224 | tf_op jit(solution)/shard_map/ppermute | solution.py:13
  55.8 41.4 %collective-permute-start.5 = (bf16[512,128]{0,1:T(8,128)(2,1)S(1)}, bf16[512,128]{0,1:T(8,128)(2,1)S(1)}, u32[]{:S(2)}, u32[]{:S(2)}) collective-permute-start(bf16[512,128]{0,1:T(8,128)(2,1)S(1)} %convolution_convert_fusion.2), channel_id=1, source_target_pairs={{0,8},{4,12},{8,16},{12,20},{16,24},{20,28},{1,9},{5,13},{9,17},{1... | collective-permute-start | bytes 393224 | tf_op jit(solution)/shard_map/ppermute | solution.py:13
  58.9 40.6 %collective-permute-start.2 = (bf16[512,128]{0,1:T(8,128)(2,1)S(1)}, bf16[512,128]{0,1:T(8,128)(2,1)S(1)}, u32[]{:S(2)}, u32[]{:S(2)}) collective-permute-start(bf16[512,128]{0,1:T(8,128)(2,1)S(1)} %convolution_convert_fusion.2), channel_id=1, source_target_pairs={{0,4},{4,8},{8,12},{12,16},{16,20},{20,24},{24,28},{1,5},{5,9},{9,... | collective-permute-start | bytes 393224 | tf_op jit(solution)/shard_map/ppermute | solution.py:13
  61.4 2.1 copy-start.9
  61.4 2.1 copy-start.12
  61.4 2.1 copy-start.13
  62.2 3.8 %collective-permute-start.6 = (bf16[512,128]{0,1:T(8,128)(2,1)S(1)}, bf16[512,128]{0,1:T(8,128)(2,1)S(1)}, u32[]{:S(2)}, u32[]{:S(2)}) collective-permute-start(bf16[512,128]{0,1:T(8,128)(2,1)S(1)} %bitcast.172), channel_id=1, source_target_pairs={{0,12},{4,16},{8,20},{12,24},{16,28},{1,13},{5,17},{9,21},{13,25},... | collective-permute-start | bytes 393224 | tf_op jit(solution)/shard_map/ppermute | solution.py:13
  66.0 7.1 %collective-permute-start.9 = (bf16[512,128]{0,1:T(8,128)(2,1)S(1)}, bf16[512,128]{0,1:T(8,128)(2,1)S(1)}, u32[]{:S(2)}, u32[]{:S(2)}) collective-permute-start(bf16[512,128]{0,1:T(8,128)(2,1)S(1)} %bitcast.173), channel_id=1, source_target_pairs={{0,16},{4,20},{8,24},{12,28},{1,17},{5,21},{9,25},{13,29},{2,18},{... | collective-permute-start | bytes 393224 | tf_op jit(solution)/shard_map/ppermute | solution.py:13
  70.4 16.4 %copy-start.7 = (pred[512,512]{0,1:T(8,128)(4,1)S(1)}, pred[512,512]{0,1:T(8,128)(4,1)}, u32[]{:S(2)}) copy-start(pred[512,512]{0,1:T(8,128)(4,1)} %get-tuple-element.34) | copy-start | bytes 786436
  70.4 16.4 %copy-start.8 = (pred[512,512]{0,1:T(8,128)(4,1)S(1)}, pred[512,512]{0,1:T(8,128)(4,1)}, u32[]{:S(2)}) copy-start(pred[512,512]{0,1:T(8,128)(4,1)} %get-tuple-element.41) | copy-start | bytes 786436
  73.0 6.3 %collective-permute-start = (bf16[512,128]{0,1:T(8,128)(2,1)S(1)}, bf16[512,128]{0,1:T(8,128)(2,1)S(1)}, u32[]{:S(2)}, u32[]{:S(2)}) collective-permute-start(bf16[512,128]{0,1:T(8,128)(2,1)S(1)} %bitcast.174), channel_id=1, source_target_pairs={{0,4},{4,8},{8,12},{12,16},{16,20},{20,24},{24,28},{1,5},{5,9},{9,... | collective-permute-start | bytes 393224 | tf_op jit(solution)/shard_map/ppermute | solution.py:13
  79.3 9.8 %collective-permute-start.3 = (bf16[512,128]{0,1:T(8,128)(2,1)S(1)}, bf16[512,128]{0,1:T(8,128)(2,1)S(1)}, u32[]{:S(2)}, u32[]{:S(2)}) collective-permute-start(bf16[512,128]{0,1:T(8,128)(2,1)S(1)} %bitcast.175), channel_id=1, source_target_pairs={{0,8},{4,12},{8,16},{12,20},{16,24},{20,28},{1,9},{5,13},{9,17},{1... | collective-permute-start | bytes 393224 | tf_op jit(solution)/shard_map/ppermute | solution.py:13
  86.8 2.3 copy-start.2
  86.8 2.3 copy-start.3
  99.5 1.2 copy-start.10
  100.6 28.7 %copy-start.4 = (bf16[512,256]{1,0:T(8,128)(2,1)S(1)}, bf16[512,256]{1,0:T(8,128)(2,1)}, u32[]{:S(2)}) copy-start(bf16[512,256]{1,0:T(8,128)(2,1)} %param.15) | copy-start | bytes 786436
  100.6 30.7 %copy-start.16 = (s32[4,1]{0,1:T(1,128)S(1)}, s32[4,1]{0,1:T(1,128)}, u32[]{:S(2)}) copy-start(s32[4,1]{0,1:T(1,128)} %copy-done.15) | copy-start | bytes 52
  100.7 30.7 %copy-start.18 = (s32[4]{0:T(128)S(1)}, s32[4]{0:T(128)}, u32[]{:S(2)}) copy-start(s32[4]{0:T(128)} %param.18) | copy-start | bytes 52
  100.7 31.0 %copy-start.17 = (s32[72]{0:T(128)S(1)}, s32[72]{0:T(128)}, u32[]{:S(2)}) copy-start(s32[72]{0:T(128)} %param.19) | copy-start | bytes 868
  100.7 31.2 %copy-start.22 = (bf16[512,128]{0,1:T(8,128)(2,1)S(1)}, bf16[512,128]{0,1:T(8,128)(2,1)}, u32[]{:S(2)}) copy-start(bf16[512,128]{0,1:T(8,128)(2,1)} %copy-done.21) | copy-start | bytes 393220
  102.2 57.3 %all-gather.5.cloned.1.call-start = ((), (), s32[]{:S(2)}) async-start(), calls=%async_computation.5 | async-start | bytes 1310720 | tf_op jit(solution)/shard_map/all_gather | solution.py:157
  131.1 73.7 %reduce-scatter.8.cloned.1.call-start = ((), (), s32[]{:S(2)}) async-start(), calls=%async_computation.7 | async-start | bytes 2654208 | tf_op jit(solution)/shard_map/reduce_scatter | solution.py:172
  134.9 0.7 copy-start.14
  135.0 99.2 %reduce-scatter.6.cloned.1.call-start = ((), (), s32[]{:S(2)}) async-start(), calls=%async_computation.6 | async-start | bytes 1310720 | tf_op jit(solution)/shard_map/reduce_scatter | solution.py:163
  161.0 4.0 %copy-start.6 = (bf16[512,1024]{1,0:T(8,128)(2,1)S(1)}, bf16[512,1024]{1,0:T(8,128)(2,1)}, u32[]{:S(2)}) copy-start(bf16[512,1024]{1,0:T(8,128)(2,1)} %all-gather.5.cloned.1.call-done) | copy-start | bytes 3145732
  164.9 69.2 %copy-start.1 = (bf16[512,256]{1,0:T(8,128)(2,1)S(1)}, bf16[512,256]{1,0:T(8,128)(2,1)}, u32[]{:S(2)}) copy-start(bf16[512,256]{1,0:T(8,128)(2,1)} %add_convert_fusion.1) | copy-start | bytes 786436
Sparse Core Ops, SparseCore 0:
  17.9 29.7 all-gather.2
  102.3 27.0 reduce-scatter.3
  131.6 27.8 all-gather.4
  163.0 41.7 reduce-scatter.7
  207.0 27.1 reduce-scatter.5
where the time goes:
time: 245 us; the launch traced here: 242 us
  waiting for transfers between devices  141 us (58%)
  starting transfers between devices  35.6 us (15%)
  matrix products  29.2 us (12%)
  other arithmetic  17.4 us (7%)
  between operations  14.4 us (6%)
  local copies, waits for them, and re-layouts  4.37 us (2%)
    ppermute x12, starting transfers between devices, passed_along(): lax.ppermute(value, axis, [(source, source + steps) for source in range(i...  35.2 us
    reduce_scatter x1, waiting for transfers between devices, per_device(): lax.psum_scatter(jnp.dot(selector, pair_rows, preferred_element_type=jnp....  33.6 us
    reduce_scatter x1, waiting for transfers between devices, per_device(): lax.psum_scatter(down_part.astype(jnp.bfloat16), 'tp', scatter_dimension=...  27.6 us
    reduce_scatter x1, waiting for transfers between devices, per_device(): lax.psum_scatter(projected.astype(jnp.bfloat16), 'tp', scatter_dimension=...  27.1 us
    all_gather x1, waiting for transfers between devices, per_device(): residual_full = lax.all_gather(residual_local, 'tp', axis=1, tiled=True)  23.8 us
    all_gather x1, waiting for transfers between devices, per_device(): token_rows = lax.all_gather(tokens, 'tp', axis=1, tiled=True)  20.4 us
    ppermute x12, waiting for transfers between devices, passed_along(): lax.ppermute(value, axis, [(source, source + steps) for source in range(i...  8.84 us
    dot_general x5, matrix products, attend(): jnp.einsum('qhd,khd->hqk', query_rows, piece_keys.reshape(piece_rows, loc...  6.35 us
  transfers between devices with their start and end apart: 17, of which 9 were waited for; matrix products, arithmetic and copies ran while one was open for 17% of the time, Pallas kernels for 0%

commit v1 on v0

v1 whole, which is shorter than its diff:
```python
import functools

import jax
import jax.numpy as jnp
from jax import lax
from jax.experimental import pallas as pl
from jax.experimental.pallas import tpu as pltpu
from jax.sharding import PartitionSpec as P

HD = 64
PAGE = 64
VARS = 4
BIAS_PARTS = 3
LANES = 128
HIDDEN_SCORE = -1e30
EPS = 1e-06

VMEM = pl.BlockSpec(memory_space=pltpu.VMEM)
SMEM = pl.BlockSpec(memory_space=pltpu.SMEM)
ANY = pl.BlockSpec(memory_space=pl.ANY)


def params(mib):
    return pltpu.CompilerParams(vmem_limit_bytes=mib << 20)


def cost(flops, nbytes, exps=0):
    return pl.CostEstimate(flops=flops, bytes_accessed=nbytes, transcendentals=exps)


def dot_f32(left, right):
    return jnp.dot(left, right, preferred_element_type=jnp.float32)


def line_gather(shard):
    far = lax.ppermute(shard, "tp", [(0, 2), (1, 3), (2, 0), (3, 1)])
    left = lax.ppermute(shard, "tp", [(0, 1), (1, 2), (2, 3)])
    right = lax.ppermute(shard, "tp", [(3, 2), (2, 1), (1, 0)])
    ends = lax.ppermute(far, "tp", [(2, 3), (1, 0)])
    return [shard, left, right, far, ends]


def gather_pieces(shard):
    if lax.axis_size("tp") == 4:
        return line_gather(shard)
    whole = lax.all_gather(shard, "tp", axis=0)
    return [whole[i] for i in range(whole.shape[0])]


def piece_count():
    return 5 if lax.axis_size("tp") == 4 else lax.axis_size("tp")


def assemble(pieces, place, target, on_line):
    width = pieces[0].shape[1]

    def put(block, value):
        target[:, pl.ds(pl.multiple_of(block * width, width), width)] = value

    if not on_line:
        for i, piece in enumerate(pieces):
            target[:, i * width : (i + 1) * width] = piece[...]
        return
    own, left, right, far, ends = pieces
    put(place, own[...])
    put(lax.rem(place + 2, 4), far[...])
    put(lax.rem(place + 3, 4), jnp.where(place == 0, ends[...], left[...]))
    put(lax.rem(place + 1, 4), jnp.where(place == 3, ends[...], right[...]))


def rotate_lanes(vectors, cosine, signed_sine):
    lane = lax.broadcasted_iota(jnp.int32, vectors.shape, 1)
    half = HD // 2
    ahead = pltpu.roll(vectors, vectors.shape[1] - half, 1)
    behind = pltpu.roll(vectors, half, 1)
    partner = jnp.where(lane % HD < half, ahead, behind)
    return vectors * cosine + partner * signed_sine


def norm_rows(values, gain):
    scale = lax.rsqrt(jnp.mean(values * values, axis=-1, keepdims=True) + EPS)
    return (values * scale * gain).astype(jnp.bfloat16)


def project_kernel(count, on_line, place_ref, *refs):
    pieces = refs[:count]
    gain, w_q, w_k, w_v, cosine, sine, tokens, queries, pairs = refs[count:]
    assemble(pieces, place_ref[0], tokens, on_line)
    rows = tokens.shape[0]
    width = w_q.shape[1]
    step = min(rows, 256)
    gain_row = gain[...].astype(jnp.float32)
    for first in range(0, rows, step):
        part = pl.ds(first, step)
        normed = norm_rows(tokens[part, :].astype(jnp.float32), gain_row)
        cos_part, sin_part = cosine[part, :], sine[part, :]
        query = rotate_lanes(dot_f32(normed, w_q[...]), cos_part, sin_part)
        queries[part, :] = query.astype(jnp.bfloat16) * jnp.bfloat16(HD**-0.5)
        key = rotate_lanes(dot_f32(normed, w_k[...]), cos_part, sin_part)
        pairs[part, :width] = key.astype(jnp.bfloat16)
        pairs[part, width:] = dot_f32(normed, w_v[...]).astype(jnp.bfloat16)


def project(pieces, place, gain, w_query, w_key, w_value, cosine, sine):
    rows, part = pieces[0].shape
    width = w_query.shape[1]
    features = w_query.shape[0]
    on_line = lax.axis_size("tp") == 4
    return pl.pallas_call(
        functools.partial(project_kernel, len(pieces), on_line),
        out_shape=[
            jax.ShapeDtypeStruct((rows, features), jnp.bfloat16),
            jax.ShapeDtypeStruct((rows, width), jnp.bfloat16),
            jax.ShapeDtypeStruct((rows, 2 * width), jnp.bfloat16),
        ],
        in_specs=[SMEM] + [VMEM] * (len(pieces) + 6),
        out_specs=[VMEM] * 3,
        compiler_params=params(24),
        cost_estimate=cost(6 * rows * features * width, 4 << 20),
        name="project",
    )(place, *pieces, gain, w_query, w_key, w_value, cosine, sine)


def seq_xor(value, mask):
    return lax.ppermute(value, "seq", [(i, i ^ mask) for i in range(lax.axis_size("seq"))])


def seq_pieces(pairs):
    if lax.axis_size("seq") == 8:
        across = seq_xor(pairs, 2)
        down = seq_xor(pairs, 4)
        twin = seq_xor(pairs, 1)
        diagonal = seq_xor(across, 4)
        across_twin = seq_xor(across, 1)
        down_twin = seq_xor(down, 1)
        diagonal_twin = seq_xor(diagonal, 1)
        return [pairs, twin, across, across_twin, down, down_twin, diagonal, diagonal_twin]
    return [lax.all_gather(pairs, "seq", axis=0)]


def piece_copies(pieces, me, wanted):
    if len(pieces) > 1:
        for m, piece in enumerate(pieces):
            wanted(piece, me ^ m)
    else:
        for j in range(pieces[0].shape[0]):
            wanted(pieces[0].at[j], j)


def attend_kernel(count, heads, reach, info, queries, query_marks, key_marks, *refs):
    pieces = refs[:count]
    out, q_buf, k_buf, v_buf, scores, peak, total, sems = refs[count:]
    me, last = info[0], info[1]
    rows = queries.shape[0]
    width = queries.shape[1]

    def copies(source, block, slot):
        return [
            pltpu.make_async_copy(
                source.at[:, pl.ds(0, width)], k_buf.at[slot, :, pl.ds(0, width)], sems.at[slot, 0]
            ),
            pltpu.make_async_copy(
                source.at[:, pl.ds(width, width)],
                v_buf.at[slot, :, pl.ds(0, width)],
                sems.at[slot, 1],
            ),
            pltpu.make_async_copy(
                key_marks.at[pl.ds(pl.multiple_of(block * rows, rows), rows), :],
                k_buf.at[slot, :, pl.ds(width, LANES)],
                sems.at[slot, 2],
            ),
        ]

    def begin(source, block):
        distance = me - block

        @pl.when((distance >= 0) & (distance <= last))
        def _():
            for copy in copies(source, block, distance):
                copy.start()

    piece_copies(pieces, me, begin)
    example = pieces[0] if count > 1 else pieces[0].at[0]

    def finish(slot):
        for copy in copies(example, 0, slot):
            copy.wait()

    lane = lax.broadcasted_iota(jnp.int32, (rows, width), 1)
    for h in range(heads):
        part = pl.ds(h * rows, rows)
        q_buf[part, :width] = jnp.where(lane // HD == h, queries[...], jnp.bfloat16(0))
        q_buf[part, width:] = query_marks[h]
    for slot in range(reach + 1):
        v_buf[slot, :, width:] = jnp.ones((rows, LANES), jnp.bfloat16)

    def narrow(tile):
        best = tile[:, :LANES]
        for first in range(LANES, rows, LANES):
            best = jnp.maximum(best, tile[:, first : first + LANES])
        return best

    def score(h, slot):
        return lax.dot_general(
            q_buf[pl.ds(h * rows, rows), :],
            k_buf[slot],
            (((1,), (1,)), ((), ())),
            preferred_element_type=jnp.float32,
        )

    finish(0)
    q_at = lax.broadcasted_iota(jnp.int32, (rows, rows), 0)
    k_at = lax.broadcasted_iota(jnp.int32, (rows, rows), 1)
    for h in range(heads):
        tile = jnp.where(k_at <= q_at, score(h, 0), HIDDEN_SCORE)
        scores[h, 0] = tile
        peak[h] = narrow(tile)

    def first_pass(slot, carry):
        finish(slot)
        for h in range(heads):
            tile = score(h, slot)
            scores[h, slot] = tile
            peak[h] = jnp.maximum(peak[h], narrow(tile))
        return carry

    lax.fori_loop(1, last + 1, first_pass, 0)
    for h in range(heads):
        best = jnp.max(peak[h], axis=1, keepdims=True)
        peak[h] = jnp.broadcast_to(best, (rows, LANES))
        total[h] = jnp.zeros_like(total[h])

    def second_pass(slot, carry):
        for h in range(heads):
            best = peak[h]
            wide = jnp.concatenate([best] * (rows // LANES), axis=1)
            weight = jnp.exp(scores[h, slot] - wide).astype(jnp.bfloat16)
            total[h] += dot_f32(weight, v_buf[slot])
        return carry

    lax.fori_loop(0, last + 1, second_pass, 0)
    result = total[0, :, :width] / total[0, :, width:]
    for h in range(1, heads):
        result = jnp.where(lane // HD == h, total[h, :, :width] / total[h, :, width:], result)
    out[...] = result.astype(jnp.bfloat16)


def attend(info, queries, query_marks, key_marks, pieces, heads, reach):
    rows, width = queries.shape
    slots = reach + 1
    return pl.pallas_call(
        functools.partial(attend_kernel, len(pieces), heads, reach),
        out_shape=jax.ShapeDtypeStruct((rows, width), jnp.bfloat16),
        in_specs=[SMEM, VMEM, VMEM, ANY] + [ANY] * len(pieces),
        out_specs=VMEM,
        scratch_shapes=[
            pltpu.VMEM((heads * rows, width + LANES), jnp.bfloat16),
            pltpu.VMEM((slots, rows, width + LANES), jnp.bfloat16),
            pltpu.VMEM((slots, rows, width + LANES), jnp.bfloat16),
            pltpu.VMEM((heads, slots, rows, rows), jnp.float32),
            pltpu.VMEM((heads, rows, LANES), jnp.float32),
            pltpu.VMEM((heads, rows, width + LANES), jnp.float32),
            pltpu.SemaphoreType.DMA((slots, 3)),
        ],
        compiler_params=params(48),
        cost_estimate=cost(
            4 * heads * rows * rows * slots * 256, 4 << 20, heads * rows * rows * slots
        ),
        name="attend",
    )(info, queries, query_marks, key_marks, *pieces)


def bias_marks(variate, segment, var_bias, requests):
    lane = jnp.arange(LANES, dtype=jnp.int32)
    chosen = variate[None, :, None] == (lane % VARS)[None, None, :]
    bias = jnp.where(chosen, var_bias[0][:, None, None], var_bias[1][:, None, None])
    high = lax.reduce_precision(bias, 8, 7)
    middle = lax.reduce_precision(bias - high, 8, 7)
    low = bias - high - middle
    part = (lane // VARS)[None, None, :]
    marks = jnp.where(part == 0, high, jnp.where(part == 1, middle, low))
    other = segment[None, :, None] != (lane - BIAS_PARTS * VARS)[None, None, :]
    marks = jnp.where(part < BIAS_PARTS, marks, jnp.where(other, HIDDEN_SCORE, 0.0))
    used = lane < BIAS_PARTS * VARS + requests
    return jnp.where(used[None, None, :], marks, 0.0).astype(jnp.bfloat16)


def key_marks_of(variate, segment, requests):
    lane = jnp.arange(LANES, dtype=jnp.int32)[None, :]
    same_variate = variate[:, None] == lane % VARS
    same_segment = segment[:, None] == lane - BIAS_PARTS * VARS
    marked = jnp.where(lane < BIAS_PARTS * VARS, same_variate, same_segment)
    used = lane < BIAS_PARTS * VARS + requests
    return (marked & used).astype(jnp.bfloat16)


def cache_kernel(count, window, me_ref, first_token, amounts, *refs):
    pieces = refs[:count]
    out, rows_buf, sems = refs[count:]
    rows = rows_buf.shape[1]
    blocks = rows_buf.shape[0]
    flat = rows_buf.shape[0] * rows
    me = me_ref[0]
    started = []

    def begin(source, block):
        copy = pltpu.make_async_copy(source, rows_buf.at[block], sems.at[len(started)])
        copy.start()
        started.append(copy)

    piece_copies(pieces, me, begin)
    for copy in started:
        copy.wait()
    row = lax.broadcasted_iota(jnp.int32, (PAGE, window), 0)
    column = lax.broadcasted_iota(jnp.int32, (PAGE, window), 1)

    def one_page(page, carry):
        first = first_token[page]
        block = first // rows
        total = None
        for ahead in range(2):
            at = jnp.minimum(block + ahead, blocks - 1)
            inside = first - block * rows
            if ahead == 0:
                start = jnp.minimum(inside // 16 * 16, rows - window)
                offset = inside - start
            else:
                start = 0
                offset = inside - rows
            wanted = (row + offset == column) & (row < amounts[page])
            if ahead == 1:
                wanted = wanted & (block + 1 < blocks)
            chooser = jnp.where(wanted, 1.0, 0.0).astype(jnp.bfloat16)
            found = dot_f32(chooser, rows_buf[at, pl.ds(pl.multiple_of(start, 16), window), :])
            total = found if total is None else total + found
        out[pl.ds(pl.multiple_of(page * PAGE, PAGE), PAGE), :] = total.astype(jnp.bfloat16)
        return carry

    lax.fori_loop(0, out.shape[0] // PAGE, one_page, 0)


def fill_cache(me, first_token, amounts, pieces):
    rows, width = pieces[0].shape[-2:]
    blocks = lax.axis_size("seq")
    pages = first_token.shape[0]
    return pl.pallas_call(
        functools.partial(cache_kernel, len(pieces), 2 * PAGE),
        out_shape=jax.ShapeDtypeStruct((pages * PAGE, width), jnp.bfloat16),
        in_specs=[SMEM] * 3 + [ANY] * len(pieces),
        out_specs=VMEM,
        scratch_shapes=[
            pltpu.VMEM((blocks, rows, width), jnp.bfloat16),
            pltpu.SemaphoreType.DMA((blocks,)),
        ],
        compiler_params=params(24),
        cost_estimate=cost(4 * pages * PAGE * 2 * PAGE * width, 3 << 20),
        name="fill_cache",
    )(me, first_token, amounts, *pieces)


def page_sources(lengths, page_table, me, devices):
    ends = jnp.cumsum(lengths)
    starts = ends - lengths
    counts = (lengths + PAGE - 1) // PAGE
    bases = jnp.cumsum(counts) - counts
    pages = page_table.shape[0] // devices
    mine = me * pages + jnp.arange(pages, dtype=jnp.int32)
    order = jnp.arange(page_table.shape[0], dtype=jnp.int32)
    logical = jnp.sum(jnp.where(page_table[None, :] == mine[:, None], order[None, :], 0), axis=1)
    within = (logical[:, None] >= bases[None, :]) & (logical[:, None] < (bases + counts)[None, :])
    first = starts[None, :] + (logical[:, None] - bases[None, :]) * PAGE
    amount = jnp.minimum(ends[None, :] - first, PAGE)
    return (
        jnp.sum(jnp.where(within, first, 0), axis=1),
        jnp.sum(jnp.where(within, amount, 0), axis=1),
    )


def hidden_kernel(count, on_line, place_ref, *refs):
    pieces = refs[:count]
    tokens, gain, w_out, w_gate, w_up, w_down = refs[count : count + 6]
    if on_line:
        hidden, kept, first_out, second_out = refs[count + 6 : count + 10]
    else:
        hidden, kept = refs[count + 6 : count + 8]
    attended, out_buf, gate_buf, up_buf, down_buf, sems = refs[-6:]
    place = place_ref[0]
    loads = [
        pltpu.make_async_copy(source, target, sems.at[i])
        for i, (source, target) in enumerate(
            [(w_out, out_buf), (w_gate, gate_buf), (w_up, up_buf), (w_down, down_buf)]
        )
    ]
    for load in loads:
        load.start()
    assemble(pieces, place, attended, on_line)
    rows, features = tokens.shape
    width = kept.shape[1]
    step = min(rows, 256)
    gain_row = gain[...].astype(jnp.float32)
    loads[0].wait()
    normed = []
    for first in range(0, rows, step):
        part = pl.ds(first, step)
        projected = dot_f32(attended[part, :], out_buf[...])
        residual = (tokens[part, :].astype(jnp.float32) + projected).astype(jnp.bfloat16)
        tokens_now = residual.astype(jnp.float32)
        normed.append(norm_rows(tokens_now, gain_row))
        gather = residual[:, :width]
        for i in range(1, features // width):
            gather = jnp.where(place == i, residual[:, i * width : (i + 1) * width], gather)
        kept[part, :] = gather
    loads[1].wait()
    loads[2].wait()
    for i, first in enumerate(range(0, rows, step)):
        part = pl.ds(first, step)
        gate = dot_f32(normed[i], gate_buf[...])
        up = dot_f32(normed[i], up_buf[...])
        hidden[part, :] = (jax.nn.silu(gate) * up).astype(jnp.bfloat16)
    loads[3].wait()
    if not on_line:
        return

    def block(index):
        return down_buf[:, pl.ds(pl.multiple_of(index * width, width), width)]

    toward_end = jnp.where(place == 3, 0, jnp.where(place == 0, 3, place))
    first_out[...] = dot_f32(hidden[...], block(toward_end)).astype(jnp.bfloat16)
    second_out[...] = dot_f32(hidden[...], block(lax.rem(place + 2, 4)))


def hidden_of(place, pieces, tokens, gain, w_out, w_gate, w_up, w_down):
    rows, features = tokens.shape
    width = features // lax.axis_size("tp")
    units = w_gate.shape[1]
    on_line = lax.axis_size("tp") == 4
    shapes = [
        jax.ShapeDtypeStruct((rows, units), jnp.bfloat16),
        jax.ShapeDtypeStruct((rows, width), jnp.bfloat16),
    ]
    if on_line:
        shapes += [
            jax.ShapeDtypeStruct((rows, width), jnp.bfloat16),
            jax.ShapeDtypeStruct((rows, width), jnp.float32),
        ]
    return pl.pallas_call(
        functools.partial(hidden_kernel, len(pieces), on_line),
        out_shape=shapes,
        in_specs=[SMEM] + [VMEM] * len(pieces) + [VMEM, VMEM] + [ANY] * 4,
        out_specs=[VMEM] * len(shapes),
        scratch_shapes=[
            pltpu.VMEM((rows, w_out.shape[0]), jnp.bfloat16),
            pltpu.VMEM(w_out.shape, jnp.bfloat16),
            pltpu.VMEM(w_gate.shape, jnp.bfloat16),
            pltpu.VMEM(w_up.shape, jnp.bfloat16),
            pltpu.VMEM(w_down.shape, jnp.bfloat16),
            pltpu.SemaphoreType.DMA((4,)),
        ],
        compiler_params=params(40),
        cost_estimate=cost(6 * rows * features * units, 10 << 20),
        name="hidden",
    )(place, *pieces, tokens, gain, w_out, w_gate, w_up, w_down)


def down_kernel(place_ref, hidden, kept, w_down, to_right, to_left, own):
    place = place_ref[0]
    width = own.shape[1]

    def product(index):
        weights = w_down[:, pl.ds(pl.multiple_of(index * width, width), width)]
        return dot_f32(hidden[...], weights)

    to_right[...] = product(lax.rem(place + 1, 4)).astype(jnp.bfloat16)
    to_left[...] = product(lax.rem(place + 3, 4)).astype(jnp.bfloat16)
    own[...] = product(place) + kept[...].astype(jnp.float32)


def down_blocks(place, hidden, kept, w_down):
    rows, width = kept.shape
    return pl.pallas_call(
        down_kernel,
        out_shape=[
            jax.ShapeDtypeStruct((rows, width), jnp.bfloat16),
            jax.ShapeDtypeStruct((rows, width), jnp.bfloat16),
            jax.ShapeDtypeStruct((rows, width), jnp.float32),
        ],
        in_specs=[SMEM, VMEM, VMEM, VMEM],
        out_specs=[VMEM] * 3,
        compiler_params=params(24),
        cost_estimate=cost(2 * rows * w_down.shape[0] * width * 3, 5 << 20),
        name="down_blocks",
    )(place, hidden, kept, w_down)


def feed_forward(place, pieces, tokens, gain, w_out, w_gate, w_up, w_down):
    outs = hidden_of(place, pieces, tokens, gain, w_out, w_gate, w_up, w_down)
    if lax.axis_size("tp") != 4:
        hidden, kept = outs
        share = lax.psum_scatter(
            dot_f32(hidden, w_down).astype(jnp.bfloat16), "tp", scatter_dimension=1, tiled=True
        )
        return (kept.astype(jnp.float32) + share.astype(jnp.float32)).astype(jnp.bfloat16)
    hidden, kept, toward_end, two_away = outs
    from_end = lax.ppermute(toward_end, "tp", [(3, 2), (0, 1)])
    to_right, to_left, own = down_blocks(place, hidden, kept, w_down)
    from_left = lax.ppermute(to_right, "tp", [(0, 1), (1, 2), (2, 3)])
    from_right = lax.ppermute(to_left, "tp", [(3, 2), (2, 1), (1, 0)])
    joined = (two_away + from_end.astype(jnp.float32)).astype(jnp.bfloat16)
    from_far = lax.ppermute(joined, "tp", [(0, 2), (1, 3), (2, 0), (3, 1)])
    arrived = from_left.astype(jnp.float32) + from_right.astype(jnp.float32)
    return (own + arrived + from_far.astype(jnp.float32)).astype(jnp.bfloat16)


def rope_tables(positions, width):
    half = HD // 2
    frequency = 10000.0 ** (-jnp.arange(half, dtype=jnp.float32) / half)
    angles = positions.astype(jnp.float32)[:, None] * frequency[None, :]
    cosine, sine = jnp.cos(angles), jnp.sin(angles)
    heads = width // HD
    return (
        jnp.concatenate([cosine, cosine] * heads, axis=1),
        jnp.concatenate([-sine, sine] * heads, axis=1),
    )


def segment_of(index, request_ends):
    return jnp.sum((index[:, None] >= request_ends[None, :]).astype(jnp.int32), axis=1)


def per_device(
    tokens,
    variate,
    positions,
    lengths,
    page_table,
    gain_attn,
    w_query,
    w_key,
    w_value,
    var_bias,
    w_out,
    gain_ffn,
    w_gate,
    w_up,
    w_down,
):
    devices = lax.axis_size("seq")
    me = lax.axis_index("seq").astype(jnp.int32)
    place = lax.axis_index("tp").astype(jnp.int32).reshape(1)
    rows = tokens.shape[0]
    width = w_query.shape[1]
    heads = width // HD
    requests = lengths.shape[0]
    reach = devices // 2

    pieces = gather_pieces(tokens)
    all_variates = lax.all_gather(variate, "seq", axis=0, tiled=True)
    slice_rows = w_out.shape[0] // devices
    w_out_slice = lax.dynamic_slice_in_dim(w_out, me * slice_rows, slice_rows, 0)
    w_out_all = lax.all_gather(w_out_slice, ("tp", "seq"), axis=0, tiled=True)

    cosine, sine = rope_tables(positions, width)
    ends = jnp.cumsum(lengths)
    row_first = me * rows
    segment = segment_of(row_first + jnp.arange(rows, dtype=jnp.int32), ends)
    query_marks = bias_marks(variate, segment, var_bias, requests)
    all_index = jnp.arange(rows * devices, dtype=jnp.int32)
    key_marks = key_marks_of(all_variates, segment_of(all_index, ends), requests)
    request_start = jnp.sum(jnp.where(ends <= row_first, lengths, 0))
    info = jnp.stack([me, me - request_start // rows]).astype(jnp.int32)
    first_token, amounts = page_sources(lengths, page_table, me, devices)

    token_rows, queries, pairs = project(
        pieces, place, gain_attn.reshape(1, -1), w_query, w_key, w_value, cosine, sine
    )
    row_pieces = seq_pieces(pairs)
    attended = attend(info, queries, query_marks, key_marks, row_pieces, heads, reach)
    attended_pieces = gather_pieces(attended)
    cache = fill_cache(me.reshape(1), first_token, amounts, row_pieces)
    mixed = feed_forward(
        place,
        attended_pieces,
        token_rows,
        gain_ffn.reshape(1, -1),
        w_out_all,
        w_gate,
        w_up,
        w_down,
    )
    return (mixed, cache.reshape(cache.shape[0], 2, width))


def solution(mesh):
    placed = (
        P("seq", "tp"),
        P("seq"),
        P("seq"),
        P(),
        P(),
        P(),
        P(None, "tp"),
        P(None, "tp"),
        P(None, "tp"),
        P(None, "tp"),
        P("tp", None),
        P(),
        P(None, "tp"),
        P(None, "tp"),
        P("tp", None),
    )
    return jax.shard_map(
        per_device,
        mesh=mesh,
        in_specs=placed,
        out_specs=(P("seq", "tp"), P("seq", None, "tp")),
        check_vma=False,
    )
```

time: 245 us -> 136 us (0.56)
  waiting for transfers between devices: 141 us -> 42.7 us
  matrix products: 29.2 us -> 0 us
  Pallas kernels: 0 us -> 16.2 us
  local copies, waits for them, and re-layouts: 4.37 us -> 15.8 us
  starting transfers between devices: 35.6 us -> 24.5 us
  blocking collectives: 0 us -> 8.91 us
  other arithmetic: 17.4 us -> 10.3 us
  between operations: 14.4 us -> 16.9 us
    reduce_scatter x3 -> x0, waiting for transfers between devices: 88.3 us -> none  [the longest x1 33.6 us: per_device(): lax.psum_scatter(jnp.dot(selector, pair_rows, preferred_element_type=jnp....]
    all_gather x2 -> x1, waiting for transfers between devices: 44.2 us -> 0.01 us  [per_device(): w_out_all = lax.all_gather(w_out_slice, ('tp', 'seq'), axis=0, tiled=True)]
    ppermute x12 -> x19, waiting for transfers between devices: 8.84 us -> 42.7 us  [the longest x2 12 us: line_gather(): ends = lax.ppermute(far, 'tp', [(2, 3), (1, 0)])]
    dot_general x17 -> x0, matrix products: 29.2 us -> none  [the longest x5 6.35 us: attend(): jnp.einsum('qhd,khd->hqk', query_rows, piece_keys.reshape(piece_rows, loc...]
    pallas_call x0 -> x5, Pallas kernels: none -> 16.2 us  [the longest x1 5.63 us: hidden_of(): pl.pallas_call(functools.partial(hidden_kernel, len(pieces), on_line), ou...]
    unnamed x46 -> x86, local copies, waits for them, and re-layouts: 1.29 us -> 13.8 us
    ppermute x12 -> x19, starting transfers between devices: 35.2 us -> 24.5 us  [the longest x2 8.01 us: line_gather(): left = lax.ppermute(shard, 'tp', [(0, 1), (1, 2), (2, 3)])]
    all_gather x0 -> x1, blocking collectives: none -> 8.91 us  [per_device(): all_variates = lax.all_gather(variate, 'seq', axis=0, tiled=True)]
  transfers between devices with their start and end apart: 17 -> 20, of which waited for: 9 -> 9; matrix products, arithmetic and copies ran while one was open for 17% -> 8% of each run, Pallas kernels for 0% -> 8%
where the time goes in v1:
time: 136 us; the launch traced here: 135 us
  waiting for transfers between devices  42.7 us (31%)
  starting transfers between devices  24.5 us (18%)
  between operations  16.9 us (12%)
  Pallas kernels  16.2 us (12%)
  local copies, waits for them, and re-layouts  15.8 us (12%)
  other arithmetic  10.3 us (8%)
  blocking collectives  8.91 us (7%)
    unnamed x86, local copies, waits for them, and re-layouts  13.8 us
    ppermute x2, waiting for transfers between devices, line_gather(): ends = lax.ppermute(far, 'tp', [(2, 3), (1, 0)])  12 us
    ppermute x1, waiting for transfers between devices, feed_forward(): from_far = lax.ppermute(joined, 'tp', [(0, 2), (1, 3), (2, 0), (3, 1)])  11.5 us
    ppermute x7, waiting for transfers between devices, seq_xor(): lax.ppermute(value, 'seq', [(i, i ^ mask) for i in range(lax.axis_size('s...  9.71 us
    all_gather x1, blocking collectives, per_device(): all_variates = lax.all_gather(variate, 'seq', axis=0, tiled=True)  8.91 us
    ppermute x2, starting transfers between devices, line_gather(): left = lax.ppermute(shard, 'tp', [(0, 1), (1, 2), (2, 3)])  8.01 us
    pallas_call x1, Pallas kernels, hidden_of(): pl.pallas_call(functools.partial(hidden_kernel, len(pieces), on_line), ou...  5.63 us
    pallas_call x1, Pallas kernels, attend(): pl.pallas_call(functools.partial(attend_kernel, len(pieces), heads, reach...  4.87 us
  transfers between devices with their start and end apart: 20, of which 9 were waited for; matrix products, arithmetic and copies ran while one was open for 8% of the time, Pallas kernels for 8%

profile of v1, /device:TPU:2, one launch (start us, length us, event | category | flops | bytes accessed | tf_op | source)
XLA Modules:
  0.0 135.4 jit_solution(2484469899693483269)
XLA Ops:
  7.3 2.7 %collective-permute-start.2 = (bf16[512,256]{1,0:T(8,128)(2,1)}, bf16[512,256]{1,0:T(8,128)(2,1)S(1)}, u32[]{:S(2)}, u32[]{:S(2)}) collective-permute-start(bf16[512,256]{1,0:T(8,128)(2,1)} %refs_0_.1), channel_id=1, source_target_pairs={{0,2},{1,3},{2,0},{3,1},{4,6},{5,7},{6,4},{7,5},{8,10},{9,11},{10,... | collective-permute-start | bytes 786440 | tf_op jit(solution)/shard_map/ppermute | solution.py:36
  9.9 3.5 %collective-permute-start = (bf16[512,256]{1,0:T(8,128)(2,1)}, bf16[512,256]{1,0:T(8,128)(2,1)S(1)}, u32[]{:S(2)}, u32[]{:S(2)}) collective-permute-start(bf16[512,256]{1,0:T(8,128)(2,1)} %refs_0_.1), channel_id=1, source_target_pairs={{0,1},{1,2},{2,3},{4,5},{5,6},{6,7},{8,9},{9,10},{10,11},{12,13},{... | collective-permute-start | bytes 786440 | tf_op jit(solution)/shard_map/ppermute | solution.py:37
  13.4 1.3 collective-permute-start.1
  16.0 0.8 reduce-window.16
  17.7 8.9 %all-gather = s32[8,1,512]{2,1,0:T(1,128)S(1)} all-gather(s32[1,1,512]{2,1,0:T(1,128)} %bitcast.17), channel_id=1, replica_groups=mesh['seq'=8,'tp'=4] {'seq'}, dimensions={0}, use_global_device_ids=true | all-gather | bytes 18432 | tf_op jit(solution)/shard_map/all_gather | solution.py:557
  26.6 1.0 fusion.3
  27.6 1.4 %and_convert_fusion.key_marks = bf16[4096,128]{1,0:T(8,128)(2,1)S(1)} fusion(s32[128]{0:T(128)S(1)} %get-tuple-element.39, s32[128]{0:T(128)S(1)} %get-tuple-element.38, s32[4096]{0:T(1024)S(1)} %convert_reduce_fusion, s32[4096]{0:T(1024)S(1)} %bitcast.16, pred[128]{0:T(512)(128)(4,1)S(1)} %get-tuple-element.34, pred[128]{0:T(512)(128)(4,1)S(1)} %iota_compare_fusion.1), kind=kLoop, calls=%fused_computation | loop fusion | flops 2621440 | bytes 1082624 | tf_op jit(solution)/shard_map/convert_element_type | solution.py:294
  29.0 1.8 %bitcast_subtract_fusion.1 = (s32[4]{0:T(128)}, s32[]{:T(128)}, s32[4]{0:T(128)}) fusion(s32[4]{0:T(128)} %param.18, s32[4,1]{0,1:T(1,128)S(1)} %reduce-window.16, s32[]{:T(128)S(6)} %mul.25), kind=kLoop, calls=%fused_computation.49 | loop fusion | flops 79 | bytes 72 | tf_op jit(solution)/shard_map/sub | solution.py:363
  31.3 1.3 collective-permute-start.3
  33.3 0.7 copy-done.26
  34.0 8.2 %collective-permute-done.3.refs_4_ = bf16[512,256]{1,0:T(8,128)(2,1)} collective-permute-done((bf16[512,256]{1,0:T(8,128)(2,1)S(1)}, bf16[512,256]{1,0:T(8,128)(2,1)}, u32[]{:S(2)}, u32[]{:S(2)}) %collective-permute-start.3) | collective-permute-done | bytes 262176 | tf_op jit(solution)/shard_map/ppermute | solution.py:39
  42.2 0.9 copy-done.27
  43.2 2.4 %project.1 = (bf16[512,1024]{1,0:T(8,128)(2,1)S(1)}, bf16[512,128]{1,0:T(8,128)(2,1)S(1)}, bf16[512,256]{1,0:T(8,128)(2,1)S(1)}) custom-call(s32[1]{0:T(128)} %bitcast.place_ref, bf16[512,256]{1,0:T(8,128)(2,1)S(1)} %copy-done.2, bf16[512,256]{1,0:T(8,128)(2,1)S(1)} %copy-done.27, bf16[512,256]{1,0:T(8,128)(2,1)} %collective-permute-done.1.refs_2_, ...), custom_call_target="tpu_custom_call" | custom-call | flops 402653184 | bytes 4194304 | tf_op jit(solution)/shard_map/project/pallas_call | solution.py:109
  45.6 1.0 copy-done.31
  47.4 1.4 %collective-permute-start.7 = (bf16[512,256]{1,0:T(8,128)(2,1)S(1)}, bf16[512,256]{1,0:T(8,128)(2,1)S(1)}, u32[]{:S(2)}, u32[]{:S(2)}) collective-permute-start(bf16[512,256]{1,0:T(8,128)(2,1)S(1)} %get-tuple-element.13.refs_0_), channel_id=1, source_target_pairs={{0,16},{4,20},{8,24},{12,28},{16,0},{20,4},{24,8},{28,12},{1,17},{... | collective-permute-start | bytes 786440 | tf_op jit(solution)/shard_map/ppermute | solution.py:125
  48.9 5.7 %collective-permute-done.5.refs_2_ = bf16[512,256]{1,0:T(8,128)(2,1)S(1)} collective-permute-done((bf16[512,256]{1,0:T(8,128)(2,1)S(1)}, bf16[512,256]{1,0:T(8,128)(2,1)S(1)}, u32[]{:S(2)}, u32[]{:S(2)}) %collective-permute-start.5) | collective-permute-done | bytes 262176 | tf_op jit(solution)/shard_map/ppermute | solution.py:125
  57.4 0.8 compare_select_fusion
  58.8 0.7 copy-done.12
  59.6 4.0 %collective-permute-done.9.refs_6_ = bf16[512,256]{1,0:T(8,128)(2,1)S(1)} collective-permute-done((bf16[512,256]{1,0:T(8,128)(2,1)S(1)}, bf16[512,256]{1,0:T(8,128)(2,1)S(1)}, u32[]{:S(2)}, u32[]{:S(2)}) %collective-permute-start.9) | collective-permute-done | bytes 262176 | tf_op jit(solution)/shard_map/ppermute | solution.py:125
  63.5 0.7 copy-done.15
  64.3 0.9 fusion.2.query_marks
  65.4 1.1 copy-done.7
  66.5 1.0 copy-done.10
  67.5 0.9 copy-done.13
  68.4 0.9 copy-done.16
  69.4 4.9 %attend.1.refs_0_ = bf16[512,128]{1,0:T(8,128)(2,1)} custom-call(s32[2]{0:T(128)S(1)} %pad_add_fusion.info, bf16[512,128]{1,0:T(8,128)(2,1)S(1)} %get-tuple-element.12.queries, bf16[2,512,128]{2,1,0:T(8,128)(2,1)S(1)} %fusion.2.query_marks, bf16[4096,128]{1,0:T(8,128)(2,1)S(1)} %and_convert_fusion.key_marks, bf16[512,256]{1,0:T(8,128)(2,1)S(1)} %copy-done.7, ...), custom_call_target="tpu_custom_call" | custom-call | flops 2684354560 | bytes 4194304 | tf_op jit(solution)/shard_map/attend/pallas_call | solution.py:251
  74.4 4.5 %collective-permute-start.11 = (bf16[512,128]{1,0:T(8,128)(2,1)}, bf16[512,128]{1,0:T(8,128)(2,1)S(1)}, u32[]{:S(2)}, u32[]{:S(2)}) collective-permute-start(bf16[512,128]{1,0:T(8,128)(2,1)} %attend.1.refs_0_), channel_id=1, source_target_pairs={{0,1},{1,2},{2,3},{4,5},{5,6},{6,7},{8,9},{9,10},{10,11},{12,13},{... | collective-permute-start | bytes 393224 | tf_op jit(solution)/shard_map/ppermute | solution.py:37
  78.9 1.3 collective-permute-start.12
  80.2 3.6 %collective-permute-done.13.refs_3_ = bf16[512,128]{1,0:T(8,128)(2,1)S(1)} collective-permute-done((bf16[512,128]{1,0:T(8,128)(2,1)}, bf16[512,128]{1,0:T(8,128)(2,1)S(1)}, u32[]{:S(2)}, u32[]{:S(2)}) %collective-permute-start.13) | collective-permute-done | bytes 131104 | tf_op jit(solution)/shard_map/ppermute | solution.py:36
  83.8 1.3 collective-permute-start.14
  85.3 2.1 %collective-permute-done.12.refs_2_ = bf16[512,128]{1,0:T(8,128)(2,1)S(1)} collective-permute-done((bf16[512,128]{1,0:T(8,128)(2,1)}, bf16[512,128]{1,0:T(8,128)(2,1)S(1)}, u32[]{:S(2)}, u32[]{:S(2)}) %collective-permute-start.12) | collective-permute-done | bytes 131104 | tf_op jit(solution)/shard_map/ppermute | solution.py:38
  87.4 3.8 %collective-permute-done.14.refs_4_ = bf16[512,128]{1,0:T(8,128)(2,1)S(1)} collective-permute-done((bf16[512,128]{1,0:T(8,128)(2,1)S(1)}, bf16[512,128]{1,0:T(8,128)(2,1)S(1)}, u32[]{:S(2)}, u32[]{:S(2)}) %collective-permute-start.14) | collective-permute-done | bytes 131104 | tf_op jit(solution)/shard_map/ppermute | solution.py:39
  91.2 1.6 %copy-done.28 = bf16[1024,1024]{1,0:T(8,128)(2,1)S(1)} copy-done((bf16[1024,1024]{1,0:T(8,128)(2,1)S(1)}, bf16[1024,1024]{1,0:T(8,128)(2,1)}, u32[]{:S(2)}) %copy-start.28) | copy-done | bytes 2097176
  92.8 1.6 %copy-done.29 = bf16[1024,1024]{1,0:T(8,128)(2,1)S(1)} copy-done((bf16[1024,1024]{1,0:T(8,128)(2,1)S(1)}, bf16[1024,1024]{1,0:T(8,128)(2,1)}, u32[]{:S(2)}) %copy-start.29) | copy-done | bytes 2097176
  94.4 1.2 copy-done.30
  95.6 1.2 copy-done.32
  96.8 5.6 %hidden.1 = (bf16[512,1024]{1,0:T(8,128)(2,1)S(1)}, bf16[512,256]{1,0:T(8,128)(2,1)S(1)}, bf16[512,256]{1,0:T(8,128)(2,1)S(1)}, f32[512,256]{1,0:T(8,128)S(1)}) custom-call(s32[1]{0:T(128)} %bitcast.place_ref, bf16[512,128]{1,0:T(8,128)(2,1)} %attend.1.refs_0_, bf16[512,128]{1,0:T(8,128)(2,1)S(1)} %collective-permute-done.11.refs_1_, ...), custom_call_target="tpu_custom_call" | custom-call | flops 3221225472 | bytes 10485760 | tf_op jit(solution)/shard_map/hidden/pallas_call | solution.py:446
  102.5 1.5 %collective-permute-start.17 = (bf16[512,256]{1,0:T(8,128)(2,1)S(1)}, bf16[512,256]{1,0:T(8,128)(2,1)S(1)}, u32[]{:S(2)}, u32[]{:S(2)}) collective-permute-start(bf16[512,256]{1,0:T(8,128)(2,1)S(1)} %get-tuple-element.21), channel_id=1, source_target_pairs={{3,2},{0,1},{7,6},{4,5},{11,10},{8,9},{15,14},{12,13},{19,18},{16,... | collective-permute-start | bytes 786440 | tf_op jit(solution)/shard_map/ppermute | solution.py:504
  104.1 1.0 down_blocks.1
  105.1 1.3 collective-permute-start.15
  106.4 1.3 collective-permute-start.16
  107.7 3.0 %collective-permute-done.17 = bf16[512,256]{1,0:T(8,128)(2,1)S(1)} collective-permute-done((bf16[512,256]{1,0:T(8,128)(2,1)S(1)}, bf16[512,256]{1,0:T(8,128)(2,1)S(1)}, u32[]{:S(2)}, u32[]{:S(2)}) %collective-permute-start.17) | collective-permute-done | bytes 262176 | tf_op jit(solution)/shard_map/ppermute | solution.py:504
  110.7 1.2 collective-permute-start.18
  112.3 2.3 %fill_cache.1 = bf16[576,256]{1,0:T(8,128)(2,1)S(1)} custom-call(s32[1]{0:T(128)} %bitcast.1.me_ref, s32[9]{0:T(128)S(1)} %get-tuple-element.23.first_token, s32[9]{0:T(128)S(1)} %get-tuple-element.22.amounts, bf16[512,256]{1,0:T(8,128)(2,1)S(1)} %copy-done.8, bf16[512,256]{1,0:T(8,128)(2,1)S(1)} %copy-done.19, bf16[512,256]{1,0:T(8,128)(2,1)S(1)} %copy-done.11, ...), custom_call_target="tpu_custom_call" | custom-call | flops 75497472 | bytes 3145728 | tf_op jit(solution)/shard_map/fill_cache/pallas_call | solution.py:346
  114.6 0.8 reshape.227
  115.4 0.9 collective-permute-done.15
  116.3 11.5 %collective-permute-done.18 = bf16[512,256]{1,0:T(8,128)(2,1)S(1)} collective-permute-done((bf16[512,256]{1,0:T(8,128)(2,1)S(1)}, bf16[512,256]{1,0:T(8,128)(2,1)S(1)}, u32[]{:S(2)}, u32[]{:S(2)}) %collective-permute-start.18) | collective-permute-done | bytes 262176 | tf_op jit(solution)/shard_map/ppermute | solution.py:509
  127.7 0.8 add_convert_fusion
  (115 shorter events, 6.2 us)
Async XLA Ops:
  7.2 35.0 %copy-start.2 = (bf16[512,256]{1,0:T(8,128)(2,1)S(1)}, bf16[512,256]{1,0:T(8,128)(2,1)}, u32[]{:S(2)}) copy-start(bf16[512,256]{1,0:T(8,128)(2,1)} %refs_0_.1) | copy-start | bytes 786436
  7.2 25.5 %copy-start.37 = (bf16[1024]{0:T(1024)(128)(2,1)S(1)}, bf16[1024]{0:T(1024)(128)(2,1)}, u32[]{:S(2)}) copy-start(bf16[1024]{0:T(1024)(128)(2,1)} %param.20) | copy-start | bytes 6148
  7.2 25.5 %copy-start.40 = (f32[2,2]{1,0:T(2,128)S(1)}, f32[2,2]{1,0:T(2,128)}, u32[]{:S(2)}) copy-start(f32[2,2]{1,0:T(2,128)} %param.24) | copy-start | bytes 52
  7.2 35.0 %copy-start.3 = (bf16[1024,128]{1,0:T(8,128)(2,1)S(1)}, bf16[1024,128]{1,0:T(8,128)(2,1)}, u32[]{:S(2)}) copy-start(bf16[1024,128]{1,0:T(8,128)(2,1)} %refs_6_.1) | copy-start | bytes 786436
  7.2 35.0 %copy-start.4 = (bf16[1024,128]{1,0:T(8,128)(2,1)S(1)}, bf16[1024,128]{1,0:T(8,128)(2,1)}, u32[]{:S(2)}) copy-start(bf16[1024,128]{1,0:T(8,128)(2,1)} %refs_7_.1) | copy-start | bytes 786436
  7.2 35.0 %copy-start.5 = (bf16[1024,128]{1,0:T(8,128)(2,1)S(1)}, bf16[1024,128]{1,0:T(8,128)(2,1)}, u32[]{:S(2)}) copy-start(bf16[1024,128]{1,0:T(8,128)(2,1)} %refs_8_.2) | copy-start | bytes 786436
  7.2 83.9 %all-gather.3.cloned.1.call-start = ((), (), s32[]{:S(2)}) async-start(), calls=%async_computation | async-start | bytes 1081344 | tf_op jit(solution)/shard_map/all_gather | solution.py:560
  7.3 24.0 %collective-permute-start.2 = (bf16[512,256]{1,0:T(8,128)(2,1)}, bf16[512,256]{1,0:T(8,128)(2,1)S(1)}, u32[]{:S(2)}, u32[]{:S(2)}) collective-permute-start(bf16[512,256]{1,0:T(8,128)(2,1)} %refs_0_.1), channel_id=1, source_target_pairs={{0,2},{1,3},{2,0},{3,1},{4,6},{5,7},{6,4},{7,5},{8,10},{9,11},{10,... | collective-permute-start | bytes 786440 | tf_op jit(solution)/shard_map/ppermute | solution.py:36
  9.9 23.3 %collective-permute-start = (bf16[512,256]{1,0:T(8,128)(2,1)}, bf16[512,256]{1,0:T(8,128)(2,1)S(1)}, u32[]{:S(2)}, u32[]{:S(2)}) collective-permute-start(bf16[512,256]{1,0:T(8,128)(2,1)} %refs_0_.1), channel_id=1, source_target_pairs={{0,1},{1,2},{2,3},{4,5},{5,6},{6,7},{8,9},{9,10},{10,11},{12,13},{... | collective-permute-start | bytes 786440 | tf_op jit(solution)/shard_map/ppermute | solution.py:37
  13.4 20.6 %collective-permute-start.1 = (bf16[512,256]{1,0:T(8,128)(2,1)}, bf16[512,256]{1,0:T(8,128)(2,1)}, u32[]{:S(2)}, u32[]{:S(2)}) collective-permute-start(bf16[512,256]{1,0:T(8,128)(2,1)} %refs_0_.1), channel_id=1, source_target_pairs={{3,2},{2,1},{1,0},{7,6},{6,5},{5,4},{11,10},{10,9},{9,8},{15,14},{... | collective-permute-start | bytes 786440 | tf_op jit(solution)/shard_map/ppermute | solution.py:38
  15.4 15.9 %copy-start.34 = (s32[128]{0:T(128)}, s32[128]{0:T(128)S(1)}, u32[]{:S(2)}) copy-start(s32[128]{0:T(128)S(1)} %get-tuple-element.39) | copy-start | bytes 1540
  15.4 26.7 %copy-start.35 = (s32[128]{0:T(128)}, s32[128]{0:T(128)S(1)}, u32[]{:S(2)}) copy-start(s32[128]{0:T(128)S(1)} %get-tuple-element.38) | copy-start | bytes 1540
  29.0 18.3 %copy-start.33 = (s32[512]{0:T(512)S(1)}, s32[512]{0:T(512)}, u32[]{:S(2)}) copy-start(s32[512]{0:T(512)} %param.16) | copy-start | bytes 6148
  31.3 10.8 %collective-permute-start.3 = (bf16[512,256]{1,0:T(8,128)(2,1)S(1)}, bf16[512,256]{1,0:T(8,128)(2,1)}, u32[]{:S(2)}, u32[]{:S(2)}) collective-permute-start(bf16[512,256]{1,0:T(8,128)(2,1)S(1)} %collective-permute-done.2.refs_3_), channel_id=1, source_target_pairs={{2,3},{1,0},{6,7},{5,4},{10,11},{9,8},{14,15},{13,12},{18,19},{17,... | collective-permute-start | bytes 786440 | tf_op jit(solution)/shard_map/ppermute | solution.py:39
  46.5 18.8 %copy-start.6 = (bf16[512,256]{1,0:T(8,128)(2,1)}, bf16[512,256]{1,0:T(8,128)(2,1)S(1)}, u32[]{:S(2)}) copy-start(bf16[512,256]{1,0:T(8,128)(2,1)S(1)} %get-tuple-element.13.refs_0_) | copy-start | bytes 786436
  46.5 8.1 %collective-permute-start.5 = (bf16[512,256]{1,0:T(8,128)(2,1)S(1)}, bf16[512,256]{1,0:T(8,128)(2,1)S(1)}, u32[]{:S(2)}, u32[]{:S(2)}) collective-permute-start(bf16[512,256]{1,0:T(8,128)(2,1)S(1)} %get-tuple-element.13.refs_0_), channel_id=1, source_target_pairs={{0,8},{4,12},{8,0},{12,4},{16,24},{20,28},{24,16},{28,20},{1,9},{5... | collective-permute-start | bytes 786440 | tf_op jit(solution)/shard_map/ppermute | solution.py:125
  47.4 11.3 %collective-permute-start.7 = (bf16[512,256]{1,0:T(8,128)(2,1)S(1)}, bf16[512,256]{1,0:T(8,128)(2,1)S(1)}, u32[]{:S(2)}, u32[]{:S(2)}) collective-permute-start(bf16[512,256]{1,0:T(8,128)(2,1)S(1)} %get-tuple-element.13.refs_0_), channel_id=1, source_target_pairs={{0,16},{4,20},{8,24},{12,28},{16,0},{20,4},{24,8},{28,12},{1,17},{... | collective-permute-start | bytes 786440 | tf_op jit(solution)/shard_map/ppermute | solution.py:125
  54.6 10.8 %copy-start.9 = (bf16[512,256]{1,0:T(8,128)(2,1)}, bf16[512,256]{1,0:T(8,128)(2,1)S(1)}, u32[]{:S(2)}) copy-start(bf16[512,256]{1,0:T(8,128)(2,1)S(1)} %collective-permute-done.5.refs_2_) | copy-start | bytes 786436
  54.6 8.9 %collective-permute-start.9 = (bf16[512,256]{1,0:T(8,128)(2,1)S(1)}, bf16[512,256]{1,0:T(8,128)(2,1)S(1)}, u32[]{:S(2)}, u32[]{:S(2)}) collective-permute-start(bf16[512,256]{1,0:T(8,128)(2,1)S(1)} %collective-permute-done.5.refs_2_), channel_id=1, source_target_pairs={{0,16},{4,20},{8,24},{12,28},{16,0},{20,4},{24,8},{28,12},{1,17},{... | collective-permute-start | bytes 786440 | tf_op jit(solution)/shard_map/ppermute | solution.py:125
  58.2 7.1 %collective-permute-start.4 = (bf16[512,256]{1,0:T(8,128)(2,1)S(1)}, bf16[512,256]{1,0:T(8,128)(2,1)S(1)}, u32[]{:S(2)}, u32[]{:S(2)}) collective-permute-start(bf16[512,256]{1,0:T(8,128)(2,1)S(1)} %get-tuple-element.13.refs_0_), channel_id=1, source_target_pairs={{0,4},{4,0},{8,12},{12,8},{16,20},{20,16},{24,28},{28,24},{1,5},{5... | collective-permute-start | bytes 786440 | tf_op jit(solution)/shard_map/ppermute | solution.py:125
  58.3 7.0 %collective-permute-start.6 = (bf16[512,256]{1,0:T(8,128)(2,1)S(1)}, bf16[512,256]{1,0:T(8,128)(2,1)S(1)}, u32[]{:S(2)}, u32[]{:S(2)}) collective-permute-start(bf16[512,256]{1,0:T(8,128)(2,1)S(1)} %collective-permute-done.5.refs_2_), channel_id=1, source_target_pairs={{0,4},{4,0},{8,12},{12,8},{16,20},{20,16},{24,28},{28,24},{1,5},{5... | collective-permute-start | bytes 786440 | tf_op jit(solution)/shard_map/ppermute | solution.py:125
  58.8 6.6 %collective-permute-start.8 = (bf16[512,256]{1,0:T(8,128)(2,1)S(1)}, bf16[512,256]{1,0:T(8,128)(2,1)S(1)}, u32[]{:S(2)}, u32[]{:S(2)}) collective-permute-start(bf16[512,256]{1,0:T(8,128)(2,1)S(1)} %collective-permute-done.7.refs_4_), channel_id=1, source_target_pairs={{0,4},{4,0},{8,12},{12,8},{16,20},{20,16},{24,28},{28,24},{1,5},{5... | collective-permute-start | bytes 786440 | tf_op jit(solution)/shard_map/ppermute | solution.py:125
  63.5 1.8 %collective-permute-start.10 = (bf16[512,256]{1,0:T(8,128)(2,1)S(1)}, bf16[512,256]{1,0:T(8,128)(2,1)S(1)}, u32[]{:S(2)}, u32[]{:S(2)}) collective-permute-start(bf16[512,256]{1,0:T(8,128)(2,1)S(1)} %collective-permute-done.9.refs_6_), channel_id=1, source_target_pairs={{0,4},{4,0},{8,12},{12,8},{16,20},{20,16},{24,28},{28,24},{1,5},{5... | collective-permute-start | bytes 786440 | tf_op jit(solution)/shard_map/ppermute | solution.py:125
  65.3 9.0 %copy-start.18 = (bf16[512,256]{1,0:T(8,128)(2,1)}, bf16[512,256]{1,0:T(8,128)(2,1)S(1)}, u32[]{:S(2)}) copy-start(bf16[512,256]{1,0:T(8,128)(2,1)S(1)} %collective-permute-done.4.refs_1_) | copy-start | bytes 786436
  65.3 9.0 %copy-start.20 = (bf16[512,256]{1,0:T(8,128)(2,1)}, bf16[512,256]{1,0:T(8,128)(2,1)S(1)}, u32[]{:S(2)}) copy-start(bf16[512,256]{1,0:T(8,128)(2,1)S(1)} %collective-permute-done.6.refs_3_) | copy-start | bytes 786436
  65.3 9.0 %copy-start.22 = (bf16[512,256]{1,0:T(8,128)(2,1)}, bf16[512,256]{1,0:T(8,128)(2,1)S(1)}, u32[]{:S(2)}) copy-start(bf16[512,256]{1,0:T(8,128)(2,1)S(1)} %collective-permute-done.8.refs_5_) | copy-start | bytes 786436
  65.4 8.9 %copy-start.24 = (bf16[512,256]{1,0:T(8,128)(2,1)}, bf16[512,256]{1,0:T(8,128)(2,1)S(1)}, u32[]{:S(2)}) copy-start(bf16[512,256]{1,0:T(8,128)(2,1)S(1)} %collective-permute-done.10.refs_7_) | copy-start | bytes 786436
  69.4 15.7 %copy-start.41 = (s32[4]{0:T(128)S(1)}, s32[4]{0:T(128)}, u32[]{:S(2)}) copy-start(s32[4]{0:T(128)} %get-tuple-element.31) | copy-start | bytes 52
  69.4 15.9 %copy-start.38 = (bf16[1024]{0:T(1024)(128)(2,1)S(1)}, bf16[1024]{0:T(1024)(128)(2,1)}, u32[]{:S(2)}) copy-start(bf16[1024]{0:T(1024)(128)(2,1)} %param.26) | copy-start | bytes 6148
  69.4 21.8 %copy-start.1 = (bf16[1024,1024]{1,0:T(8,128)(2,1)S(1)}, bf16[1024,1024]{1,0:T(8,128)(2,1)}, u32[]{:S(2)}) copy-start(bf16[1024,1024]{1,0:T(8,128)(2,1)} %w_down.1) | copy-start | bytes 6291460
  74.3 9.5 %collective-permute-start.13 = (bf16[512,128]{1,0:T(8,128)(2,1)}, bf16[512,128]{1,0:T(8,128)(2,1)S(1)}, u32[]{:S(2)}, u32[]{:S(2)}) collective-permute-start(bf16[512,128]{1,0:T(8,128)(2,1)} %attend.1.refs_0_), channel_id=1, source_target_pairs={{0,2},{1,3},{2,0},{3,1},{4,6},{5,7},{6,4},{7,5},{8,10},{9,11},{10,... | collective-permute-start | bytes 393224 | tf_op jit(solution)/shard_map/ppermute | solution.py:36
  74.4 10.9 %collective-permute-start.11 = (bf16[512,128]{1,0:T(8,128)(2,1)}, bf16[512,128]{1,0:T(8,128)(2,1)S(1)}, u32[]{:S(2)}, u32[]{:S(2)}) collective-permute-start(bf16[512,128]{1,0:T(8,128)(2,1)} %attend.1.refs_0_), channel_id=1, source_target_pairs={{0,1},{1,2},{2,3},{4,5},{5,6},{6,7},{8,9},{9,10},{10,11},{12,13},{... | collective-permute-start | bytes 393224 | tf_op jit(solution)/shard_map/ppermute | solution.py:37
  78.9 8.4 %collective-permute-start.12 = (bf16[512,128]{1,0:T(8,128)(2,1)}, bf16[512,128]{1,0:T(8,128)(2,1)S(1)}, u32[]{:S(2)}, u32[]{:S(2)}) collective-permute-start(bf16[512,128]{1,0:T(8,128)(2,1)} %attend.1.refs_0_), channel_id=1, source_target_pairs={{3,2},{2,1},{1,0},{7,6},{6,5},{5,4},{11,10},{10,9},{9,8},{15,14},{... | collective-permute-start | bytes 393224 | tf_op jit(solution)/shard_map/ppermute | solution.py:38
  83.8 7.4 %collective-permute-start.14 = (bf16[512,128]{1,0:T(8,128)(2,1)S(1)}, bf16[512,128]{1,0:T(8,128)(2,1)S(1)}, u32[]{:S(2)}, u32[]{:S(2)}) collective-permute-start(bf16[512,128]{1,0:T(8,128)(2,1)S(1)} %collective-permute-done.13.refs_3_), channel_id=1, source_target_pairs={{2,3},{1,0},{6,7},{5,4},{10,11},{9,8},{14,15},{13,12},{18,19},{17,... | collective-permute-start | bytes 393224 | tf_op jit(solution)/shard_map/ppermute | solution.py:39
  102.5 8.2 %collective-permute-start.17 = (bf16[512,256]{1,0:T(8,128)(2,1)S(1)}, bf16[512,256]{1,0:T(8,128)(2,1)S(1)}, u32[]{:S(2)}, u32[]{:S(2)}) collective-permute-start(bf16[512,256]{1,0:T(8,128)(2,1)S(1)} %get-tuple-element.21), channel_id=1, source_target_pairs={{3,2},{0,1},{7,6},{4,5},{11,10},{8,9},{15,14},{12,13},{19,18},{16,... | collective-permute-start | bytes 786440 | tf_op jit(solution)/shard_map/ppermute | solution.py:504
  103.9 8.0 %copy-start.42 = (s32[72]{0:T(128)S(1)}, s32[72]{0:T(128)}, u32[]{:S(2)}) copy-start(s32[72]{0:T(128)} %param.19) | copy-start | bytes 868
  104.0 8.2 %copy-start.39 = (s32[4]{0:T(128)S(1)}, s32[4]{0:T(128)}, u32[]{:S(2)}) copy-start(s32[4]{0:T(128)} %get-tuple-element.27) | copy-start | bytes 52
  104.0 8.2 %copy-start.8 = (bf16[512,256]{1,0:T(8,128)(2,1)S(1)}, bf16[512,256]{1,0:T(8,128)(2,1)}, u32[]{:S(2)}) copy-start(bf16[512,256]{1,0:T(8,128)(2,1)} %copy-done.6) | copy-start | bytes 786436
  104.0 8.2 %copy-start.11 = (bf16[512,256]{1,0:T(8,128)(2,1)S(1)}, bf16[512,256]{1,0:T(8,128)(2,1)}, u32[]{:S(2)}) copy-start(bf16[512,256]{1,0:T(8,128)(2,1)} %copy-done.9) | copy-start | bytes 786436
  104.0 8.2 %copy-start.14 = (bf16[512,256]{1,0:T(8,128)(2,1)S(1)}, bf16[512,256]{1,0:T(8,128)(2,1)}, u32[]{:S(2)}) copy-start(bf16[512,256]{1,0:T(8,128)(2,1)} %copy-done.12) | copy-start | bytes 786436
  104.0 8.2 %copy-start.17 = (bf16[512,256]{1,0:T(8,128)(2,1)S(1)}, bf16[512,256]{1,0:T(8,128)(2,1)}, u32[]{:S(2)}) copy-start(bf16[512,256]{1,0:T(8,128)(2,1)} %copy-done.15) | copy-start | bytes 786436
  104.0 8.2 %copy-start.19 = (bf16[512,256]{1,0:T(8,128)(2,1)S(1)}, bf16[512,256]{1,0:T(8,128)(2,1)}, u32[]{:S(2)}) copy-start(bf16[512,256]{1,0:T(8,128)(2,1)} %copy-done.18) | copy-start | bytes 786436
  104.0 8.2 %copy-start.21 = (bf16[512,256]{1,0:T(8,128)(2,1)S(1)}, bf16[512,256]{1,0:T(8,128)(2,1)}, u32[]{:S(2)}) copy-start(bf16[512,256]{1,0:T(8,128)(2,1)} %copy-done.20) | copy-start | bytes 786436
  104.0 8.2 %copy-start.23 = (bf16[512,256]{1,0:T(8,128)(2,1)S(1)}, bf16[512,256]{1,0:T(8,128)(2,1)}, u32[]{:S(2)}) copy-start(bf16[512,256]{1,0:T(8,128)(2,1)} %copy-done.22) | copy-start | bytes 786436
  104.0 8.2 %copy-start.25 = (bf16[512,256]{1,0:T(8,128)(2,1)S(1)}, bf16[512,256]{1,0:T(8,128)(2,1)}, u32[]{:S(2)}) copy-start(bf16[512,256]{1,0:T(8,128)(2,1)} %copy-done.24) | copy-start | bytes 786436
  105.1 11.2 %collective-permute-start.15 = (bf16[512,256]{1,0:T(8,128)(2,1)S(1)}, bf16[512,256]{1,0:T(8,128)(2,1)S(1)}, u32[]{:S(2)}, u32[]{:S(2)}) collective-permute-start(bf16[512,256]{1,0:T(8,128)(2,1)S(1)} %get-tuple-element.18), channel_id=1, source_target_pairs={{0,1},{1,2},{2,3},{4,5},{5,6},{6,7},{8,9},{9,10},{10,11},{12,13},{... | collective-permute-start | bytes 786440 | tf_op jit(solution)/shard_map/ppermute | solution.py:506
  106.4 9.9 %collective-permute-start.16 = (bf16[512,256]{1,0:T(8,128)(2,1)S(1)}, bf16[512,256]{1,0:T(8,128)(2,1)S(1)}, u32[]{:S(2)}, u32[]{:S(2)}) collective-permute-start(bf16[512,256]{1,0:T(8,128)(2,1)S(1)} %get-tuple-element.19), channel_id=1, source_target_pairs={{3,2},{2,1},{1,0},{7,6},{6,5},{5,4},{11,10},{10,9},{9,8},{15,14},{... | collective-permute-start | bytes 786440 | tf_op jit(solution)/shard_map/ppermute | solution.py:507
  110.7 17.0 %collective-permute-start.18 = (bf16[512,256]{1,0:T(8,128)(2,1)S(1)}, bf16[512,256]{1,0:T(8,128)(2,1)S(1)}, u32[]{:S(2)}, u32[]{:S(2)}) collective-permute-start(bf16[512,256]{1,0:T(8,128)(2,1)S(1)} %add_convert_fusion.1), channel_id=1, source_target_pairs={{0,2},{1,3},{2,0},{3,1},{4,6},{5,7},{6,4},{7,5},{8,10},{9,11},{10,... | collective-permute-start | bytes 786440 | tf_op jit(solution)/shard_map/ppermute | solution.py:509
  (15 other events, 25.4 us)
Sparse Core Ops, SparseCore 0:
  15.5 54.7 all-gather.2

commit v2 on v1

--- a/solution.py
+++ b/solution.py
@@ -40,26 +40,31 @@
     return [shard, left, right, far, ends]
 
 
+def turn_gather(shard):
+    count = lax.axis_size("tp")
+    turns = [2, 1, 3] if count == 4 else list(range(1, count))
+    moved = {
+        turn: lax.ppermute(shard, "tp", [(i, (i + turn) % count) for i in range(count)])
+        for turn in turns
+    }
+    return [shard] + [moved[turn] for turn in range(1, count)]
+
+
 def gather_pieces(shard):
     if lax.axis_size("tp") == 4:
         return line_gather(shard)
-    whole = lax.all_gather(shard, "tp", axis=0)
-    return [whole[i] for i in range(whole.shape[0])]
-
-
-def piece_count():
-    return 5 if lax.axis_size("tp") == 4 else lax.axis_size("tp")
-
-
-def assemble(pieces, place, target, on_line):
+    return turn_gather(shard)
+
+
+def assemble(pieces, place, count, target):
     width = pieces[0].shape[1]
 
     def put(block, value):
         target[:, pl.ds(pl.multiple_of(block * width, width), width)] = value
 
-    if not on_line:
-        for i, piece in enumerate(pieces):
-            target[:, i * width : (i + 1) * width] = piece[...]
+    if len(pieces) == count:
+        for turn, piece in enumerate(pieces):
+            put(lax.rem(place + count - turn, count), piece[...])
         return
     own, left, right, far, ends = pieces
     put(place, own[...])
@@ -82,10 +87,10 @@
     return (values * scale * gain).astype(jnp.bfloat16)
 
 
-def project_kernel(count, on_line, place_ref, *refs):
+def project_kernel(places, count, place_ref, *refs):
     pieces = refs[:count]
     gain, w_q, w_k, w_v, cosine, sine, tokens, queries, pairs = refs[count:]
-    assemble(pieces, place_ref[0], tokens, on_line)
+    assemble(pieces, place_ref[0], places, tokens)
     rows = tokens.shape[0]
     width = w_q.shape[1]
     step = min(rows, 256)
@@ -105,9 +110,8 @@
     rows, part = pieces[0].shape
     width = w_query.shape[1]
     features = w_query.shape[0]
-    on_line = lax.axis_size("tp") == 4
     return pl.pallas_call(
-        functools.partial(project_kernel, len(pieces), on_line),
+        functools.partial(project_kernel, lax.axis_size("tp"), len(pieces)),
         out_shape=[
             jax.ShapeDtypeStruct((rows, features), jnp.bfloat16),
             jax.ShapeDtypeStruct((rows, width), jnp.bfloat16),
@@ -115,7 +119,7 @@
         ],
         in_specs=[SMEM] + [VMEM] * (len(pieces) + 6),
         out_specs=[VMEM] * 3,
-        compiler_params=params(24),
+        compiler_params=params(12),
         cost_estimate=cost(6 * rows * features * width, 4 << 20),
         name="project",
     )(place, *pieces, gain, w_query, w_key, w_value, cosine, sine)
@@ -262,7 +266,7 @@
             pltpu.VMEM((heads, rows, width + LANES), jnp.float32),
             pltpu.SemaphoreType.DMA((slots, 3)),
         ],
-        compiler_params=params(48),
+        compiler_params=params(12 + 2 * slots),
         cost_estimate=cost(
             4 * heads * rows * rows * slots * 256, 4 << 20, heads * rows * rows * slots
         ),
@@ -272,17 +276,18 @@
 
 def bias_marks(variate, segment, var_bias, requests):
     lane = jnp.arange(LANES, dtype=jnp.int32)
-    chosen = variate[None, :, None] == (lane % VARS)[None, None, :]
-    bias = jnp.where(chosen, var_bias[0][:, None, None], var_bias[1][:, None, None])
-    high = lax.reduce_precision(bias, 8, 7)
-    middle = lax.reduce_precision(bias - high, 8, 7)
-    low = bias - high - middle
-    part = (lane // VARS)[None, None, :]
-    marks = jnp.where(part == 0, high, jnp.where(part == 1, middle, low))
-    other = segment[None, :, None] != (lane - BIAS_PARTS * VARS)[None, None, :]
-    marks = jnp.where(part < BIAS_PARTS, marks, jnp.where(other, HIDDEN_SCORE, 0.0))
-    used = lane < BIAS_PARTS * VARS + requests
-    return jnp.where(used[None, None, :], marks, 0.0).astype(jnp.bfloat16)
+    high = lax.reduce_precision(var_bias, 8, 7)
+    middle = lax.reduce_precision(var_bias - high, 8, 7)
+    parts = jnp.stack([high, middle, var_bias - high - middle], axis=2)
+    by_lane = jnp.repeat(parts, VARS, axis=2)
+    by_lane = jnp.pad(by_lane, ((0, 0), (0, 0), (0, LANES - by_lane.shape[2])))
+    by_lane = by_lane.astype(jnp.bfloat16)
+    same = variate[None, :, None] == (lane % VARS)[None, None, :]
+    marks = jnp.where(same, by_lane[0][:, None, :], by_lane[1][:, None, :])
+    request = lane - BIAS_PARTS * VARS
+    other = segment[None, :, None] != request[None, None, :]
+    hidden = other & ((request >= 0) & (request < requests))[None, None, :]
+    return jnp.where(hidden, jnp.bfloat16(HIDDEN_SCORE), marks)
 
 
 def key_marks_of(variate, segment, requests):
@@ -352,17 +357,22 @@
             pltpu.VMEM((blocks, rows, width), jnp.bfloat16),
             pltpu.SemaphoreType.DMA((blocks,)),
         ],
-        compiler_params=params(24),
+        compiler_params=params(8),
         cost_estimate=cost(4 * pages * PAGE * 2 * PAGE * width, 3 << 20),
         name="fill_cache",
     )(me, first_token, amounts, *pieces)
 
 
+def running_sum(values):
+    at = jnp.arange(values.shape[0], dtype=jnp.int32)
+    return jnp.sum(jnp.where(at[None, :] <= at[:, None], values[None, :], 0), axis=1)
+
+
 def page_sources(lengths, page_table, me, devices):
-    ends = jnp.cumsum(lengths)
+    ends = running_sum(lengths)
     starts = ends - lengths
     counts = (lengths + PAGE - 1) // PAGE
-    bases = jnp.cumsum(counts) - counts
+    bases = running_sum(counts) - counts
     pages = page_table.shape[0] // devices
     mine = me * pages + jnp.arange(pages, dtype=jnp.int32)
     order = jnp.arange(page_table.shape[0], dtype=jnp.int32)
@@ -376,139 +386,100 @@
     )
 
 
-def hidden_kernel(count, on_line, place_ref, *refs):
+def feed_kernel(places, count, on_line, place_ref, *refs):
     pieces = refs[:count]
     tokens, gain, w_out, w_gate, w_up, w_down = refs[count : count + 6]
+    outs, attended = refs[count + 6 : -1], refs[-1]
+    place = place_ref[0]
+    assemble(pieces, place, places, attended)
+    features = tokens.shape[1]
+    width = features // places
+    columns = w_out.shape[2]
+    projected = jnp.concatenate(
+        [dot_f32(attended[...], w_out[i, : attended.shape[1], :]) for i in range(w_out.shape[0])],
+        axis=1,
+    )
+    residual = (tokens[...].astype(jnp.float32) + projected).astype(jnp.bfloat16)
+    normed = norm_rows(residual.astype(jnp.float32), gain[...].astype(jnp.float32))
+    kept = residual[:, :width]
+    for i in range(1, places):
+        kept = jnp.where(place == i, residual[:, i * width : (i + 1) * width], kept)
+    gate = dot_f32(normed, w_gate[...])
+    up = dot_f32(normed, w_up[...])
+    hidden = (jax.nn.silu(gate) * up).astype(jnp.bfloat16)
+    if not on_line:
+        outs[0][...] = dot_f32(hidden, w_down[...]).astype(jnp.bfloat16)
+        outs[1][...] = kept.astype(jnp.float32)
+        return
+
+    def product(index):
+        return dot_f32(hidden, w_down[:, pl.ds(pl.multiple_of(index * width, width), width)])
+
+    far, to_right, to_left, toward_end, own = outs
+    far[...] = product(lax.rem(place + 2, 4))
+    right = product(lax.rem(place + 1, 4)).astype(jnp.bfloat16)
+    left = product(lax.rem(place + 3, 4)).astype(jnp.bfloat16)
+    to_right[...] = right
+    to_left[...] = left
+    toward_end[...] = jnp.where(place == 3, right, left)
+    own[...] = product(place) + kept.astype(jnp.float32)
+
+
+def feed_share(place, pieces, tokens, gain, w_out, w_gate, w_up, w_down, part, parts):
+    places = lax.axis_size("tp")
+    rows, features = tokens.shape[0] // parts, tokens.shape[1]
+    width = features // places
+    on_line = places == 4
     if on_line:
-        hidden, kept, first_out, second_out = refs[count + 6 : count + 10]
+        kinds = [jnp.float32, jnp.bfloat16, jnp.bfloat16, jnp.bfloat16, jnp.float32]
+        shapes = [jax.ShapeDtypeStruct((rows, width), kind) for kind in kinds]
     else:
-        hidden, kept = refs[count + 6 : count + 8]
-    attended, out_buf, gate_buf, up_buf, down_buf, sems = refs[-6:]
-    place = place_ref[0]
-    loads = [
-        pltpu.make_async_copy(source, target, sems.at[i])
-        for i, (source, target) in enumerate(
-            [(w_out, out_buf), (w_gate, gate_buf), (w_up, up_buf), (w_down, down_buf)]
-        )
-    ]
-    for load in loads:
-        load.start()
-    assemble(pieces, place, attended, on_line)
-    rows, features = tokens.shape
-    width = kept.shape[1]
-    step = min(rows, 256)
-    gain_row = gain[...].astype(jnp.float32)
-    loads[0].wait()
-    normed = []
-    for first in range(0, rows, step):
-        part = pl.ds(first, step)
-        projected = dot_f32(attended[part, :], out_buf[...])
-        residual = (tokens[part, :].astype(jnp.float32) + projected).astype(jnp.bfloat16)
-        tokens_now = residual.astype(jnp.float32)
-        normed.append(norm_rows(tokens_now, gain_row))
-        gather = residual[:, :width]
-        for i in range(1, features // width):
-            gather = jnp.where(place == i, residual[:, i * width : (i + 1) * width], gather)
-        kept[part, :] = gather
-    loads[1].wait()
-    loads[2].wait()
-    for i, first in enumerate(range(0, rows, step)):
-        part = pl.ds(first, step)
-        gate = dot_f32(normed[i], gate_buf[...])
-        up = dot_f32(normed[i], up_buf[...])
-        hidden[part, :] = (jax.nn.silu(gate) * up).astype(jnp.bfloat16)
-    loads[3].wait()
-    if not on_line:
-        return
-
-    def block(index):
-        return down_buf[:, pl.ds(pl.multiple_of(index * width, width), width)]
-
-    toward_end = jnp.where(place == 3, 0, jnp.where(place == 0, 3, place))
-    first_out[...] = dot_f32(hidden[...], block(toward_end)).astype(jnp.bfloat16)
-    second_out[...] = dot_f32(hidden[...], block(lax.rem(place + 2, 4)))
-
-
-def hidden_of(place, pieces, tokens, gain, w_out, w_gate, w_up, w_down):
-    rows, features = tokens.shape
-    width = features // lax.axis_size("tp")
-    units = w_gate.shape[1]
-    on_line = lax.axis_size("tp") == 4
-    shapes = [
-        jax.ShapeDtypeStruct((rows, units), jnp.bfloat16),
-        jax.ShapeDtypeStruct((rows, width), jnp.bfloat16),
-    ]
-    if on_line:
-        shapes += [
-            jax.ShapeDtypeStruct((rows, width), jnp.bfloat16),
+        shapes = [
+            jax.ShapeDtypeStruct((rows, features), jnp.bfloat16),
             jax.ShapeDtypeStruct((rows, width), jnp.float32),
         ]
+
+    def rows_of(array):
+        return pl.BlockSpec((rows, array.shape[1]), lambda i: (part, 0))
+
+    def whole(array):
+        return pl.BlockSpec(array.shape, lambda i: (0,) * array.ndim)
+
+    weights = [gain, w_out, w_gate, w_up, w_down]
     return pl.pallas_call(
-        functools.partial(hidden_kernel, len(pieces), on_line),
+        functools.partial(feed_kernel, places, len(pieces), on_line),
+        grid=(1,),
         out_shape=shapes,
-        in_specs=[SMEM] + [VMEM] * len(pieces) + [VMEM, VMEM] + [ANY] * 4,
-        out_specs=[VMEM] * len(shapes),
-        scratch_shapes=[
-            pltpu.VMEM((rows, w_out.shape[0]), jnp.bfloat16),
-            pltpu.VMEM(w_out.shape, jnp.bfloat16),
-            pltpu.VMEM(w_gate.shape, jnp.bfloat16),
-            pltpu.VMEM(w_up.shape, jnp.bfloat16),
-            pltpu.VMEM(w_down.shape, jnp.bfloat16),
-            pltpu.SemaphoreType.DMA((4,)),
-        ],
-        compiler_params=params(40),
-        cost_estimate=cost(6 * rows * features * units, 10 << 20),
-        name="hidden",
-    )(place, *pieces, tokens, gain, w_out, w_gate, w_up, w_down)
-
-
-def down_kernel(place_ref, hidden, kept, w_down, to_right, to_left, own):
-    place = place_ref[0]
-    width = own.shape[1]
-
-    def product(index):
-        weights = w_down[:, pl.ds(pl.multiple_of(index * width, width), width)]
-        return dot_f32(hidden[...], weights)
-
-    to_right[...] = product(lax.rem(place + 1, 4)).astype(jnp.bfloat16)
-    to_left[...] = product(lax.rem(place + 3, 4)).astype(jnp.bfloat16)
-    own[...] = product(place) + kept[...].astype(jnp.float32)
-
-
-def down_blocks(place, hidden, kept, w_down):
-    rows, width = kept.shape
-    return pl.pallas_call(
-        down_kernel,
-        out_shape=[
-            jax.ShapeDtypeStruct((rows, width), jnp.bfloat16),
-            jax.ShapeDtypeStruct((rows, width), jnp.bfloat16),
-            jax.ShapeDtypeStruct((rows, width), jnp.float32),
-        ],
-        in_specs=[SMEM, VMEM, VMEM, VMEM],
-        out_specs=[VMEM] * 3,
-        compiler_params=params(24),
-        cost_estimate=cost(2 * rows * w_down.shape[0] * width * 3, 5 << 20),
-        name="down_blocks",
-    )(place, hidden, kept, w_down)
+        in_specs=[SMEM]
+        + [rows_of(piece) for piece in pieces]
+        + [rows_of(tokens)]
+        + [whole(weight) for weight in weights],
+        out_specs=[whole(shape) for shape in shapes],
+        scratch_shapes=[pltpu.VMEM((rows, places * pieces[0].shape[1]), jnp.bfloat16)],
+        compiler_params=params(28),
+        cost_estimate=cost(6 * rows * features * w_gate.shape[1], 10 << 20),
+        name="feed",
+    )(place, *pieces, tokens, *weights)
 
 
 def feed_forward(place, pieces, tokens, gain, w_out, w_gate, w_up, w_down):
-    outs = hidden_of(place, pieces, tokens, gain, w_out, w_gate, w_up, w_down)
-    if lax.axis_size("tp") != 4:
-        hidden, kept = outs
-        share = lax.psum_scatter(
-            dot_f32(hidden, w_down).astype(jnp.bfloat16), "tp", scatter_dimension=1, tiled=True
-        )
-        return (kept.astype(jnp.float32) + share.astype(jnp.float32)).astype(jnp.bfloat16)
-    hidden, kept, toward_end, two_away = outs
-    from_end = lax.ppermute(toward_end, "tp", [(3, 2), (0, 1)])
-    to_right, to_left, own = down_blocks(place, hidden, kept, w_down)
-    from_left = lax.ppermute(to_right, "tp", [(0, 1), (1, 2), (2, 3)])
-    from_right = lax.ppermute(to_left, "tp", [(3, 2), (2, 1), (1, 0)])
-    joined = (two_away + from_end.astype(jnp.float32)).astype(jnp.bfloat16)
-    from_far = lax.ppermute(joined, "tp", [(0, 2), (1, 3), (2, 0), (3, 1)])
-    arrived = from_left.astype(jnp.float32) + from_right.astype(jnp.float32)
-    return (own + arrived + from_far.astype(jnp.float32)).astype(jnp.bfloat16)
+    parts = 2
+    mixed = []
+    for part in range(parts):
+        outs = feed_share(place, pieces, tokens, gain, w_out, w_gate, w_up, w_down, part, parts)
+        if lax.axis_size("tp") != 4:
+            share = lax.psum_scatter(outs[0], "tp", scatter_dimension=1, tiled=True)
+            mixed.append((outs[1] + share.astype(jnp.float32)).astype(jnp.bfloat16))
+            continue
+        far, to_right, to_left, toward_end, own = outs
+        from_end = lax.ppermute(toward_end, "tp", [(3, 2), (0, 1)])
+        from_left = lax.ppermute(to_right, "tp", [(0, 1), (1, 2), (2, 3)])
+        from_right = lax.ppermute(to_left, "tp", [(3, 2), (2, 1), (1, 0)])
+        joined = (far + from_end.astype(jnp.float32)).astype(jnp.bfloat16)
+        from_far = lax.ppermute(joined, "tp", [(0, 2), (1, 3), (2, 0), (3, 1)])
+        arrived = from_left.astype(jnp.float32) + from_right.astype(jnp.float32)
+        mixed.append((own + arrived + from_far.astype(jnp.float32)).astype(jnp.bfloat16))
+    return jnp.concatenate(mixed, axis=0)
 
 
 def rope_tables(positions, width):
@@ -521,6 +492,19 @@
         jnp.concatenate([cosine, cosine] * heads, axis=1),
         jnp.concatenate([-sine, sine] * heads, axis=1),
     )
+
+
+def gather_w_out(w_out, variate, me, devices):
+    columns = w_out.shape[1] // devices
+    block = lax.dynamic_slice_in_dim(w_out, me * columns, columns, 1)
+    block = lax.all_gather(block, "tp", axis=0, tiled=True)
+    extra = variate.astype(jnp.bfloat16).reshape(-1, columns)
+    height = block.shape[0]
+    pad = -extra.shape[0] % 16
+    block = jnp.concatenate([block, jnp.pad(extra, ((0, pad), (0, 0)))], axis=0)
+    blocks = lax.all_gather(block, "seq", axis=0)
+    variates = blocks[:, height : height + extra.shape[0], :]
+    return blocks, variates.reshape(-1).astype(jnp.int32)
 
 
 def segment_of(index, request_ends):
@@ -554,13 +538,10 @@
     reach = devices // 2
 
     pieces = gather_pieces(tokens)
-    all_variates = lax.all_gather(variate, "seq", axis=0, tiled=True)
-    slice_rows = w_out.shape[0] // devices
-    w_out_slice = lax.dynamic_slice_in_dim(w_out, me * slice_rows, slice_rows, 0)
-    w_out_all = lax.all_gather(w_out_slice, ("tp", "seq"), axis=0, tiled=True)
+    w_out_all, all_variates = gather_w_out(w_out, variate, me, devices)
 
     cosine, sine = rope_tables(positions, width)
-    ends = jnp.cumsum(lengths)
+    ends = running_sum(lengths)
     row_first = me * rows
     segment = segment_of(row_first + jnp.arange(rows, dtype=jnp.int32), ends)
     query_marks = bias_marks(variate, segment, var_bias, requests)
@@ -575,7 +556,7 @@
     )
     row_pieces = seq_pieces(pairs)
     attended = attend(info, queries, query_marks, key_marks, row_pieces, heads, reach)
-    attended_pieces = gather_pieces(attended)
+    attended_pieces = turn_gather(attended)
     cache = fill_cache(me.reshape(1), first_token, amounts, row_pieces)
     mixed = feed_forward(
         place,

time: 136 us -> 154 us (1.13); the launches traced: 135 us -> 152 us
  waiting for transfers between devices: 42.7 us -> 25.7 us
  starting transfers between devices: 24.5 us -> 39.5 us
  blocking collectives: 8.91 us -> 21.4 us
  local copies, waits for them, and re-layouts: 15.8 us -> 20.5 us
  other arithmetic: 10.3 us -> 12.8 us
  Pallas kernels: 16.2 us -> 14.6 us
    all_gather x1, blocking collectives: 8.91 us -> 21.4 us  [gather_w_out(): block = lax.all_gather(block, 'tp', axis=0, tiled=True)]
    ppermute x1 -> x2, starting transfers between devices: 1.31 us -> 9.3 us  [feed_forward(): from_left = lax.ppermute(to_right, 'tp', [(0, 1), (1, 2), (2, 3)])]
    ppermute x2 -> x1, waiting for transfers between devices: 12 us -> 6.75 us  [line_gather(): ends = lax.ppermute(far, 'tp', [(2, 3), (1, 0)])]
    ppermute x0 -> x3, starting transfers between devices: none -> 4.93 us  [turn_gather(): lax.ppermute(shard, 'tp', [(i, (i + turn) % count) for i in range(count)])]
    ppermute x2 -> x1, starting transfers between devices: 8.01 us -> 3.63 us  [line_gather(): left = lax.ppermute(shard, 'tp', [(0, 1), (1, 2), (2, 3)])]
    ppermute x1 -> x2, starting transfers between devices: 1.47 us -> 5.55 us  [feed_forward(): from_end = lax.ppermute(toward_end, 'tp', [(3, 2), (0, 1)])]
    unnamed x86 -> x80, local copies, waits for them, and re-layouts: 13.8 us -> 17.5 us
    ppermute x2 -> x1, waiting for transfers between devices: 3.55 us -> 0.01 us  [line_gather(): far = lax.ppermute(shard, 'tp', [(0, 2), (1, 3), (2, 0), (3, 1)])]
  transfers between devices with their start and end apart: 20 -> 23, of which waited for: 9 -> 6; matrix products, arithmetic and copies ran while one was open for 8% -> 10% of each run, Pallas kernels for 8% -> 5%
where the time goes in v2:
time: 154 us; the launch traced here: 152 us
  starting transfers between devices  39.5 us (26%)
  waiting for transfers between devices  25.7 us (17%)
  blocking collectives  21.4 us (14%)
  local copies, waits for them, and re-layouts  20.5 us (13%)
  between operations  17.2 us (11%)
  Pallas kernels  14.6 us (9%)
  other arithmetic  12.8 us (8%)
    all_gather x1, blocking collectives, gather_w_out(): block = lax.all_gather(block, 'tp', axis=0, tiled=True)  21.4 us
    unnamed x80, local copies, waits for them, and re-layouts  17.5 us
    ppermute x2, waiting for transfers between devices, feed_forward(): from_far = lax.ppermute(joined, 'tp', [(0, 2), (1, 3), (2, 0), (3, 1)])  10.5 us
    ppermute x2, starting transfers between devices, feed_forward(): from_left = lax.ppermute(to_right, 'tp', [(0, 1), (1, 2), (2, 3)])  9.3 us
    ppermute x7, waiting for transfers between devices, seq_xor(): lax.ppermute(value, 'seq', [(i, i ^ mask) for i in range(lax.axis_size('s...  8.39 us
    pallas_call x2, Pallas kernels, feed_share(): pl.pallas_call(functools.partial(feed_kernel, places, len(pieces), on_lin...  7.15 us
    ppermute x1, waiting for transfers between devices, line_gather(): ends = lax.ppermute(far, 'tp', [(2, 3), (1, 0)])  6.75 us
    ppermute x2, starting transfers between devices, feed_forward(): from_end = lax.ppermute(toward_end, 'tp', [(3, 2), (0, 1)])  5.55 us
  transfers between devices with their start and end apart: 23, of which 6 were waited for; matrix products, arithmetic and copies ran while one was open for 10% of the time, Pallas kernels for 5%

profile of v2, /device:TPU:2, one launch (start us, length us, event | category | flops | bytes accessed | tf_op | source)
XLA Modules:
  0.0 151.8 jit_solution(13386256301528266403)
XLA Ops:
  7.3 3.6 %collective-permute-start = (bf16[512,256]{1,0:T(8,128)(2,1)}, bf16[512,256]{1,0:T(8,128)(2,1)S(1)}, u32[]{:S(2)}, u32[]{:S(2)}) collective-permute-start(bf16[512,256]{1,0:T(8,128)(2,1)} %refs_0_.1), channel_id=1, source_target_pairs={{0,1},{1,2},{2,3},{4,5},{5,6},{6,7},{8,9},{9,10},{10,11},{12,13},{... | collective-permute-start | bytes 786440 | tf_op jit(solution)/shard_map/ppermute | solution.py:37
  10.9 1.3 collective-permute-start.1
  12.2 3.7 %collective-permute-start.2 = (bf16[512,256]{1,0:T(8,128)(2,1)}, bf16[512,256]{1,0:T(8,128)(2,1)S(1)}, u32[]{:S(2)}, u32[]{:S(2)}) collective-permute-start(bf16[512,256]{1,0:T(8,128)(2,1)} %refs_0_.1), channel_id=1, source_target_pairs={{0,2},{1,3},{2,0},{3,1},{4,6},{5,7},{6,4},{7,5},{8,10},{9,11},{10,... | collective-permute-start | bytes 786440 | tf_op jit(solution)/shard_map/ppermute | solution.py:36
  16.6 21.4 %all_gather.9 = bf16[512,128]{1,0:T(8,128)(2,1)S(1)} all-gather(bf16[128,128]{1,0:T(8,128)(2,1)S(1)} %constant_dynamic-slice_fusion), channel_id=1, replica_groups=mesh['seq'=8,'tp'=4] {'tp'}, dimensions={0}, use_global_device_ids=true | all-gather | bytes 163840 | tf_op jit(solution)/shard_map/all_gather | solution.py:500
  39.3 0.8 select_reduce_fusion.4
  40.9 1.4 select_reduce_fusion
  43.5 1.0 fusion.2
  45.2 1.2 fusion.7
  46.4 1.3 collective-permute-start.3
  47.9 6.8 %collective-permute-done.3.refs_4_ = bf16[512,256]{1,0:T(8,128)(2,1)S(1)} collective-permute-done((bf16[512,256]{1,0:T(8,128)(2,1)S(1)}, bf16[512,256]{1,0:T(8,128)(2,1)S(1)}, u32[]{:S(2)}, u32[]{:S(2)}) %collective-permute-start.3) | collective-permute-done | bytes 262176 | tf_op jit(solution)/shard_map/ppermute | solution.py:39
  54.7 1.3 project.1
  56.0 1.0 copy-done.5
  60.3 1.6 %collective-permute-start.7 = (bf16[512,256]{1,0:T(8,128)(2,1)S(1)}, bf16[512,256]{1,0:T(8,128)(2,1)S(1)}, u32[]{:S(2)}, u32[]{:S(2)}) collective-permute-start(bf16[512,256]{1,0:T(8,128)(2,1)S(1)} %get-tuple-element.16.refs_0_), channel_id=1, source_target_pairs={{0,16},{4,20},{8,24},{12,28},{16,0},{20,4},{24,8},{28,12},{1,17},{... | collective-permute-start | bytes 786440 | tf_op jit(solution)/shard_map/ppermute | solution.py:129
  61.9 2.8 %collective-permute-done.5.refs_2_ = bf16[512,256]{1,0:T(8,128)(2,1)S(1)} collective-permute-done((bf16[512,256]{1,0:T(8,128)(2,1)S(1)}, bf16[512,256]{1,0:T(8,128)(2,1)S(1)}, u32[]{:S(2)}, u32[]{:S(2)}) %collective-permute-start.5) | collective-permute-done | bytes 262176 | tf_op jit(solution)/shard_map/ppermute | solution.py:129
  64.7 1.5 %collective-permute-start.9 = (bf16[512,256]{1,0:T(8,128)(2,1)S(1)}, bf16[512,256]{1,0:T(8,128)(2,1)S(1)}, u32[]{:S(2)}, u32[]{:S(2)}) collective-permute-start(bf16[512,256]{1,0:T(8,128)(2,1)S(1)} %collective-permute-done.5.refs_2_), channel_id=1, source_target_pairs={{0,16},{4,20},{8,24},{12,28},{16,0},{20,4},{24,8},{28,12},{1,17},{... | collective-permute-start | bytes 786440 | tf_op jit(solution)/shard_map/ppermute | solution.py:129
  66.3 0.8 select_select_fusion.query_marks
  67.5 2.2 %collective-permute-done.7.refs_4_ = bf16[512,256]{1,0:T(8,128)(2,1)S(1)} collective-permute-done((bf16[512,256]{1,0:T(8,128)(2,1)S(1)}, bf16[512,256]{1,0:T(8,128)(2,1)S(1)}, u32[]{:S(2)}, u32[]{:S(2)}) %collective-permute-start.7) | collective-permute-done | bytes 262176 | tf_op jit(solution)/shard_map/ppermute | solution.py:129
  69.7 3.4 %collective-permute-done.9.refs_6_ = bf16[512,256]{1,0:T(8,128)(2,1)S(1)} collective-permute-done((bf16[512,256]{1,0:T(8,128)(2,1)S(1)}, bf16[512,256]{1,0:T(8,128)(2,1)S(1)}, u32[]{:S(2)}, u32[]{:S(2)}) %collective-permute-start.9) | collective-permute-done | bytes 262176 | tf_op jit(solution)/shard_map/ppermute | solution.py:129
  73.1 0.7 slice.12
  73.9 2.1 %and_convert_fusion.key_marks = bf16[4096,128]{1,0:T(8,128)(2,1)S(1)} fusion(s32[128]{0:T(128)} %copy-done.33, s32[128]{0:T(128)} %copy-done.32, s32[4096]{0:T(1024)S(1)} %convert_reduce_fusion, s32[4096]{0:T(1024)S(1)} %convert.8, pred[128]{0:T(512)(128)(4,1)} %get-tuple-element.45, pred[128]{0:T(512)(128)(4,1)} %get-tuple-element.46), kind=kLoop, calls=%fused_computation | loop fusion | flops 2621440 | bytes 1082624 | tf_op jit(solution)/shard_map/convert_element_type | solution.py:299
  76.8 0.9 copy-done.27
  77.7 0.9 copy-done.28
  78.7 3.8 %attend.1.refs_0_ = bf16[512,128]{1,0:T(8,128)(2,1)} custom-call(s32[2]{0:T(128)S(1)} %pad_add_fusion.info, bf16[512,128]{1,0:T(8,128)(2,1)S(1)} %get-tuple-element.15.queries, bf16[2,512,128]{2,1,0:T(8,128)(2,1)S(1)} %copy-done.28, bf16[4096,128]{1,0:T(8,128)(2,1)S(1)} %and_convert_fusion.key_marks, bf16[512,256]{1,0:T(8,128)(2,1)S(1)} %get-tuple-element.16.refs_0_, ...), custom_call_target="tpu_custom_call" | custom-call | flops 2684354560 | bytes 4194304 | tf_op jit(solution)/shard_map/attend/pallas_call | solution.py:255
  84.7 4.6 %collective-permute-start.12 = (bf16[512,128]{1,0:T(8,128)(2,1)}, bf16[512,128]{1,0:T(8,128)(2,1)}, u32[]{:S(2)}, u32[]{:S(2)}) collective-permute-start(bf16[512,128]{1,0:T(8,128)(2,1)} %attend.1.refs_0_), channel_id=1, source_target_pairs={{0,2},{1,3},{2,0},{3,1},{4,6},{5,7},{6,4},{7,5},{8,10},{9,11},{10,... | collective-permute-start | bytes 393224 | tf_op jit(solution)/shard_map/ppermute | solution.py:47
  89.9 0.9 copy-done.13
  90.8 0.9 copy-done.15
  91.8 0.9 copy-done.17
  92.7 0.9 copy-done.19
  93.7 0.9 copy-done.21
  94.6 0.9 copy-done.23
  95.6 0.9 copy-done.25
  96.5 2.3 %fill_cache.1 = bf16[576,256]{1,0:T(8,128)(2,1)S(1)} custom-call(s32[1]{0:T(128)} %bitcast.1.me_ref, s32[9]{0:T(128)S(1)} %get-tuple-element.29.first_token, s32[9]{0:T(128)S(1)} %get-tuple-element.28.amounts, bf16[512,256]{1,0:T(8,128)(2,1)S(1)} %copy-done.13, bf16[512,256]{1,0:T(8,128)(2,1)S(1)} %copy-done.21, bf16[512,256]{1,0:T(8,128)(2,1)S(1)} %copy-done.15, ...), custom_call_target="tpu_custom_call" | custom-call | flops 75497472 | bytes 3145728 | tf_op jit(solution)/shard_map/fill_cache/pallas_call | solution.py:351
  99.6 1.7 %reshape.191 = bf16[576,2,128]{2,1,0:T(2,128)(2,1)} reshape(bf16[576,256]{1,0:T(8,128)(2,1)} %copy-done.7) | data formatting | bytes 589824 | tf_op jit(solution)/shard_map/reshape | solution.py:571
  101.3 1.6 %copy-done.2 = bf16[1024,1024]{1,0:T(8,128)(2,1)S(1)} copy-done((bf16[1024,1024]{1,0:T(8,128)(2,1)S(1)}, bf16[1024,1024]{1,0:T(8,128)(2,1)}, u32[]{:S(2)}) %copy-start.2) | copy-done | bytes 2097176
  102.9 1.6 %copy-done.3 = bf16[1024,1024]{1,0:T(8,128)(2,1)S(1)} copy-done((bf16[1024,1024]{1,0:T(8,128)(2,1)S(1)}, bf16[1024,1024]{1,0:T(8,128)(2,1)}, u32[]{:S(2)}) %copy-start.3) | copy-done | bytes 2097176
  104.5 1.2 copy-done.6
  105.7 3.6 %feed.3 = (f32[256,256]{1,0:T(8,128)S(1)}, bf16[256,256]{1,0:T(8,128)(2,1)S(1)}, bf16[256,256]{1,0:T(8,128)(2,1)S(1)}, bf16[256,256]{1,0:T(8,128)(2,1)S(1)}, f32[256,256]{1,0:T(8,128)S(1)}) custom-call(s32[1]{0:T(128)} %bitcast.place_ref, bf16[512,128]{1,0:T(8,128)(2,1)} %attend.1.refs_0_, bf16[512,128]{1,0:T(8,128)(2,1)} %collective-permute-done.11.refs_1_, ...), custom_call_target="tpu_custom_call" | custom-call | flops 1610612736 | bytes 10485760 | tf_op jit(solution)/shard_map/feed/pallas_call | solution.py:449
  109.3 3.6 %collective-permute-start.20 = (bf16[256,256]{1,0:T(8,128)(2,1)S(1)}, bf16[256,256]{1,0:T(8,128)(2,1)S(1)}, u32[]{:S(2)}, u32[]{:S(2)}) collective-permute-start(bf16[256,256]{1,0:T(8,128)(2,1)S(1)} %get-tuple-element.27), channel_id=1, source_target_pairs={{3,2},{0,1},{7,6},{4,5},{11,10},{8,9},{15,14},{12,13},{19,18},{16,... | collective-permute-start | bytes 393224 | tf_op jit(solution)/shard_map/ppermute | solution.py:475
  112.9 1.3 collective-permute-start.19
  114.2 4.7 %collective-permute-start.18 = (bf16[256,256]{1,0:T(8,128)(2,1)S(1)}, bf16[256,256]{1,0:T(8,128)(2,1)S(1)}, u32[]{:S(2)}, u32[]{:S(2)}) collective-permute-start(bf16[256,256]{1,0:T(8,128)(2,1)S(1)} %get-tuple-element.24), channel_id=1, source_target_pairs={{0,1},{1,2},{2,3},{4,5},{5,6},{6,7},{8,9},{9,10},{10,11},{12,13},{... | collective-permute-start | bytes 393224 | tf_op jit(solution)/shard_map/ppermute | solution.py:476
  119.0 3.6 %feed.2 = (f32[256,256]{1,0:T(8,128)S(1)}, bf16[256,256]{1,0:T(8,128)(2,1)S(1)}, bf16[256,256]{1,0:T(8,128)(2,1)S(1)}, bf16[256,256]{1,0:T(8,128)(2,1)S(1)}, f32[256,256]{1,0:T(8,128)S(1)}) custom-call(s32[1]{0:T(128)} %bitcast.place_ref, bf16[512,128]{1,0:T(8,128)(2,1)} %attend.1.refs_0_, bf16[512,128]{1,0:T(8,128)(2,1)} %collective-permute-done.11.refs_1_, ...), custom_call_target="tpu_custom_call" | custom-call | flops 1610612736 | bytes 10485760 | tf_op jit(solution)/shard_map/feed/pallas_call | solution.py:449
  122.6 1.9 %collective-permute-start.16 = (bf16[256,256]{1,0:T(8,128)(2,1)S(1)}, bf16[256,256]{1,0:T(8,128)(2,1)S(1)}, u32[]{:S(2)}, u32[]{:S(2)}) collective-permute-start(bf16[256,256]{1,0:T(8,128)(2,1)S(1)} %get-tuple-element.22), channel_id=1, source_target_pairs={{3,2},{0,1},{7,6},{4,5},{11,10},{8,9},{15,14},{12,13},{19,18},{16,... | collective-permute-start | bytes 393224 | tf_op jit(solution)/shard_map/ppermute | solution.py:475
  124.5 1.3 collective-permute-start.15
  125.8 4.6 %collective-permute-start.14 = (bf16[256,256]{1,0:T(8,128)(2,1)S(1)}, bf16[256,256]{1,0:T(8,128)(2,1)S(1)}, u32[]{:S(2)}, u32[]{:S(2)}) collective-permute-start(bf16[256,256]{1,0:T(8,128)(2,1)S(1)} %get-tuple-element.19), channel_id=1, source_target_pairs={{0,1},{1,2},{2,3},{4,5},{5,6},{6,7},{8,9},{9,10},{10,11},{12,13},{... | collective-permute-start | bytes 393224 | tf_op jit(solution)/shard_map/ppermute | solution.py:476
  130.6 3.0 %collective-permute-start.17 = (bf16[256,256]{1,0:T(8,128)(2,1)S(1)}, bf16[256,256]{1,0:T(8,128)(2,1)S(1)}, u32[]{:S(2)}, u32[]{:S(2)}) collective-permute-start(bf16[256,256]{1,0:T(8,128)(2,1)S(1)} %add_convert_fusion.3), channel_id=1, source_target_pairs={{0,2},{1,3},{2,0},{3,1},{4,6},{5,7},{6,4},{7,5},{8,10},{9,11},{10,... | collective-permute-start | bytes 393224 | tf_op jit(solution)/shard_map/ppermute | solution.py:479
  133.6 7.9 %collective-permute-done.21 = bf16[256,256]{1,0:T(8,128)(2,1)S(1)} collective-permute-done((bf16[256,256]{1,0:T(8,128)(2,1)S(1)}, bf16[256,256]{1,0:T(8,128)(2,1)S(1)}, u32[]{:S(2)}, u32[]{:S(2)}) %collective-permute-start.21) | collective-permute-done | bytes 131104 | tf_op jit(solution)/shard_map/ppermute | solution.py:479
  141.5 2.6 %collective-permute-done.17 = bf16[256,256]{1,0:T(8,128)(2,1)S(1)} collective-permute-done((bf16[256,256]{1,0:T(8,128)(2,1)S(1)}, bf16[256,256]{1,0:T(8,128)(2,1)S(1)}, u32[]{:S(2)}, u32[]{:S(2)}) %collective-permute-start.17) | collective-permute-done | bytes 131104 | tf_op jit(solution)/shard_map/ppermute | solution.py:479
  144.3 0.7 pad_maximum_fusion.2
  (128 shorter events, 10.5 us)
Async XLA Ops:
  7.2 9.5 %copy-start = (bf16[128,1024]{1,0:T(8,128)(2,1)S(1)}, bf16[128,1024]{1,0:T(8,128)(2,1)}, u32[]{:S(2)}) copy-start(bf16[128,1024]{1,0:T(8,128)(2,1)} %param.25) | copy-start | bytes 786436
  7.2 47.5 %copy-start.8 = (bf16[512,256]{1,0:T(8,128)(2,1)S(1)}, bf16[512,256]{1,0:T(8,128)(2,1)}, u32[]{:S(2)}) copy-start(bf16[512,256]{1,0:T(8,128)(2,1)} %refs_0_.1) | copy-start | bytes 786436
  7.2 40.5 %copy-start.29 = (s32[512]{0:T(512)S(1)}, s32[512]{0:T(512)}, u32[]{:S(2)}) copy-start(s32[512]{0:T(512)} %param.16) | copy-start | bytes 6148
  7.2 38.0 %copy-start.38 = (s32[4]{0:T(128)S(1)}, s32[4]{0:T(128)}, u32[]{:S(2)}) copy-start(s32[4]{0:T(128)} %param.18) | copy-start | bytes 52
  7.2 40.5 %copy-start.34 = (bf16[1024]{0:T(1024)(128)(2,1)S(1)}, bf16[1024]{0:T(1024)(128)(2,1)}, u32[]{:S(2)}) copy-start(bf16[1024]{0:T(1024)(128)(2,1)} %param.20) | copy-start | bytes 6148
  7.2 47.4 %copy-start.9 = (bf16[1024,128]{1,0:T(8,128)(2,1)S(1)}, bf16[1024,128]{1,0:T(8,128)(2,1)}, u32[]{:S(2)}) copy-start(bf16[1024,128]{1,0:T(8,128)(2,1)} %refs_6_.1) | copy-start | bytes 786436
  7.2 47.4 %copy-start.10 = (bf16[1024,128]{1,0:T(8,128)(2,1)S(1)}, bf16[1024,128]{1,0:T(8,128)(2,1)}, u32[]{:S(2)}) copy-start(bf16[1024,128]{1,0:T(8,128)(2,1)} %refs_7_.3) | copy-start | bytes 786436
  7.2 47.4 %copy-start.11 = (bf16[1024,128]{1,0:T(8,128)(2,1)S(1)}, bf16[1024,128]{1,0:T(8,128)(2,1)}, u32[]{:S(2)}) copy-start(bf16[1024,128]{1,0:T(8,128)(2,1)} %refs_8_.3) | copy-start | bytes 786436
  7.3 65.9 %all-gather.3.cloned.1.call-start = ((), (), s32[]{:S(2)}) async-start(), calls=%async_computation | async-start | bytes 1216512 | tf_op jit(solution)/shard_map/all_gather | solution.py:505
  7.3 40.6 %collective-permute-start = (bf16[512,256]{1,0:T(8,128)(2,1)}, bf16[512,256]{1,0:T(8,128)(2,1)S(1)}, u32[]{:S(2)}, u32[]{:S(2)}) collective-permute-start(bf16[512,256]{1,0:T(8,128)(2,1)} %refs_0_.1), channel_id=1, source_target_pairs={{0,1},{1,2},{2,3},{4,5},{5,6},{6,7},{8,9},{9,10},{10,11},{12,13},{... | collective-permute-start | bytes 786440 | tf_op jit(solution)/shard_map/ppermute | solution.py:37
  10.9 37.0 %collective-permute-start.1 = (bf16[512,256]{1,0:T(8,128)(2,1)}, bf16[512,256]{1,0:T(8,128)(2,1)S(1)}, u32[]{:S(2)}, u32[]{:S(2)}) collective-permute-start(bf16[512,256]{1,0:T(8,128)(2,1)} %refs_0_.1), channel_id=1, source_target_pairs={{3,2},{2,1},{1,0},{7,6},{6,5},{5,4},{11,10},{10,9},{9,8},{15,14},{... | collective-permute-start | bytes 786440 | tf_op jit(solution)/shard_map/ppermute | solution.py:38
  12.2 34.2 %collective-permute-start.2 = (bf16[512,256]{1,0:T(8,128)(2,1)}, bf16[512,256]{1,0:T(8,128)(2,1)S(1)}, u32[]{:S(2)}, u32[]{:S(2)}) collective-permute-start(bf16[512,256]{1,0:T(8,128)(2,1)} %refs_0_.1), channel_id=1, source_target_pairs={{0,2},{1,3},{2,0},{3,1},{4,6},{5,7},{6,4},{7,5},{8,10},{9,11},{10,... | collective-permute-start | bytes 786440 | tf_op jit(solution)/shard_map/ppermute | solution.py:36
  38.8 21.4 %copy-start.32 = (s32[128]{0:T(128)}, s32[128]{0:T(128)S(1)}, u32[]{:S(2)}) copy-start(s32[128]{0:T(128)S(1)} %get-tuple-element.43) | copy-start | bytes 1540
  38.8 28.8 %copy-start.33 = (s32[128]{0:T(128)}, s32[128]{0:T(128)S(1)}, u32[]{:S(2)}) copy-start(s32[128]{0:T(128)S(1)} %get-tuple-element.44) | copy-start | bytes 1540
  40.1 15.9 %copy-start.30 = (s32[4]{0:T(128)}, s32[4]{0:T(128)S(1)}, u32[]{:S(2)}) copy-start(s32[4]{0:T(128)S(1)} %select_reduce_fusion.4) | copy-start | bytes 52
  46.4 8.3 %collective-permute-start.3 = (bf16[512,256]{1,0:T(8,128)(2,1)S(1)}, bf16[512,256]{1,0:T(8,128)(2,1)S(1)}, u32[]{:S(2)}, u32[]{:S(2)}) collective-permute-start(bf16[512,256]{1,0:T(8,128)(2,1)S(1)} %collective-permute-done.2.refs_3_), channel_id=1, source_target_pairs={{2,3},{1,0},{6,7},{5,4},{10,11},{9,8},{14,15},{13,12},{18,19},{17,... | collective-permute-start | bytes 786440 | tf_op jit(solution)/shard_map/ppermute | solution.py:39
  57.0 19.8 %copy-start.12 = (bf16[512,256]{1,0:T(8,128)(2,1)}, bf16[512,256]{1,0:T(8,128)(2,1)S(1)}, u32[]{:S(2)}) copy-start(bf16[512,256]{1,0:T(8,128)(2,1)S(1)} %get-tuple-element.16.refs_0_) | copy-start | bytes 786436
  57.0 7.7 %collective-permute-start.5 = (bf16[512,256]{1,0:T(8,128)(2,1)S(1)}, bf16[512,256]{1,0:T(8,128)(2,1)S(1)}, u32[]{:S(2)}, u32[]{:S(2)}) collective-permute-start(bf16[512,256]{1,0:T(8,128)(2,1)S(1)} %get-tuple-element.16.refs_0_), channel_id=1, source_target_pairs={{0,8},{4,12},{8,0},{12,4},{16,24},{20,28},{24,16},{28,20},{1,9},{5... | collective-permute-start | bytes 786440 | tf_op jit(solution)/shard_map/ppermute | solution.py:129
  60.3 9.4 %collective-permute-start.7 = (bf16[512,256]{1,0:T(8,128)(2,1)S(1)}, bf16[512,256]{1,0:T(8,128)(2,1)S(1)}, u32[]{:S(2)}, u32[]{:S(2)}) collective-permute-start(bf16[512,256]{1,0:T(8,128)(2,1)S(1)} %get-tuple-element.16.refs_0_), channel_id=1, source_target_pairs={{0,16},{4,20},{8,24},{12,28},{16,0},{20,4},{24,8},{28,12},{1,17},{... | collective-permute-start | bytes 786440 | tf_op jit(solution)/shard_map/ppermute | solution.py:129
  64.7 12.1 %copy-start.14 = (bf16[512,256]{1,0:T(8,128)(2,1)}, bf16[512,256]{1,0:T(8,128)(2,1)S(1)}, u32[]{:S(2)}) copy-start(bf16[512,256]{1,0:T(8,128)(2,1)S(1)} %collective-permute-done.5.refs_2_) | copy-start | bytes 786436
  64.7 8.5 %collective-permute-start.9 = (bf16[512,256]{1,0:T(8,128)(2,1)S(1)}, bf16[512,256]{1,0:T(8,128)(2,1)S(1)}, u32[]{:S(2)}, u32[]{:S(2)}) collective-permute-start(bf16[512,256]{1,0:T(8,128)(2,1)S(1)} %collective-permute-done.5.refs_2_), channel_id=1, source_target_pairs={{0,16},{4,20},{8,24},{12,28},{16,0},{20,4},{24,8},{28,12},{1,17},{... | collective-permute-start | bytes 786440 | tf_op jit(solution)/shard_map/ppermute | solution.py:129
  67.0 9.0 %collective-permute-start.4 = (bf16[512,256]{1,0:T(8,128)(2,1)S(1)}, bf16[512,256]{1,0:T(8,128)(2,1)S(1)}, u32[]{:S(2)}, u32[]{:S(2)}) collective-permute-start(bf16[512,256]{1,0:T(8,128)(2,1)S(1)} %get-tuple-element.16.refs_0_), channel_id=1, source_target_pairs={{0,4},{4,0},{8,12},{12,8},{16,20},{20,16},{24,28},{28,24},{1,5},{5... | collective-permute-start | bytes 786440 | tf_op jit(solution)/shard_map/ppermute | solution.py:129
  67.0 9.0 %collective-permute-start.6 = (bf16[512,256]{1,0:T(8,128)(2,1)S(1)}, bf16[512,256]{1,0:T(8,128)(2,1)S(1)}, u32[]{:S(2)}, u32[]{:S(2)}) collective-permute-start(bf16[512,256]{1,0:T(8,128)(2,1)S(1)} %collective-permute-done.5.refs_2_), channel_id=1, source_target_pairs={{0,4},{4,0},{8,12},{12,8},{16,20},{20,16},{24,28},{28,24},{1,5},{5... | collective-permute-start | bytes 786440 | tf_op jit(solution)/shard_map/ppermute | solution.py:129
  69.7 7.1 %copy-start.16 = (bf16[512,256]{1,0:T(8,128)(2,1)}, bf16[512,256]{1,0:T(8,128)(2,1)S(1)}, u32[]{:S(2)}) copy-start(bf16[512,256]{1,0:T(8,128)(2,1)S(1)} %collective-permute-done.7.refs_4_) | copy-start | bytes 786436
  69.7 6.3 %collective-permute-start.8 = (bf16[512,256]{1,0:T(8,128)(2,1)S(1)}, bf16[512,256]{1,0:T(8,128)(2,1)S(1)}, u32[]{:S(2)}, u32[]{:S(2)}) collective-permute-start(bf16[512,256]{1,0:T(8,128)(2,1)S(1)} %collective-permute-done.7.refs_4_), channel_id=1, source_target_pairs={{0,4},{4,0},{8,12},{12,8},{16,20},{20,16},{24,28},{28,24},{1,5},{5... | collective-permute-start | bytes 786440 | tf_op jit(solution)/shard_map/ppermute | solution.py:129
  73.1 3.6 %copy-start.18 = (bf16[512,256]{1,0:T(8,128)(2,1)}, bf16[512,256]{1,0:T(8,128)(2,1)S(1)}, u32[]{:S(2)}) copy-start(bf16[512,256]{1,0:T(8,128)(2,1)S(1)} %collective-permute-done.9.refs_6_) | copy-start | bytes 786436
  73.1 2.9 %collective-permute-start.10 = (bf16[512,256]{1,0:T(8,128)(2,1)S(1)}, bf16[512,256]{1,0:T(8,128)(2,1)S(1)}, u32[]{:S(2)}, u32[]{:S(2)}) collective-permute-start(bf16[512,256]{1,0:T(8,128)(2,1)S(1)} %collective-permute-done.9.refs_6_), channel_id=1, source_target_pairs={{0,4},{4,0},{8,12},{12,8},{16,20},{20,16},{24,28},{28,24},{1,5},{5... | collective-permute-start | bytes 786440 | tf_op jit(solution)/shard_map/ppermute | solution.py:129
  78.7 10.9 %copy-start.39 = (s32[4]{0:T(128)S(1)}, s32[4]{0:T(128)}, u32[]{:S(2)}) copy-start(s32[4]{0:T(128)} %get-tuple-element.40) | copy-start | bytes 52
  78.7 11.0 %copy-start.35 = (bf16[1024]{0:T(1024)(128)(2,1)S(1)}, bf16[1024]{0:T(1024)(128)(2,1)}, u32[]{:S(2)}) copy-start(bf16[1024]{0:T(1024)(128)(2,1)} %param.26) | copy-start | bytes 6148
  78.7 11.1 %copy-start.31 = (s32[4]{0:T(128)S(1)}, s32[4]{0:T(128)}, u32[]{:S(2)}) copy-start(s32[4]{0:T(128)} %copy-done.30) | copy-start | bytes 52
  78.7 11.1 %copy-start.36 = (s32[4]{0:T(128)S(1)}, s32[4]{0:T(128)}, u32[]{:S(2)}) copy-start(s32[4]{0:T(128)} %get-tuple-element.33) | copy-start | bytes 52
  78.7 11.1 %copy-start.37 = (s32[9]{0:T(128)S(1)}, s32[9]{0:T(128)}, u32[]{:S(2)}) copy-start(s32[9]{0:T(128)} %select_reduce_fusion) | copy-start | bytes 112
  78.7 22.6 %copy-start.4 = (bf16[4224,128]{1,0:T(8,128)(2,1)S(1)}, bf16[4224,128]{1,0:T(8,128)(2,1)}, u32[]{:S(2)}) copy-start(bf16[4224,128]{1,0:T(8,128)(2,1)} %all-gather.3.cloned.1.call-done) | copy-start | bytes 3244036
  84.7 16.7 %copy-start.1 = (bf16[1024,1024]{1,0:T(8,128)(2,1)S(1)}, bf16[1024,1024]{1,0:T(8,128)(2,1)}, u32[]{:S(2)}) copy-start(bf16[1024,1024]{1,0:T(8,128)(2,1)} %refs_7_.5) | copy-start | bytes 6291460
  84.7 16.6 %collective-permute-start.11 = (bf16[512,128]{1,0:T(8,128)(2,1)}, bf16[512,128]{1,0:T(8,128)(2,1)}, u32[]{:S(2)}, u32[]{:S(2)}) collective-permute-start(bf16[512,128]{1,0:T(8,128)(2,1)} %attend.1.refs_0_), channel_id=1, source_target_pairs={{0,1},{1,2},{2,3},{3,0},{4,5},{5,6},{6,7},{7,4},{8,9},{9,10},{10,1... | collective-permute-start | bytes 393224 | tf_op jit(solution)/shard_map/ppermute | solution.py:47
  84.7 16.6 %collective-permute-start.12 = (bf16[512,128]{1,0:T(8,128)(2,1)}, bf16[512,128]{1,0:T(8,128)(2,1)}, u32[]{:S(2)}, u32[]{:S(2)}) collective-permute-start(bf16[512,128]{1,0:T(8,128)(2,1)} %attend.1.refs_0_), channel_id=1, source_target_pairs={{0,2},{1,3},{2,0},{3,1},{4,6},{5,7},{6,4},{7,5},{8,10},{9,11},{10,... | collective-permute-start | bytes 393224 | tf_op jit(solution)/shard_map/ppermute | solution.py:47
  89.3 12.0 %collective-permute-start.13 = (bf16[512,128]{1,0:T(8,128)(2,1)}, bf16[512,128]{1,0:T(8,128)(2,1)}, u32[]{:S(2)}, u32[]{:S(2)}) collective-permute-start(bf16[512,128]{1,0:T(8,128)(2,1)} %attend.1.refs_0_), channel_id=1, source_target_pairs={{0,3},{1,0},{2,1},{3,2},{4,7},{5,4},{6,5},{7,6},{8,11},{9,8},{10,9... | collective-permute-start | bytes 393224 | tf_op jit(solution)/shard_map/ppermute | solution.py:47
  101.3 1.6 %copy-start.2 = (bf16[1024,1024]{1,0:T(8,128)(2,1)S(1)}, bf16[1024,1024]{1,0:T(8,128)(2,1)}, u32[]{:S(2)}) copy-start(bf16[1024,1024]{1,0:T(8,128)(2,1)} %refs_8_.5) | copy-start | bytes 6291460
  102.9 1.6 %copy-start.3 = (bf16[1024,1024]{1,0:T(8,128)(2,1)S(1)}, bf16[1024,1024]{1,0:T(8,128)(2,1)}, u32[]{:S(2)}) copy-start(bf16[1024,1024]{1,0:T(8,128)(2,1)} %refs_9_.3) | copy-start | bytes 6291460
  104.5 1.2 copy-start.6
  109.3 16.5 %collective-permute-start.20 = (bf16[256,256]{1,0:T(8,128)(2,1)S(1)}, bf16[256,256]{1,0:T(8,128)(2,1)S(1)}, u32[]{:S(2)}, u32[]{:S(2)}) collective-permute-start(bf16[256,256]{1,0:T(8,128)(2,1)S(1)} %get-tuple-element.27), channel_id=1, source_target_pairs={{3,2},{0,1},{7,6},{4,5},{11,10},{8,9},{15,14},{12,13},{19,18},{16,... | collective-permute-start | bytes 393224 | tf_op jit(solution)/shard_map/ppermute | solution.py:475
  112.9 17.6 %collective-permute-start.19 = (bf16[256,256]{1,0:T(8,128)(2,1)S(1)}, bf16[256,256]{1,0:T(8,128)(2,1)S(1)}, u32[]{:S(2)}, u32[]{:S(2)}) collective-permute-start(bf16[256,256]{1,0:T(8,128)(2,1)S(1)} %get-tuple-element.25), channel_id=1, source_target_pairs={{3,2},{2,1},{1,0},{7,6},{6,5},{5,4},{11,10},{10,9},{9,8},{15,14},{... | collective-permute-start | bytes 393224 | tf_op jit(solution)/shard_map/ppermute | solution.py:477
  114.2 19.3 %collective-permute-start.18 = (bf16[256,256]{1,0:T(8,128)(2,1)S(1)}, bf16[256,256]{1,0:T(8,128)(2,1)S(1)}, u32[]{:S(2)}, u32[]{:S(2)}) collective-permute-start(bf16[256,256]{1,0:T(8,128)(2,1)S(1)} %get-tuple-element.24), channel_id=1, source_target_pairs={{0,1},{1,2},{2,3},{4,5},{5,6},{6,7},{8,9},{9,10},{10,11},{12,13},{... | collective-permute-start | bytes 393224 | tf_op jit(solution)/shard_map/ppermute | solution.py:476
  122.6 7.9 %collective-permute-start.16 = (bf16[256,256]{1,0:T(8,128)(2,1)S(1)}, bf16[256,256]{1,0:T(8,128)(2,1)S(1)}, u32[]{:S(2)}, u32[]{:S(2)}) collective-permute-start(bf16[256,256]{1,0:T(8,128)(2,1)S(1)} %get-tuple-element.22), channel_id=1, source_target_pairs={{3,2},{0,1},{7,6},{4,5},{11,10},{8,9},{15,14},{12,13},{19,18},{16,... | collective-permute-start | bytes 393224 | tf_op jit(solution)/shard_map/ppermute | solution.py:475
  124.5 17.0 %collective-permute-start.15 = (bf16[256,256]{1,0:T(8,128)(2,1)S(1)}, bf16[256,256]{1,0:T(8,128)(2,1)S(1)}, u32[]{:S(2)}, u32[]{:S(2)}) collective-permute-start(bf16[256,256]{1,0:T(8,128)(2,1)S(1)} %get-tuple-element.20), channel_id=1, source_target_pairs={{3,2},{2,1},{1,0},{7,6},{6,5},{5,4},{11,10},{10,9},{9,8},{15,14},{... | collective-permute-start | bytes 393224 | tf_op jit(solution)/shard_map/ppermute | solution.py:477
  125.8 15.7 %collective-permute-start.14 = (bf16[256,256]{1,0:T(8,128)(2,1)S(1)}, bf16[256,256]{1,0:T(8,128)(2,1)S(1)}, u32[]{:S(2)}, u32[]{:S(2)}) collective-permute-start(bf16[256,256]{1,0:T(8,128)(2,1)S(1)} %get-tuple-element.19), channel_id=1, source_target_pairs={{0,1},{1,2},{2,3},{4,5},{5,6},{6,7},{8,9},{9,10},{10,11},{12,13},{... | collective-permute-start | bytes 393224 | tf_op jit(solution)/shard_map/ppermute | solution.py:476
  130.5 11.0 %collective-permute-start.21 = (bf16[256,256]{1,0:T(8,128)(2,1)S(1)}, bf16[256,256]{1,0:T(8,128)(2,1)S(1)}, u32[]{:S(2)}, u32[]{:S(2)}) collective-permute-start(bf16[256,256]{1,0:T(8,128)(2,1)S(1)} %add_convert_fusion.1), channel_id=1, source_target_pairs={{0,2},{1,3},{2,0},{3,1},{4,6},{5,7},{6,4},{7,5},{8,10},{9,11},{10,... | collective-permute-start | bytes 393224 | tf_op jit(solution)/shard_map/ppermute | solution.py:479
  130.6 13.6 %collective-permute-start.17 = (bf16[256,256]{1,0:T(8,128)(2,1)S(1)}, bf16[256,256]{1,0:T(8,128)(2,1)S(1)}, u32[]{:S(2)}, u32[]{:S(2)}) collective-permute-start(bf16[256,256]{1,0:T(8,128)(2,1)S(1)} %add_convert_fusion.3), channel_id=1, source_target_pairs={{0,2},{1,3},{2,0},{3,1},{4,6},{5,7},{6,4},{7,5},{8,10},{9,11},{10,... | collective-permute-start | bytes 393224 | tf_op jit(solution)/shard_map/ppermute | solution.py:479
  (15 other events, 13.1 us)
Sparse Core Ops, SparseCore 0:
  38.9 26.9 all-gather.2

commit v3 on v2

--- a/solution.py
+++ b/solution.py
@@ -26,6 +26,10 @@
 
 def cost(flops, nbytes, exps=0):
     return pl.CostEstimate(flops=flops, bytes_accessed=nbytes, transcendentals=exps)
+
+
+def round_up(amount, unit):
+    return (amount + unit - 1) // unit * unit
 
 
 def dot_f32(left, right):
@@ -89,7 +93,8 @@
 
 def project_kernel(places, count, place_ref, *refs):
     pieces = refs[:count]
-    gain, w_q, w_k, w_v, cosine, sine, tokens, queries, pairs = refs[count:]
+    gain, w_q, w_k, w_v, cosine, sine, extra, tokens, queries, pairs = refs[count:]
+    pairs[tokens.shape[0] :, :] = extra[...]
     assemble(pieces, place_ref[0], places, tokens)
     rows = tokens.shape[0]
     width = w_q.shape[1]
@@ -106,7 +111,7 @@
         pairs[part, width:] = dot_f32(normed, w_v[...]).astype(jnp.bfloat16)
 
 
-def project(pieces, place, gain, w_query, w_key, w_value, cosine, sine):
+def project(pieces, place, gain, w_query, w_key, w_value, cosine, sine, extra):
     rows, part = pieces[0].shape
     width = w_query.shape[1]
     features = w_query.shape[0]
@@ -115,14 +120,14 @@
         out_shape=[
             jax.ShapeDtypeStruct((rows, features), jnp.bfloat16),
             jax.ShapeDtypeStruct((rows, width), jnp.bfloat16),
-            jax.ShapeDtypeStruct((rows, 2 * width), jnp.bfloat16),
+            jax.ShapeDtypeStruct((rows + extra.shape[0], 2 * width), jnp.bfloat16),
         ],
-        in_specs=[SMEM] + [VMEM] * (len(pieces) + 6),
+        in_specs=[SMEM] + [VMEM] * (len(pieces) + 7),
         out_specs=[VMEM] * 3,
         compiler_params=params(12),
         cost_estimate=cost(6 * rows * features * width, 4 << 20),
         name="project",
-    )(place, *pieces, gain, w_query, w_key, w_value, cosine, sine)
+    )(place, *pieces, gain, w_query, w_key, w_value, cosine, sine, extra)
 
 
 def seq_xor(value, mask):
@@ -131,10 +136,10 @@
 
 def seq_pieces(pairs):
     if lax.axis_size("seq") == 8:
+        diagonal = seq_xor(pairs, 6)
         across = seq_xor(pairs, 2)
         down = seq_xor(pairs, 4)
         twin = seq_xor(pairs, 1)
-        diagonal = seq_xor(across, 4)
         across_twin = seq_xor(across, 1)
         down_twin = seq_xor(down, 1)
         diagonal_twin = seq_xor(diagonal, 1)
@@ -151,27 +156,27 @@
             wanted(pieces[0].at[j], j)
 
 
-def attend_kernel(count, heads, reach, info, queries, query_marks, key_marks, *refs):
+def attend_kernel(count, heads, reach, requests, info, queries, query_marks, *refs):
     pieces = refs[:count]
-    out, q_buf, k_buf, v_buf, scores, peak, total, sems = refs[count:]
+    out, q_buf, k_buf, v_buf, extra_buf, scores, peak, total, sems = refs[count:]
     me, last = info[0], info[1]
     rows = queries.shape[0]
     width = queries.shape[1]
 
-    def copies(source, block, slot):
+    def copies(source, slot):
         return [
             pltpu.make_async_copy(
-                source.at[:, pl.ds(0, width)], k_buf.at[slot, :, pl.ds(0, width)], sems.at[slot, 0]
+                source.at[pl.ds(0, rows), pl.ds(0, width)],
+                k_buf.at[slot, :, pl.ds(0, width)],
+                sems.at[slot, 0],
             ),
             pltpu.make_async_copy(
-                source.at[:, pl.ds(width, width)],
+                source.at[pl.ds(0, rows), pl.ds(width, width)],
                 v_buf.at[slot, :, pl.ds(0, width)],
                 sems.at[slot, 1],
             ),
             pltpu.make_async_copy(
-                key_marks.at[pl.ds(pl.multiple_of(block * rows, rows), rows), :],
-                k_buf.at[slot, :, pl.ds(width, LANES)],
-                sems.at[slot, 2],
+                source.at[pl.ds(rows, extra_buf.shape[1]), :], extra_buf.at[slot], sems.at[slot, 2]
             ),
         ]
 
@@ -180,15 +185,32 @@
 
         @pl.when((distance >= 0) & (distance <= last))
         def _():
-            for copy in copies(source, block, distance):
+            for copy in copies(source, distance):
                 copy.start()
 
     piece_copies(pieces, me, begin)
     example = pieces[0] if count > 1 else pieces[0].at[0]
 
+    mark_count = round_up(BIAS_PARTS * VARS + requests, 16)
+
     def finish(slot):
-        for copy in copies(example, 0, slot):
+        for copy in copies(example, slot):
             copy.wait()
+        extra = extra_buf[slot].astype(jnp.float32)
+        pair_width = extra.shape[1]
+        variates = jnp.concatenate([extra[i : i + 1] for i in range(rows // pair_width)], axis=1)
+        mark = lax.broadcasted_iota(jnp.int32, (mark_count, rows), 0)
+        key = lax.broadcasted_iota(jnp.int32, (mark_count, rows), 1) + (me - slot) * rows
+        segment = jnp.zeros_like(key)
+        for r in range(requests):
+            segment += (key >= info[2 + r]).astype(jnp.int32)
+        same_variate = (mark % VARS).astype(jnp.float32) == variates
+        same_segment = mark - BIAS_PARTS * VARS == segment
+        marked = (same_variate & (mark < BIAS_PARTS * VARS)) | (
+            same_segment & (mark >= BIAS_PARTS * VARS)
+        )
+        columns = jnp.transpose(jnp.where(marked, 1.0, 0.0))
+        k_buf[slot, :, width : width + mark_count] = columns.astype(jnp.bfloat16)
 
     lane = lax.broadcasted_iota(jnp.int32, (rows, width), 1)
     for h in range(heads):
@@ -197,6 +219,7 @@
         q_buf[part, width:] = query_marks[h]
     for slot in range(reach + 1):
         v_buf[slot, :, width:] = jnp.ones((rows, LANES), jnp.bfloat16)
+        k_buf[slot, :, width:] = jnp.zeros((rows, LANES), jnp.bfloat16)
 
     def narrow(tile):
         best = tile[:, :LANES]
@@ -249,18 +272,19 @@
     out[...] = result.astype(jnp.bfloat16)
 
 
-def attend(info, queries, query_marks, key_marks, pieces, heads, reach):
+def attend(info, queries, query_marks, pieces, heads, reach, requests):
     rows, width = queries.shape
     slots = reach + 1
     return pl.pallas_call(
-        functools.partial(attend_kernel, len(pieces), heads, reach),
+        functools.partial(attend_kernel, len(pieces), heads, reach, requests),
         out_shape=jax.ShapeDtypeStruct((rows, width), jnp.bfloat16),
-        in_specs=[SMEM, VMEM, VMEM, ANY] + [ANY] * len(pieces),
+        in_specs=[SMEM, VMEM, VMEM] + [ANY] * len(pieces),
         out_specs=VMEM,
         scratch_shapes=[
             pltpu.VMEM((heads * rows, width + LANES), jnp.bfloat16),
             pltpu.VMEM((slots, rows, width + LANES), jnp.bfloat16),
             pltpu.VMEM((slots, rows, width + LANES), jnp.bfloat16),
+            pltpu.VMEM((slots, pieces[0].shape[-2] - rows, pieces[0].shape[-1]), jnp.bfloat16),
             pltpu.VMEM((heads, slots, rows, rows), jnp.float32),
             pltpu.VMEM((heads, rows, LANES), jnp.float32),
             pltpu.VMEM((heads, rows, width + LANES), jnp.float32),
@@ -271,7 +295,7 @@
             4 * heads * rows * rows * slots * 256, 4 << 20, heads * rows * rows * slots
         ),
         name="attend",
-    )(info, queries, query_marks, key_marks, *pieces)
+    )(info, queries, query_marks, *pieces)
 
 
 def bias_marks(variate, segment, var_bias, requests):
@@ -290,13 +314,9 @@
     return jnp.where(hidden, jnp.bfloat16(HIDDEN_SCORE), marks)
 
 
-def key_marks_of(variate, segment, requests):
-    lane = jnp.arange(LANES, dtype=jnp.int32)[None, :]
-    same_variate = variate[:, None] == lane % VARS
-    same_segment = segment[:, None] == lane - BIAS_PARTS * VARS
-    marked = jnp.where(lane < BIAS_PARTS * VARS, same_variate, same_segment)
-    used = lane < BIAS_PARTS * VARS + requests
-    return (marked & used).astype(jnp.bfloat16)
+def extra_rows(variate, width):
+    extra = variate.astype(jnp.bfloat16).reshape(-1, width)
+    return jnp.pad(extra, ((0, round_up(extra.shape[0], 16) - extra.shape[0]), (0, 0)))
 
 
 def cache_kernel(count, window, me_ref, first_token, amounts, *refs):
@@ -309,7 +329,9 @@
     started = []
 
     def begin(source, block):
-        copy = pltpu.make_async_copy(source, rows_buf.at[block], sems.at[len(started)])
+        copy = pltpu.make_async_copy(
+            source.at[pl.ds(0, rows), :], rows_buf.at[block], sems.at[len(started)]
+        )
         copy.start()
         started.append(copy)
 
@@ -344,8 +366,8 @@
     lax.fori_loop(0, out.shape[0] // PAGE, one_page, 0)
 
 
-def fill_cache(me, first_token, amounts, pieces):
-    rows, width = pieces[0].shape[-2:]
+def fill_cache(me, first_token, amounts, pieces, rows):
+    width = pieces[0].shape[-1]
     blocks = lax.axis_size("seq")
     pages = first_token.shape[0]
     return pl.pallas_call(
@@ -386,100 +408,125 @@
     )
 
 
-def feed_kernel(places, count, on_line, place_ref, *refs):
+def hidden_kernel(places, count, on_line, place_ref, *refs):
     pieces = refs[:count]
     tokens, gain, w_out, w_gate, w_up, w_down = refs[count : count + 6]
     outs, attended = refs[count + 6 : -1], refs[-1]
+    hidden, kept = outs[:2]
     place = place_ref[0]
     assemble(pieces, place, places, attended)
-    features = tokens.shape[1]
+    rows, features = tokens.shape
+    width = kept.shape[1]
+    step = min(rows, 256)
+    gain_row = gain[...].astype(jnp.float32)
+    for first in range(0, rows, step):
+        part = pl.ds(first, step)
+        projected = dot_f32(attended[part, :], w_out[...])
+        residual = (tokens[part, :].astype(jnp.float32) + projected).astype(jnp.bfloat16)
+        mine = residual[:, :width]
+        for i in range(1, places):
+            mine = jnp.where(place == i, residual[:, i * width : (i + 1) * width], mine)
+        kept[part, :] = mine
+        normed = norm_rows(residual.astype(jnp.float32), gain_row)
+        gate = dot_f32(normed, w_gate[...])
+        up = dot_f32(normed, w_up[...])
+        hidden[part, :] = (jax.nn.silu(gate) * up).astype(jnp.bfloat16)
+    if not on_line:
+        return
+
+    def block(index):
+        return w_down[:, pl.ds(pl.multiple_of(index * width, width), width)]
+
+    toward_end = jnp.where(place == 3, 0, jnp.where(place == 0, 3, place))
+    outs[2][...] = dot_f32(hidden[...], block(toward_end)).astype(jnp.bfloat16)
+
+
+def hidden_of(place, pieces, tokens, gain, w_out, w_gate, w_up, w_down):
+    rows, features = tokens.shape
+    places = lax.axis_size("tp")
     width = features // places
-    columns = w_out.shape[2]
-    projected = jnp.concatenate(
-        [dot_f32(attended[...], w_out[i, : attended.shape[1], :]) for i in range(w_out.shape[0])],
-        axis=1,
-    )
-    residual = (tokens[...].astype(jnp.float32) + projected).astype(jnp.bfloat16)
-    normed = norm_rows(residual.astype(jnp.float32), gain[...].astype(jnp.float32))
-    kept = residual[:, :width]
-    for i in range(1, places):
-        kept = jnp.where(place == i, residual[:, i * width : (i + 1) * width], kept)
-    gate = dot_f32(normed, w_gate[...])
-    up = dot_f32(normed, w_up[...])
-    hidden = (jax.nn.silu(gate) * up).astype(jnp.bfloat16)
-    if not on_line:
-        outs[0][...] = dot_f32(hidden, w_down[...]).astype(jnp.bfloat16)
-        outs[1][...] = kept.astype(jnp.float32)
-        return
+    units = w_gate.shape[1]
+    on_line = places == 4
+    shapes = [
+        jax.ShapeDtypeStruct((rows, units), jnp.bfloat16),
+        jax.ShapeDtypeStruct((rows, width), jnp.bfloat16),
+    ]
+    if on_line:
+        shapes.append(jax.ShapeDtypeStruct((rows, width), jnp.bfloat16))
+    return pl.pallas_call(
+        functools.partial(hidden_kernel, places, len(pieces), on_line),
+        out_shape=shapes,
+        in_specs=[SMEM] + [VMEM] * (len(pieces) + 6),
+        out_specs=[VMEM] * len(shapes),
+        scratch_shapes=[pltpu.VMEM((rows, w_out.shape[0]), jnp.bfloat16)],
+        compiler_params=params(24),
+        cost_estimate=cost(6 * rows * features * units, 10 << 20),
+        name="hidden",
+    )(place, *pieces, tokens, gain, w_out, w_gate, w_up, w_down)
+
+
+def down_kernel(place_ref, hidden, kept, w_down, far, to_right, to_left, own):
+    place = place_ref[0]
+    width = own.shape[1]
 
     def product(index):
-        return dot_f32(hidden, w_down[:, pl.ds(pl.multiple_of(index * width, width), width)])
-
-    far, to_right, to_left, toward_end, own = outs
+        weights = w_down[:, pl.ds(pl.multiple_of(index * width, width), width)]
+        return dot_f32(hidden[...], weights)
+
     far[...] = product(lax.rem(place + 2, 4))
-    right = product(lax.rem(place + 1, 4)).astype(jnp.bfloat16)
-    left = product(lax.rem(place + 3, 4)).astype(jnp.bfloat16)
-    to_right[...] = right
-    to_left[...] = left
-    toward_end[...] = jnp.where(place == 3, right, left)
-    own[...] = product(place) + kept.astype(jnp.float32)
-
-
-def feed_share(place, pieces, tokens, gain, w_out, w_gate, w_up, w_down, part, parts):
-    places = lax.axis_size("tp")
-    rows, features = tokens.shape[0] // parts, tokens.shape[1]
-    width = features // places
-    on_line = places == 4
-    if on_line:
-        kinds = [jnp.float32, jnp.bfloat16, jnp.bfloat16, jnp.bfloat16, jnp.float32]
-        shapes = [jax.ShapeDtypeStruct((rows, width), kind) for kind in kinds]
-    else:
-        shapes = [
-            jax.ShapeDtypeStruct((rows, features), jnp.bfloat16),
-            jax.ShapeDtypeStruct((rows, width), jnp.float32),
-        ]
-
-    def rows_of(array):
-        return pl.BlockSpec((rows, array.shape[1]), lambda i: (part, 0))
-
-    def whole(array):
-        return pl.BlockSpec(array.shape, lambda i: (0,) * array.ndim)
-
-    weights = [gain, w_out, w_gate, w_up, w_down]
+    to_right[...] = product(lax.rem(place + 1, 4)).astype(jnp.bfloat16)
+    to_left[...] = product(lax.rem(place + 3, 4)).astype(jnp.bfloat16)
+    own[...] = product(place) + kept[...].astype(jnp.float32)
+
+
+def down_blocks(place, hidden, kept, w_down):
+    rows, width = kept.shape
+    kinds = [jnp.float32, jnp.bfloat16, jnp.bfloat16, jnp.float32]
     return pl.pallas_call(
-        functools.partial(feed_kernel, places, len(pieces), on_line),
-        grid=(1,),
-        out_shape=shapes,
-        in_specs=[SMEM]
-        + [rows_of(piece) for piece in pieces]
-        + [rows_of(tokens)]
-        + [whole(weight) for weight in weights],
-        out_specs=[whole(shape) for shape in shapes],
-        scratch_shapes=[pltpu.VMEM((rows, places * pieces[0].shape[1]), jnp.bfloat16)],
-        compiler_params=params(28),
-        cost_estimate=cost(6 * rows * features * w_gate.shape[1], 10 << 20),
-        name="feed",
-    )(place, *pieces, tokens, *weights)
+        down_kernel,
+        out_shape=[jax.ShapeDtypeStruct((rows, width), kind) for kind in kinds],
+        in_specs=[SMEM, VMEM, VMEM, VMEM],
+        out_specs=[VMEM] * 4,
+        compiler_params=params(12),
+        cost_estimate=cost(2 * rows * w_down.shape[0] * width * 4, 5 << 20),
+        name="down_blocks",
+    )(place, hidden, kept, w_down)
+
+
+def add_kernel(*refs):
+    total = refs[0][...].astype(jnp.float32)
+    for ref in refs[1:-1]:
+        total = total + ref[...].astype(jnp.float32)
+    refs[-1][...] = total.astype(jnp.bfloat16)
+
+
+def add_up(*terms):
+    return pl.pallas_call(
+        add_kernel,
+        out_shape=jax.ShapeDtypeStruct(terms[0].shape, jnp.bfloat16),
+        in_specs=[VMEM] * len(terms),
+        out_specs=VMEM,
+        compiler_params=params(6),
+        cost_estimate=cost(terms[0].size * len(terms), 4 * terms[0].size * len(terms)),
+        name="add_up",
+    )(*terms)
 
 
 def feed_forward(place, pieces, tokens, gain, w_out, w_gate, w_up, w_down):
-    parts = 2
-    mixed = []
-    for part in range(parts):
-        outs = feed_share(place, pieces, tokens, gain, w_out, w_gate, w_up, w_down, part, parts)
-        if lax.axis_size("tp") != 4:
-            share = lax.psum_scatter(outs[0], "tp", scatter_dimension=1, tiled=True)
-            mixed.append((outs[1] + share.astype(jnp.float32)).astype(jnp.bfloat16))
-            continue
-        far, to_right, to_left, toward_end, own = outs
-        from_end = lax.ppermute(toward_end, "tp", [(3, 2), (0, 1)])
-        from_left = lax.ppermute(to_right, "tp", [(0, 1), (1, 2), (2, 3)])
-        from_right = lax.ppermute(to_left, "tp", [(3, 2), (2, 1), (1, 0)])
-        joined = (far + from_end.astype(jnp.float32)).astype(jnp.bfloat16)
-        from_far = lax.ppermute(joined, "tp", [(0, 2), (1, 3), (2, 0), (3, 1)])
-        arrived = from_left.astype(jnp.float32) + from_right.astype(jnp.float32)
-        mixed.append((own + arrived + from_far.astype(jnp.float32)).astype(jnp.bfloat16))
-    return jnp.concatenate(mixed, axis=0)
+    outs = hidden_of(place, pieces, tokens, gain, w_out, w_gate, w_up, w_down)
+    hidden, kept = outs[:2]
+    if lax.axis_size("tp") != 4:
+        share = lax.psum_scatter(
+            dot_f32(hidden, w_down).astype(jnp.bfloat16), "tp", scatter_dimension=1, tiled=True
+        )
+        return add_up(kept, share), hidden
+    from_end = lax.ppermute(outs[2], "tp", [(3, 2), (0, 1)])
+    far, to_right, to_left, own = down_blocks(place, hidden, kept, w_down)
+    from_left = lax.ppermute(to_right, "tp", [(0, 1), (1, 2), (2, 3)])
+    from_right = lax.ppermute(to_left, "tp", [(3, 2), (2, 1), (1, 0)])
+    joined = add_up(far, from_end)
+    from_far = lax.ppermute(joined, "tp", [(0, 2), (1, 3), (2, 0), (3, 1)])
+    return add_up(own, from_left, from_right, from_far), joined
 
 
 def rope_tables(positions, width):
@@ -492,19 +539,6 @@
         jnp.concatenate([cosine, cosine] * heads, axis=1),
         jnp.concatenate([-sine, sine] * heads, axis=1),
     )
-
-
-def gather_w_out(w_out, variate, me, devices):
-    columns = w_out.shape[1] // devices
-    block = lax.dynamic_slice_in_dim(w_out, me * columns, columns, 1)
-    block = lax.all_gather(block, "tp", axis=0, tiled=True)
-    extra = variate.astype(jnp.bfloat16).reshape(-1, columns)
-    height = block.shape[0]
-    pad = -extra.shape[0] % 16
-    block = jnp.concatenate([block, jnp.pad(extra, ((0, pad), (0, 0)))], axis=0)
-    blocks = lax.all_gather(block, "seq", axis=0)
-    variates = blocks[:, height : height + extra.shape[0], :]
-    return blocks, variates.reshape(-1).astype(jnp.int32)
 
 
 def segment_of(index, request_ends):
@@ -538,36 +572,33 @@
     reach = devices // 2
 
     pieces = gather_pieces(tokens)
-    w_out_all, all_variates = gather_w_out(w_out, variate, me, devices)
-
     cosine, sine = rope_tables(positions, width)
     ends = running_sum(lengths)
     row_first = me * rows
     segment = segment_of(row_first + jnp.arange(rows, dtype=jnp.int32), ends)
     query_marks = bias_marks(variate, segment, var_bias, requests)
-    all_index = jnp.arange(rows * devices, dtype=jnp.int32)
-    key_marks = key_marks_of(all_variates, segment_of(all_index, ends), requests)
     request_start = jnp.sum(jnp.where(ends <= row_first, lengths, 0))
-    info = jnp.stack([me, me - request_start // rows]).astype(jnp.int32)
+    info = jnp.concatenate([jnp.stack([me, me - request_start // rows]), ends]).astype(jnp.int32)
     first_token, amounts = page_sources(lengths, page_table, me, devices)
+    extra = extra_rows(variate, 2 * width)
+    gains = gain_attn.reshape(1, -1), gain_ffn.reshape(1, -1)
+
+    ready = (pieces[-1], w_out, cosine, sine, query_marks, info, first_token, amounts, extra, gains)
+    ready = lax.optimization_barrier(ready)
+    pieces[-1], w_out, cosine, sine, query_marks, info, first_token, amounts, extra, gains = ready
+    w_out_all = lax.all_gather(w_out, "tp", axis=0, tiled=True)
 
     token_rows, queries, pairs = project(
-        pieces, place, gain_attn.reshape(1, -1), w_query, w_key, w_value, cosine, sine
+        pieces, place, gains[0], w_query, w_key, w_value, cosine, sine, extra
     )
     row_pieces = seq_pieces(pairs)
-    attended = attend(info, queries, query_marks, key_marks, row_pieces, heads, reach)
+    attended = attend(info, queries, query_marks, row_pieces, heads, reach, requests)
     attended_pieces = turn_gather(attended)
-    cache = fill_cache(me.reshape(1), first_token, amounts, row_pieces)
-    mixed = feed_forward(
-        place,
-        attended_pieces,
-        token_rows,
-        gain_ffn.reshape(1, -1),
-        w_out_all,
-        w_gate,
-        w_up,
-        w_down,
+    cache = fill_cache(me.reshape(1), first_token, amounts, row_pieces, rows)
+    mixed, joined = feed_forward(
+        place, attended_pieces, token_rows, gains[1], w_out_all, w_gate, w_up, w_down
     )
+    cache, _ = lax.optimization_barrier((cache, joined))
     return (mixed, cache.reshape(cache.shape[0], 2, width))
 
 

time: 154 us -> 131 us (0.85)
  waiting for transfers between devices: 25.7 us -> 53.9 us
  blocking collectives: 21.4 us -> 0 us
  starting transfers between devices: 39.5 us -> 26.5 us
  local copies, waits for them, and re-layouts: 20.5 us -> 9.54 us
  other arithmetic: 12.8 us -> 6.5 us
  Pallas kernels: 14.6 us -> 16.7 us
    all_gather x1 -> x0, blocking collectives: 21.4 us -> none  [gather_w_out(): block = lax.all_gather(block, 'tp', axis=0, tiled=True)]
    unnamed x80 -> x26, local copies, waits for them, and re-layouts: 17.5 us -> 8.21 us
    ppermute x2 -> x1, starting transfers between devices: 9.3 us -> 1.29 us  [feed_forward(): from_left = lax.ppermute(to_right, 'tp', [(0, 1), (1, 2), (2, 3)])]
    ppermute x3, waiting for transfers between devices: 0.01 us -> 7.44 us  [turn_gather(): lax.ppermute(shard, 'tp', [(i, (i + turn) % count) for i in range(count)])]
    ppermute x1, waiting for transfers between devices: 0.01 us -> 6.99 us  [line_gather(): right = lax.ppermute(shard, 'tp', [(3, 2), (2, 1), (1, 0)])]
    ppermute x7, waiting for transfers between devices: 8.39 us -> 11.4 us  [seq_xor(): lax.ppermute(value, 'seq', [(i, i ^ mask) for i in range(lax.axis_size('s...]
    ppermute x1, waiting for transfers between devices: 0.01 us -> 2.66 us  [line_gather(): far = lax.ppermute(shard, 'tp', [(0, 2), (1, 3), (2, 0), (3, 1)])]
    ppermute x1, waiting for transfers between devices: 0.01 us -> 2.58 us  [line_gather(): left = lax.ppermute(shard, 'tp', [(0, 1), (1, 2), (2, 3)])]
  transfers between devices with their start and end apart: 23 -> 19, of which waited for: 6 -> 14; matrix products, arithmetic and copies ran while one was open for 10% -> 6% of each run, Pallas kernels for 5% -> 9%
where the time goes in v3:
time: 131 us; the launch traced here: 130 us
  waiting for transfers between devices  53.9 us (41%)
  starting transfers between devices  26.5 us (20%)
  between operations  16.9 us (13%)
  Pallas kernels  16.7 us (13%)
  local copies, waits for them, and re-layouts  9.54 us (7%)
  other arithmetic  6.5 us (5%)
    ppermute x1, waiting for transfers between devices, feed_forward(): from_far = lax.ppermute(joined, 'tp', [(0, 2), (1, 3), (2, 0), (3, 1)])  11.5 us
    ppermute x7, waiting for transfers between devices, seq_xor(): lax.ppermute(value, 'seq', [(i, i ^ mask) for i in range(lax.axis_size('s...  11.4 us
    unnamed x26, local copies, waits for them, and re-layouts  8.21 us
    ppermute x1, waiting for transfers between devices, line_gather(): ends = lax.ppermute(far, 'tp', [(2, 3), (1, 0)])  7.57 us
    ppermute x3, waiting for transfers between devices, turn_gather(): lax.ppermute(shard, 'tp', [(i, (i + turn) % count) for i in range(count)])  7.44 us
    ppermute x1, waiting for transfers between devices, line_gather(): right = lax.ppermute(shard, 'tp', [(3, 2), (2, 1), (1, 0)])  6.99 us
    ppermute x3, starting transfers between devices, turn_gather(): lax.ppermute(shard, 'tp', [(i, (i + turn) % count) for i in range(count)])  6.39 us
    ppermute x1, starting transfers between devices, feed_forward(): from_end = lax.ppermute(outs[2], 'tp', [(3, 2), (0, 1)])  5.28 us
  transfers between devices with their start and end apart: 19, of which 14 were waited for; matrix products, arithmetic and copies ran while one was open for 6% of the time, Pallas kernels for 9%

profile of v3, /device:TPU:2, one launch (start us, length us, event | category | flops | bytes accessed | tf_op | source)
XLA Modules:
  0.0 130.1 jit_solution(15831351662848204361)
XLA Ops:
  7.3 2.7 %collective-permute-start = (bf16[512,256]{1,0:T(8,128)(2,1)}, bf16[512,256]{1,0:T(8,128)(2,1)S(1)}, u32[]{:S(2)}, u32[]{:S(2)}) collective-permute-start(bf16[512,256]{1,0:T(8,128)(2,1)} %refs_0_.1), channel_id=1, source_target_pairs={{0,2},{1,3},{2,0},{3,1},{4,6},{5,7},{6,4},{7,5},{8,10},{9,11},{10,... | collective-permute-start | bytes 786440 | tf_op jit(solution)/shard_map/ppermute | solution.py:40
  10.0 0.8 select_reduce_fusion.4
  10.7 1.3 fusion.5
  12.3 0.7 reduce-precision_bitcast_fusion.1
  13.5 0.7 convert_element_type.14
  14.2 0.8 select_reduce_fusion
  15.1 1.0 fusion
  16.1 0.5 pad_maximum_fusion
  19.5 2.7 %collective-permute-done.refs_3_ = bf16[512,256]{1,0:T(8,128)(2,1)S(1)} collective-permute-done((bf16[512,256]{1,0:T(8,128)(2,1)}, bf16[512,256]{1,0:T(8,128)(2,1)S(1)}, u32[]{:S(2)}, u32[]{:S(2)}) %collective-permute-start) | collective-permute-done | bytes 262176 | tf_op jit(solution)/shard_map/ppermute | solution.py:40
  22.1 1.3 collective-permute-start.1
  23.6 7.6 %collective-permute-done.1.refs_4_ = bf16[512,256]{1,0:T(8,128)(2,1)S(1)} collective-permute-done((bf16[512,256]{1,0:T(8,128)(2,1)S(1)}, bf16[512,256]{1,0:T(8,128)(2,1)S(1)}, u32[]{:S(2)}, u32[]{:S(2)}) %collective-permute-start.1) | collective-permute-done | bytes 262176 | tf_op jit(solution)/shard_map/ppermute | solution.py:43
  31.2 1.5 %collective-permute-start.2 = (bf16[512,256]{1,0:T(8,128)(2,1)S(1)}, bf16[512,256]{1,0:T(8,128)(2,1)S(1)}, u32[]{:S(2)}, u32[]{:S(2)}) collective-permute-start(bf16[512,256]{1,0:T(8,128)(2,1)S(1)} %copy-done), channel_id=1, source_target_pairs={{0,1},{1,2},{2,3},{4,5},{5,6},{6,7},{8,9},{9,10},{10,11},{12,13},{... | collective-permute-start | bytes 786440 | tf_op jit(solution)/shard_map/ppermute | solution.py:41
  32.7 1.3 collective-permute-start.3
  34.0 2.6 %collective-permute-done.2.refs_1_ = bf16[512,256]{1,0:T(8,128)(2,1)S(1)} collective-permute-done((bf16[512,256]{1,0:T(8,128)(2,1)S(1)}, bf16[512,256]{1,0:T(8,128)(2,1)S(1)}, u32[]{:S(2)}, u32[]{:S(2)}) %collective-permute-start.2) | collective-permute-done | bytes 262176 | tf_op jit(solution)/shard_map/ppermute | solution.py:41
  36.6 7.0 %collective-permute-done.3.refs_2_ = bf16[512,256]{1,0:T(8,128)(2,1)S(1)} collective-permute-done((bf16[512,256]{1,0:T(8,128)(2,1)S(1)}, bf16[512,256]{1,0:T(8,128)(2,1)S(1)}, u32[]{:S(2)}, u32[]{:S(2)}) %collective-permute-start.3) | collective-permute-done | bytes 262176 | tf_op jit(solution)/shard_map/ppermute | solution.py:42
  43.6 1.4 %project.1 = (bf16[512,1024]{1,0:T(8,128)(2,1)S(1)}, bf16[512,128]{1,0:T(8,128)(2,1)S(1)}, bf16[528,256]{1,0:T(8,128)(2,1)S(1)}) custom-call(s32[1]{0:T(128)} %bitcast.place_ref, bf16[512,256]{1,0:T(8,128)(2,1)S(1)} %copy-done, bf16[512,256]{1,0:T(8,128)(2,1)S(1)} %collective-permute-done.2.refs_1_, bf16[512,256]{1,0:T(8,128)(2,1)S(1)} %collective-permute-done.3.refs_2_, ...), custom_call_target="tpu_custom_call" | custom-call | flops 402653184 | bytes 4194304 | tf_op jit(solution)/shard_map/project/pallas_call | solution.py:118
  45.0 1.0 copy-done.8
  45.9 1.5 %collective-permute-start.9 = (bf16[528,256]{1,0:T(8,128)(2,1)S(1)}, bf16[528,256]{1,0:T(8,128)(2,1)S(1)}, u32[]{:S(2)}, u32[]{:S(2)}) collective-permute-start(bf16[528,256]{1,0:T(8,128)(2,1)S(1)} %get-tuple-element.32.refs_0_), channel_id=1, source_target_pairs={{0,24},{4,28},{8,16},{12,20},{16,8},{20,12},{24,0},{28,4},{1,25},{... | collective-permute-start | bytes 811016 | tf_op jit(solution)/shard_map/ppermute | solution.py:134
  47.4 1.5 %collective-permute-start.5 = (bf16[528,256]{1,0:T(8,128)(2,1)S(1)}, bf16[528,256]{1,0:T(8,128)(2,1)S(1)}, u32[]{:S(2)}, u32[]{:S(2)}) collective-permute-start(bf16[528,256]{1,0:T(8,128)(2,1)S(1)} %get-tuple-element.32.refs_0_), channel_id=1, source_target_pairs={{0,8},{4,12},{8,0},{12,4},{16,24},{20,28},{24,16},{28,20},{1,9},{5... | collective-permute-start | bytes 811016 | tf_op jit(solution)/shard_map/ppermute | solution.py:134
  48.9 0.5 collective-permute-start.7
  49.4 6.8 %collective-permute-done.9.refs_6_ = bf16[528,256]{1,0:T(8,128)(2,1)S(1)} collective-permute-done((bf16[528,256]{1,0:T(8,128)(2,1)S(1)}, bf16[528,256]{1,0:T(8,128)(2,1)S(1)}, u32[]{:S(2)}, u32[]{:S(2)}) %collective-permute-start.9) | collective-permute-done | bytes 270368 | tf_op jit(solution)/shard_map/ppermute | solution.py:134
  56.2 3.1 %collective-permute-done.5.refs_2_ = bf16[528,256]{1,0:T(8,128)(2,1)S(1)} collective-permute-done((bf16[528,256]{1,0:T(8,128)(2,1)S(1)}, bf16[528,256]{1,0:T(8,128)(2,1)S(1)}, u32[]{:S(2)}, u32[]{:S(2)}) %collective-permute-start.5) | collective-permute-done | bytes 270368 | tf_op jit(solution)/shard_map/ppermute | solution.py:134
  59.4 0.5 collective-permute-start.8
  59.9 1.0 collective-permute-done.6.refs_3_
  61.3 4.7 %attend.1.refs_0_ = bf16[512,128]{1,0:T(8,128)(2,1)S(1)} custom-call(s32[6]{0:T(128)S(1)} %pad_add_fusion.info, bf16[512,128]{1,0:T(8,128)(2,1)S(1)} %get-tuple-element.30.queries, bf16[2,512,128]{2,1,0:T(8,128)(2,1)S(1)} %select_select_fusion.query_marks, bf16[528,256]{1,0:T(8,128)(2,1)S(1)} %get-tuple-element.32.refs_0_, ...), custom_call_target="tpu_custom_call" | custom-call | flops 2684354560 | bytes 4194304 | tf_op jit(solution)/shard_map/attend/pallas_call | solution.py:278
  66.0 2.6 %collective-permute-start.11 = (bf16[512,128]{1,0:T(8,128)(2,1)S(1)}, bf16[512,128]{1,0:T(8,128)(2,1)S(1)}, u32[]{:S(2)}, u32[]{:S(2)}) collective-permute-start(bf16[512,128]{1,0:T(8,128)(2,1)S(1)} %attend.1.refs_0_), channel_id=1, source_target_pairs={{0,1},{1,2},{2,3},{3,0},{4,5},{5,6},{6,7},{7,4},{8,9},{9,10},{10,1... | collective-permute-start | bytes 393224 | tf_op jit(solution)/shard_map/ppermute | solution.py:51
  68.6 1.0 collective-permute-start.12
  69.6 2.8 %collective-permute-start.13 = (bf16[512,128]{1,0:T(8,128)(2,1)S(1)}, bf16[512,128]{1,0:T(8,128)(2,1)S(1)}, u32[]{:S(2)}, u32[]{:S(2)}) collective-permute-start(bf16[512,128]{1,0:T(8,128)(2,1)S(1)} %attend.1.refs_0_), channel_id=1, source_target_pairs={{0,3},{1,0},{2,1},{3,2},{4,7},{5,4},{6,5},{7,6},{8,11},{9,8},{10,9... | collective-permute-start | bytes 393224 | tf_op jit(solution)/shard_map/ppermute | solution.py:51
  72.4 1.7 %collective-permute-done.11.refs_1_ = bf16[512,128]{1,0:T(8,128)(2,1)S(1)} collective-permute-done((bf16[512,128]{1,0:T(8,128)(2,1)S(1)}, bf16[512,128]{1,0:T(8,128)(2,1)S(1)}, u32[]{:S(2)}, u32[]{:S(2)}) %collective-permute-start.11) | collective-permute-done | bytes 131104 | tf_op jit(solution)/shard_map/ppermute | solution.py:51
  74.1 5.7 %collective-permute-done.12.refs_2_ = bf16[512,128]{1,0:T(8,128)(2,1)S(1)} collective-permute-done((bf16[512,128]{1,0:T(8,128)(2,1)S(1)}, bf16[512,128]{1,0:T(8,128)(2,1)S(1)}, u32[]{:S(2)}, u32[]{:S(2)}) %collective-permute-start.12) | collective-permute-done | bytes 131104 | tf_op jit(solution)/shard_map/ppermute | solution.py:51
  79.8 1.6 %copy-done.4 = bf16[1024,1024]{1,0:T(8,128)(2,1)S(1)} copy-done((bf16[1024,1024]{1,0:T(8,128)(2,1)S(1)}, bf16[1024,1024]{1,0:T(8,128)(2,1)}, u32[]{:S(2)}) %copy-start.4) | copy-done | bytes 2097176
  81.4 1.6 %copy-done.5 = bf16[1024,1024]{1,0:T(8,128)(2,1)S(1)} copy-done((bf16[1024,1024]{1,0:T(8,128)(2,1)S(1)}, bf16[1024,1024]{1,0:T(8,128)(2,1)}, u32[]{:S(2)}) %copy-start.5) | copy-done | bytes 2097176
  83.0 1.6 %copy-done.6 = bf16[1024,1024]{1,0:T(8,128)(2,1)S(1)} copy-done((bf16[1024,1024]{1,0:T(8,128)(2,1)S(1)}, bf16[1024,1024]{1,0:T(8,128)(2,1)}, u32[]{:S(2)}) %copy-start.6) | copy-done | bytes 2097176
  84.6 1.2 copy-done.7
  85.9 1.2 copy-done.9
  87.1 3.8 %hidden.1 = (bf16[512,1024]{1,0:T(8,128)(2,1)S(1)}, bf16[512,256]{1,0:T(8,128)(2,1)S(1)}, bf16[512,256]{1,0:T(8,128)(2,1)S(1)}) custom-call(s32[1]{0:T(128)} %bitcast.place_ref, bf16[512,128]{1,0:T(8,128)(2,1)S(1)} %attend.1.refs_0_, bf16[512,128]{1,0:T(8,128)(2,1)S(1)} %collective-permute-done.11.refs_1_, ...), custom_call_target="tpu_custom_call" | custom-call | flops 3221225472 | bytes 10485760 | tf_op jit(solution)/shard_map/hidden/pallas_call | solution.py:456
  90.9 5.3 %collective-permute-start.16 = (bf16[512,256]{1,0:T(8,128)(2,1)S(1)}, bf16[512,256]{1,0:T(8,128)(2,1)S(1)}, u32[]{:S(2)}, u32[]{:S(2)}) collective-permute-start(bf16[512,256]{1,0:T(8,128)(2,1)S(1)} %get-tuple-element.42), channel_id=1, source_target_pairs={{3,2},{0,1},{7,6},{4,5},{11,10},{8,9},{15,14},{12,13},{19,18},{16,... | collective-permute-start | bytes 786440 | tf_op jit(solution)/shard_map/ppermute | solution.py:523
  96.2 2.0 %down_blocks.1 = (f32[512,256]{1,0:T(8,128)S(1)}, bf16[512,256]{1,0:T(8,128)(2,1)}, bf16[512,256]{1,0:T(8,128)(2,1)}, f32[512,256]{1,0:T(8,128)S(1)}) custom-call(s32[1]{0:T(128)} %bitcast.place_ref, bf16[512,1024]{1,0:T(8,128)(2,1)S(1)} %get-tuple-element.36.hidden, bf16[512,256]{1,0:T(8,128)(2,1)S(1)} %get-tuple-element.37.kept, ...), custom_call_target="tpu_custom_call" | custom-call | flops 1073741824 | bytes 5242880 | tf_op jit(solution)/shard_map/down_blocks/pallas_call | solution.py:485
  98.2 1.3 collective-permute-start.14
  99.5 1.3 collective-permute-start.15
  100.8 2.1 %collective-permute-done.16.refs_1_ = bf16[512,256]{1,0:T(8,128)(2,1)S(1)} collective-permute-done((bf16[512,256]{1,0:T(8,128)(2,1)S(1)}, bf16[512,256]{1,0:T(8,128)(2,1)S(1)}, u32[]{:S(2)}, u32[]{:S(2)}) %collective-permute-start.16) | collective-permute-done | bytes 262176 | tf_op jit(solution)/shard_map/ppermute | solution.py:523
  102.8 0.7 add_up.2
  103.6 1.5 %collective-permute-start.17 = (bf16[512,256]{1,0:T(8,128)(2,1)}, bf16[512,256]{1,0:T(8,128)(2,1)}, u32[]{:S(2)}, u32[]{:S(2)}) collective-permute-start(bf16[512,256]{1,0:T(8,128)(2,1)} %add_up.2), channel_id=1, source_target_pairs={{0,2},{1,3},{2,0},{3,1},{4,6},{5,7},{6,4},{7,5},{8,10},{9,11},{10,... | collective-permute-start | bytes 786440 | tf_op jit(solution)/shard_map/ppermute | solution.py:528
  105.1 2.3 %fill_cache.1 = bf16[576,256]{1,0:T(8,128)(2,1)S(1)} custom-call(s32[1]{0:T(128)} %bitcast.6.me_ref, s32[9]{0:T(128)S(1)} %get-tuple-element.43.first_token, s32[9]{0:T(128)S(1)} %get-tuple-element.44.amounts, bf16[528,256]{1,0:T(8,128)(2,1)S(1)} %get-tuple-element.32.refs_0_, bf16[528,256]{1,0:T(8,128)(2,1)S(1)} %collective-permute-done.4.refs_1_, ...), custom_call_target="tpu_custom_call" | custom-call | flops 75497472 | bytes 3145728 | tf_op jit(solution)/shard_map/fill_cache/pallas_call | solution.py:373
  107.4 0.8 reshape.152
  108.6 1.4 %collective-permute-done.15.refs_2_ = bf16[512,256]{1,0:T(8,128)(2,1)S(1)} collective-permute-done((bf16[512,256]{1,0:T(8,128)(2,1)}, bf16[512,256]{1,0:T(8,128)(2,1)S(1)}, u32[]{:S(2)}, u32[]{:S(2)}) %collective-permute-start.15) | collective-permute-done | bytes 262176 | tf_op jit(solution)/shard_map/ppermute | solution.py:526
  110.0 11.5 %collective-permute-done.17.refs_3_ = bf16[512,256]{1,0:T(8,128)(2,1)} collective-permute-done((bf16[512,256]{1,0:T(8,128)(2,1)}, bf16[512,256]{1,0:T(8,128)(2,1)}, u32[]{:S(2)}, u32[]{:S(2)}) %collective-permute-start.17) | collective-permute-done | bytes 262176 | tf_op jit(solution)/shard_map/ppermute | solution.py:528
  121.5 1.8 %add_up.3 = bf16[512,256]{1,0:T(8,128)(2,1)} custom-call(f32[512,256]{1,0:T(8,128)S(1)} %get-tuple-element.38.refs_0_, bf16[512,256]{1,0:T(8,128)(2,1)S(1)} %collective-permute-done.14.refs_1_, bf16[512,256]{1,0:T(8,128)(2,1)S(1)} %collective-permute-done.15.refs_2_, bf16[512,256]{1,0:T(8,128)(2,1)} %collective-permute-done.17.refs_3_), custom_call_target="tpu_custom_call" | custom-call | flops 524288 | bytes 2097152 | tf_op jit(solution)/shard_map/add_up/pallas_call | solution.py:504
  (57 shorter events, 2.1 us)
Async XLA Ops:
  7.2 24.1 %copy-start = (bf16[512,256]{1,0:T(8,128)(2,1)S(1)}, bf16[512,256]{1,0:T(8,128)(2,1)}, u32[]{:S(2)}) copy-start(bf16[512,256]{1,0:T(8,128)(2,1)} %refs_0_.1) | copy-start | bytes 786436
  7.2 12.1 %copy-start.10 = (s32[512]{0:T(512)S(1)}, s32[512]{0:T(512)}, u32[]{:S(2)}) copy-start(s32[512]{0:T(512)} %param.16) | copy-start | bytes 6148
  7.2 16.3 %copy-start.11 = (bf16[1024]{0:T(1024)(128)(2,1)S(1)}, bf16[1024]{0:T(1024)(128)(2,1)}, u32[]{:S(2)}) copy-start(bf16[1024]{0:T(1024)(128)(2,1)} %param.20) | copy-start | bytes 6148
  7.2 16.3 %copy-start.12 = (bf16[1024]{0:T(1024)(128)(2,1)S(1)}, bf16[1024]{0:T(1024)(128)(2,1)}, u32[]{:S(2)}) copy-start(bf16[1024]{0:T(1024)(128)(2,1)} %param.26) | copy-start | bytes 6148
  7.2 36.4 %copy-start.1 = (bf16[1024,128]{1,0:T(8,128)(2,1)S(1)}, bf16[1024,128]{1,0:T(8,128)(2,1)}, u32[]{:S(2)}) copy-start(bf16[1024,128]{1,0:T(8,128)(2,1)} %refs_6_.1) | copy-start | bytes 786436
  7.2 36.4 %copy-start.2 = (bf16[1024,128]{1,0:T(8,128)(2,1)S(1)}, bf16[1024,128]{1,0:T(8,128)(2,1)}, u32[]{:S(2)}) copy-start(bf16[1024,128]{1,0:T(8,128)(2,1)} %refs_7_.2) | copy-start | bytes 786436
  7.2 36.4 %copy-start.3 = (bf16[1024,128]{1,0:T(8,128)(2,1)S(1)}, bf16[1024,128]{1,0:T(8,128)(2,1)}, u32[]{:S(2)}) copy-start(bf16[1024,128]{1,0:T(8,128)(2,1)} %refs_8_.2) | copy-start | bytes 786436
  7.2 72.6 %all-gather.2.cloned.1.call-start = ((), (), s32[]{:S(2)}) async-start(), calls=%async_computation | async-start | bytes 1310720 | tf_op jit(solution)/shard_map/all_gather | solution.py:589
  7.3 14.8 %collective-permute-start = (bf16[512,256]{1,0:T(8,128)(2,1)}, bf16[512,256]{1,0:T(8,128)(2,1)S(1)}, u32[]{:S(2)}, u32[]{:S(2)}) collective-permute-start(bf16[512,256]{1,0:T(8,128)(2,1)} %refs_0_.1), channel_id=1, source_target_pairs={{0,2},{1,3},{2,0},{3,1},{4,6},{5,7},{6,4},{7,5},{8,10},{9,11},{10,... | collective-permute-start | bytes 786440 | tf_op jit(solution)/shard_map/ppermute | solution.py:40
  22.1 9.1 %collective-permute-start.1 = (bf16[512,256]{1,0:T(8,128)(2,1)S(1)}, bf16[512,256]{1,0:T(8,128)(2,1)S(1)}, u32[]{:S(2)}, u32[]{:S(2)}) collective-permute-start(bf16[512,256]{1,0:T(8,128)(2,1)S(1)} %collective-permute-done.refs_3_), channel_id=1, source_target_pairs={{2,3},{1,0},{6,7},{5,4},{10,11},{9,8},{14,15},{13,12},{18,19},{17,... | collective-permute-start | bytes 786440 | tf_op jit(solution)/shard_map/ppermute | solution.py:43
  31.2 5.4 %collective-permute-start.2 = (bf16[512,256]{1,0:T(8,128)(2,1)S(1)}, bf16[512,256]{1,0:T(8,128)(2,1)S(1)}, u32[]{:S(2)}, u32[]{:S(2)}) collective-permute-start(bf16[512,256]{1,0:T(8,128)(2,1)S(1)} %copy-done), channel_id=1, source_target_pairs={{0,1},{1,2},{2,3},{4,5},{5,6},{6,7},{8,9},{9,10},{10,11},{12,13},{... | collective-permute-start | bytes 786440 | tf_op jit(solution)/shard_map/ppermute | solution.py:41
  32.7 10.9 %collective-permute-start.3 = (bf16[512,256]{1,0:T(8,128)(2,1)S(1)}, bf16[512,256]{1,0:T(8,128)(2,1)S(1)}, u32[]{:S(2)}, u32[]{:S(2)}) collective-permute-start(bf16[512,256]{1,0:T(8,128)(2,1)S(1)} %copy-done), channel_id=1, source_target_pairs={{3,2},{2,1},{1,0},{7,6},{6,5},{5,4},{11,10},{10,9},{9,8},{15,14},{... | collective-permute-start | bytes 786440 | tf_op jit(solution)/shard_map/ppermute | solution.py:42
  44.9 1.0 copy-start.8
  45.9 10.3 %collective-permute-start.9 = (bf16[528,256]{1,0:T(8,128)(2,1)S(1)}, bf16[528,256]{1,0:T(8,128)(2,1)S(1)}, u32[]{:S(2)}, u32[]{:S(2)}) collective-permute-start(bf16[528,256]{1,0:T(8,128)(2,1)S(1)} %get-tuple-element.32.refs_0_), channel_id=1, source_target_pairs={{0,24},{4,28},{8,16},{12,20},{16,8},{20,12},{24,0},{28,4},{1,25},{... | collective-permute-start | bytes 811016 | tf_op jit(solution)/shard_map/ppermute | solution.py:134
  47.4 11.9 %collective-permute-start.5 = (bf16[528,256]{1,0:T(8,128)(2,1)S(1)}, bf16[528,256]{1,0:T(8,128)(2,1)S(1)}, u32[]{:S(2)}, u32[]{:S(2)}) collective-permute-start(bf16[528,256]{1,0:T(8,128)(2,1)S(1)} %get-tuple-element.32.refs_0_), channel_id=1, source_target_pairs={{0,8},{4,12},{8,0},{12,4},{16,24},{20,28},{24,16},{28,20},{1,9},{5... | collective-permute-start | bytes 811016 | tf_op jit(solution)/shard_map/ppermute | solution.py:134
  48.9 10.5 %collective-permute-start.7 = (bf16[528,256]{1,0:T(8,128)(2,1)S(1)}, bf16[528,256]{1,0:T(8,128)(2,1)S(1)}, u32[]{:S(2)}, u32[]{:S(2)}) collective-permute-start(bf16[528,256]{1,0:T(8,128)(2,1)S(1)} %get-tuple-element.32.refs_0_), channel_id=1, source_target_pairs={{0,16},{4,20},{8,24},{12,28},{16,0},{20,4},{24,8},{28,12},{1,17},{... | collective-permute-start | bytes 811016 | tf_op jit(solution)/shard_map/ppermute | solution.py:134
  49.4 10.5 %collective-permute-start.4 = (bf16[528,256]{1,0:T(8,128)(2,1)S(1)}, bf16[528,256]{1,0:T(8,128)(2,1)S(1)}, u32[]{:S(2)}, u32[]{:S(2)}) collective-permute-start(bf16[528,256]{1,0:T(8,128)(2,1)S(1)} %get-tuple-element.32.refs_0_), channel_id=1, source_target_pairs={{0,4},{4,0},{8,12},{12,8},{16,20},{20,16},{24,28},{28,24},{1,5},{5... | collective-permute-start | bytes 811016 | tf_op jit(solution)/shard_map/ppermute | solution.py:134
  56.2 3.6 %collective-permute-start.10 = (bf16[528,256]{1,0:T(8,128)(2,1)S(1)}, bf16[528,256]{1,0:T(8,128)(2,1)S(1)}, u32[]{:S(2)}, u32[]{:S(2)}) collective-permute-start(bf16[528,256]{1,0:T(8,128)(2,1)S(1)} %collective-permute-done.9.refs_6_), channel_id=1, source_target_pairs={{0,4},{4,0},{8,12},{12,8},{16,20},{20,16},{24,28},{28,24},{1,5},{5... | collective-permute-start | bytes 811016 | tf_op jit(solution)/shard_map/ppermute | solution.py:134
  59.3 1.5 %collective-permute-start.6 = (bf16[528,256]{1,0:T(8,128)(2,1)S(1)}, bf16[528,256]{1,0:T(8,128)(2,1)S(1)}, u32[]{:S(2)}, u32[]{:S(2)}) collective-permute-start(bf16[528,256]{1,0:T(8,128)(2,1)S(1)} %collective-permute-done.5.refs_2_), channel_id=1, source_target_pairs={{0,4},{4,0},{8,12},{12,8},{16,20},{20,16},{24,28},{28,24},{1,5},{5... | collective-permute-start | bytes 811016 | tf_op jit(solution)/shard_map/ppermute | solution.py:134
  59.4 1.9 %collective-permute-start.8 = (bf16[528,256]{1,0:T(8,128)(2,1)S(1)}, bf16[528,256]{1,0:T(8,128)(2,1)S(1)}, u32[]{:S(2)}, u32[]{:S(2)}) collective-permute-start(bf16[528,256]{1,0:T(8,128)(2,1)S(1)} %collective-permute-done.7.refs_4_), channel_id=1, source_target_pairs={{0,4},{4,0},{8,12},{12,8},{16,20},{20,16},{24,28},{28,24},{1,5},{5... | collective-permute-start | bytes 811016 | tf_op jit(solution)/shard_map/ppermute | solution.py:134
  66.0 8.1 %collective-permute-start.11 = (bf16[512,128]{1,0:T(8,128)(2,1)S(1)}, bf16[512,128]{1,0:T(8,128)(2,1)S(1)}, u32[]{:S(2)}, u32[]{:S(2)}) collective-permute-start(bf16[512,128]{1,0:T(8,128)(2,1)S(1)} %attend.1.refs_0_), channel_id=1, source_target_pairs={{0,1},{1,2},{2,3},{3,0},{4,5},{5,6},{6,7},{7,4},{8,9},{9,10},{10,1... | collective-permute-start | bytes 393224 | tf_op jit(solution)/shard_map/ppermute | solution.py:51
  68.6 11.3 %collective-permute-start.12 = (bf16[512,128]{1,0:T(8,128)(2,1)S(1)}, bf16[512,128]{1,0:T(8,128)(2,1)S(1)}, u32[]{:S(2)}, u32[]{:S(2)}) collective-permute-start(bf16[512,128]{1,0:T(8,128)(2,1)S(1)} %attend.1.refs_0_), channel_id=1, source_target_pairs={{0,2},{1,3},{2,0},{3,1},{4,6},{5,7},{6,4},{7,5},{8,10},{9,11},{10,... | collective-permute-start | bytes 393224 | tf_op jit(solution)/shard_map/ppermute | solution.py:51
  69.6 10.3 %collective-permute-start.13 = (bf16[512,128]{1,0:T(8,128)(2,1)S(1)}, bf16[512,128]{1,0:T(8,128)(2,1)S(1)}, u32[]{:S(2)}, u32[]{:S(2)}) collective-permute-start(bf16[512,128]{1,0:T(8,128)(2,1)S(1)} %attend.1.refs_0_), channel_id=1, source_target_pairs={{0,3},{1,0},{2,1},{3,2},{4,7},{5,4},{6,5},{7,6},{8,11},{9,8},{10,9... | collective-permute-start | bytes 393224 | tf_op jit(solution)/shard_map/ppermute | solution.py:51
  79.8 1.6 %copy-start.4 = (bf16[1024,1024]{1,0:T(8,128)(2,1)S(1)}, bf16[1024,1024]{1,0:T(8,128)(2,1)}, u32[]{:S(2)}) copy-start(bf16[1024,1024]{1,0:T(8,128)(2,1)} %refs_7_.3) | copy-start | bytes 6291460
  81.4 1.6 %copy-start.5 = (bf16[1024,1024]{1,0:T(8,128)(2,1)S(1)}, bf16[1024,1024]{1,0:T(8,128)(2,1)}, u32[]{:S(2)}) copy-start(bf16[1024,1024]{1,0:T(8,128)(2,1)} %refs_8_.3) | copy-start | bytes 6291460
  83.0 1.6 %copy-start.6 = (bf16[1024,1024]{1,0:T(8,128)(2,1)S(1)}, bf16[1024,1024]{1,0:T(8,128)(2,1)}, u32[]{:S(2)}) copy-start(bf16[1024,1024]{1,0:T(8,128)(2,1)} %w_down.1) | copy-start | bytes 6291460
  84.6 1.2 copy-start.7
  85.8 1.2 copy-start.9
  90.9 11.9 %collective-permute-start.16 = (bf16[512,256]{1,0:T(8,128)(2,1)S(1)}, bf16[512,256]{1,0:T(8,128)(2,1)S(1)}, u32[]{:S(2)}, u32[]{:S(2)}) collective-permute-start(bf16[512,256]{1,0:T(8,128)(2,1)S(1)} %get-tuple-element.42), channel_id=1, source_target_pairs={{3,2},{0,1},{7,6},{4,5},{11,10},{8,9},{15,14},{12,13},{19,18},{16,... | collective-permute-start | bytes 786440 | tf_op jit(solution)/shard_map/ppermute | solution.py:523
  98.2 10.4 %collective-permute-start.14 = (bf16[512,256]{1,0:T(8,128)(2,1)}, bf16[512,256]{1,0:T(8,128)(2,1)S(1)}, u32[]{:S(2)}, u32[]{:S(2)}) collective-permute-start(bf16[512,256]{1,0:T(8,128)(2,1)} %get-tuple-element.39), channel_id=1, source_target_pairs={{0,1},{1,2},{2,3},{4,5},{5,6},{6,7},{8,9},{9,10},{10,11},{12,13},{... | collective-permute-start | bytes 786440 | tf_op jit(solution)/shard_map/ppermute | solution.py:525
  99.5 10.5 %collective-permute-start.15 = (bf16[512,256]{1,0:T(8,128)(2,1)}, bf16[512,256]{1,0:T(8,128)(2,1)S(1)}, u32[]{:S(2)}, u32[]{:S(2)}) collective-permute-start(bf16[512,256]{1,0:T(8,128)(2,1)} %get-tuple-element.40), channel_id=1, source_target_pairs={{3,2},{2,1},{1,0},{7,6},{6,5},{5,4},{11,10},{10,9},{9,8},{15,14},{... | collective-permute-start | bytes 786440 | tf_op jit(solution)/shard_map/ppermute | solution.py:526
  103.6 17.9 %collective-permute-start.17 = (bf16[512,256]{1,0:T(8,128)(2,1)}, bf16[512,256]{1,0:T(8,128)(2,1)}, u32[]{:S(2)}, u32[]{:S(2)}) collective-permute-start(bf16[512,256]{1,0:T(8,128)(2,1)} %add_up.2), channel_id=1, source_target_pairs={{0,2},{1,3},{2,0},{3,1},{4,6},{5,7},{6,4},{7,5},{8,10},{9,11},{10,... | collective-permute-start | bytes 786440 | tf_op jit(solution)/shard_map/ppermute | solution.py:528
Sparse Core Ops, SparseCore 0:
  31.3 30.6 all-gather.1

commit v4 on v3

--- a/solution.py
+++ b/solution.py
@@ -18,6 +18,7 @@
 VMEM = pl.BlockSpec(memory_space=pltpu.VMEM)
 SMEM = pl.BlockSpec(memory_space=pltpu.SMEM)
 ANY = pl.BlockSpec(memory_space=pl.ANY)
+HBM = pl.BlockSpec(memory_space=pltpu.HBM)
 
 
 def params(mib):
@@ -37,11 +38,13 @@
 
 
 def line_gather(shard):
-    far = lax.ppermute(shard, "tp", [(0, 2), (1, 3), (2, 0), (3, 1)])
+    half = shard.shape[0] // 2
+    two_away = [(0, 2), (1, 3), (2, 0), (3, 1)]
+    far = [lax.ppermute(part, "tp", two_away) for part in (shard[:half], shard[half:])]
     left = lax.ppermute(shard, "tp", [(0, 1), (1, 2), (2, 3)])
     right = lax.ppermute(shard, "tp", [(3, 2), (2, 1), (1, 0)])
-    ends = lax.ppermute(far, "tp", [(2, 3), (1, 0)])
-    return [shard, left, right, far, ends]
+    ends = [lax.ppermute(part, "tp", [(2, 3), (1, 0)]) for part in far]
+    return [shard, left, right] + far + ends
 
 
 def turn_gather(shard):
@@ -63,18 +66,22 @@
 def assemble(pieces, place, count, target):
     width = pieces[0].shape[1]
 
-    def put(block, value):
-        target[:, pl.ds(pl.multiple_of(block * width, width), width)] = value
+    def put(block, value, first=0):
+        columns = pl.ds(pl.multiple_of(block * width, width), width)
+        target[pl.ds(first, value.shape[0]), columns] = value
 
     if len(pieces) == count:
         for turn, piece in enumerate(pieces):
             put(lax.rem(place + count - turn, count), piece[...])
         return
-    own, left, right, far, ends = pieces
+    own, left, right = pieces[:3]
     put(place, own[...])
-    put(lax.rem(place + 2, 4), far[...])
-    put(lax.rem(place + 3, 4), jnp.where(place == 0, ends[...], left[...]))
-    put(lax.rem(place + 1, 4), jnp.where(place == 3, ends[...], right[...]))
+    half = own.shape[0] // 2
+    for first, far, ends in zip((0, half), pieces[3:5], pieces[5:]):
+        part = pl.ds(first, half)
+        put(lax.rem(place + 2, 4), far[...], first)
+        put(lax.rem(place + 3, 4), jnp.where(place == 0, ends[...], left[part, :]), first)
+        put(lax.rem(place + 1, 4), jnp.where(place == 3, ends[...], right[part, :]), first)
 
 
 def rotate_lanes(vectors, cosine, signed_sine):
@@ -93,9 +100,12 @@
 
 def project_kernel(places, count, place_ref, *refs):
     pieces = refs[:count]
-    gain, w_q, w_k, w_v, cosine, sine, extra, tokens, queries, pairs = refs[count:]
+    gain, w_q, w_k, w_v, cosine, sine, extra, tokens_out, queries, pairs = refs[count:-2]
+    tokens, sem = refs[-2:]
     pairs[tokens.shape[0] :, :] = extra[...]
     assemble(pieces, place_ref[0], places, tokens)
+    keep = pltpu.make_async_copy(tokens, tokens_out, sem)
+    keep.start()
     rows = tokens.shape[0]
     width = w_q.shape[1]
     step = min(rows, 256)
@@ -109,6 +119,7 @@
         key = rotate_lanes(dot_f32(normed, w_k[...]), cos_part, sin_part)
         pairs[part, :width] = key.astype(jnp.bfloat16)
         pairs[part, width:] = dot_f32(normed, w_v[...]).astype(jnp.bfloat16)
+    keep.wait()
 
 
 def project(pieces, place, gain, w_query, w_key, w_value, cosine, sine, extra):
@@ -123,8 +134,9 @@
             jax.ShapeDtypeStruct((rows + extra.shape[0], 2 * width), jnp.bfloat16),
         ],
         in_specs=[SMEM] + [VMEM] * (len(pieces) + 7),
-        out_specs=[VMEM] * 3,
-        compiler_params=params(12),
+        out_specs=[HBM, VMEM, VMEM],
+        scratch_shapes=[pltpu.VMEM((rows, features), jnp.bfloat16), pltpu.SemaphoreType.DMA],
+        compiler_params=params(6),
         cost_estimate=cost(6 * rows * features * width, 4 << 20),
         name="project",
     )(place, *pieces, gain, w_query, w_key, w_value, cosine, sine, extra)
@@ -290,7 +302,7 @@
             pltpu.VMEM((heads, rows, width + LANES), jnp.float32),
             pltpu.SemaphoreType.DMA((slots, 3)),
         ],
-        compiler_params=params(12 + 2 * slots),
+        compiler_params=params(8 + 2 * slots),
         cost_estimate=cost(
             4 * heads * rows * rows * slots * 256, 4 << 20, heads * rows * rows * slots
         ),
@@ -406,6 +418,31 @@
         jnp.sum(jnp.where(within, first, 0), axis=1),
         jnp.sum(jnp.where(within, amount, 0), axis=1),
     )
+
+
+def fetch_kernel(count, *refs):
+    sems = refs[-1]
+    loads = [
+        pltpu.make_async_copy(source, target, sems.at[i])
+        for i, (source, target) in enumerate(zip(refs[:count], refs[count:-1]))
+    ]
+    for load in loads:
+        load.start()
+    for load in loads:
+        load.wait()
+
+
+def fetch(arrays):
+    return pl.pallas_call(
+        functools.partial(fetch_kernel, len(arrays)),
+        out_shape=[jax.ShapeDtypeStruct(array.shape, array.dtype) for array in arrays],
+        in_specs=[HBM] * len(arrays),
+        out_specs=[VMEM] * len(arrays),
+        scratch_shapes=[pltpu.SemaphoreType.DMA((len(arrays),))],
+        compiler_params=params(10),
+        cost_estimate=cost(0, 4 * sum(array.size for array in arrays)),
+        name="fetch",
+    )(*arrays)
 
 
 def hidden_kernel(places, count, on_line, place_ref, *refs):
@@ -438,7 +475,9 @@
         return w_down[:, pl.ds(pl.multiple_of(index * width, width), width)]
 
     toward_end = jnp.where(place == 3, 0, jnp.where(place == 0, 3, place))
-    outs[2][...] = dot_f32(hidden[...], block(toward_end)).astype(jnp.bfloat16)
+    for out, first in zip(outs[2:], (0, rows // 2)):
+        part = pl.ds(first, rows // 2)
+        out[...] = dot_f32(hidden[part, :], block(toward_end)).astype(jnp.bfloat16)
 
 
 def hidden_of(place, pieces, tokens, gain, w_out, w_gate, w_up, w_down):
@@ -452,62 +491,73 @@
         jax.ShapeDtypeStruct((rows, width), jnp.bfloat16),
     ]
     if on_line:
-        shapes.append(jax.ShapeDtypeStruct((rows, width), jnp.bfloat16))
+        shapes += [jax.ShapeDtypeStruct((rows // 2, width), jnp.bfloat16)] * 2
     return pl.pallas_call(
         functools.partial(hidden_kernel, places, len(pieces), on_line),
         out_shape=shapes,
         in_specs=[SMEM] + [VMEM] * (len(pieces) + 6),
         out_specs=[VMEM] * len(shapes),
         scratch_shapes=[pltpu.VMEM((rows, w_out.shape[0]), jnp.bfloat16)],
-        compiler_params=params(24),
+        compiler_params=params(12),
         cost_estimate=cost(6 * rows * features * units, 10 << 20),
         name="hidden",
     )(place, *pieces, tokens, gain, w_out, w_gate, w_up, w_down)
 
 
-def down_kernel(place_ref, hidden, kept, w_down, far, to_right, to_left, own):
+def down_kernel(place_ref, hidden, kept, w_down, far_top, far_low, to_right, to_left, own):
     place = place_ref[0]
-    width = own.shape[1]
+    rows, width = own.shape
 
     def product(index):
         weights = w_down[:, pl.ds(pl.multiple_of(index * width, width), width)]
         return dot_f32(hidden[...], weights)
 
-    far[...] = product(lax.rem(place + 2, 4))
+    to_left[...] = product(lax.rem(place + 3, 4)).astype(jnp.bfloat16)
     to_right[...] = product(lax.rem(place + 1, 4)).astype(jnp.bfloat16)
-    to_left[...] = product(lax.rem(place + 3, 4)).astype(jnp.bfloat16)
+    far = product(lax.rem(place + 2, 4))
+    far_top[...] = far[: rows // 2]
+    far_low[...] = far[rows // 2 :]
     own[...] = product(place) + kept[...].astype(jnp.float32)
 
 
 def down_blocks(place, hidden, kept, w_down):
     rows, width = kept.shape
-    kinds = [jnp.float32, jnp.bfloat16, jnp.bfloat16, jnp.float32]
+    shapes = [((rows // 2, width), jnp.float32)] * 2
+    shapes += [((rows, width), jnp.bfloat16)] * 2 + [((rows, width), jnp.float32)]
     return pl.pallas_call(
         down_kernel,
-        out_shape=[jax.ShapeDtypeStruct((rows, width), kind) for kind in kinds],
+        out_shape=[jax.ShapeDtypeStruct(*shape) for shape in shapes],
         in_specs=[SMEM, VMEM, VMEM, VMEM],
-        out_specs=[VMEM] * 4,
-        compiler_params=params(12),
+        out_specs=[VMEM] * 5,
+        compiler_params=params(6),
         cost_estimate=cost(2 * rows * w_down.shape[0] * width * 4, 5 << 20),
         name="down_blocks",
     )(place, hidden, kept, w_down)
 
 
-def add_kernel(*refs):
-    total = refs[0][...].astype(jnp.float32)
-    for ref in refs[1:-1]:
-        total = total + ref[...].astype(jnp.float32)
-    refs[-1][...] = total.astype(jnp.bfloat16)
-
-
-def add_up(*terms):
+def add_kernel(out_parts, *refs):
+    whole, parts, out = refs[: -1 - out_parts], refs[-1 - out_parts : -1], refs[-1]
+    step = out.shape[0] // max(out_parts, 1)
+    for i, first in enumerate(range(0, out.shape[0], step)):
+        rows = pl.ds(first, step)
+        total = whole[0][rows, :].astype(jnp.float32)
+        for ref in whole[1:]:
+            total = total + ref[rows, :].astype(jnp.float32)
+        if out_parts:
+            total = total + parts[i][...].astype(jnp.float32)
+        out[rows, :] = total.astype(jnp.bfloat16)
+
+
+def add_up(whole, parts=()):
+    terms = [*whole, *parts]
+    size = whole[0].size
     return pl.pallas_call(
-        add_kernel,
-        out_shape=jax.ShapeDtypeStruct(terms[0].shape, jnp.bfloat16),
+        functools.partial(add_kernel, len(parts)),
+        out_shape=jax.ShapeDtypeStruct(whole[0].shape, jnp.bfloat16),
         in_specs=[VMEM] * len(terms),
         out_specs=VMEM,
         compiler_params=params(6),
-        cost_estimate=cost(terms[0].size * len(terms), 4 * terms[0].size * len(terms)),
+        cost_estimate=cost(size * len(terms), 4 * size * len(terms)),
         name="add_up",
     )(*terms)
 
@@ -519,14 +569,15 @@
         share = lax.psum_scatter(
             dot_f32(hidden, w_down).astype(jnp.bfloat16), "tp", scatter_dimension=1, tiled=True
         )
-        return add_up(kept, share), hidden
-    from_end = lax.ppermute(outs[2], "tp", [(3, 2), (0, 1)])
-    far, to_right, to_left, own = down_blocks(place, hidden, kept, w_down)
+        return add_up([kept, share]), hidden
+    from_end = [lax.ppermute(part, "tp", [(3, 2), (0, 1)]) for part in outs[2:]]
+    *far, to_right, to_left, own = down_blocks(place, hidden, kept, w_down)
+    from_right = lax.ppermute(to_left, "tp", [(3, 2), (2, 1), (1, 0)])
     from_left = lax.ppermute(to_right, "tp", [(0, 1), (1, 2), (2, 3)])
-    from_right = lax.ppermute(to_left, "tp", [(3, 2), (2, 1), (1, 0)])
-    joined = add_up(far, from_end)
-    from_far = lax.ppermute(joined, "tp", [(0, 2), (1, 3), (2, 0), (3, 1)])
-    return add_up(own, from_left, from_right, from_far), joined
+    two_away = [(0, 2), (1, 3), (2, 0), (3, 1)]
+    joined = [add_up([part, end]) for part, end in zip(far, from_end)]
+    from_far = [lax.ppermute(part, "tp", two_away) for part in joined]
+    return add_up([own, from_left, from_right], from_far), joined[-1]
 
 
 def rope_tables(positions, width):
@@ -583,9 +634,9 @@
     extra = extra_rows(variate, 2 * width)
     gains = gain_attn.reshape(1, -1), gain_ffn.reshape(1, -1)
 
-    ready = (pieces[-1], w_out, cosine, sine, query_marks, info, first_token, amounts, extra, gains)
+    ready = (pieces, w_out, cosine, sine, query_marks, info, first_token, amounts, extra, gains)
     ready = lax.optimization_barrier(ready)
-    pieces[-1], w_out, cosine, sine, query_marks, info, first_token, amounts, extra, gains = ready
+    pieces, w_out, cosine, sine, query_marks, info, first_token, amounts, extra, gains = ready
     w_out_all = lax.all_gather(w_out, "tp", axis=0, tiled=True)
 
     token_rows, queries, pairs = project(
@@ -595,6 +646,8 @@
     attended = attend(info, queries, query_marks, row_pieces, heads, reach, requests)
     attended_pieces = turn_gather(attended)
     cache = fill_cache(me.reshape(1), first_token, amounts, row_pieces, rows)
+    large = lax.optimization_barrier(((token_rows, w_out_all, w_gate, w_up, w_down), attended))[0]
+    token_rows, w_out_all, w_gate, w_up, w_down = fetch(large)
     mixed, joined = feed_forward(
         place, attended_pieces, token_rows, gains[1], w_out_all, w_gate, w_up, w_down
     )

time: 131 us -> 126 us (0.962)
  waiting for transfers between devices: 53.9 us -> 33.5 us
  local copies, waits for them, and re-layouts: 9.54 us -> 14.9 us
  starting transfers between devices: 26.5 us -> 31.4 us
  other arithmetic: 6.5 us -> 9.59 us
  Pallas kernels: 16.7 us -> 18.4 us
    ppermute x4 -> x8, waiting for transfers between devices: 23.8 us -> 15.8 us  [the longest x2 10.3 us: feed_forward(): from_far = [lax.ppermute(part, 'tp', two_away) for part in joined]]
    ppermute x1, waiting for transfers between devices: 6.99 us -> 0.01 us  [line_gather(): right = lax.ppermute(shard, 'tp', [(3, 2), (2, 1), (1, 0)])]
    ppermute x4 -> x8, starting transfers between devices: 10.8 us -> 15.8 us  [the longest x2 6.55 us: feed_forward(): from_end = [lax.ppermute(part, 'tp', [(3, 2), (0, 1)]) for part in outs[2:]]]
    ppermute x1, waiting for transfers between devices: 2.58 us -> 0.01 us  [line_gather(): left = lax.ppermute(shard, 'tp', [(0, 1), (1, 2), (2, 3)])]
    reshape x2, local copies, waits for them, and re-layouts: 0.01 us -> 2.55 us  [per_device(): gains = (gain_attn.reshape(1, -1), gain_ffn.reshape(1, -1))]
    ppermute x3, waiting for transfers between devices: 7.44 us -> 4.93 us  [turn_gather(): lax.ppermute(shard, 'tp', [(i, (i + turn) % count) for i in range(count)])]
    ppermute x3, starting transfers between devices: 6.39 us -> 4.01 us  [turn_gather(): lax.ppermute(shard, 'tp', [(i, (i + turn) % count) for i in range(count)])]
    ppermute x1, starting transfers between devices: 1.46 us -> 3.63 us  [line_gather(): left = lax.ppermute(shard, 'tp', [(0, 1), (1, 2), (2, 3)])]
  transfers between devices with their start and end apart: 19 -> 23, of which waited for: 14 -> 13; matrix products, arithmetic and copies ran while one was open for 6% -> 12% of each run, Pallas kernels for 9% -> 9%
where the time goes in v4:
time: 126 us; the launch traced here: 125 us
  waiting for transfers between devices  33.5 us (27%)
  starting transfers between devices  31.4 us (25%)
  Pallas kernels  18.4 us (15%)
  between operations  17.1 us (14%)
  local copies, waits for them, and re-layouts  14.9 us (12%)
  other arithmetic  9.59 us (8%)
    ppermute x7, waiting for transfers between devices, seq_xor(): lax.ppermute(value, 'seq', [(i, i ^ mask) for i in range(lax.axis_size('s...  10.7 us
    ppermute x2, waiting for transfers between devices, feed_forward(): from_far = [lax.ppermute(part, 'tp', two_away) for part in joined]  10.3 us
    unnamed x68, local copies, waits for them, and re-layouts  10.1 us
    ppermute x2, starting transfers between devices, feed_forward(): from_end = [lax.ppermute(part, 'tp', [(3, 2), (0, 1)]) for part in outs[2:]]  6.55 us
    ppermute x3, waiting for transfers between devices, turn_gather(): lax.ppermute(shard, 'tp', [(i, (i + turn) % count) for i in range(count)])  4.93 us
    pallas_call x1, Pallas kernels, hidden_of(): pl.pallas_call(functools.partial(hidden_kernel, places, len(pieces), on_l...  4.78 us
    pallas_call x1, Pallas kernels, attend(): pl.pallas_call(functools.partial(attend_kernel, len(pieces), heads, reach...  4.72 us
    ppermute x7, starting transfers between devices, seq_xor(): lax.ppermute(value, 'seq', [(i, i ^ mask) for i in range(lax.axis_size('s...  4.06 us
  transfers between devices with their start and end apart: 23, of which 13 were waited for; matrix products, arithmetic and copies ran while one was open for 12% of the time, Pallas kernels for 9%

profile of v4, /device:TPU:2, one launch (start us, length us, event | category | flops | bytes accessed | tf_op | source)
XLA Modules:
  0.0 125.0 jit_solution(156020401965704090)
XLA Ops:
  7.2 3.6 %collective-permute-start = (bf16[512,256]{1,0:T(8,128)(2,1)}, bf16[512,256]{1,0:T(8,128)(2,1)S(1)}, u32[]{:S(2)}, u32[]{:S(2)}) collective-permute-start(bf16[512,256]{1,0:T(8,128)(2,1)} %refs_0_), channel_id=1, source_target_pairs={{0,1},{1,2},{2,3},{4,5},{5,6},{6,7},{8,9},{9,10},{10,11},{12,13},{... | collective-permute-start | bytes 786440 | tf_op jit(solution)/shard_map/ppermute | solution.py:44
  10.9 1.3 %collective-permute-start.1 = (bf16[512,256]{1,0:T(8,128)(2,1)}, bf16[512,256]{1,0:T(8,128)(2,1)S(1)}, u32[]{:S(2)}, u32[]{:S(2)}) collective-permute-start(bf16[512,256]{1,0:T(8,128)(2,1)} %refs_0_), channel_id=1, source_target_pairs={{3,2},{2,1},{1,0},{7,6},{6,5},{5,4},{11,10},{10,9},{9,8},{15,14},{... | collective-permute-start | bytes 786440 | tf_op jit(solution)/shard_map/ppermute | solution.py:45
  12.2 1.0 fusion.5
  13.2 3.7 %collective-permute-start.2 = (bf16[256,256]{1,0:T(8,128)(2,1)S(1)}, bf16[256,256]{1,0:T(8,128)(2,1)S(1)}, u32[]{:S(2)}, u32[]{:S(2)}) collective-permute-start(bf16[256,256]{1,0:T(8,128)(2,1)S(1)} %get-tuple-element.85), channel_id=1, source_target_pairs={{0,2},{1,3},{2,0},{3,1},{4,6},{5,7},{6,4},{7,5},{8,10},{9,11},{10,... | collective-permute-start | bytes 393224 | tf_op jit(solution)/shard_map/ppermute | solution.py:43
  17.0 0.8 select_reduce_fusion.4
  17.8 1.3 %fusion.6 = (s32[4]{0:T(128)S(1)}, s32[]{:T(128)}, s32[4]{0:T(128)S(1)}) fusion(s32[4]{0:T(128)S(1)} %select_reduce_fusion.4, s32[4]{0:T(128)} %param.18, s32[]{:T(128)S(6)} %mul.25), kind=kLoop, calls=%fused_computation.41 | loop fusion | flops 79 | bytes 72 | tf_op jit(solution)/shard_map/sub | solution.py:407
  21.1 0.8 select_reduce_fusion
  22.0 1.0 fusion
  23.0 0.9 compare_and_fusion
  23.9 0.8 select_select_fusion.query_marks
  28.0 3.6 %collective-permute-done.2.refs_3_ = bf16[256,256]{1,0:T(8,128)(2,1)S(1)} collective-permute-done((bf16[256,256]{1,0:T(8,128)(2,1)S(1)}, bf16[256,256]{1,0:T(8,128)(2,1)S(1)}, u32[]{:S(2)}, u32[]{:S(2)}) %collective-permute-start.2) | collective-permute-done | bytes 131104 | tf_op jit(solution)/shard_map/ppermute | solution.py:43
  31.6 1.3 %collective-permute-start.4 = (bf16[256,256]{1,0:T(8,128)(2,1)S(1)}, bf16[256,256]{1,0:T(8,128)(2,1)S(1)}, u32[]{:S(2)}, u32[]{:S(2)}) collective-permute-start(bf16[256,256]{1,0:T(8,128)(2,1)S(1)} %collective-permute-done.2.refs_3_), channel_id=1, source_target_pairs={{2,3},{1,0},{6,7},{5,4},{10,11},{9,8},{14,15},{13,12},{18,19},{17,... | collective-permute-start | bytes 393224 | tf_op jit(solution)/shard_map/ppermute | solution.py:46
  33.0 1.3 %collective-permute-start.5 = (bf16[256,256]{1,0:T(8,128)(2,1)S(1)}, bf16[256,256]{1,0:T(8,128)(2,1)S(1)}, u32[]{:S(2)}, u32[]{:S(2)}) collective-permute-start(bf16[256,256]{1,0:T(8,128)(2,1)S(1)} %collective-permute-done.3.refs_4_), channel_id=1, source_target_pairs={{2,3},{1,0},{6,7},{5,4},{10,11},{9,8},{14,15},{13,12},{18,19},{17,... | collective-permute-start | bytes 393224 | tf_op jit(solution)/shard_map/ppermute | solution.py:46
  35.5 1.3 %reshape.150.refs_7_ = bf16[1,1024]{1,0:T(2,128)(2,1)} reshape(bf16[1024]{0:T(1024)(128)(2,1)} %param.20) | data formatting | bytes 4096 | tf_op jit(solution)/shard_map/reshape | solution.py:635
  36.8 1.3 %reshape.151.refs_5_ = bf16[1,1024]{1,0:T(2,128)(2,1)} reshape(bf16[1024]{0:T(1024)(128)(2,1)} %param.26) | data formatting | bytes 4096 | tf_op jit(solution)/shard_map/reshape | solution.py:635
  38.9 1.4 %collective-permute-done.5.refs_6_ = bf16[256,256]{1,0:T(8,128)(2,1)S(1)} collective-permute-done((bf16[256,256]{1,0:T(8,128)(2,1)S(1)}, bf16[256,256]{1,0:T(8,128)(2,1)S(1)}, u32[]{:S(2)}, u32[]{:S(2)}) %collective-permute-start.5) | collective-permute-done | bytes 131104 | tf_op jit(solution)/shard_map/ppermute | solution.py:46
  41.0 0.9 copy-done.24
  41.9 0.9 copy-done.26
  42.8 0.9 copy-done.28
  44.4 1.3 %project.1 = (bf16[512,1024]{1,0:T(8,128)(2,1)S(1)}, bf16[512,128]{1,0:T(8,128)(2,1)S(1)}, bf16[528,256]{1,0:T(8,128)(2,1)S(1)}) custom-call(s32[1]{0:T(128)} %bitcast.place_ref, bf16[512,256]{1,0:T(8,128)(2,1)S(1)} %copy-done.3, bf16[512,256]{1,0:T(8,128)(2,1)S(1)} %collective-permute-done.refs_1_, bf16[512,256]{1,0:T(8,128)(2,1)S(1)} %collective-permute-done.1.refs_2_, ...), custom_call_target="tpu_custom_call" | custom-call | flops 402653184 | bytes 4194304 | tf_op jit(solution)/shard_map/project/pallas_call | solution.py:129
  45.7 1.6 %collective-permute-start.9 = (bf16[528,256]{1,0:T(8,128)(2,1)S(1)}, bf16[528,256]{1,0:T(8,128)(2,1)S(1)}, u32[]{:S(2)}, u32[]{:S(2)}) collective-permute-start(bf16[528,256]{1,0:T(8,128)(2,1)S(1)} %get-tuple-element.56.refs_0_), channel_id=1, source_target_pairs={{0,16},{4,20},{8,24},{12,28},{16,0},{20,4},{24,8},{28,12},{1,17},{... | collective-permute-start | bytes 811016 | tf_op jit(solution)/shard_map/ppermute | solution.py:146
  47.8 1.5 %collective-permute-start.7 = (bf16[528,256]{1,0:T(8,128)(2,1)S(1)}, bf16[528,256]{1,0:T(8,128)(2,1)S(1)}, u32[]{:S(2)}, u32[]{:S(2)}) collective-permute-start(bf16[528,256]{1,0:T(8,128)(2,1)S(1)} %get-tuple-element.56.refs_0_), channel_id=1, source_target_pairs={{0,8},{4,12},{8,0},{12,4},{16,24},{20,28},{24,16},{28,20},{1,9},{5... | collective-permute-start | bytes 811016 | tf_op jit(solution)/shard_map/ppermute | solution.py:146
  49.3 8.5 %collective-permute-done.9.refs_4_ = bf16[528,256]{1,0:T(8,128)(2,1)S(1)} collective-permute-done((bf16[528,256]{1,0:T(8,128)(2,1)S(1)}, bf16[528,256]{1,0:T(8,128)(2,1)S(1)}, u32[]{:S(2)}, u32[]{:S(2)}) %collective-permute-start.9) | collective-permute-done | bytes 270368 | tf_op jit(solution)/shard_map/ppermute | solution.py:146
  58.3 0.7 collective-permute-done.7.refs_2_
  59.7 0.8 collective-permute-done.8.refs_3_
  60.5 1.0 copy-done.22
  62.2 4.7 %attend.1.refs_0_ = bf16[512,128]{1,0:T(8,128)(2,1)S(1)} custom-call(s32[6]{0:T(128)S(1)} %copy-done.33, bf16[512,128]{1,0:T(8,128)(2,1)S(1)} %get-tuple-element.54.queries, bf16[2,512,128]{2,1,0:T(8,128)(2,1)S(1)} %copy-done.22, bf16[528,256]{1,0:T(8,128)(2,1)S(1)} %get-tuple-element.56.refs_0_, bf16[528,256]{1,0:T(8,128)(2,1)S(1)} %collective-permute-done.6.refs_1_, ...), custom_call_target="tpu_custom_call" | custom-call | flops 2684354560 | bytes 4194304 | tf_op jit(solution)/shard_map/attend/pallas_call | solution.py:290
  67.0 1.6 %collective-permute-start.13 = (bf16[512,128]{1,0:T(8,128)(2,1)S(1)}, bf16[512,128]{1,0:T(8,128)(2,1)}, u32[]{:S(2)}, u32[]{:S(2)}) collective-permute-start(bf16[512,128]{1,0:T(8,128)(2,1)S(1)} %attend.1.refs_0_), channel_id=1, source_target_pairs={{0,1},{1,2},{2,3},{3,0},{4,5},{5,6},{6,7},{7,4},{8,9},{9,10},{10,1... | collective-permute-start | bytes 393224 | tf_op jit(solution)/shard_map/ppermute | solution.py:54
  68.5 2.4 %collective-permute-start.15 = (bf16[512,128]{1,0:T(8,128)(2,1)S(1)}, bf16[512,128]{1,0:T(8,128)(2,1)}, u32[]{:S(2)}, u32[]{:S(2)}) collective-permute-start(bf16[512,128]{1,0:T(8,128)(2,1)S(1)} %attend.1.refs_0_), channel_id=1, source_target_pairs={{0,3},{1,0},{2,1},{3,2},{4,7},{5,4},{6,5},{7,6},{8,11},{9,8},{10,9... | collective-permute-start | bytes 393224 | tf_op jit(solution)/shard_map/ppermute | solution.py:54
  71.0 1.6 %copy-done.1 = bf16[1024,1024]{1,0:T(8,128)(2,1)S(1)} copy-done((bf16[1024,1024]{1,0:T(8,128)(2,1)S(1)}, bf16[1024,1024]{1,0:T(8,128)(2,1)}, u32[]{:S(2)}) %copy-start.1) | copy-done | bytes 2097176
  72.6 1.6 %copy-done.2 = bf16[1024,1024]{1,0:T(8,128)(2,1)S(1)} copy-done((bf16[1024,1024]{1,0:T(8,128)(2,1)S(1)}, bf16[1024,1024]{1,0:T(8,128)(2,1)}, u32[]{:S(2)}) %copy-start.2) | copy-done | bytes 2097176
  74.2 1.2 copy-done.4
  76.0 4.9 %collective-permute-done.14.refs_2_ = bf16[512,128]{1,0:T(8,128)(2,1)} collective-permute-done((bf16[512,128]{1,0:T(8,128)(2,1)S(1)}, bf16[512,128]{1,0:T(8,128)(2,1)}, u32[]{:S(2)}, u32[]{:S(2)}) %collective-permute-start.14) | collective-permute-done | bytes 131104 | tf_op jit(solution)/shard_map/ppermute | solution.py:54
  81.0 4.8 %hidden.1 = (bf16[512,1024]{1,0:T(8,128)(2,1)S(1)}, bf16[512,256]{1,0:T(8,128)(2,1)S(1)}, bf16[256,256]{1,0:T(8,128)(2,1)S(1)}, bf16[256,256]{1,0:T(8,128)(2,1)S(1)}) custom-call(s32[1]{0:T(128)} %bitcast.place_ref, bf16[512,128]{1,0:T(8,128)(2,1)S(1)} %attend.1.refs_0_, bf16[512,128]{1,0:T(8,128)(2,1)} %collective-permute-done.13.refs_1_, ...), custom_call_target="tpu_custom_call" | custom-call | flops 3221225472 | bytes 10485760 | tf_op jit(solution)/shard_map/hidden/pallas_call | solution.py:495
  85.7 5.3 %collective-permute-start.20 = (bf16[256,256]{1,0:T(8,128)(2,1)S(1)}, bf16[256,256]{1,0:T(8,128)(2,1)S(1)}, u32[]{:S(2)}, u32[]{:S(2)}) collective-permute-start(bf16[256,256]{1,0:T(8,128)(2,1)S(1)} %get-tuple-element.78), channel_id=1, source_target_pairs={{3,2},{0,1},{7,6},{4,5},{11,10},{8,9},{15,14},{12,13},{19,18},{16,... | collective-permute-start | bytes 393224 | tf_op jit(solution)/shard_map/ppermute | solution.py:573
  91.0 1.3 %collective-permute-start.18 = (bf16[256,256]{1,0:T(8,128)(2,1)S(1)}, bf16[256,256]{1,0:T(8,128)(2,1)S(1)}, u32[]{:S(2)}, u32[]{:S(2)}) collective-permute-start(bf16[256,256]{1,0:T(8,128)(2,1)S(1)} %get-tuple-element.76), channel_id=1, source_target_pairs={{3,2},{0,1},{7,6},{4,5},{11,10},{8,9},{15,14},{12,13},{19,18},{16,... | collective-permute-start | bytes 393224 | tf_op jit(solution)/shard_map/ppermute | solution.py:573
  92.4 1.5 %down_blocks.1 = (f32[256,256]{1,0:T(8,128)S(1)}, f32[256,256]{1,0:T(8,128)S(1)}, bf16[512,256]{1,0:T(8,128)(2,1)}, bf16[512,256]{1,0:T(8,128)(2,1)}, f32[512,256]{1,0:T(8,128)S(1)}) custom-call(s32[1]{0:T(128)} %bitcast.place_ref, bf16[512,1024]{1,0:T(8,128)(2,1)S(1)} %get-tuple-element.70.hidden, bf16[512,256]{1,0:T(8,128)(2,1)S(1)} %get-tuple-element.71.kept, ...), custom_call_target="tpu_custom_call" | custom-call | flops 1073741824 | bytes 5242880 | tf_op jit(solution)/shard_map/down_blocks/pallas_call | solution.py:527
  93.9 1.3 %collective-permute-start.16 = (bf16[512,256]{1,0:T(8,128)(2,1)}, bf16[512,256]{1,0:T(8,128)(2,1)S(1)}, u32[]{:S(2)}, u32[]{:S(2)}) collective-permute-start(bf16[512,256]{1,0:T(8,128)(2,1)} %get-tuple-element.73), channel_id=1, source_target_pairs={{0,1},{1,2},{2,3},{4,5},{5,6},{6,7},{8,9},{9,10},{10,11},{12,13},{... | collective-permute-start | bytes 786440 | tf_op jit(solution)/shard_map/ppermute | solution.py:576
  95.2 1.3 %collective-permute-start.17 = (bf16[512,256]{1,0:T(8,128)(2,1)}, bf16[512,256]{1,0:T(8,128)(2,1)}, u32[]{:S(2)}, u32[]{:S(2)}) collective-permute-start(bf16[512,256]{1,0:T(8,128)(2,1)} %get-tuple-element.74), channel_id=1, source_target_pairs={{3,2},{2,1},{1,0},{7,6},{6,5},{5,4},{11,10},{10,9},{9,8},{15,14},{... | collective-permute-start | bytes 786440 | tf_op jit(solution)/shard_map/ppermute | solution.py:575
  97.2 2.1 %collective-permute-start.21 = (bf16[256,256]{1,0:T(8,128)(2,1)}, bf16[256,256]{1,0:T(8,128)(2,1)S(1)}, u32[]{:S(2)}, u32[]{:S(2)}) collective-permute-start(bf16[256,256]{1,0:T(8,128)(2,1)} %add_up.4), channel_id=1, source_target_pairs={{0,2},{1,3},{2,0},{3,1},{4,6},{5,7},{6,4},{7,5},{8,10},{9,11},{10,... | collective-permute-start | bytes 393224 | tf_op jit(solution)/shard_map/ppermute | solution.py:579
  99.4 0.7 add_up.3
  100.1 0.8 collective-permute-start.19
  100.9 2.3 %fill_cache.1 = bf16[576,256]{1,0:T(8,128)(2,1)S(1)} custom-call(s32[1]{0:T(128)} %bitcast.6.me_ref, s32[9]{0:T(128)S(1)} %copy-done.32, s32[9]{0:T(128)S(1)} %copy-done.31, bf16[528,256]{1,0:T(8,128)(2,1)S(1)} %get-tuple-element.56.refs_0_, bf16[528,256]{1,0:T(8,128)(2,1)S(1)} %copy-done.12, bf16[528,256]{1,0:T(8,128)(2,1)S(1)} %copy-done.10, ...), custom_call_target="tpu_custom_call" | custom-call | flops 75497472 | bytes 3145728 | tf_op jit(solution)/shard_map/fill_cache/pallas_call | solution.py:385
  103.2 0.8 reshape.152
  104.0 2.0 %collective-permute-done.17.refs_2_ = bf16[512,256]{1,0:T(8,128)(2,1)} collective-permute-done((bf16[512,256]{1,0:T(8,128)(2,1)}, bf16[512,256]{1,0:T(8,128)(2,1)}, u32[]{:S(2)}, u32[]{:S(2)}) %collective-permute-start.17) | collective-permute-done | bytes 262176 | tf_op jit(solution)/shard_map/ppermute | solution.py:575
  106.1 8.4 %collective-permute-done.21.refs_4_ = bf16[256,256]{1,0:T(8,128)(2,1)S(1)} collective-permute-done((bf16[256,256]{1,0:T(8,128)(2,1)}, bf16[256,256]{1,0:T(8,128)(2,1)S(1)}, u32[]{:S(2)}, u32[]{:S(2)}) %collective-permute-start.21) | collective-permute-done | bytes 131104 | tf_op jit(solution)/shard_map/ppermute | solution.py:579
  114.4 1.9 %collective-permute-done.19.refs_3_ = bf16[256,256]{1,0:T(8,128)(2,1)S(1)} collective-permute-done((bf16[256,256]{1,0:T(8,128)(2,1)}, bf16[256,256]{1,0:T(8,128)(2,1)S(1)}, u32[]{:S(2)}, u32[]{:S(2)}) %collective-permute-start.19) | collective-permute-done | bytes 131104 | tf_op jit(solution)/shard_map/ppermute | solution.py:579
  116.3 1.8 %add_up.5 = bf16[512,256]{1,0:T(8,128)(2,1)} custom-call(f32[512,256]{1,0:T(8,128)S(1)} %get-tuple-element.72.refs_0_, bf16[512,256]{1,0:T(8,128)(2,1)S(1)} %collective-permute-done.16.refs_1_, bf16[512,256]{1,0:T(8,128)(2,1)} %collective-permute-done.17.refs_2_, bf16[256,256]{1,0:T(8,128)(2,1)S(1)} %collective-permute-done.19.refs_3_, ...), custom_call_target="tpu_custom_call" | custom-call | flops 655360 | bytes 2621440 | tf_op jit(solution)/shard_map/add_up/pallas_call | solution.py:554
  (110 shorter events, 10.1 us)
Async XLA Ops:
  7.2 33.8 %copy-start.3 = (bf16[512,256]{1,0:T(8,128)(2,1)S(1)}, bf16[512,256]{1,0:T(8,128)(2,1)}, u32[]{:S(2)}) copy-start(bf16[512,256]{1,0:T(8,128)(2,1)} %refs_0_) | copy-start | bytes 786436
  7.2 33.8 %copy-start.19 = (bf16[1024,128]{1,0:T(8,128)(2,1)S(1)}, bf16[1024,128]{1,0:T(8,128)(2,1)}, u32[]{:S(2)}) copy-start(bf16[1024,128]{1,0:T(8,128)(2,1)} %refs_8_.1) | copy-start | bytes 786436
  7.2 33.8 %copy-start.20 = (bf16[1024,128]{1,0:T(8,128)(2,1)S(1)}, bf16[1024,128]{1,0:T(8,128)(2,1)}, u32[]{:S(2)}) copy-start(bf16[1024,128]{1,0:T(8,128)(2,1)} %refs_9_.1) | copy-start | bytes 786436
  7.2 33.8 %copy-start.21 = (bf16[1024,128]{1,0:T(8,128)(2,1)S(1)}, bf16[1024,128]{1,0:T(8,128)(2,1)}, u32[]{:S(2)}) copy-start(bf16[1024,128]{1,0:T(8,128)(2,1)} %refs_10_.1) | copy-start | bytes 786436
  7.2 63.8 %all-gather.2.cloned.1.call-start = ((), (), s32[]{:S(2)}) async-start(), calls=%async_computation | async-start | bytes 1310720 | tf_op jit(solution)/shard_map/all_gather | solution.py:640
  7.2 33.1 %collective-permute-start = (bf16[512,256]{1,0:T(8,128)(2,1)}, bf16[512,256]{1,0:T(8,128)(2,1)S(1)}, u32[]{:S(2)}, u32[]{:S(2)}) collective-permute-start(bf16[512,256]{1,0:T(8,128)(2,1)} %refs_0_), channel_id=1, source_target_pairs={{0,1},{1,2},{2,3},{4,5},{5,6},{6,7},{8,9},{9,10},{10,11},{12,13},{... | collective-permute-start | bytes 786440 | tf_op jit(solution)/shard_map/ppermute | solution.py:44
  10.9 29.5 %collective-permute-start.1 = (bf16[512,256]{1,0:T(8,128)(2,1)}, bf16[512,256]{1,0:T(8,128)(2,1)S(1)}, u32[]{:S(2)}, u32[]{:S(2)}) collective-permute-start(bf16[512,256]{1,0:T(8,128)(2,1)} %refs_0_), channel_id=1, source_target_pairs={{3,2},{2,1},{1,0},{7,6},{6,5},{5,4},{11,10},{10,9},{9,8},{15,14},{... | collective-permute-start | bytes 786440 | tf_op jit(solution)/shard_map/ppermute | solution.py:45
  13.2 18.4 %collective-permute-start.2 = (bf16[256,256]{1,0:T(8,128)(2,1)S(1)}, bf16[256,256]{1,0:T(8,128)(2,1)S(1)}, u32[]{:S(2)}, u32[]{:S(2)}) collective-permute-start(bf16[256,256]{1,0:T(8,128)(2,1)S(1)} %get-tuple-element.85), channel_id=1, source_target_pairs={{0,2},{1,3},{2,0},{3,1},{4,6},{5,7},{6,4},{7,5},{8,10},{9,11},{10,... | collective-permute-start | bytes 393224 | tf_op jit(solution)/shard_map/ppermute | solution.py:43
  16.9 16.1 %collective-permute-start.3 = (bf16[256,256]{1,0:T(8,128)(2,1)S(1)}, bf16[256,256]{1,0:T(8,128)(2,1)S(1)}, u32[]{:S(2)}, u32[]{:S(2)}) collective-permute-start(bf16[256,256]{1,0:T(8,128)(2,1)S(1)} %get-tuple-element.84), channel_id=1, source_target_pairs={{0,2},{1,3},{2,0},{3,1},{4,6},{5,7},{6,4},{7,5},{8,10},{9,11},{10,... | collective-permute-start | bytes 393224 | tf_op jit(solution)/shard_map/ppermute | solution.py:43
  31.6 7.3 %collective-permute-start.4 = (bf16[256,256]{1,0:T(8,128)(2,1)S(1)}, bf16[256,256]{1,0:T(8,128)(2,1)S(1)}, u32[]{:S(2)}, u32[]{:S(2)}) collective-permute-start(bf16[256,256]{1,0:T(8,128)(2,1)S(1)} %collective-permute-done.2.refs_3_), channel_id=1, source_target_pairs={{2,3},{1,0},{6,7},{5,4},{10,11},{9,8},{14,15},{13,12},{18,19},{17,... | collective-permute-start | bytes 393224 | tf_op jit(solution)/shard_map/ppermute | solution.py:46
  33.0 7.4 %copy-start.23 = (bf16[256,256]{1,0:T(8,128)(2,1)}, bf16[256,256]{1,0:T(8,128)(2,1)S(1)}, u32[]{:S(2)}) copy-start(bf16[256,256]{1,0:T(8,128)(2,1)S(1)} %collective-permute-done.3.refs_4_) | copy-start | bytes 393220
  33.0 7.3 %collective-permute-start.5 = (bf16[256,256]{1,0:T(8,128)(2,1)S(1)}, bf16[256,256]{1,0:T(8,128)(2,1)S(1)}, u32[]{:S(2)}, u32[]{:S(2)}) collective-permute-start(bf16[256,256]{1,0:T(8,128)(2,1)S(1)} %collective-permute-done.3.refs_4_), channel_id=1, source_target_pairs={{2,3},{1,0},{6,7},{5,4},{10,11},{9,8},{14,15},{13,12},{18,19},{17,... | collective-permute-start | bytes 393224 | tf_op jit(solution)/shard_map/ppermute | solution.py:46
  45.7 12.0 %collective-permute-start.9 = (bf16[528,256]{1,0:T(8,128)(2,1)S(1)}, bf16[528,256]{1,0:T(8,128)(2,1)S(1)}, u32[]{:S(2)}, u32[]{:S(2)}) collective-permute-start(bf16[528,256]{1,0:T(8,128)(2,1)S(1)} %get-tuple-element.56.refs_0_), channel_id=1, source_target_pairs={{0,16},{4,20},{8,24},{12,28},{16,0},{20,4},{24,8},{28,12},{1,17},{... | collective-permute-start | bytes 811016 | tf_op jit(solution)/shard_map/ppermute | solution.py:146
  47.3 10.5 %collective-permute-start.11 = (bf16[528,256]{1,0:T(8,128)(2,1)S(1)}, bf16[528,256]{1,0:T(8,128)(2,1)S(1)}, u32[]{:S(2)}, u32[]{:S(2)}) collective-permute-start(bf16[528,256]{1,0:T(8,128)(2,1)S(1)} %get-tuple-element.56.refs_0_), channel_id=1, source_target_pairs={{0,24},{4,28},{8,16},{12,20},{16,8},{20,12},{24,0},{28,4},{1,25},{... | collective-permute-start | bytes 811016 | tf_op jit(solution)/shard_map/ppermute | solution.py:146
  47.8 11.2 %collective-permute-start.7 = (bf16[528,256]{1,0:T(8,128)(2,1)S(1)}, bf16[528,256]{1,0:T(8,128)(2,1)S(1)}, u32[]{:S(2)}, u32[]{:S(2)}) collective-permute-start(bf16[528,256]{1,0:T(8,128)(2,1)S(1)} %get-tuple-element.56.refs_0_), channel_id=1, source_target_pairs={{0,8},{4,12},{8,0},{12,4},{16,24},{20,28},{24,16},{28,20},{1,9},{5... | collective-permute-start | bytes 811016 | tf_op jit(solution)/shard_map/ppermute | solution.py:146
  49.3 9.7 %collective-permute-start.6 = (bf16[528,256]{1,0:T(8,128)(2,1)S(1)}, bf16[528,256]{1,0:T(8,128)(2,1)S(1)}, u32[]{:S(2)}, u32[]{:S(2)}) collective-permute-start(bf16[528,256]{1,0:T(8,128)(2,1)S(1)} %get-tuple-element.56.refs_0_), channel_id=1, source_target_pairs={{0,4},{4,0},{8,12},{12,8},{16,20},{20,16},{24,28},{28,24},{1,5},{5... | collective-permute-start | bytes 811016 | tf_op jit(solution)/shard_map/ppermute | solution.py:146
  57.8 9.1 %copy-start.5 = (bf16[528,256]{1,0:T(8,128)(2,1)}, bf16[528,256]{1,0:T(8,128)(2,1)S(1)}, u32[]{:S(2)}) copy-start(bf16[528,256]{1,0:T(8,128)(2,1)S(1)} %collective-permute-done.9.refs_4_) | copy-start | bytes 811012
  57.8 1.5 %collective-permute-start.10 = (bf16[528,256]{1,0:T(8,128)(2,1)S(1)}, bf16[528,256]{1,0:T(8,128)(2,1)S(1)}, u32[]{:S(2)}, u32[]{:S(2)}) collective-permute-start(bf16[528,256]{1,0:T(8,128)(2,1)S(1)} %collective-permute-done.9.refs_4_), channel_id=1, source_target_pairs={{0,4},{4,0},{8,12},{12,8},{16,20},{20,16},{24,28},{28,24},{1,5},{5... | collective-permute-start | bytes 811016 | tf_op jit(solution)/shard_map/ppermute | solution.py:146
  57.8 9.1 %copy-start.7 = (bf16[528,256]{1,0:T(8,128)(2,1)}, bf16[528,256]{1,0:T(8,128)(2,1)S(1)}, u32[]{:S(2)}) copy-start(bf16[528,256]{1,0:T(8,128)(2,1)S(1)} %collective-permute-done.11.refs_6_) | copy-start | bytes 811012
  57.8 1.9 %collective-permute-start.12 = (bf16[528,256]{1,0:T(8,128)(2,1)S(1)}, bf16[528,256]{1,0:T(8,128)(2,1)S(1)}, u32[]{:S(2)}, u32[]{:S(2)}) collective-permute-start(bf16[528,256]{1,0:T(8,128)(2,1)S(1)} %collective-permute-done.11.refs_6_), channel_id=1, source_target_pairs={{0,4},{4,0},{8,12},{12,8},{16,20},{20,16},{24,28},{28,24},{1,5},{5... | collective-permute-start | bytes 811016 | tf_op jit(solution)/shard_map/ppermute | solution.py:146
  59.0 7.9 %copy-start.9 = (bf16[528,256]{1,0:T(8,128)(2,1)}, bf16[528,256]{1,0:T(8,128)(2,1)S(1)}, u32[]{:S(2)}) copy-start(bf16[528,256]{1,0:T(8,128)(2,1)S(1)} %collective-permute-done.7.refs_2_) | copy-start | bytes 811012
  59.0 1.5 %collective-permute-start.8 = (bf16[528,256]{1,0:T(8,128)(2,1)S(1)}, bf16[528,256]{1,0:T(8,128)(2,1)S(1)}, u32[]{:S(2)}, u32[]{:S(2)}) collective-permute-start(bf16[528,256]{1,0:T(8,128)(2,1)S(1)} %collective-permute-done.7.refs_2_), channel_id=1, source_target_pairs={{0,4},{4,0},{8,12},{12,8},{16,20},{20,16},{24,28},{28,24},{1,5},{5... | collective-permute-start | bytes 811016 | tf_op jit(solution)/shard_map/ppermute | solution.py:146
  59.0 7.9 %copy-start.11 = (bf16[528,256]{1,0:T(8,128)(2,1)}, bf16[528,256]{1,0:T(8,128)(2,1)S(1)}, u32[]{:S(2)}) copy-start(bf16[528,256]{1,0:T(8,128)(2,1)S(1)} %collective-permute-done.6.refs_1_) | copy-start | bytes 811012
  59.3 7.6 %copy-start.13 = (bf16[528,256]{1,0:T(8,128)(2,1)}, bf16[528,256]{1,0:T(8,128)(2,1)S(1)}, u32[]{:S(2)}) copy-start(bf16[528,256]{1,0:T(8,128)(2,1)S(1)} %collective-permute-done.10.refs_5_) | copy-start | bytes 811012
  59.7 7.2 %copy-start.15 = (bf16[528,256]{1,0:T(8,128)(2,1)}, bf16[528,256]{1,0:T(8,128)(2,1)S(1)}, u32[]{:S(2)}) copy-start(bf16[528,256]{1,0:T(8,128)(2,1)S(1)} %collective-permute-done.12.refs_7_) | copy-start | bytes 811012
  60.5 6.4 %copy-start.17 = (bf16[528,256]{1,0:T(8,128)(2,1)}, bf16[528,256]{1,0:T(8,128)(2,1)S(1)}, u32[]{:S(2)}) copy-start(bf16[528,256]{1,0:T(8,128)(2,1)S(1)} %collective-permute-done.8.refs_3_) | copy-start | bytes 811012
  62.2 8.8 %copy-start = (bf16[1024,1024]{1,0:T(8,128)(2,1)S(1)}, bf16[1024,1024]{1,0:T(8,128)(2,1)}, u32[]{:S(2)}) copy-start(bf16[1024,1024]{1,0:T(8,128)(2,1)} %refs_2_) | copy-start | bytes 6291460
  67.0 9.1 %collective-permute-start.13 = (bf16[512,128]{1,0:T(8,128)(2,1)S(1)}, bf16[512,128]{1,0:T(8,128)(2,1)}, u32[]{:S(2)}, u32[]{:S(2)}) collective-permute-start(bf16[512,128]{1,0:T(8,128)(2,1)S(1)} %attend.1.refs_0_), channel_id=1, source_target_pairs={{0,1},{1,2},{2,3},{3,0},{4,5},{5,6},{6,7},{7,4},{8,9},{9,10},{10,1... | collective-permute-start | bytes 393224 | tf_op jit(solution)/shard_map/ppermute | solution.py:54
  68.5 12.4 %collective-permute-start.14 = (bf16[512,128]{1,0:T(8,128)(2,1)S(1)}, bf16[512,128]{1,0:T(8,128)(2,1)}, u32[]{:S(2)}, u32[]{:S(2)}) collective-permute-start(bf16[512,128]{1,0:T(8,128)(2,1)S(1)} %attend.1.refs_0_), channel_id=1, source_target_pairs={{0,2},{1,3},{2,0},{3,1},{4,6},{5,7},{6,4},{7,5},{8,10},{9,11},{10,... | collective-permute-start | bytes 393224 | tf_op jit(solution)/shard_map/ppermute | solution.py:54
  68.5 12.4 %collective-permute-start.15 = (bf16[512,128]{1,0:T(8,128)(2,1)S(1)}, bf16[512,128]{1,0:T(8,128)(2,1)}, u32[]{:S(2)}, u32[]{:S(2)}) collective-permute-start(bf16[512,128]{1,0:T(8,128)(2,1)S(1)} %attend.1.refs_0_), channel_id=1, source_target_pairs={{0,3},{1,0},{2,1},{3,2},{4,7},{5,4},{6,5},{7,6},{8,11},{9,8},{10,9... | collective-permute-start | bytes 393224 | tf_op jit(solution)/shard_map/ppermute | solution.py:54
  71.0 1.6 %copy-start.1 = (bf16[1024,1024]{1,0:T(8,128)(2,1)S(1)}, bf16[1024,1024]{1,0:T(8,128)(2,1)}, u32[]{:S(2)}) copy-start(bf16[1024,1024]{1,0:T(8,128)(2,1)} %refs_3_) | copy-start | bytes 6291460
  72.6 1.6 %copy-start.2 = (bf16[1024,1024]{1,0:T(8,128)(2,1)S(1)}, bf16[1024,1024]{1,0:T(8,128)(2,1)}, u32[]{:S(2)}) copy-start(bf16[1024,1024]{1,0:T(8,128)(2,1)} %refs_4_) | copy-start | bytes 6291460
  75.4 5.6 %copy-start.30 = (bf16[1,1024]{1,0:T(2,128)(2,1)S(1)}, bf16[1,1024]{1,0:T(2,128)(2,1)}, u32[]{:S(2)}) copy-start(bf16[1,1024]{1,0:T(2,128)(2,1)} %reshape.151.refs_5_) | copy-start | bytes 6148
  85.7 10.8 %collective-permute-start.20 = (bf16[256,256]{1,0:T(8,128)(2,1)S(1)}, bf16[256,256]{1,0:T(8,128)(2,1)S(1)}, u32[]{:S(2)}, u32[]{:S(2)}) collective-permute-start(bf16[256,256]{1,0:T(8,128)(2,1)S(1)} %get-tuple-element.78), channel_id=1, source_target_pairs={{3,2},{0,1},{7,6},{4,5},{11,10},{8,9},{15,14},{12,13},{19,18},{16,... | collective-permute-start | bytes 393224 | tf_op jit(solution)/shard_map/ppermute | solution.py:573
  91.0 8.4 %collective-permute-start.18 = (bf16[256,256]{1,0:T(8,128)(2,1)S(1)}, bf16[256,256]{1,0:T(8,128)(2,1)S(1)}, u32[]{:S(2)}, u32[]{:S(2)}) collective-permute-start(bf16[256,256]{1,0:T(8,128)(2,1)S(1)} %get-tuple-element.76), channel_id=1, source_target_pairs={{3,2},{0,1},{7,6},{4,5},{11,10},{8,9},{15,14},{12,13},{19,18},{16,... | collective-permute-start | bytes 393224 | tf_op jit(solution)/shard_map/ppermute | solution.py:573
  92.3 8.5 %copy-start.6 = (bf16[528,256]{1,0:T(8,128)(2,1)S(1)}, bf16[528,256]{1,0:T(8,128)(2,1)}, u32[]{:S(2)}) copy-start(bf16[528,256]{1,0:T(8,128)(2,1)} %copy-done.5) | copy-start | bytes 811012
  92.3 8.5 %copy-start.8 = (bf16[528,256]{1,0:T(8,128)(2,1)S(1)}, bf16[528,256]{1,0:T(8,128)(2,1)}, u32[]{:S(2)}) copy-start(bf16[528,256]{1,0:T(8,128)(2,1)} %copy-done.7) | copy-start | bytes 811012
  92.3 8.5 %copy-start.10 = (bf16[528,256]{1,0:T(8,128)(2,1)S(1)}, bf16[528,256]{1,0:T(8,128)(2,1)}, u32[]{:S(2)}) copy-start(bf16[528,256]{1,0:T(8,128)(2,1)} %copy-done.9) | copy-start | bytes 811012
  92.3 8.5 %copy-start.12 = (bf16[528,256]{1,0:T(8,128)(2,1)S(1)}, bf16[528,256]{1,0:T(8,128)(2,1)}, u32[]{:S(2)}) copy-start(bf16[528,256]{1,0:T(8,128)(2,1)} %copy-done.11) | copy-start | bytes 811012
  92.4 8.5 %copy-start.14 = (bf16[528,256]{1,0:T(8,128)(2,1)S(1)}, bf16[528,256]{1,0:T(8,128)(2,1)}, u32[]{:S(2)}) copy-start(bf16[528,256]{1,0:T(8,128)(2,1)} %copy-done.13) | copy-start | bytes 811012
  92.4 8.5 %copy-start.16 = (bf16[528,256]{1,0:T(8,128)(2,1)S(1)}, bf16[528,256]{1,0:T(8,128)(2,1)}, u32[]{:S(2)}) copy-start(bf16[528,256]{1,0:T(8,128)(2,1)} %copy-done.15) | copy-start | bytes 811012
  92.4 8.5 %copy-start.18 = (bf16[528,256]{1,0:T(8,128)(2,1)S(1)}, bf16[528,256]{1,0:T(8,128)(2,1)}, u32[]{:S(2)}) copy-start(bf16[528,256]{1,0:T(8,128)(2,1)} %copy-done.17) | copy-start | bytes 811012
  92.4 8.5 %copy-start.31 = (s32[9]{0:T(128)S(1)}, s32[9]{0:T(128)}, u32[]{:S(2)}) copy-start(s32[9]{0:T(128)} %get-tuple-element.80.amounts) | copy-start | bytes 112
  92.4 8.5 %copy-start.32 = (s32[9]{0:T(128)S(1)}, s32[9]{0:T(128)}, u32[]{:S(2)}) copy-start(s32[9]{0:T(128)} %get-tuple-element.79.first_token) | copy-start | bytes 112
  93.9 10.1 %collective-permute-start.16 = (bf16[512,256]{1,0:T(8,128)(2,1)}, bf16[512,256]{1,0:T(8,128)(2,1)S(1)}, u32[]{:S(2)}, u32[]{:S(2)}) collective-permute-start(bf16[512,256]{1,0:T(8,128)(2,1)} %get-tuple-element.73), channel_id=1, source_target_pairs={{0,1},{1,2},{2,3},{4,5},{5,6},{6,7},{8,9},{9,10},{10,11},{12,13},{... | collective-permute-start | bytes 786440 | tf_op jit(solution)/shard_map/ppermute | solution.py:576
  95.2 10.8 %collective-permute-start.17 = (bf16[512,256]{1,0:T(8,128)(2,1)}, bf16[512,256]{1,0:T(8,128)(2,1)}, u32[]{:S(2)}, u32[]{:S(2)}) collective-permute-start(bf16[512,256]{1,0:T(8,128)(2,1)} %get-tuple-element.74), channel_id=1, source_target_pairs={{3,2},{2,1},{1,0},{7,6},{6,5},{5,4},{11,10},{10,9},{9,8},{15,14},{... | collective-permute-start | bytes 786440 | tf_op jit(solution)/shard_map/ppermute | solution.py:575
  97.2 17.2 %collective-permute-start.21 = (bf16[256,256]{1,0:T(8,128)(2,1)}, bf16[256,256]{1,0:T(8,128)(2,1)S(1)}, u32[]{:S(2)}, u32[]{:S(2)}) collective-permute-start(bf16[256,256]{1,0:T(8,128)(2,1)} %add_up.4), channel_id=1, source_target_pairs={{0,2},{1,3},{2,0},{3,1},{4,6},{5,7},{6,4},{7,5},{8,10},{9,11},{10,... | collective-permute-start | bytes 393224 | tf_op jit(solution)/shard_map/ppermute | solution.py:579
  100.1 16.3 %collective-permute-start.19 = (bf16[256,256]{1,0:T(8,128)(2,1)}, bf16[256,256]{1,0:T(8,128)(2,1)S(1)}, u32[]{:S(2)}, u32[]{:S(2)}) collective-permute-start(bf16[256,256]{1,0:T(8,128)(2,1)} %add_up.3), channel_id=1, source_target_pairs={{0,2},{1,3},{2,0},{3,1},{4,6},{5,7},{6,4},{7,5},{8,10},{9,11},{10,... | collective-permute-start | bytes 393224 | tf_op jit(solution)/shard_map/ppermute | solution.py:579
  (9 other events, 8.3 us)
Sparse Core Ops, SparseCore 0:
  40.5 26.4 all-gather.1

commit v5 on v4

v5 whole, which is shorter than its diff:
```python
import functools

import jax
import jax.numpy as jnp
import numpy as np
from jax import lax
from jax.experimental import pallas as pl
from jax.experimental.pallas import tpu as pltpu
from jax.sharding import PartitionSpec as P

HD = 64
PAGE = 64
VARS = 4
BIAS_PARTS = 3
LANES = 128
HIDDEN_SCORE = -1e30
EPS = 1e-06

VMEM = pl.BlockSpec(memory_space=pltpu.VMEM)
SMEM = pl.BlockSpec(memory_space=pltpu.SMEM)
ANY = pl.BlockSpec(memory_space=pl.ANY)
HBM = pl.BlockSpec(memory_space=pltpu.HBM)


def params(mib):
    return pltpu.CompilerParams(vmem_limit_bytes=mib << 20)


def cost(flops, nbytes, exps=0):
    return pl.CostEstimate(flops=flops, bytes_accessed=nbytes, transcendentals=exps)


def round_up(amount, unit):
    return (amount + unit - 1) // unit * unit


def dot_f32(left, right):
    return jnp.dot(left, right, preferred_element_type=jnp.float32)


def start_loads(sources, targets, sems):
    loads = [
        pltpu.make_async_copy(source, target, sems.at[i])
        for i, (source, target) in enumerate(zip(sources, targets))
    ]
    for load in loads:
        load.start()
    return loads


def finish_loads(loads):
    for load in loads:
        load.wait()


def tp_xor(value, mask):
    return lax.ppermute(value, "tp", [(i, i ^ mask) for i in range(lax.axis_size("tp"))])


def pair_gather(shard, parts, first=None):
    step = shard.shape[0] // parts
    split = [shard]
    if parts > 1:
        split = [shard[i * step : (i + 1) * step] for i in range(parts)]
        split, shard = lax.optimization_barrier((split, shard))
    far = [tp_xor(part, 2) for part in split]
    near = tp_xor(shard, 1)
    if first is not None:
        far[0], _ = lax.optimization_barrier((far[0], first))
    return [shard, near] + far + [tp_xor(part, 1) for part in far]


def turn_gather(shard):
    count = lax.axis_size("tp")
    pairs = [[(i, (i + turn) % count) for i in range(count)] for turn in range(1, count)]
    return [shard] + [lax.ppermute(shard, "tp", each) for each in pairs]


def gather_pieces(shard, parts, first=None):
    if lax.axis_size("tp") == 4:
        return pair_gather(shard, parts, first)
    return turn_gather(shard)


def assemble(pieces, place, count, target):
    width = pieces[0].shape[1]

    def put(block, value, first=0):
        columns = pl.ds(pl.multiple_of(block * width, width), width)
        target[pl.ds(first, value.shape[0]), columns] = value

    if count != 4:
        for turn, piece in enumerate(pieces):
            put(lax.rem(place + count - turn, count), piece[...])
        return
    put(place, pieces[0][...])
    put(place ^ 1, pieces[1][...])
    parts = (len(pieces) - 2) // 2
    for i in range(parts):
        first = i * (target.shape[0] // parts)
        put(place ^ 2, pieces[2 + i][...], first)
        put(place ^ 3, pieces[2 + parts + i][...], first)


def request_bounds(lengths):
    starts, ends, total = [], [], 0
    for r in range(lengths.shape[0]):
        starts.append(total)
        total = total + lengths[r]
        ends.append(total)
    return starts, ends


def segments_of(index, ends):
    segment = jnp.zeros_like(index)
    for end in ends:
        segment += (index >= end).astype(jnp.int32)
    return segment


def mark_count(requests):
    return round_up(BIAS_PARTS * VARS + requests, 16)


def tables_kernel(count, lengths, bias, frequency, positions, variate, *refs):
    cosine, sine, extra, marks = refs[count : count + 4]
    loads = start_loads(refs[:count], refs[count + 4 : -1], refs[-1])
    rows = positions.shape[1]
    width = cosine.shape[1]
    angles = frequency[...] * positions[...].astype(jnp.float32)
    cos_rows, sin_rows = jnp.cos(angles), jnp.sin(angles)
    copies = width // HD
    cosine[...] = jnp.transpose(jnp.concatenate([cos_rows, cos_rows] * copies, axis=0))
    sine[...] = jnp.transpose(jnp.concatenate([-sin_rows, sin_rows] * copies, axis=0))

    ids = variate[...].astype(jnp.float32)
    row = lax.broadcasted_iota(jnp.int32, extra.shape, 0)
    below = jnp.zeros(extra.shape, jnp.float32)
    for i in range(rows // extra.shape[1]):
        below = jnp.where(row == i, ids[:, i * extra.shape[1] : (i + 1) * extra.shape[1]], below)
    extra[...] = below.astype(jnp.bfloat16)

    requests = lengths.shape[0]
    shape = (mark_count(requests), rows)
    _, ends = request_bounds(lengths)
    me = lax.axis_index("seq")
    index = lax.broadcasted_iota(jnp.int32, shape, 1) + me * rows
    mark = lax.broadcasted_iota(jnp.int32, shape, 0)
    request = mark - BIAS_PARTS * VARS
    other = (segments_of(index, ends) != request) & (request >= 0) & (request < requests)
    same = (mark % VARS).astype(jnp.float32) == ids
    part = mark // VARS
    for h in range(marks.shape[0]):
        value = jnp.where(same, bias[0, h], bias[1, h])
        high = value.astype(jnp.bfloat16).astype(jnp.float32)
        middle = (value - high).astype(jnp.bfloat16).astype(jnp.float32)
        low = value - high - middle
        column = jnp.where(part == 0, high, jnp.where(part == 1, middle, low))
        column = jnp.where(part < BIAS_PARTS, column, 0.0)
        column = jnp.where(other, HIDDEN_SCORE, column)
        rest = jnp.zeros((LANES - shape[0], rows), jnp.float32)
        marks[h] = jnp.transpose(jnp.concatenate([column, rest], axis=0)).astype(jnp.bfloat16)
    finish_loads(loads)


def tables(lengths, bias, positions, variate, width, arrays):
    rows = positions.shape[0]
    half = HD // 2
    heads = width // HD
    frequency = 10000.0 ** (-np.arange(half, dtype=np.float32) / np.float32(half))
    extra = round_up(rows // (2 * width), 16)
    return pl.pallas_call(
        functools.partial(tables_kernel, len(arrays)),
        out_shape=[
            jax.ShapeDtypeStruct((rows, width), jnp.float32),
            jax.ShapeDtypeStruct((rows, width), jnp.float32),
            jax.ShapeDtypeStruct((extra, 2 * width), jnp.bfloat16),
            jax.ShapeDtypeStruct((heads, rows, LANES), jnp.bfloat16),
        ]
        + [jax.ShapeDtypeStruct(array.shape, array.dtype) for array in arrays],
        in_specs=[SMEM, SMEM, VMEM, VMEM, VMEM] + [ANY] * len(arrays),
        out_specs=[VMEM] * (4 + len(arrays)),
        scratch_shapes=[pltpu.SemaphoreType.DMA((len(arrays),))],
        compiler_params=params(6),
        cost_estimate=cost(rows * 1024, 1 << 20, rows * 64),
        name="tables",
    )(
        lengths,
        bias,
        jnp.asarray(frequency.astype(np.float32).reshape(half, 1)),
        positions.reshape(1, rows),
        variate.reshape(1, rows),
        *arrays,
    )


def rotate_lanes(vectors, cosine, signed_sine):
    lane = lax.broadcasted_iota(jnp.int32, vectors.shape, 1)
    half = HD // 2
    ahead = pltpu.roll(vectors, vectors.shape[1] - half, 1)
    behind = pltpu.roll(vectors, half, 1)
    partner = jnp.where(lane % HD < half, ahead, behind)
    return vectors * cosine + partner * signed_sine


def norm_rows(values, gain):
    scale = lax.rsqrt(jnp.mean(values * values, axis=-1, keepdims=True) + EPS)
    return (values * scale * gain).astype(jnp.bfloat16)


def project_kernel(places, count, *refs):
    pieces = refs[:count]
    gain, w_q, w_k, w_v, cosine, sine, extra, tokens_out, queries, pairs = refs[count:-2]
    tokens, sem = refs[-2:]
    pairs[tokens.shape[0] :, :] = extra[...]
    assemble(pieces, lax.axis_index("tp"), places, tokens)
    keep = pltpu.make_async_copy(tokens, tokens_out, sem)
    keep.start()
    rows = tokens.shape[0]
    width = w_q.shape[1]
    step = min(rows, 256)
    gain_row = gain[...].astype(jnp.float32).reshape(1, -1)
    for first in range(0, rows, step):
        part = pl.ds(first, step)
        normed = norm_rows(tokens[part, :].astype(jnp.float32), gain_row)
        cos_part, sin_part = cosine[part, :], sine[part, :]
        query = rotate_lanes(dot_f32(normed, w_q[...]), cos_part, sin_part)
        queries[part, :] = query.astype(jnp.bfloat16) * jnp.bfloat16(HD**-0.5)
        key = rotate_lanes(dot_f32(normed, w_k[...]), cos_part, sin_part)
        pairs[part, :width] = key.astype(jnp.bfloat16)
        pairs[part, width:] = dot_f32(normed, w_v[...]).astype(jnp.bfloat16)
    keep.wait()


def project(pieces, gain, w_query, w_key, w_value, cosine, sine, extra):
    rows, part = pieces[0].shape
    width = w_query.shape[1]
    features = w_query.shape[0]
    return pl.pallas_call(
        functools.partial(project_kernel, lax.axis_size("tp"), len(pieces)),
        out_shape=[
            jax.ShapeDtypeStruct((rows, features), jnp.bfloat16),
            jax.ShapeDtypeStruct((rows, width), jnp.bfloat16),
            jax.ShapeDtypeStruct((rows + extra.shape[0], 2 * width), jnp.bfloat16),
        ],
        in_specs=[VMEM] * (len(pieces) + 7),
        out_specs=[HBM, VMEM, VMEM],
        scratch_shapes=[pltpu.VMEM((rows, features), jnp.bfloat16), pltpu.SemaphoreType.DMA],
        compiler_params=params(6),
        cost_estimate=cost(6 * rows * features * width, 4 << 20),
        name="project",
    )(*pieces, gain, w_query, w_key, w_value, cosine, sine, extra)


def seq_xor(value, mask):
    return lax.ppermute(value, "seq", [(i, i ^ mask) for i in range(lax.axis_size("seq"))])


def seq_pieces(pairs):
    if lax.axis_size("seq") == 8:
        diagonal = seq_xor(pairs, 6)
        across = seq_xor(pairs, 2)
        down = seq_xor(pairs, 4)
        twin = seq_xor(pairs, 1)
        across_twin = seq_xor(across, 1)
        down_twin = seq_xor(down, 1)
        diagonal_twin = seq_xor(diagonal, 1)
        return [pairs, twin, across, across_twin, down, down_twin, diagonal, diagonal_twin]
    return [lax.all_gather(pairs, "seq", axis=0)]


def piece_copies(pieces, me, wanted):
    if len(pieces) > 1:
        for m, piece in enumerate(pieces):
            wanted(piece, me ^ m)
    else:
        for j in range(pieces[0].shape[0]):
            wanted(pieces[0].at[j], j)


def attend_kernel(count, heads, reach, lengths, queries, query_marks, *refs):
    pieces = refs[:count]
    out, q_buf, k_buf, v_buf, extra_buf, scores, peak, total, sems = refs[count:]
    me = lax.axis_index("seq")
    rows = queries.shape[0]
    _, ends = request_bounds(lengths)
    request_start = 0
    for end in ends:
        request_start = jnp.where(end <= me * rows, end, request_start)
    last = me - request_start // rows
    width = queries.shape[1]

    def copies(source, slot):
        return [
            pltpu.make_async_copy(
                source.at[pl.ds(0, rows), pl.ds(0, width)],
                k_buf.at[slot, :, pl.ds(0, width)],
                sems.at[slot, 0],
            ),
            pltpu.make_async_copy(
                source.at[pl.ds(0, rows), pl.ds(width, width)],
                v_buf.at[slot, :, pl.ds(0, width)],
                sems.at[slot, 1],
            ),
            pltpu.make_async_copy(
                source.at[pl.ds(rows, extra_buf.shape[1]), :], extra_buf.at[slot], sems.at[slot, 2]
            ),
        ]

    def begin(source, block):
        distance = me - block

        @pl.when((distance >= 0) & (distance <= last))
        def _():
            for copy in copies(source, distance):
                copy.start()

    piece_copies(pieces, me, begin)
    example = pieces[0] if count > 1 else pieces[0].at[0]

    marks = mark_count(lengths.shape[0])

    def finish(slot):
        for copy in copies(example, slot):
            copy.wait()
        extra = extra_buf[slot].astype(jnp.float32)
        pair_width = extra.shape[1]
        variates = jnp.concatenate([extra[i : i + 1] for i in range(rows // pair_width)], axis=1)
        mark = lax.broadcasted_iota(jnp.int32, (marks, rows), 0)
        key = lax.broadcasted_iota(jnp.int32, (marks, rows), 1) + (me - slot) * rows
        segment = segments_of(key, ends)
        same_variate = (mark % VARS).astype(jnp.float32) == variates
        same_segment = mark - BIAS_PARTS * VARS == segment
        marked = (same_variate & (mark < BIAS_PARTS * VARS)) | (
            same_segment & (mark >= BIAS_PARTS * VARS)
        )
        columns = jnp.transpose(jnp.where(marked, 1.0, 0.0))
        k_buf[slot, :, width : width + marks] = columns.astype(jnp.bfloat16)

    lane = lax.broadcasted_iota(jnp.int32, (rows, width), 1)
    for h in range(heads):
        part = pl.ds(h * rows, rows)
        q_buf[part, :width] = jnp.where(lane // HD == h, queries[...], jnp.bfloat16(0))
        q_buf[part, width:] = query_marks[h]
    for slot in range(reach + 1):
        v_buf[slot, :, width:] = jnp.ones((rows, LANES), jnp.bfloat16)
        k_buf[slot, :, width:] = jnp.zeros((rows, LANES), jnp.bfloat16)

    def narrow(tile):
        best = tile[:, :LANES]
        for first in range(LANES, rows, LANES):
            best = jnp.maximum(best, tile[:, first : first + LANES])
        return best

    def score(h, slot):
        return lax.dot_general(
            q_buf[pl.ds(h * rows, rows), :],
            k_buf[slot],
            (((1,), (1,)), ((), ())),
            preferred_element_type=jnp.float32,
        )

    finish(0)
    q_at = lax.broadcasted_iota(jnp.int32, (rows, rows), 0)
    k_at = lax.broadcasted_iota(jnp.int32, (rows, rows), 1)
    for h in range(heads):
        tile = jnp.where(k_at <= q_at, score(h, 0), HIDDEN_SCORE)
        scores[h, 0] = tile
        peak[h] = narrow(tile)

    def first_pass(slot, carry):
        finish(slot)
        for h in range(heads):
            tile = score(h, slot)
            scores[h, slot] = tile
            peak[h] = jnp.maximum(peak[h], narrow(tile))
        return carry

    lax.fori_loop(1, last + 1, first_pass, 0)
    for h in range(heads):
        best = jnp.max(peak[h], axis=1, keepdims=True)
        peak[h] = jnp.broadcast_to(best, (rows, LANES))
        total[h] = jnp.zeros_like(total[h])

    def second_pass(slot, carry):
        for h in range(heads):
            best = peak[h]
            wide = jnp.concatenate([best] * (rows // LANES), axis=1)
            weight = jnp.exp(scores[h, slot] - wide).astype(jnp.bfloat16)
            total[h] += dot_f32(weight, v_buf[slot])
        return carry

    lax.fori_loop(0, last + 1, second_pass, 0)
    result = total[0, :, :width] / total[0, :, width:]
    for h in range(1, heads):
        result = jnp.where(lane // HD == h, total[h, :, :width] / total[h, :, width:], result)
    out[...] = result.astype(jnp.bfloat16)


def attend(lengths, queries, query_marks, pieces, heads, reach):
    rows, width = queries.shape
    slots = reach + 1
    return pl.pallas_call(
        functools.partial(attend_kernel, len(pieces), heads, reach),
        out_shape=jax.ShapeDtypeStruct((rows, width), jnp.bfloat16),
        in_specs=[SMEM, VMEM, VMEM] + [ANY] * len(pieces),
        out_specs=VMEM,
        scratch_shapes=[
            pltpu.VMEM((heads * rows, width + LANES), jnp.bfloat16),
            pltpu.VMEM((slots, rows, width + LANES), jnp.bfloat16),
            pltpu.VMEM((slots, rows, width + LANES), jnp.bfloat16),
            pltpu.VMEM((slots, pieces[0].shape[-2] - rows, pieces[0].shape[-1]), jnp.bfloat16),
            pltpu.VMEM((heads, slots, rows, rows), jnp.float32),
            pltpu.VMEM((heads, rows, LANES), jnp.float32),
            pltpu.VMEM((heads, rows, width + LANES), jnp.float32),
            pltpu.SemaphoreType.DMA((slots, 3)),
        ],
        compiler_params=params(8 + 2 * slots),
        cost_estimate=cost(
            4 * heads * rows * rows * slots * 256, 4 << 20, heads * rows * rows * slots
        ),
        name="attend",
    )(lengths, queries, query_marks, *pieces)


def cache_kernel(count, window, lengths, page_table, *refs):
    pieces = refs[:count]
    out, rows_buf, logical, sems = refs[count:]
    rows = rows_buf.shape[1]
    blocks = rows_buf.shape[0]
    width = out.shape[2]
    pages = out.shape[0] // PAGE
    me = lax.axis_index("seq")
    started = []

    def begin(source, block):
        copy = pltpu.make_async_copy(
            source.at[pl.ds(0, rows), :], rows_buf.at[block], sems.at[len(started)]
        )
        copy.start()
        started.append(copy)

    piece_copies(pieces, me, begin)

    def place_page(page, carry):
        local = page_table[page] - me * pages

        @pl.when((local >= 0) & (local < pages))
        def _():
            logical[local] = page

        return carry

    lax.fori_loop(0, page_table.shape[0], place_page, 0)
    starts, _ = request_bounds(lengths)
    for copy in started:
        copy.wait()
    row = lax.broadcasted_iota(jnp.int32, (PAGE, window), 0)
    column = lax.broadcasted_iota(jnp.int32, (PAGE, window), 1)

    def one_page(page, carry):
        first, amount, base = 0, 0, 0
        for r, start in enumerate(starts):
            count_r = (lengths[r] + PAGE - 1) // PAGE
            ahead = (logical[page] - base) * PAGE
            within = (ahead >= 0) & (ahead < lengths[r])
            first = jnp.where(within, start + ahead, first)
            amount = jnp.where(within, jnp.minimum(lengths[r] - ahead, PAGE), amount)
            base = base + count_r
        block = first // rows
        total = None
        for ahead in range(2):
            at = jnp.minimum(block + ahead, blocks - 1)
            inside = first - block * rows
            if ahead == 0:
                start = jnp.minimum(inside // 16 * 16, rows - window)
                offset = inside - start
            else:
                start = 0
                offset = inside - rows
            wanted = (row + offset == column) & (row < amount)
            if ahead == 1:
                wanted = wanted & (block + 1 < blocks)
            chooser = jnp.where(wanted, 1.0, 0.0).astype(jnp.bfloat16)
            found = dot_f32(chooser, rows_buf[at, pl.ds(pl.multiple_of(start, 16), window), :])
            total = found if total is None else total + found
        part = pl.ds(pl.multiple_of(page * PAGE, PAGE), PAGE)
        out[part, 0, :] = total[:, :width].astype(jnp.bfloat16)
        out[part, 1, :] = total[:, width:].astype(jnp.bfloat16)
        return carry

    lax.fori_loop(0, pages, one_page, 0)


def fill_cache(lengths, page_table, pieces, rows):
    width = pieces[0].shape[-1]
    blocks = lax.axis_size("seq")
    pages = page_table.shape[0] // blocks
    return pl.pallas_call(
        functools.partial(cache_kernel, len(pieces), 2 * PAGE),
        out_shape=jax.ShapeDtypeStruct((pages * PAGE, 2, width // 2), jnp.bfloat16),
        in_specs=[SMEM] * 2 + [ANY] * len(pieces),
        out_specs=VMEM,
        scratch_shapes=[
            pltpu.VMEM((blocks, rows, width), jnp.bfloat16),
            pltpu.SMEM((pages,), jnp.int32),
            pltpu.SemaphoreType.DMA((blocks,)),
        ],
        compiler_params=params(8),
        cost_estimate=cost(4 * pages * PAGE * 2 * PAGE * width, 3 << 20),
        name="fill_cache",
    )(lengths, page_table, *pieces)


def fetch_kernel(count, *refs):
    finish_loads(start_loads(refs[:count], refs[count:-1], refs[-1]))


def fetch(arrays):
    return pl.pallas_call(
        functools.partial(fetch_kernel, len(arrays)),
        out_shape=[jax.ShapeDtypeStruct(array.shape, array.dtype) for array in arrays],
        in_specs=[HBM] * len(arrays),
        out_specs=[VMEM] * len(arrays),
        scratch_shapes=[pltpu.SemaphoreType.DMA((len(arrays),))],
        compiler_params=params(10),
        cost_estimate=cost(0, 4 * sum(array.size for array in arrays)),
        name="fetch",
    )(*arrays)


def hidden_kernel(places, count, on_line, *refs):
    pieces = refs[:count]
    tokens, gain, w_out, w_gate, w_up, w_down = refs[count : count + 6]
    outs, attended = refs[count + 6 : -1], refs[-1]
    hidden, kept = outs[:2]
    place = lax.axis_index("tp")
    assemble(pieces, place, places, attended)
    rows, features = tokens.shape
    width = kept.shape[1]
    step = min(rows, 256)
    gain_row = gain[...].astype(jnp.float32).reshape(1, -1)
    for first in range(0, rows, step):
        part = pl.ds(first, step)
        projected = dot_f32(attended[part, :], w_out[...])
        residual = (tokens[part, :].astype(jnp.float32) + projected).astype(jnp.bfloat16)
        mine = residual[:, :width]
        for i in range(1, places):
            mine = jnp.where(place == i, residual[:, i * width : (i + 1) * width], mine)
        kept[part, :] = mine
        normed = norm_rows(residual.astype(jnp.float32), gain_row)
        gate = dot_f32(normed, w_gate[...])
        up = dot_f32(normed, w_up[...])
        hidden[part, :] = (jax.nn.silu(gate) * up).astype(jnp.bfloat16)
    if not on_line:
        return

    weights = w_down[:, pl.ds(pl.multiple_of((place ^ 3) * width, width), width)]
    through = dot_f32(hidden[...], weights).astype(jnp.bfloat16)
    outs[2][...] = through[: rows // 2]
    outs[3][...] = through[rows // 2 :]


def hidden_of(pieces, tokens, gain, w_out, w_gate, w_up, w_down):
    rows, features = tokens.shape
    places = lax.axis_size("tp")
    width = features // places
    units = w_gate.shape[1]
    on_line = places == 4
    shapes = [
        jax.ShapeDtypeStruct((rows, units), jnp.bfloat16),
        jax.ShapeDtypeStruct((rows, width), jnp.bfloat16),
    ]
    if on_line:
        shapes += [jax.ShapeDtypeStruct((rows // 2, width), jnp.bfloat16)] * 2
    return pl.pallas_call(
        functools.partial(hidden_kernel, places, len(pieces), on_line),
        out_shape=shapes,
        in_specs=[VMEM] * (len(pieces) + 6),
        out_specs=[VMEM] * len(shapes),
        scratch_shapes=[pltpu.VMEM((rows, w_out.shape[0]), jnp.bfloat16)],
        compiler_params=params(12),
        cost_estimate=cost(6 * rows * features * units, 10 << 20),
        name="hidden",
    )(*pieces, tokens, gain, w_out, w_gate, w_up, w_down)


def down_kernel(hidden, kept, w_down, far_top, far_low, near, own):
    place = lax.axis_index("tp")
    rows, width = own.shape

    def product(index):
        weights = w_down[:, pl.ds(pl.multiple_of(index * width, width), width)]
        return dot_f32(hidden[...], weights)

    far = product(place ^ 2)
    far_top[...] = far[: rows // 2]
    far_low[...] = far[rows // 2 :]
    near[...] = product(place ^ 1).astype(jnp.bfloat16)
    own[...] = product(place) + kept[...].astype(jnp.float32)


def down_blocks(hidden, kept, w_down):
    rows, width = kept.shape
    shapes = [((rows // 2, width), jnp.float32)] * 2
    shapes += [((rows, width), jnp.bfloat16), ((rows, width), jnp.float32)]
    return pl.pallas_call(
        down_kernel,
        out_shape=[jax.ShapeDtypeStruct(*shape) for shape in shapes],
        in_specs=[VMEM] * 3,
        out_specs=[VMEM] * 4,
        compiler_params=params(6),
        cost_estimate=cost(2 * rows * w_down.shape[0] * width * 3, 5 << 20),
        name="down_blocks",
    )(hidden, kept, w_down)


def add_kernel(out_parts, *refs):
    whole, parts, out = refs[: -1 - out_parts], refs[-1 - out_parts : -1], refs[-1]
    step = out.shape[0] // max(out_parts, 1)
    for i, first in enumerate(range(0, out.shape[0], step)):
        rows = pl.ds(first, step)
        total = whole[0][rows, :].astype(jnp.float32)
        for ref in whole[1:]:
            total = total + ref[rows, :].astype(jnp.float32)
        if out_parts:
            total = total + parts[i][...].astype(jnp.float32)
        out[rows, :] = total.astype(jnp.bfloat16)


def add_up(whole, parts=()):
    terms = [*whole, *parts]
    size = whole[0].size
    return pl.pallas_call(
        functools.partial(add_kernel, len(parts)),
        out_shape=jax.ShapeDtypeStruct(whole[0].shape, jnp.bfloat16),
        in_specs=[VMEM] * len(terms),
        out_specs=VMEM,
        compiler_params=params(6),
        cost_estimate=cost(size * len(terms), 4 * size * len(terms)),
        name="add_up",
    )(*terms)


def feed_forward(pieces, tokens, gain, w_out, w_gate, w_up, w_down):
    hidden, kept, *through = hidden_of(pieces, tokens, gain, w_out, w_gate, w_up, w_down)
    if lax.axis_size("tp") != 4:
        share = lax.psum_scatter(
            dot_f32(hidden, w_down).astype(jnp.bfloat16), "tp", scatter_dimension=1, tiled=True
        )
        return add_up([kept, share]), hidden
    through = [tp_xor(part, 1) for part in through]
    far_top, far_low, near, own = down_blocks(hidden, kept, w_down)
    joined = [add_up([part, other]) for part, other in zip((far_top, far_low), through)]
    near = tp_xor(near, 1)
    far = [tp_xor(part, 2) for part in joined]
    return add_up([own, near], far), joined[-1]


def per_device(
    tokens,
    variate,
    positions,
    lengths,
    page_table,
    gain_attn,
    w_query,
    w_key,
    w_value,
    var_bias,
    w_out,
    gain_ffn,
    w_gate,
    w_up,
    w_down,
):
    rows = tokens.shape[0]
    width = w_query.shape[1]
    heads = width // HD
    reach = lax.axis_size("seq") // 2

    weights = (tokens, gain_attn, w_query, w_key, w_value)
    cosine, sine, extra, marks, *weights = tables(
        lengths, var_bias, positions, variate, width, weights
    )
    pieces = gather_pieces(tokens, 2, extra)
    pieces, w_out = lax.optimization_barrier((pieces, w_out))
    w_out_all = lax.all_gather(w_out, "tp", axis=0, tiled=True)
    pieces[0] = weights[0]
    token_rows, queries, pairs = project(pieces, *weights[1:], cosine, sine, extra)
    row_pieces = seq_pieces(pairs)
    attended = attend(lengths, queries, marks, row_pieces, heads, reach)
    attended_pieces = gather_pieces(attended, 1)
    large = (token_rows, gain_ffn, w_out_all, w_gate, w_up, w_down)
    large = lax.optimization_barrier((large, attended))[0]
    mixed, joined = feed_forward(attended_pieces, *fetch(large))
    row_pieces, _ = lax.optimization_barrier((row_pieces, joined))
    cache = fill_cache(lengths, page_table, row_pieces, rows)
    return (mixed, cache)


def solution(mesh):
    placed = (
        P("seq", "tp"),
        P("seq"),
        P("seq"),
        P(),
        P(),
        P(),
        P(None, "tp"),
        P(None, "tp"),
        P(None, "tp"),
        P(None, "tp"),
        P("tp", None),
        P(),
        P(None, "tp"),
        P(None, "tp"),
        P("tp", None),
    )
    return jax.shard_map(
        per_device,
        mesh=mesh,
        in_specs=placed,
        out_specs=(P("seq", "tp"), P("seq", None, "tp")),
        check_vma=False,
    )
```

time: 126 us -> 107 us (0.85)
  starting transfers between devices: 31.4 us -> 20.2 us
  other arithmetic: 9.59 us -> 0 us
  between operations: 17.1 us -> 14.4 us
  local copies, waits for them, and re-layouts: 14.9 us -> 17.5 us
    ppermute x15 -> x13, starting transfers between devices: 27.3 us -> 16.1 us  [tp_xor(): lax.ppermute(value, 'tp', [(i, i ^ mask) for i in range(lax.axis_size('tp...]
    unnamed x68 -> x76, local copies, waits for them, and re-layouts: 10.1 us -> 16.5 us
    reshape x5 -> x0, local copies, waits for them, and re-layouts: 3.44 us -> none  [the longest x2 2.55 us: per_device(): gains = (gain_attn.reshape(1, -1), gain_ffn.reshape(1, -1))]
    reduce_sum x5 -> x0, other arithmetic: 2.44 us -> none  [the longest x2 0.89 us: running_sum(): jnp.sum(jnp.where(at[None, :] <= at[:, None], values[None, :], 0), axis=1)]
    pallas_call x1, Pallas kernels: 2.31 us -> 4.69 us  [fill_cache(): pl.pallas_call(functools.partial(cache_kernel, len(pieces), 2 * PAGE), ou...]
    pallas_call x3, Pallas kernels: 3.13 us -> 0.86 us  [add_up(): pl.pallas_call(functools.partial(add_kernel, len(parts)), out_shape=jax.S...]
    convert_element_type x2 -> x0, other arithmetic: 1.37 us -> none  [the longest x1 0.69 us: rope_tables(): angles = positions.astype(jnp.float32)[:, None] * frequency[None, :]]
    sub x3 -> x0, other arithmetic: 1.31 us -> none  [the longest x1 1.3 us: page_sources(): starts = ends - lengths]
  transfers between devices with their start and end apart: 23 -> 21, of which waited for: 13 -> 11; matrix products, arithmetic and copies ran while one was open for 12% -> 0% of each run, Pallas kernels for 9% -> 12%
where the time goes in v5:
time: 107 us; the launch traced here: 105 us
  waiting for transfers between devices  34.5 us (32%)
  starting transfers between devices  20.2 us (19%)
  Pallas kernels  18.2 us (17%)
  local copies, waits for them, and re-layouts  17.5 us (16%)
  between operations  14.4 us (13%)
    ppermute x13, waiting for transfers between devices, tp_xor(): lax.ppermute(value, 'tp', [(i, i ^ mask) for i in range(lax.axis_size('tp...  23.4 us
    unnamed x76, local copies, waits for them, and re-layouts  16.5 us
    ppermute x13, starting transfers between devices, tp_xor(): lax.ppermute(value, 'tp', [(i, i ^ mask) for i in range(lax.axis_size('tp...  16.1 us
    ppermute x7, waiting for transfers between devices, seq_xor(): lax.ppermute(value, 'seq', [(i, i ^ mask) for i in range(lax.axis_size('s...  11.2 us
    pallas_call x1, Pallas kernels, hidden_of(): pl.pallas_call(functools.partial(hidden_kernel, places, len(pieces), on_l...  4.87 us
    pallas_call x1, Pallas kernels, fill_cache(): pl.pallas_call(functools.partial(cache_kernel, len(pieces), 2 * PAGE), ou...  4.69 us
    ppermute x7, starting transfers between devices, seq_xor(): lax.ppermute(value, 'seq', [(i, i ^ mask) for i in range(lax.axis_size('s...  4.06 us
    pallas_call x1, Pallas kernels, attend(): pl.pallas_call(functools.partial(attend_kernel, len(pieces), heads, reach...  3.61 us
  transfers between devices with their start and end apart: 21, of which 11 were waited for; matrix products, arithmetic and copies ran while one was open for 0% of the time, Pallas kernels for 12%

profile of v5, /device:TPU:2, one launch (start us, length us, event | category | flops | bytes accessed | tf_op | source)
XLA Modules:
  0.0 104.9 jit_solution(16475291800681788072)
XLA Ops:
  7.2 1.0 fusion
  8.2 2.7 %collective-permute-start.1 = (bf16[256,256]{1,0:T(8,128)(2,1)S(1)}, bf16[256,256]{1,0:T(8,128)(2,1)S(1)}, u32[]{:S(2)}, u32[]{:S(2)}) collective-permute-start(bf16[256,256]{1,0:T(8,128)(2,1)S(1)} %get-tuple-element.54), channel_id=1, source_target_pairs={{0,2},{1,3},{2,0},{3,1},{4,6},{5,7},{6,4},{7,5},{8,10},{9,11},{10,... | collective-permute-start | bytes 393224 | tf_op jit(solution)/shard_map/ppermute | solution.py:57
  11.2 1.6 %collective-permute-start = (bf16[512,256]{1,0:T(8,128)(2,1)}, bf16[512,256]{1,0:T(8,128)(2,1)S(1)}, u32[]{:S(2)}, u32[]{:S(2)}) collective-permute-start(bf16[512,256]{1,0:T(8,128)(2,1)} %refs_0_.1), channel_id=1, source_target_pairs={{0,1},{1,0},{2,3},{3,2},{4,5},{5,4},{6,7},{7,6},{8,9},{9,8},{10,11... | collective-permute-start | bytes 786440 | tf_op jit(solution)/shard_map/ppermute | solution.py:57
  12.8 1.0 copy-done.4
  13.8 0.9 copy-done.19
  14.7 0.9 copy-done.20
  15.7 0.9 copy-done.21
  16.6 0.7 copy-done.24
  17.3 0.7 copy-done.25
  18.0 0.7 copy-done.26
  18.7 0.7 copy-done.27
  19.4 0.7 copy-done.29
  20.0 0.7 copy-done.34
  20.7 1.2 %tables.1 = (f32[512,128]{1,0:T(8,128)S(1)}, f32[512,128]{1,0:T(8,128)S(1)}, bf16[16,256]{1,0:T(8,128)(2,1)S(1)}, bf16[2,512,128]{2,1,0:T(8,128)(2,1)S(1)}, bf16...) custom-call(s32[4]{0:T(128)S(1)} %copy-done.29, ...), custom_call_target="tpu_custom_call" | custom-call | flops 524288 | bytes 1048576 | tf_op jit(solution)/shard_map/tables/pallas_call | solution.py:172
  22.5 0.7 copy-done.36
  23.7 1.6 %collective-permute-start.4 = (bf16[256,256]{1,0:T(8,128)(2,1)S(1)}, bf16[256,256]{1,0:T(8,128)(2,1)S(1)}, u32[]{:S(2)}, u32[]{:S(2)}) collective-permute-start(bf16[256,256]{1,0:T(8,128)(2,1)S(1)} %collective-permute-done.2.refs_3_), channel_id=1, source_target_pairs={{0,1},{1,0},{2,3},{3,2},{4,5},{5,4},{6,7},{7,6},{8,9},{9,8},{10,11... | collective-permute-start | bytes 393224 | tf_op jit(solution)/shard_map/ppermute | solution.py:57
  25.3 3.8 %collective-permute-done.3.refs_4_ = bf16[256,256]{1,0:T(8,128)(2,1)S(1)} collective-permute-done((bf16[256,256]{1,0:T(8,128)(2,1)S(1)}, bf16[256,256]{1,0:T(8,128)(2,1)S(1)}, u32[]{:S(2)}, u32[]{:S(2)}) %collective-permute-start.3) | collective-permute-done | bytes 131104 | tf_op jit(solution)/shard_map/ppermute | solution.py:57
  29.1 1.4 %collective-permute-done.4.refs_5_ = bf16[256,256]{1,0:T(8,128)(2,1)S(1)} collective-permute-done((bf16[256,256]{1,0:T(8,128)(2,1)S(1)}, bf16[256,256]{1,0:T(8,128)(2,1)S(1)}, u32[]{:S(2)}, u32[]{:S(2)}) %collective-permute-start.4) | collective-permute-done | bytes 131104 | tf_op jit(solution)/shard_map/ppermute | solution.py:57
  30.5 0.6 copy-done.22
  31.1 0.9 copy-done.23
  32.0 0.7 copy-done.33
  32.7 1.4 %project.1 = (bf16[512,1024]{1,0:T(8,128)(2,1)S(1)}, bf16[512,128]{1,0:T(8,128)(2,1)S(1)}, bf16[528,256]{1,0:T(8,128)(2,1)S(1)}) custom-call(bf16[512,256]{1,0:T(8,128)(2,1)S(1)} %get-tuple-element.52.refs_0_, bf16[512,256]{1,0:T(8,128)(2,1)S(1)} %collective-permute-done.refs_1_, bf16[256,256]{1,0:T(8,128)(2,1)S(1)} %collective-permute-done.1.refs_2_, ...), custom_call_target="tpu_custom_call" | custom-call | flops 402653184 | bytes 4194304 | tf_op jit(solution)/shard_map/project/pallas_call | solution.py:239
  34.1 1.6 %collective-permute-start.10 = (bf16[528,256]{1,0:T(8,128)(2,1)S(1)}, bf16[528,256]{1,0:T(8,128)(2,1)S(1)}, u32[]{:S(2)}, u32[]{:S(2)}) collective-permute-start(bf16[528,256]{1,0:T(8,128)(2,1)S(1)} %get-tuple-element.94.refs_0_), channel_id=1, source_target_pairs={{0,24},{4,28},{8,16},{12,20},{16,8},{20,12},{24,0},{28,4},{1,25},{... | collective-permute-start | bytes 811016 | tf_op jit(solution)/shard_map/ppermute | solution.py:256
  35.6 1.5 %collective-permute-start.6 = (bf16[528,256]{1,0:T(8,128)(2,1)S(1)}, bf16[528,256]{1,0:T(8,128)(2,1)S(1)}, u32[]{:S(2)}, u32[]{:S(2)}) collective-permute-start(bf16[528,256]{1,0:T(8,128)(2,1)S(1)} %get-tuple-element.94.refs_0_), channel_id=1, source_target_pairs={{0,8},{4,12},{8,0},{12,4},{16,24},{20,28},{24,16},{28,20},{1,9},{5... | collective-permute-start | bytes 811016 | tf_op jit(solution)/shard_map/ppermute | solution.py:256
  37.6 6.8 %collective-permute-done.10.refs_6_ = bf16[528,256]{1,0:T(8,128)(2,1)S(1)} collective-permute-done((bf16[528,256]{1,0:T(8,128)(2,1)S(1)}, bf16[528,256]{1,0:T(8,128)(2,1)S(1)}, u32[]{:S(2)}, u32[]{:S(2)}) %collective-permute-start.10) | collective-permute-done | bytes 270368 | tf_op jit(solution)/shard_map/ppermute | solution.py:256
  44.4 3.0 %collective-permute-done.6.refs_2_ = bf16[528,256]{1,0:T(8,128)(2,1)S(1)} collective-permute-done((bf16[528,256]{1,0:T(8,128)(2,1)S(1)}, bf16[528,256]{1,0:T(8,128)(2,1)S(1)}, u32[]{:S(2)}, u32[]{:S(2)}) %collective-permute-start.6) | collective-permute-done | bytes 270368 | tf_op jit(solution)/shard_map/ppermute | solution.py:256
  48.0 1.0 collective-permute-done.7.refs_3_
  49.4 0.7 copy-done.30
  50.0 3.6 %attend.1.refs_0_ = bf16[512,128]{1,0:T(8,128)(2,1)S(1)} custom-call(s32[4]{0:T(128)S(1)} %copy-done.30, bf16[512,128]{1,0:T(8,128)(2,1)S(1)} %get-tuple-element.69.queries, bf16[2,512,128]{2,1,0:T(8,128)(2,1)S(1)} %copy-done.37, bf16[528,256]{1,0:T(8,128)(2,1)S(1)} %get-tuple-element.94.refs_0_, bf16[528,256]{1,0:T(8,128)(2,1)S(1)} %collective-permute-done.5.refs_1_, ...), custom_call_target="tpu_custom_call" | custom-call | flops 2684354560 | bytes 4194304 | tf_op jit(solution)/shard_map/attend/pallas_call | solution.py:403
  53.7 2.6 %collective-permute-start.13 = (bf16[512,128]{1,0:T(8,128)(2,1)S(1)}, bf16[512,128]{1,0:T(8,128)(2,1)}, u32[]{:S(2)}, u32[]{:S(2)}) collective-permute-start(bf16[512,128]{1,0:T(8,128)(2,1)S(1)} %attend.1.refs_0_), channel_id=1, source_target_pairs={{0,2},{1,3},{2,0},{3,1},{4,6},{5,7},{6,4},{7,5},{8,10},{9,11},{10,... | collective-permute-start | bytes 393224 | tf_op jit(solution)/shard_map/ppermute | solution.py:57
  56.3 1.9 %collective-permute-start.12 = (bf16[512,128]{1,0:T(8,128)(2,1)S(1)}, bf16[512,128]{1,0:T(8,128)(2,1)}, u32[]{:S(2)}, u32[]{:S(2)}) collective-permute-start(bf16[512,128]{1,0:T(8,128)(2,1)S(1)} %attend.1.refs_0_), channel_id=1, source_target_pairs={{0,1},{1,0},{2,3},{3,2},{4,5},{5,4},{6,7},{7,6},{8,9},{9,8},{10,11... | collective-permute-start | bytes 393224 | tf_op jit(solution)/shard_map/ppermute | solution.py:57
  58.2 7.1 %collective-permute-done.13.refs_2_ = bf16[512,128]{1,0:T(8,128)(2,1)} collective-permute-done((bf16[512,128]{1,0:T(8,128)(2,1)S(1)}, bf16[512,128]{1,0:T(8,128)(2,1)}, u32[]{:S(2)}, u32[]{:S(2)}) %collective-permute-start.13) | collective-permute-done | bytes 131104 | tf_op jit(solution)/shard_map/ppermute | solution.py:57
  65.3 1.6 %copy-done.1 = bf16[1024,1024]{1,0:T(8,128)(2,1)S(1)} copy-done((bf16[1024,1024]{1,0:T(8,128)(2,1)S(1)}, bf16[1024,1024]{1,0:T(8,128)(2,1)}, u32[]{:S(2)}) %copy-start.1) | copy-done | bytes 2097176
  66.9 1.6 %copy-done.2 = bf16[1024,1024]{1,0:T(8,128)(2,1)S(1)} copy-done((bf16[1024,1024]{1,0:T(8,128)(2,1)S(1)}, bf16[1024,1024]{1,0:T(8,128)(2,1)}, u32[]{:S(2)}) %copy-start.2) | copy-done | bytes 2097176
  68.5 1.2 %copy-done.3 = bf16[512,1024]{1,0:T(8,128)(2,1)S(1)} copy-done((bf16[512,1024]{1,0:T(8,128)(2,1)S(1)}, bf16[512,1024]{1,0:T(8,128)(2,1)}, u32[]{:S(2)}) %copy-start.3) | copy-done | bytes 1048600
  69.7 0.6 fetch.1
  70.4 0.7 collective-permute-done.14.refs_3_
  71.0 4.9 %hidden.1 = (bf16[512,1024]{1,0:T(8,128)(2,1)S(1)}, bf16[512,256]{1,0:T(8,128)(2,1)S(1)}, bf16[256,256]{1,0:T(8,128)(2,1)S(1)}, bf16[256,256]{1,0:T(8,128)(2,1)S(1)}) custom-call(bf16[512,128]{1,0:T(8,128)(2,1)S(1)} %attend.1.refs_0_, bf16[512,128]{1,0:T(8,128)(2,1)} %collective-permute-done.12.refs_1_, bf16[512,128]{1,0:T(8,128)(2,1)} %collective-permute-done.13.refs_2_, ...), custom_call_target="tpu_custom_call" | custom-call | flops 3221225472 | bytes 10485760 | tf_op jit(solution)/shard_map/hidden/pallas_call | solution.py:576
  75.9 1.4 %collective-permute-start.18 = (bf16[256,256]{1,0:T(8,128)(2,1)S(1)}, bf16[256,256]{1,0:T(8,128)(2,1)S(1)}, u32[]{:S(2)}, u32[]{:S(2)}) collective-permute-start(bf16[256,256]{1,0:T(8,128)(2,1)S(1)} %get-tuple-element.93), channel_id=1, source_target_pairs={{0,1},{1,0},{2,3},{3,2},{4,5},{5,4},{6,7},{7,6},{8,9},{9,8},{10,11... | collective-permute-start | bytes 393224 | tf_op jit(solution)/shard_map/ppermute | solution.py:57
  77.3 0.7 collective-permute-start.16
  78.1 1.0 down_blocks.1
  79.1 1.4 %collective-permute-start.15 = (bf16[512,256]{1,0:T(8,128)(2,1)S(1)}, bf16[512,256]{1,0:T(8,128)(2,1)S(1)}, u32[]{:S(2)}, u32[]{:S(2)}) collective-permute-start(bf16[512,256]{1,0:T(8,128)(2,1)S(1)} %get-tuple-element.89), channel_id=1, source_target_pairs={{0,1},{1,0},{2,3},{3,2},{4,5},{5,4},{6,7},{7,6},{8,9},{9,8},{10,11... | collective-permute-start | bytes 786440 | tf_op jit(solution)/shard_map/ppermute | solution.py:57
  80.5 1.8 %collective-permute-done.18.refs_1_ = bf16[256,256]{1,0:T(8,128)(2,1)S(1)} collective-permute-done((bf16[256,256]{1,0:T(8,128)(2,1)S(1)}, bf16[256,256]{1,0:T(8,128)(2,1)S(1)}, u32[]{:S(2)}, u32[]{:S(2)}) %collective-permute-start.18) | collective-permute-done | bytes 131104 | tf_op jit(solution)/shard_map/ppermute | solution.py:57
  82.4 1.4 %collective-permute-start.19 = (bf16[256,256]{1,0:T(8,128)(2,1)S(1)}, bf16[256,256]{1,0:T(8,128)(2,1)S(1)}, u32[]{:S(2)}, u32[]{:S(2)}) collective-permute-start(bf16[256,256]{1,0:T(8,128)(2,1)S(1)} %add_up.4), channel_id=1, source_target_pairs={{0,2},{1,3},{2,0},{3,1},{4,6},{5,7},{6,4},{7,5},{8,10},{9,11},{10,... | collective-permute-start | bytes 393224 | tf_op jit(solution)/shard_map/ppermute | solution.py:57
  83.7 5.6 %collective-permute-done.16.refs_1_ = bf16[256,256]{1,0:T(8,128)(2,1)S(1)} collective-permute-done((bf16[256,256]{1,0:T(8,128)(2,1)S(1)}, bf16[256,256]{1,0:T(8,128)(2,1)S(1)}, u32[]{:S(2)}, u32[]{:S(2)}) %collective-permute-start.16) | collective-permute-done | bytes 131104 | tf_op jit(solution)/shard_map/ppermute | solution.py:57
  89.5 4.7 %fill_cache.1 = bf16[576,2,128]{2,1,0:T(2,128)(2,1)} custom-call(s32[4]{0:T(128)S(1)} %copy-done.31, s32[72]{0:T(128)S(1)} %copy-done.35, bf16[528,256]{1,0:T(8,128)(2,1)S(1)} %get-tuple-element.94.refs_0_, bf16[528,256]{1,0:T(8,128)(2,1)S(1)} %copy-done.12, bf16[528,256]{1,0:T(8,128)(2,1)S(1)} %copy-done.8, bf16[528,256]{1,0:T(8,128)(2,1)S(1)} %copy-done.16, ...), custom_call_target="tpu_custom_call" | custom-call | flops 75497472 | bytes 3145728 | tf_op jit(solution)/shard_map/fill_cache/pallas_call | solution.py:499
  94.3 3.0 %collective-permute-done.17.refs_2_ = bf16[256,256]{1,0:T(8,128)(2,1)S(1)} collective-permute-done((bf16[256,256]{1,0:T(8,128)(2,1)S(1)}, bf16[256,256]{1,0:T(8,128)(2,1)S(1)}, u32[]{:S(2)}, u32[]{:S(2)}) %collective-permute-start.17) | collective-permute-done | bytes 131104 | tf_op jit(solution)/shard_map/ppermute | solution.py:57
  97.2 0.8 add_up.5
  (82 shorter events, 3.1 us)
Async XLA Ops:
  7.2 58.1 %all-gather.2.cloned.1.call-start = ((), (), s32[]{:S(2)}) async-start(), calls=%async_computation | async-start | bytes 1310720 | tf_op jit(solution)/shard_map/all_gather | solution.py:688
  8.2 15.0 %collective-permute-start.1 = (bf16[256,256]{1,0:T(8,128)(2,1)S(1)}, bf16[256,256]{1,0:T(8,128)(2,1)S(1)}, u32[]{:S(2)}, u32[]{:S(2)}) collective-permute-start(bf16[256,256]{1,0:T(8,128)(2,1)S(1)} %get-tuple-element.54), channel_id=1, source_target_pairs={{0,2},{1,3},{2,0},{3,1},{4,6},{5,7},{6,4},{7,5},{8,10},{9,11},{10,... | collective-permute-start | bytes 393224 | tf_op jit(solution)/shard_map/ppermute | solution.py:57
  10.9 12.8 %collective-permute-start.2 = (bf16[256,256]{1,0:T(8,128)(2,1)S(1)}, bf16[256,256]{1,0:T(8,128)(2,1)S(1)}, u32[]{:S(2)}, u32[]{:S(2)}) collective-permute-start(bf16[256,256]{1,0:T(8,128)(2,1)S(1)} %get-tuple-element.57), channel_id=1, source_target_pairs={{0,2},{1,3},{2,0},{3,1},{4,6},{5,7},{6,4},{7,5},{8,10},{9,11},{10,... | collective-permute-start | bytes 393224 | tf_op jit(solution)/shard_map/ppermute | solution.py:57
  11.2 19.3 %collective-permute-start = (bf16[512,256]{1,0:T(8,128)(2,1)}, bf16[512,256]{1,0:T(8,128)(2,1)S(1)}, u32[]{:S(2)}, u32[]{:S(2)}) collective-permute-start(bf16[512,256]{1,0:T(8,128)(2,1)} %refs_0_.1), channel_id=1, source_target_pairs={{0,1},{1,0},{2,3},{3,2},{4,5},{5,4},{6,7},{7,6},{8,9},{9,8},{10,11... | collective-permute-start | bytes 786440 | tf_op jit(solution)/shard_map/ppermute | solution.py:57
  12.8 1.0 copy-start.4
  13.8 0.9 copy-start.19
  14.7 0.9 copy-start.20
  15.7 0.9 copy-start.21
  23.2 5.8 %collective-permute-start.3 = (bf16[256,256]{1,0:T(8,128)(2,1)S(1)}, bf16[256,256]{1,0:T(8,128)(2,1)S(1)}, u32[]{:S(2)}, u32[]{:S(2)}) collective-permute-start(bf16[256,256]{1,0:T(8,128)(2,1)S(1)} %collective-permute-done.1.refs_2_), channel_id=1, source_target_pairs={{0,1},{1,0},{2,3},{3,2},{4,5},{5,4},{6,7},{7,6},{8,9},{9,8},{10,11... | collective-permute-start | bytes 393224 | tf_op jit(solution)/shard_map/ppermute | solution.py:57
  23.7 6.8 %collective-permute-start.4 = (bf16[256,256]{1,0:T(8,128)(2,1)S(1)}, bf16[256,256]{1,0:T(8,128)(2,1)S(1)}, u32[]{:S(2)}, u32[]{:S(2)}) collective-permute-start(bf16[256,256]{1,0:T(8,128)(2,1)S(1)} %collective-permute-done.2.refs_3_), channel_id=1, source_target_pairs={{0,1},{1,0},{2,3},{3,2},{4,5},{5,4},{6,7},{7,6},{8,9},{9,8},{10,11... | collective-permute-start | bytes 393224 | tf_op jit(solution)/shard_map/ppermute | solution.py:57
  31.1 0.9 copy-start.23
  32.7 16.7 %copy-start.37 = (bf16[2,512,128]{2,1,0:T(8,128)(2,1)S(1)}, bf16[2,512,128]{2,1,0:T(8,128)(2,1)}, u32[]{:S(2)}) copy-start(bf16[2,512,128]{2,1,0:T(8,128)(2,1)} %copy-done.36) | copy-start | bytes 786436
  34.1 10.3 %collective-permute-start.10 = (bf16[528,256]{1,0:T(8,128)(2,1)S(1)}, bf16[528,256]{1,0:T(8,128)(2,1)S(1)}, u32[]{:S(2)}, u32[]{:S(2)}) collective-permute-start(bf16[528,256]{1,0:T(8,128)(2,1)S(1)} %get-tuple-element.94.refs_0_), channel_id=1, source_target_pairs={{0,24},{4,28},{8,16},{12,20},{16,8},{20,12},{24,0},{28,4},{1,25},{... | collective-permute-start | bytes 811016 | tf_op jit(solution)/shard_map/ppermute | solution.py:256
  35.6 11.8 %collective-permute-start.6 = (bf16[528,256]{1,0:T(8,128)(2,1)S(1)}, bf16[528,256]{1,0:T(8,128)(2,1)S(1)}, u32[]{:S(2)}, u32[]{:S(2)}) collective-permute-start(bf16[528,256]{1,0:T(8,128)(2,1)S(1)} %get-tuple-element.94.refs_0_), channel_id=1, source_target_pairs={{0,8},{4,12},{8,0},{12,4},{16,24},{20,28},{24,16},{28,20},{1,9},{5... | collective-permute-start | bytes 811016 | tf_op jit(solution)/shard_map/ppermute | solution.py:256
  37.1 10.3 %collective-permute-start.8 = (bf16[528,256]{1,0:T(8,128)(2,1)S(1)}, bf16[528,256]{1,0:T(8,128)(2,1)S(1)}, u32[]{:S(2)}, u32[]{:S(2)}) collective-permute-start(bf16[528,256]{1,0:T(8,128)(2,1)S(1)} %get-tuple-element.94.refs_0_), channel_id=1, source_target_pairs={{0,16},{4,20},{8,24},{12,28},{16,0},{20,4},{24,8},{28,12},{1,17},{... | collective-permute-start | bytes 811016 | tf_op jit(solution)/shard_map/ppermute | solution.py:256
  37.6 10.3 %collective-permute-start.5 = (bf16[528,256]{1,0:T(8,128)(2,1)S(1)}, bf16[528,256]{1,0:T(8,128)(2,1)S(1)}, u32[]{:S(2)}, u32[]{:S(2)}) collective-permute-start(bf16[528,256]{1,0:T(8,128)(2,1)S(1)} %get-tuple-element.94.refs_0_), channel_id=1, source_target_pairs={{0,4},{4,0},{8,12},{12,8},{16,20},{20,16},{24,28},{28,24},{1,5},{5... | collective-permute-start | bytes 811016 | tf_op jit(solution)/shard_map/ppermute | solution.py:256
  44.4 9.2 %copy-start.5 = (bf16[528,256]{1,0:T(8,128)(2,1)}, bf16[528,256]{1,0:T(8,128)(2,1)S(1)}, u32[]{:S(2)}) copy-start(bf16[528,256]{1,0:T(8,128)(2,1)S(1)} %collective-permute-done.10.refs_6_) | copy-start | bytes 811012
  44.4 3.5 %collective-permute-start.11 = (bf16[528,256]{1,0:T(8,128)(2,1)S(1)}, bf16[528,256]{1,0:T(8,128)(2,1)S(1)}, u32[]{:S(2)}, u32[]{:S(2)}) collective-permute-start(bf16[528,256]{1,0:T(8,128)(2,1)S(1)} %collective-permute-done.10.refs_6_), channel_id=1, source_target_pairs={{0,4},{4,0},{8,12},{12,8},{16,20},{20,16},{24,28},{28,24},{1,5},{5... | collective-permute-start | bytes 811016 | tf_op jit(solution)/shard_map/ppermute | solution.py:256
  47.4 6.2 %copy-start.7 = (bf16[528,256]{1,0:T(8,128)(2,1)}, bf16[528,256]{1,0:T(8,128)(2,1)S(1)}, u32[]{:S(2)}) copy-start(bf16[528,256]{1,0:T(8,128)(2,1)S(1)} %collective-permute-done.6.refs_2_) | copy-start | bytes 811012
  47.4 1.5 %collective-permute-start.7 = (bf16[528,256]{1,0:T(8,128)(2,1)S(1)}, bf16[528,256]{1,0:T(8,128)(2,1)S(1)}, u32[]{:S(2)}, u32[]{:S(2)}) collective-permute-start(bf16[528,256]{1,0:T(8,128)(2,1)S(1)} %collective-permute-done.6.refs_2_), channel_id=1, source_target_pairs={{0,4},{4,0},{8,12},{12,8},{16,20},{20,16},{24,28},{28,24},{1,5},{5... | collective-permute-start | bytes 811016 | tf_op jit(solution)/shard_map/ppermute | solution.py:256
  47.4 6.2 %copy-start.9 = (bf16[528,256]{1,0:T(8,128)(2,1)}, bf16[528,256]{1,0:T(8,128)(2,1)S(1)}, u32[]{:S(2)}) copy-start(bf16[528,256]{1,0:T(8,128)(2,1)S(1)} %collective-permute-done.8.refs_4_) | copy-start | bytes 811012
  47.4 1.9 %collective-permute-start.9 = (bf16[528,256]{1,0:T(8,128)(2,1)S(1)}, bf16[528,256]{1,0:T(8,128)(2,1)S(1)}, u32[]{:S(2)}, u32[]{:S(2)}) collective-permute-start(bf16[528,256]{1,0:T(8,128)(2,1)S(1)} %collective-permute-done.8.refs_4_), channel_id=1, source_target_pairs={{0,4},{4,0},{8,12},{12,8},{16,20},{20,16},{24,28},{28,24},{1,5},{5... | collective-permute-start | bytes 811016 | tf_op jit(solution)/shard_map/ppermute | solution.py:256
  47.9 5.7 %copy-start.11 = (bf16[528,256]{1,0:T(8,128)(2,1)}, bf16[528,256]{1,0:T(8,128)(2,1)S(1)}, u32[]{:S(2)}) copy-start(bf16[528,256]{1,0:T(8,128)(2,1)S(1)} %collective-permute-done.5.refs_1_) | copy-start | bytes 811012
  47.9 5.7 %copy-start.13 = (bf16[528,256]{1,0:T(8,128)(2,1)}, bf16[528,256]{1,0:T(8,128)(2,1)S(1)}, u32[]{:S(2)}) copy-start(bf16[528,256]{1,0:T(8,128)(2,1)S(1)} %collective-permute-done.11.refs_7_) | copy-start | bytes 811012
  49.0 4.7 %copy-start.15 = (bf16[528,256]{1,0:T(8,128)(2,1)}, bf16[528,256]{1,0:T(8,128)(2,1)S(1)}, u32[]{:S(2)}) copy-start(bf16[528,256]{1,0:T(8,128)(2,1)S(1)} %collective-permute-done.7.refs_3_) | copy-start | bytes 811012
  49.3 4.3 %copy-start.17 = (bf16[528,256]{1,0:T(8,128)(2,1)}, bf16[528,256]{1,0:T(8,128)(2,1)S(1)}, u32[]{:S(2)}) copy-start(bf16[528,256]{1,0:T(8,128)(2,1)S(1)} %collective-permute-done.9.refs_5_) | copy-start | bytes 811012
  50.0 15.3 %copy-start = (bf16[1024,1024]{1,0:T(8,128)(2,1)S(1)}, bf16[1024,1024]{1,0:T(8,128)(2,1)}, u32[]{:S(2)}) copy-start(bf16[1024,1024]{1,0:T(8,128)(2,1)} %refs_3_.2) | copy-start | bytes 6291460
  50.0 15.3 %copy-start.28 = (bf16[1024]{0:T(1024)(128)(2,1)S(1)}, bf16[1024]{0:T(1024)(128)(2,1)}, u32[]{:S(2)}) copy-start(bf16[1024]{0:T(1024)(128)(2,1)} %refs_1_.2) | copy-start | bytes 6148
  53.7 11.6 %collective-permute-start.13 = (bf16[512,128]{1,0:T(8,128)(2,1)S(1)}, bf16[512,128]{1,0:T(8,128)(2,1)}, u32[]{:S(2)}, u32[]{:S(2)}) collective-permute-start(bf16[512,128]{1,0:T(8,128)(2,1)S(1)} %attend.1.refs_0_), channel_id=1, source_target_pairs={{0,2},{1,3},{2,0},{3,1},{4,6},{5,7},{6,4},{7,5},{8,10},{9,11},{10,... | collective-permute-start | bytes 393224 | tf_op jit(solution)/shard_map/ppermute | solution.py:57
  56.3 14.0 %collective-permute-start.12 = (bf16[512,128]{1,0:T(8,128)(2,1)S(1)}, bf16[512,128]{1,0:T(8,128)(2,1)}, u32[]{:S(2)}, u32[]{:S(2)}) collective-permute-start(bf16[512,128]{1,0:T(8,128)(2,1)S(1)} %attend.1.refs_0_), channel_id=1, source_target_pairs={{0,1},{1,0},{2,3},{3,2},{4,5},{5,4},{6,7},{7,6},{8,9},{9,8},{10,11... | collective-permute-start | bytes 393224 | tf_op jit(solution)/shard_map/ppermute | solution.py:57
  65.3 5.7 %collective-permute-start.14 = (bf16[512,128]{1,0:T(8,128)(2,1)}, bf16[512,128]{1,0:T(8,128)(2,1)}, u32[]{:S(2)}, u32[]{:S(2)}) collective-permute-start(bf16[512,128]{1,0:T(8,128)(2,1)} %collective-permute-done.13.refs_2_), channel_id=1, source_target_pairs={{0,1},{1,0},{2,3},{3,2},{4,5},{5,4},{6,7},{7,6},{8,9},{9,8},{10,11... | collective-permute-start | bytes 393224 | tf_op jit(solution)/shard_map/ppermute | solution.py:57
  65.3 1.6 %copy-start.1 = (bf16[1024,1024]{1,0:T(8,128)(2,1)S(1)}, bf16[1024,1024]{1,0:T(8,128)(2,1)}, u32[]{:S(2)}) copy-start(bf16[1024,1024]{1,0:T(8,128)(2,1)} %refs_4_.2) | copy-start | bytes 6291460
  66.9 1.6 %copy-start.2 = (bf16[1024,1024]{1,0:T(8,128)(2,1)S(1)}, bf16[1024,1024]{1,0:T(8,128)(2,1)}, u32[]{:S(2)}) copy-start(bf16[1024,1024]{1,0:T(8,128)(2,1)} %refs_5_) | copy-start | bytes 6291460
  68.5 1.2 %copy-start.3 = (bf16[512,1024]{1,0:T(8,128)(2,1)S(1)}, bf16[512,1024]{1,0:T(8,128)(2,1)}, u32[]{:S(2)}) copy-start(bf16[512,1024]{1,0:T(8,128)(2,1)} %all-gather.2.cloned.1.call-done.refs_2_) | copy-start | bytes 3145732
  75.9 6.4 %collective-permute-start.18 = (bf16[256,256]{1,0:T(8,128)(2,1)S(1)}, bf16[256,256]{1,0:T(8,128)(2,1)S(1)}, u32[]{:S(2)}, u32[]{:S(2)}) collective-permute-start(bf16[256,256]{1,0:T(8,128)(2,1)S(1)} %get-tuple-element.93), channel_id=1, source_target_pairs={{0,1},{1,0},{2,3},{3,2},{4,5},{5,4},{6,7},{7,6},{8,9},{9,8},{10,11... | collective-permute-start | bytes 393224 | tf_op jit(solution)/shard_map/ppermute | solution.py:57
  77.3 12.0 %collective-permute-start.16 = (bf16[256,256]{1,0:T(8,128)(2,1)S(1)}, bf16[256,256]{1,0:T(8,128)(2,1)S(1)}, u32[]{:S(2)}, u32[]{:S(2)}) collective-permute-start(bf16[256,256]{1,0:T(8,128)(2,1)S(1)} %get-tuple-element.91), channel_id=1, source_target_pairs={{0,1},{1,0},{2,3},{3,2},{4,5},{5,4},{6,7},{7,6},{8,9},{9,8},{10,11... | collective-permute-start | bytes 393224 | tf_op jit(solution)/shard_map/ppermute | solution.py:57
  78.0 11.5 %copy-start.6 = (bf16[528,256]{1,0:T(8,128)(2,1)S(1)}, bf16[528,256]{1,0:T(8,128)(2,1)}, u32[]{:S(2)}) copy-start(bf16[528,256]{1,0:T(8,128)(2,1)} %copy-done.5) | copy-start | bytes 811012
  78.0 11.5 %copy-start.8 = (bf16[528,256]{1,0:T(8,128)(2,1)S(1)}, bf16[528,256]{1,0:T(8,128)(2,1)}, u32[]{:S(2)}) copy-start(bf16[528,256]{1,0:T(8,128)(2,1)} %copy-done.7) | copy-start | bytes 811012
  78.0 11.5 %copy-start.10 = (bf16[528,256]{1,0:T(8,128)(2,1)S(1)}, bf16[528,256]{1,0:T(8,128)(2,1)}, u32[]{:S(2)}) copy-start(bf16[528,256]{1,0:T(8,128)(2,1)} %copy-done.9) | copy-start | bytes 811012
  78.0 11.5 %copy-start.12 = (bf16[528,256]{1,0:T(8,128)(2,1)S(1)}, bf16[528,256]{1,0:T(8,128)(2,1)}, u32[]{:S(2)}) copy-start(bf16[528,256]{1,0:T(8,128)(2,1)} %copy-done.11) | copy-start | bytes 811012
  78.0 11.5 %copy-start.14 = (bf16[528,256]{1,0:T(8,128)(2,1)S(1)}, bf16[528,256]{1,0:T(8,128)(2,1)}, u32[]{:S(2)}) copy-start(bf16[528,256]{1,0:T(8,128)(2,1)} %copy-done.13) | copy-start | bytes 811012
  78.0 11.5 %copy-start.16 = (bf16[528,256]{1,0:T(8,128)(2,1)S(1)}, bf16[528,256]{1,0:T(8,128)(2,1)}, u32[]{:S(2)}) copy-start(bf16[528,256]{1,0:T(8,128)(2,1)} %copy-done.15) | copy-start | bytes 811012
  78.0 11.5 %copy-start.18 = (bf16[528,256]{1,0:T(8,128)(2,1)S(1)}, bf16[528,256]{1,0:T(8,128)(2,1)}, u32[]{:S(2)}) copy-start(bf16[528,256]{1,0:T(8,128)(2,1)} %copy-done.17) | copy-start | bytes 811012
  78.0 11.5 %copy-start.31 = (s32[4]{0:T(128)S(1)}, s32[4]{0:T(128)}, u32[]{:S(2)}) copy-start(s32[4]{0:T(128)} %lengths.5) | copy-start | bytes 52
  78.0 11.5 %copy-start.35 = (s32[72]{0:T(128)S(1)}, s32[72]{0:T(128)}, u32[]{:S(2)}) copy-start(s32[72]{0:T(128)} %page_table.1) | copy-start | bytes 868
  79.1 15.2 %collective-permute-start.15 = (bf16[512,256]{1,0:T(8,128)(2,1)S(1)}, bf16[512,256]{1,0:T(8,128)(2,1)S(1)}, u32[]{:S(2)}, u32[]{:S(2)}) collective-permute-start(bf16[512,256]{1,0:T(8,128)(2,1)S(1)} %get-tuple-element.89), channel_id=1, source_target_pairs={{0,1},{1,0},{2,3},{3,2},{4,5},{5,4},{6,7},{7,6},{8,9},{9,8},{10,11... | collective-permute-start | bytes 786440 | tf_op jit(solution)/shard_map/ppermute | solution.py:57
  82.4 11.9 %collective-permute-start.19 = (bf16[256,256]{1,0:T(8,128)(2,1)S(1)}, bf16[256,256]{1,0:T(8,128)(2,1)S(1)}, u32[]{:S(2)}, u32[]{:S(2)}) collective-permute-start(bf16[256,256]{1,0:T(8,128)(2,1)S(1)} %add_up.4), channel_id=1, source_target_pairs={{0,2},{1,3},{2,0},{3,1},{4,6},{5,7},{6,4},{7,5},{8,10},{9,11},{10,... | collective-permute-start | bytes 393224 | tf_op jit(solution)/shard_map/ppermute | solution.py:57
  89.4 7.8 %collective-permute-start.17 = (bf16[256,256]{1,0:T(8,128)(2,1)S(1)}, bf16[256,256]{1,0:T(8,128)(2,1)S(1)}, u32[]{:S(2)}, u32[]{:S(2)}) collective-permute-start(bf16[256,256]{1,0:T(8,128)(2,1)S(1)} %add_up.3), channel_id=1, source_target_pairs={{0,2},{1,3},{2,0},{3,1},{4,6},{5,7},{6,4},{7,5},{8,10},{9,11},{10,... | collective-permute-start | bytes 393224 | tf_op jit(solution)/shard_map/ppermute | solution.py:57
  (11 other events, 7.4 us)
Sparse Core Ops, SparseCore 0:
  30.6 33.0 all-gather.1

commit v6 on v5

--- a/solution.py
+++ b/solution.py
@@ -57,7 +57,7 @@
     return lax.ppermute(value, "tp", [(i, i ^ mask) for i in range(lax.axis_size("tp"))])
 
 
-def pair_gather(shard, parts, first=None):
+def pair_gather(shard, parts):
     step = shard.shape[0] // parts
     split = [shard]
     if parts > 1:
@@ -65,33 +65,35 @@
         split, shard = lax.optimization_barrier((split, shard))
     far = [tp_xor(part, 2) for part in split]
     near = tp_xor(shard, 1)
-    if first is not None:
-        far[0], _ = lax.optimization_barrier((far[0], first))
     return [shard, near] + far + [tp_xor(part, 1) for part in far]
 
 
 def turn_gather(shard):
     count = lax.axis_size("tp")
-    pairs = [[(i, (i + turn) % count) for i in range(count)] for turn in range(1, count)]
-    return [shard] + [lax.ppermute(shard, "tp", each) for each in pairs]
-
-
-def gather_pieces(shard, parts, first=None):
+    turns = sorted(range(1, count), key=lambda turn: -min(turn, count - turn))
+    moved = {
+        turn: lax.ppermute(shard, "tp", [(i, (i + turn) % count) for i in range(count)])
+        for turn in turns
+    }
+    return [shard] + [moved[turn] for turn in range(1, count)]
+
+
+def gather_pieces(shard, parts):
     if lax.axis_size("tp") == 4:
-        return pair_gather(shard, parts, first)
+        return pair_gather(shard, parts)
     return turn_gather(shard)
 
 
-def assemble(pieces, place, count, target):
+def assemble(pieces, place, count, target, part=slice(None)):
     width = pieces[0].shape[1]
 
     def put(block, value, first=0):
         columns = pl.ds(pl.multiple_of(block * width, width), width)
         target[pl.ds(first, value.shape[0]), columns] = value
 
-    if count != 4:
+    if len(pieces) == count:
         for turn, piece in enumerate(pieces):
-            put(lax.rem(place + count - turn, count), piece[...])
+            put(lax.rem(place + count - turn, count), piece[part, :])
         return
     put(place, pieces[0][...])
     put(place ^ 1, pieces[1][...])
@@ -122,9 +124,9 @@
     return round_up(BIAS_PARTS * VARS + requests, 16)
 
 
-def tables_kernel(count, lengths, bias, frequency, positions, variate, *refs):
-    cosine, sine, extra, marks = refs[count : count + 4]
-    loads = start_loads(refs[:count], refs[count + 4 : -1], refs[-1])
+def tables_kernel(
+    lengths, bias, frequency, positions, variate, cosine, sine, extra, marks
+):
     rows = positions.shape[1]
     width = cosine.shape[1]
     angles = frequency[...] * positions[...].astype(jnp.float32)
@@ -160,28 +162,25 @@
         column = jnp.where(other, HIDDEN_SCORE, column)
         rest = jnp.zeros((LANES - shape[0], rows), jnp.float32)
         marks[h] = jnp.transpose(jnp.concatenate([column, rest], axis=0)).astype(jnp.bfloat16)
-    finish_loads(loads)
-
-
-def tables(lengths, bias, positions, variate, width, arrays):
+
+
+def tables(lengths, bias, positions, variate, width):
     rows = positions.shape[0]
     half = HD // 2
     heads = width // HD
     frequency = 10000.0 ** (-np.arange(half, dtype=np.float32) / np.float32(half))
     extra = round_up(rows // (2 * width), 16)
     return pl.pallas_call(
-        functools.partial(tables_kernel, len(arrays)),
+        tables_kernel,
         out_shape=[
             jax.ShapeDtypeStruct((rows, width), jnp.float32),
             jax.ShapeDtypeStruct((rows, width), jnp.float32),
             jax.ShapeDtypeStruct((extra, 2 * width), jnp.bfloat16),
             jax.ShapeDtypeStruct((heads, rows, LANES), jnp.bfloat16),
-        ]
-        + [jax.ShapeDtypeStruct(array.shape, array.dtype) for array in arrays],
-        in_specs=[SMEM, SMEM, VMEM, VMEM, VMEM] + [ANY] * len(arrays),
-        out_specs=[VMEM] * (4 + len(arrays)),
-        scratch_shapes=[pltpu.SemaphoreType.DMA((len(arrays),))],
-        compiler_params=params(6),
+        ],
+        in_specs=[SMEM, SMEM, VMEM, VMEM, VMEM],
+        out_specs=[VMEM] * 4,
+        compiler_params=params(60),
         cost_estimate=cost(rows * 1024, 1 << 20, rows * 64),
         name="tables",
     )(
@@ -190,7 +189,6 @@
         jnp.asarray(frequency.astype(np.float32).reshape(half, 1)),
         positions.reshape(1, rows),
         variate.reshape(1, rows),
-        *arrays,
     )
 
 
@@ -246,7 +244,7 @@
         in_specs=[VMEM] * (len(pieces) + 7),
         out_specs=[HBM, VMEM, VMEM],
         scratch_shapes=[pltpu.VMEM((rows, features), jnp.bfloat16), pltpu.SemaphoreType.DMA],
-        compiler_params=params(6),
+        compiler_params=params(60),
         cost_estimate=cost(6 * rows * features * width, 4 << 20),
         name="project",
     )(*pieces, gain, w_query, w_key, w_value, cosine, sine, extra)
@@ -529,55 +527,42 @@
     )(*arrays)
 
 
-def hidden_kernel(places, count, on_line, *refs):
+def hidden_kernel(places, count, first, *refs):
     pieces = refs[:count]
     tokens, gain, w_out, w_gate, w_up, w_down = refs[count : count + 6]
     outs, attended = refs[count + 6 : -1], refs[-1]
     hidden, kept = outs[:2]
     place = lax.axis_index("tp")
-    assemble(pieces, place, places, attended)
-    rows, features = tokens.shape
-    width = kept.shape[1]
-    step = min(rows, 256)
+    rows, width = kept.shape
+    part = pl.ds(first, rows)
+    assemble(pieces, place, places, attended, part)
+    projected = dot_f32(attended[...], w_out[...])
+    residual = (tokens[part, :].astype(jnp.float32) + projected).astype(jnp.bfloat16)
+    mine = residual[:, :width]
+    for i in range(1, places):
+        mine = jnp.where(place == i, residual[:, i * width : (i + 1) * width], mine)
+    kept[...] = mine
     gain_row = gain[...].astype(jnp.float32).reshape(1, -1)
-    for first in range(0, rows, step):
-        part = pl.ds(first, step)
-        projected = dot_f32(attended[part, :], w_out[...])
-        residual = (tokens[part, :].astype(jnp.float32) + projected).astype(jnp.bfloat16)
-        mine = residual[:, :width]
-        for i in range(1, places):
-            mine = jnp.where(place == i, residual[:, i * width : (i + 1) * width], mine)
-        kept[part, :] = mine
-        normed = norm_rows(residual.astype(jnp.float32), gain_row)
-        gate = dot_f32(normed, w_gate[...])
-        up = dot_f32(normed, w_up[...])
-        hidden[part, :] = (jax.nn.silu(gate) * up).astype(jnp.bfloat16)
-    if not on_line:
-        return
-
-    weights = w_down[:, pl.ds(pl.multiple_of((place ^ 3) * width, width), width)]
-    through = dot_f32(hidden[...], weights).astype(jnp.bfloat16)
-    outs[2][...] = through[: rows // 2]
-    outs[3][...] = through[rows // 2 :]
-
-
-def hidden_of(pieces, tokens, gain, w_out, w_gate, w_up, w_down):
-    rows, features = tokens.shape
+    normed = norm_rows(residual.astype(jnp.float32), gain_row)
+    gate = dot_f32(normed, w_gate[...])
+    up = dot_f32(normed, w_up[...])
+    hidden[...] = (jax.nn.silu(gate) * up).astype(jnp.bfloat16)
+    if len(outs) > 2:
+        weights = w_down[:, pl.ds(pl.multiple_of((place ^ 3) * width, width), width)]
+        outs[2][...] = dot_f32(hidden[...], weights).astype(jnp.bfloat16)
+
+
+def hidden_of(pieces, tokens, gain, w_out, w_gate, w_up, w_down, part, parts):
+    rows, features = tokens.shape[0] // parts, tokens.shape[1]
     places = lax.axis_size("tp")
     width = features // places
     units = w_gate.shape[1]
-    on_line = places == 4
-    shapes = [
-        jax.ShapeDtypeStruct((rows, units), jnp.bfloat16),
-        jax.ShapeDtypeStruct((rows, width), jnp.bfloat16),
-    ]
-    if on_line:
-        shapes += [jax.ShapeDtypeStruct((rows // 2, width), jnp.bfloat16)] * 2
+    widths = [units, width] + [width] * (places == 4)
     return pl.pallas_call(
-        functools.partial(hidden_kernel, places, len(pieces), on_line),
-        out_shape=shapes,
+        functools.partial(hidden_kernel, places, len(pieces), part * rows),
+        out_shape=[jax.ShapeDtypeStruct((rows, each), jnp.bfloat16) for each in widths],
         in_specs=[VMEM] * (len(pieces) + 6),
-        out_specs=[VMEM] * len(shapes),
+        out_specs=[VMEM] * len(widths),
         scratch_shapes=[pltpu.VMEM((rows, w_out.shape[0]), jnp.bfloat16)],
         compiler_params=params(12),
         cost_estimate=cost(6 * rows * features * units, 10 << 20),
@@ -585,34 +570,41 @@
     )(*pieces, tokens, gain, w_out, w_gate, w_up, w_down)
 
 
-def down_kernel(hidden, kept, w_down, far_top, far_low, near, own):
+def down_kernel(parts, *refs):
+    hidden, kept, w_down = refs[:parts], refs[parts : 2 * parts], refs[2 * parts]
+    far, near, own = refs[2 * parts + 1 : 3 * parts + 1], refs[-2], refs[-1]
     place = lax.axis_index("tp")
-    rows, width = own.shape
-
-    def product(index):
-        weights = w_down[:, pl.ds(pl.multiple_of(index * width, width), width)]
-        return dot_f32(hidden[...], weights)
-
-    far = product(place ^ 2)
-    far_top[...] = far[: rows // 2]
-    far_low[...] = far[rows // 2 :]
-    near[...] = product(place ^ 1).astype(jnp.bfloat16)
-    own[...] = product(place) + kept[...].astype(jnp.float32)
+    width = own.shape[1]
+    rows = own.shape[0] // parts
+
+    def weights(index):
+        return w_down[:, pl.ds(pl.multiple_of(index * width, width), width)]
+
+    for i in range(parts):
+        far[i][...] = dot_f32(hidden[i][...], weights(place ^ 2))
+    for i in range(parts):
+        part = pl.ds(i * rows, rows)
+        near[part, :] = dot_f32(hidden[i][...], weights(place ^ 1)).astype(jnp.bfloat16)
+    for i in range(parts):
+        part = pl.ds(i * rows, rows)
+        own[part, :] = dot_f32(hidden[i][...], weights(place)) + kept[i][...].astype(jnp.float32)
 
 
 def down_blocks(hidden, kept, w_down):
-    rows, width = kept.shape
-    shapes = [((rows // 2, width), jnp.float32)] * 2
-    shapes += [((rows, width), jnp.bfloat16), ((rows, width), jnp.float32)]
-    return pl.pallas_call(
-        down_kernel,
+    parts = len(hidden)
+    rows, width = kept[0].shape
+    shapes = [((rows, width), jnp.float32)] * parts
+    shapes += [((rows * parts, width), jnp.bfloat16), ((rows * parts, width), jnp.float32)]
+    *far, near, own = pl.pallas_call(
+        functools.partial(down_kernel, parts),
         out_shape=[jax.ShapeDtypeStruct(*shape) for shape in shapes],
-        in_specs=[VMEM] * 3,
-        out_specs=[VMEM] * 4,
+        in_specs=[VMEM] * (2 * parts + 1),
+        out_specs=[VMEM] * len(shapes),
         compiler_params=params(6),
-        cost_estimate=cost(2 * rows * w_down.shape[0] * width * 3, 5 << 20),
+        cost_estimate=cost(2 * rows * parts * w_down.shape[0] * width * 3, 5 << 20),
         name="down_blocks",
-    )(hidden, kept, w_down)
+    )(*hidden, *kept, w_down)
+    return far, near, own
 
 
 def add_kernel(out_parts, *refs):
@@ -642,16 +634,20 @@
     )(*terms)
 
 
-def feed_forward(pieces, tokens, gain, w_out, w_gate, w_up, w_down):
-    hidden, kept, *through = hidden_of(pieces, tokens, gain, w_out, w_gate, w_up, w_down)
+def feed_forward(pieces, *arrays):
+    w_down = arrays[-1]
     if lax.axis_size("tp") != 4:
+        hidden, kept = hidden_of(pieces, *arrays, 0, 1)
         share = lax.psum_scatter(
             dot_f32(hidden, w_down).astype(jnp.bfloat16), "tp", scatter_dimension=1, tiled=True
         )
         return add_up([kept, share]), hidden
+    parts = 2
+    outs = [hidden_of(pieces, *arrays, part, parts) for part in range(parts)]
+    hidden, kept, through = zip(*outs)
     through = [tp_xor(part, 1) for part in through]
-    far_top, far_low, near, own = down_blocks(hidden, kept, w_down)
-    joined = [add_up([part, other]) for part, other in zip((far_top, far_low), through)]
+    far, near, own = down_blocks(hidden, kept, w_down)
+    joined = [add_up([part, other]) for part, other in zip(far, through)]
     near = tp_xor(near, 1)
     far = [tp_xor(part, 2) for part in joined]
     return add_up([own, near], far), joined[-1]
@@ -679,18 +675,16 @@
     heads = width // HD
     reach = lax.axis_size("seq") // 2
 
-    weights = (tokens, gain_attn, w_query, w_key, w_value)
-    cosine, sine, extra, marks, *weights = tables(
-        lengths, var_bias, positions, variate, width, weights
-    )
-    pieces = gather_pieces(tokens, 2, extra)
+    pieces = gather_pieces(tokens, 2)
+    cosine, sine, extra, marks = tables(lengths, var_bias, positions, variate, width)
     pieces, w_out = lax.optimization_barrier((pieces, w_out))
     w_out_all = lax.all_gather(w_out, "tp", axis=0, tiled=True)
-    pieces[0] = weights[0]
-    token_rows, queries, pairs = project(pieces, *weights[1:], cosine, sine, extra)
+    token_rows, queries, pairs = project(
+        pieces, gain_attn, w_query, w_key, w_value, cosine, sine, extra
+    )
     row_pieces = seq_pieces(pairs)
     attended = attend(lengths, queries, marks, row_pieces, heads, reach)
-    attended_pieces = gather_pieces(attended, 1)
+    attended_pieces = turn_gather(attended)
     large = (token_rows, gain_ffn, w_out_all, w_gate, w_up, w_down)
     large = lax.optimization_barrier((large, attended))[0]
     mixed, joined = feed_forward(attended_pieces, *fetch(large))

time: 107 us -> 108 us (level)
  local copies, waits for them, and re-layouts: 17.5 us -> 7.45 us
  Pallas kernels: 18.2 us -> 24.1 us
  waiting for transfers between devices: 34.5 us -> 38.4 us
  starting transfers between devices: 20.2 us -> 21.5 us
    unnamed x76 -> x62, local copies, waits for them, and re-layouts: 16.5 us -> 6.46 us
    ppermute x0 -> x3, starting transfers between devices: none -> 5.6 us  [turn_gather(): lax.ppermute(shard, 'tp', [(i, (i + turn) % count) for i in range(count)])]
    ppermute x13 -> x10, starting transfers between devices: 16.1 us -> 11.8 us  [tp_xor(): lax.ppermute(value, 'tp', [(i, i ^ mask) for i in range(lax.axis_size('tp...]
    ppermute x0 -> x3, waiting for transfers between devices: none -> 2.55 us  [turn_gather(): lax.ppermute(shard, 'tp', [(i, (i + turn) % count) for i in range(count)])]
    pallas_call x3 -> x4, Pallas kernels: 7.11 us -> 9.52 us  [the longest x2 6.35 us: hidden_of(): pl.pallas_call(functools.partial(hidden_kernel, places, len(pieces), part...]
    pallas_call x1, Pallas kernels: 1.37 us -> 3.71 us  [project(): pl.pallas_call(functools.partial(project_kernel, lax.axis_size('tp'), len...]
    pallas_call x1, Pallas kernels: 3.61 us -> 4.73 us  [attend(): pl.pallas_call(functools.partial(attend_kernel, len(pieces), heads, reach...]
    ppermute x13 -> x10, waiting for transfers between devices: 23.4 us -> 23.9 us  [tp_xor(): lax.ppermute(value, 'tp', [(i, i ^ mask) for i in range(lax.axis_size('tp...]
  transfers between devices with their start and end apart: 21 -> 21, of which waited for: 11 -> 13; matrix products, arithmetic and copies ran while one was open for 0% -> 0% of each run, Pallas kernels for 12% -> 19%
where the time goes in v6:
time: 108 us; the launch traced here: 106 us
  waiting for transfers between devices  38.4 us (36%)
  Pallas kernels  24.1 us (22%)
  starting transfers between devices  21.5 us (20%)
  between operations  14.4 us (13%)
  local copies, waits for them, and re-layouts  7.45 us (7%)
    ppermute x10, waiting for transfers between devices, tp_xor(): lax.ppermute(value, 'tp', [(i, i ^ mask) for i in range(lax.axis_size('tp...  23.9 us
    ppermute x7, waiting for transfers between devices, seq_xor(): lax.ppermute(value, 'seq', [(i, i ^ mask) for i in range(lax.axis_size('s...  11.9 us
    ppermute x10, starting transfers between devices, tp_xor(): lax.ppermute(value, 'tp', [(i, i ^ mask) for i in range(lax.axis_size('tp...  11.8 us
    unnamed x62, local copies, waits for them, and re-layouts  6.46 us
    pallas_call x2, Pallas kernels, hidden_of(): pl.pallas_call(functools.partial(hidden_kernel, places, len(pieces), part...  6.35 us
    ppermute x3, starting transfers between devices, turn_gather(): lax.ppermute(shard, 'tp', [(i, (i + turn) % count) for i in range(count)])  5.6 us
    pallas_call x1, Pallas kernels, attend(): pl.pallas_call(functools.partial(attend_kernel, len(pieces), heads, reach...  4.73 us
    pallas_call x1, Pallas kernels, fill_cache(): pl.pallas_call(functools.partial(cache_kernel, len(pieces), 2 * PAGE), ou...  4.69 us
  transfers between devices with their start and end apart: 21, of which 13 were waited for; matrix products, arithmetic and copies ran while one was open for 0% of the time, Pallas kernels for 19%

profile of v6, /device:TPU:2, one launch (start us, length us, event | category | flops | bytes accessed | tf_op | source)
XLA Modules:
  0.0 105.9 jit_solution(9664803646912474337)
XLA Ops:
  7.2 0.0 copy-start.22
  7.2 0.0 all-gather.2.cloned.1.call-start
  7.2 1.0 fusion
  8.2 2.7 %collective-permute-start.1 = (bf16[256,256]{1,0:T(8,128)(2,1)S(1)}, bf16[256,256]{1,0:T(8,128)(2,1)S(1)}, u32[]{:S(2)}, u32[]{:S(2)}) collective-permute-start(bf16[256,256]{1,0:T(8,128)(2,1)S(1)} %get-tuple-element.50), channel_id=1, source_target_pairs={{0,2},{1,3},{2,0},{3,1},{4,6},{5,7},{6,4},{7,5},{8,10},{9,11},{10,... | collective-permute-start | bytes 393224 | tf_op jit(solution)/shard_map/ppermute | solution.py:57
  10.9 0.3 collective-permute-start.2
  11.2 1.6 %collective-permute-start = (bf16[512,256]{1,0:T(8,128)(2,1)}, bf16[512,256]{1,0:T(8,128)(2,1)S(1)}, u32[]{:S(2)}, u32[]{:S(2)}) collective-permute-start(bf16[512,256]{1,0:T(8,128)(2,1)} %refs_0_), channel_id=1, source_target_pairs={{0,1},{1,0},{2,3},{3,2},{4,5},{5,4},{6,7},{7,6},{8,9},{9,8},{10,11... | collective-permute-start | bytes 786440 | tf_op jit(solution)/shard_map/ppermute | solution.py:57
  12.8 8.5 %collective-permute-done.1.refs_2_ = bf16[256,256]{1,0:T(8,128)(2,1)S(1)} collective-permute-done((bf16[256,256]{1,0:T(8,128)(2,1)S(1)}, bf16[256,256]{1,0:T(8,128)(2,1)S(1)}, u32[]{:S(2)}, u32[]{:S(2)}) %collective-permute-start.1) | collective-permute-done | bytes 131104 | tf_op jit(solution)/shard_map/ppermute | solution.py:57
  21.3 1.7 %collective-permute-done.2.refs_3_ = bf16[256,256]{1,0:T(8,128)(2,1)S(1)} collective-permute-done((bf16[256,256]{1,0:T(8,128)(2,1)S(1)}, bf16[256,256]{1,0:T(8,128)(2,1)S(1)}, u32[]{:S(2)}, u32[]{:S(2)}) %collective-permute-start.2) | collective-permute-done | bytes 131104 | tf_op jit(solution)/shard_map/ppermute | solution.py:57
  23.0 0.6 collective-permute-start.4
  23.6 4.1 %collective-permute-done.3.refs_4_ = bf16[256,256]{1,0:T(8,128)(2,1)S(1)} collective-permute-done((bf16[256,256]{1,0:T(8,128)(2,1)S(1)}, bf16[256,256]{1,0:T(8,128)(2,1)S(1)}, u32[]{:S(2)}, u32[]{:S(2)}) %collective-permute-start.3) | collective-permute-done | bytes 131104 | tf_op jit(solution)/shard_map/ppermute | solution.py:57
  27.6 1.4 %collective-permute-done.4.refs_5_ = bf16[256,256]{1,0:T(8,128)(2,1)S(1)} collective-permute-done((bf16[256,256]{1,0:T(8,128)(2,1)S(1)}, bf16[256,256]{1,0:T(8,128)(2,1)S(1)}, u32[]{:S(2)}, u32[]{:S(2)}) %collective-permute-start.4) | collective-permute-done | bytes 131104 | tf_op jit(solution)/shard_map/ppermute | solution.py:57
  29.1 0.0 all-gather.2.cloned.1.call-update
  29.1 2.2 %tables.1 = (f32[512,128]{1,0:T(8,128)}, f32[512,128]{1,0:T(8,128)}, bf16[16,256]{1,0:T(8,128)(2,1)}, bf16[2,512,128]{2,1,0:T(8,128)(2,1)}) custom-call(s32[4]{0:T(128)} %lengths.5, f32[2,2]{1,0:T(2,128)} %bias.1, f32[32,1]{1,0:T(8,128)} %constant.2.clone.frequency, s32[1,512]{1,0:T(1,128)} %bitcast.2, s32[1,512]{1,0:T(1,128)} %bitcast.3), custom_call_target="tpu_custom_call" | custom-call | flops 524288 | bytes 1048576 | tf_op jit(solution)/shard_map/tables/pallas_call | solution.py:173
  31.3 3.7 %project.1 = (bf16[512,1024]{1,0:T(8,128)(2,1)}, bf16[512,128]{1,0:T(8,128)(2,1)}, bf16[528,256]{1,0:T(8,128)(2,1)}) custom-call(bf16[512,256]{1,0:T(8,128)(2,1)} %refs_0_, bf16[512,256]{1,0:T(8,128)(2,1)} %copy-done.26, bf16[256,256]{1,0:T(8,128)(2,1)} %copy-done.27, bf16[256,256]{1,0:T(8,128)(2,1)} %copy-done.28, bf16[256,256]{1,0:T(8,128)(2,1)} %copy-done.29, ...), custom_call_target="tpu_custom_call" | custom-call | flops 402653184 | bytes 4194304 | tf_op jit(solution)/shard_map/project/pallas_call | solution.py:237
  35.0 1.6 %collective-permute-start.10 = (bf16[528,256]{1,0:T(8,128)(2,1)}, bf16[528,256]{1,0:T(8,128)(2,1)S(1)}, u32[]{:S(2)}, u32[]{:S(2)}) collective-permute-start(bf16[528,256]{1,0:T(8,128)(2,1)} %get-tuple-element.88.refs_0_), channel_id=1, source_target_pairs={{0,24},{4,28},{8,16},{12,20},{16,8},{20,12},{24,0},{28,4},{1,25},{... | collective-permute-start | bytes 811016 | tf_op jit(solution)/shard_map/ppermute | solution.py:254
  36.6 1.5 %collective-permute-start.6 = (bf16[528,256]{1,0:T(8,128)(2,1)}, bf16[528,256]{1,0:T(8,128)(2,1)S(1)}, u32[]{:S(2)}, u32[]{:S(2)}) collective-permute-start(bf16[528,256]{1,0:T(8,128)(2,1)} %get-tuple-element.88.refs_0_), channel_id=1, source_target_pairs={{0,8},{4,12},{8,0},{12,4},{16,24},{20,28},{24,16},{28,20},{1,9},{5... | collective-permute-start | bytes 811016 | tf_op jit(solution)/shard_map/ppermute | solution.py:254
  38.1 0.5 collective-permute-start.8
  38.6 7.1 %collective-permute-done.10.refs_6_ = bf16[528,256]{1,0:T(8,128)(2,1)S(1)} collective-permute-done((bf16[528,256]{1,0:T(8,128)(2,1)}, bf16[528,256]{1,0:T(8,128)(2,1)S(1)}, u32[]{:S(2)}, u32[]{:S(2)}) %collective-permute-start.10) | collective-permute-done | bytes 270368 | tf_op jit(solution)/shard_map/ppermute | solution.py:254
  45.6 3.5 %collective-permute-done.6.refs_2_ = bf16[528,256]{1,0:T(8,128)(2,1)S(1)} collective-permute-done((bf16[528,256]{1,0:T(8,128)(2,1)}, bf16[528,256]{1,0:T(8,128)(2,1)S(1)}, u32[]{:S(2)}, u32[]{:S(2)}) %collective-permute-start.6) | collective-permute-done | bytes 270368 | tf_op jit(solution)/shard_map/ppermute | solution.py:254
  49.1 0.5 collective-permute-start.9
  49.6 1.0 collective-permute-done.7.refs_3_
  50.7 0.4 collective-permute-done.9.refs_5_
  51.1 1.0 copy-done.5
  52.1 0.9 copy-done.24
  53.0 4.7 %attend.1.refs_0_ = bf16[512,128]{1,0:T(8,128)(2,1)S(1)} custom-call(s32[4]{0:T(128)S(1)} %copy-done.22, bf16[512,128]{1,0:T(8,128)(2,1)S(1)} %copy-done.24, bf16[2,512,128]{2,1,0:T(8,128)(2,1)S(1)} %copy-done.25, bf16[528,256]{1,0:T(8,128)(2,1)S(1)} %copy-done.5, bf16[528,256]{1,0:T(8,128)(2,1)S(1)} %collective-permute-done.5.refs_1_, ...), custom_call_target="tpu_custom_call" | custom-call | flops 2684354560 | bytes 4194304 | tf_op jit(solution)/shard_map/attend/pallas_call | solution.py:401
  57.8 1.5 %collective-permute-start.12 = (bf16[512,128]{1,0:T(8,128)(2,1)S(1)}, bf16[512,128]{1,0:T(8,128)(2,1)S(1)}, u32[]{:S(2)}, u32[]{:S(2)}) collective-permute-start(bf16[512,128]{1,0:T(8,128)(2,1)S(1)} %attend.1.refs_0_), channel_id=1, source_target_pairs={{0,1},{1,2},{2,3},{3,0},{4,5},{5,6},{6,7},{7,4},{8,9},{9,10},{10,1... | collective-permute-start | bytes 393224 | tf_op jit(solution)/shard_map/ppermute | solution.py:75
  59.3 3.6 %collective-permute-start.13 = (bf16[512,128]{1,0:T(8,128)(2,1)S(1)}, bf16[512,128]{1,0:T(8,128)(2,1)S(1)}, u32[]{:S(2)}, u32[]{:S(2)}) collective-permute-start(bf16[512,128]{1,0:T(8,128)(2,1)S(1)} %attend.1.refs_0_), channel_id=1, source_target_pairs={{0,2},{1,3},{2,0},{3,1},{4,6},{5,7},{6,4},{7,5},{8,10},{9,11},{10,... | collective-permute-start | bytes 393224 | tf_op jit(solution)/shard_map/ppermute | solution.py:75
  63.0 0.5 collective-permute-start.14
  63.5 1.6 %copy-done.1 = bf16[1024,1024]{1,0:T(8,128)(2,1)S(1)} copy-done((bf16[1024,1024]{1,0:T(8,128)(2,1)S(1)}, bf16[1024,1024]{1,0:T(8,128)(2,1)}, u32[]{:S(2)}) %copy-start.1) | copy-done | bytes 2097176
  65.0 1.6 %copy-done.2 = bf16[1024,1024]{1,0:T(8,128)(2,1)S(1)} copy-done((bf16[1024,1024]{1,0:T(8,128)(2,1)S(1)}, bf16[1024,1024]{1,0:T(8,128)(2,1)}, u32[]{:S(2)}) %copy-start.2) | copy-done | bytes 2097176
  66.6 1.2 %copy-done.3 = bf16[512,1024]{1,0:T(8,128)(2,1)S(1)} copy-done((bf16[512,1024]{1,0:T(8,128)(2,1)S(1)}, bf16[512,1024]{1,0:T(8,128)(2,1)}, u32[]{:S(2)}) %copy-start.3) | copy-done | bytes 1048600
  67.9 0.6 fetch.1
  68.5 2.3 %collective-permute-done.13.refs_2_ = bf16[512,128]{1,0:T(8,128)(2,1)S(1)} collective-permute-done((bf16[512,128]{1,0:T(8,128)(2,1)S(1)}, bf16[512,128]{1,0:T(8,128)(2,1)S(1)}, u32[]{:S(2)}, u32[]{:S(2)}) %collective-permute-start.13) | collective-permute-done | bytes 131104 | tf_op jit(solution)/shard_map/ppermute | solution.py:75
  70.8 0.3 collective-permute-done.14.refs_3_
  71.0 3.2 %hidden.3 = (bf16[256,1024]{1,0:T(8,128)(2,1)S(1)}, bf16[256,256]{1,0:T(8,128)(2,1)S(1)}, bf16[256,256]{1,0:T(8,128)(2,1)S(1)}) custom-call(bf16[512,128]{1,0:T(8,128)(2,1)S(1)} %attend.1.refs_0_, bf16[512,128]{1,0:T(8,128)(2,1)S(1)} %collective-permute-done.12.refs_1_, bf16[512,128]{1,0:T(8,128)(2,1)S(1)} %collective-permute-done.13.refs_2_, ...), custom_call_target="tpu_custom_call" | custom-call | flops 1610612736 | bytes 10485760 | tf_op jit(solution)/shard_map/hidden/pallas_call | solution.py:561
  74.2 3.2 %collective-permute-start.18 = (bf16[256,256]{1,0:T(8,128)(2,1)S(1)}, bf16[256,256]{1,0:T(8,128)(2,1)S(1)}, u32[]{:S(2)}, u32[]{:S(2)}) collective-permute-start(bf16[256,256]{1,0:T(8,128)(2,1)S(1)} %get-tuple-element.87), channel_id=1, source_target_pairs={{0,1},{1,0},{2,3},{3,2},{4,5},{5,4},{6,7},{7,6},{8,9},{9,8},{10,11... | collective-permute-start | bytes 393224 | tf_op jit(solution)/shard_map/ppermute | solution.py:57
  77.4 3.2 %hidden.2 = (bf16[256,1024]{1,0:T(8,128)(2,1)S(1)}, bf16[256,256]{1,0:T(8,128)(2,1)S(1)}, bf16[256,256]{1,0:T(8,128)(2,1)S(1)}) custom-call(bf16[512,128]{1,0:T(8,128)(2,1)S(1)} %attend.1.refs_0_, bf16[512,128]{1,0:T(8,128)(2,1)S(1)} %collective-permute-done.12.refs_1_, bf16[512,128]{1,0:T(8,128)(2,1)S(1)} %collective-permute-done.13.refs_2_, ...), custom_call_target="tpu_custom_call" | custom-call | flops 1610612736 | bytes 10485760 | tf_op jit(solution)/shard_map/hidden/pallas_call | solution.py:561
  80.6 0.1 collective-permute-start.16
  80.7 0.0 copy-start.6
  80.8 1.0 down_blocks.1
  81.8 2.0 %collective-permute-start.15 = (bf16[512,256]{1,0:T(8,128)(2,1)S(1)}, bf16[512,256]{1,0:T(8,128)(2,1)S(1)}, u32[]{:S(2)}, u32[]{:S(2)}) collective-permute-start(bf16[512,256]{1,0:T(8,128)(2,1)S(1)} %get-tuple-element.83), channel_id=1, source_target_pairs={{0,1},{1,0},{2,3},{3,2},{4,5},{5,4},{6,7},{7,6},{8,9},{9,8},{10,11... | collective-permute-start | bytes 786440 | tf_op jit(solution)/shard_map/ppermute | solution.py:57
  83.9 1.3 %collective-permute-start.19 = (bf16[256,256]{1,0:T(8,128)(2,1)S(1)}, bf16[256,256]{1,0:T(8,128)(2,1)S(1)}, u32[]{:S(2)}, u32[]{:S(2)}) collective-permute-start(bf16[256,256]{1,0:T(8,128)(2,1)S(1)} %add_up.4), channel_id=1, source_target_pairs={{0,2},{1,3},{2,0},{3,1},{4,6},{5,7},{6,4},{7,5},{8,10},{9,11},{10,... | collective-permute-start | bytes 393224 | tf_op jit(solution)/shard_map/ppermute | solution.py:57
  85.1 4.5 %collective-permute-done.16.refs_1_ = bf16[256,256]{1,0:T(8,128)(2,1)S(1)} collective-permute-done((bf16[256,256]{1,0:T(8,128)(2,1)S(1)}, bf16[256,256]{1,0:T(8,128)(2,1)S(1)}, u32[]{:S(2)}, u32[]{:S(2)}) %collective-permute-start.16) | collective-permute-done | bytes 131104 | tf_op jit(solution)/shard_map/ppermute | solution.py:57
  89.7 0.1 collective-permute-start.17
  89.9 4.7 %fill_cache.1 = bf16[576,2,128]{2,1,0:T(2,128)(2,1)} custom-call(s32[4]{0:T(128)S(1)} %copy-done.22, s32[72]{0:T(128)S(1)} %copy-done.23, bf16[528,256]{1,0:T(8,128)(2,1)S(1)} %copy-done.6, bf16[528,256]{1,0:T(8,128)(2,1)S(1)} %copy-done.14, bf16[528,256]{1,0:T(8,128)(2,1)S(1)} %copy-done.10, bf16[528,256]{1,0:T(8,128)(2,1)S(1)} %copy-done.18, ...), custom_call_target="tpu_custom_call" | custom-call | flops 75497472 | bytes 3145728 | tf_op jit(solution)/shard_map/fill_cache/pallas_call | solution.py:497
  94.6 1.2 %collective-permute-done.15.refs_1_ = bf16[512,256]{1,0:T(8,128)(2,1)S(1)} collective-permute-done((bf16[512,256]{1,0:T(8,128)(2,1)S(1)}, bf16[512,256]{1,0:T(8,128)(2,1)S(1)}, u32[]{:S(2)}, u32[]{:S(2)}) %collective-permute-start.15) | collective-permute-done | bytes 262176 | tf_op jit(solution)/shard_map/ppermute | solution.py:57
  95.7 2.5 %collective-permute-done.17.refs_2_ = bf16[256,256]{1,0:T(8,128)(2,1)S(1)} collective-permute-done((bf16[256,256]{1,0:T(8,128)(2,1)S(1)}, bf16[256,256]{1,0:T(8,128)(2,1)S(1)}, u32[]{:S(2)}, u32[]{:S(2)}) %collective-permute-start.17) | collective-permute-done | bytes 131104 | tf_op jit(solution)/shard_map/ppermute | solution.py:57
  98.2 0.8 add_up.5
  (69 shorter events, 0.2 us)
Async XLA Ops:
  7.2 43.9 %copy-start.22 = (s32[4]{0:T(128)S(1)}, s32[4]{0:T(128)}, u32[]{:S(2)}) copy-start(s32[4]{0:T(128)} %lengths.5) | copy-start | bytes 52
  7.2 56.3 %all-gather.2.cloned.1.call-start = ((), (), s32[]{:S(2)}) async-start(), calls=%async_computation | async-start | bytes 1310720 | tf_op jit(solution)/shard_map/all_gather | solution.py:681
  8.2 13.0 %collective-permute-start.1 = (bf16[256,256]{1,0:T(8,128)(2,1)S(1)}, bf16[256,256]{1,0:T(8,128)(2,1)S(1)}, u32[]{:S(2)}, u32[]{:S(2)}) collective-permute-start(bf16[256,256]{1,0:T(8,128)(2,1)S(1)} %get-tuple-element.50), channel_id=1, source_target_pairs={{0,2},{1,3},{2,0},{3,1},{4,6},{5,7},{6,4},{7,5},{8,10},{9,11},{10,... | collective-permute-start | bytes 393224 | tf_op jit(solution)/shard_map/ppermute | solution.py:57
  10.9 12.1 %collective-permute-start.2 = (bf16[256,256]{1,0:T(8,128)(2,1)S(1)}, bf16[256,256]{1,0:T(8,128)(2,1)S(1)}, u32[]{:S(2)}, u32[]{:S(2)}) collective-permute-start(bf16[256,256]{1,0:T(8,128)(2,1)S(1)} %get-tuple-element.51), channel_id=1, source_target_pairs={{0,2},{1,3},{2,0},{3,1},{4,6},{5,7},{6,4},{7,5},{8,10},{9,11},{10,... | collective-permute-start | bytes 393224 | tf_op jit(solution)/shard_map/ppermute | solution.py:57
  11.2 17.8 %collective-permute-start = (bf16[512,256]{1,0:T(8,128)(2,1)}, bf16[512,256]{1,0:T(8,128)(2,1)S(1)}, u32[]{:S(2)}, u32[]{:S(2)}) collective-permute-start(bf16[512,256]{1,0:T(8,128)(2,1)} %refs_0_), channel_id=1, source_target_pairs={{0,1},{1,0},{2,3},{3,2},{4,5},{5,4},{6,7},{7,6},{8,9},{9,8},{10,11... | collective-permute-start | bytes 786440 | tf_op jit(solution)/shard_map/ppermute | solution.py:57
  21.3 10.0 %copy-start.27 = (bf16[256,256]{1,0:T(8,128)(2,1)}, bf16[256,256]{1,0:T(8,128)(2,1)S(1)}, u32[]{:S(2)}) copy-start(bf16[256,256]{1,0:T(8,128)(2,1)S(1)} %collective-permute-done.1.refs_2_) | copy-start | bytes 393220
  21.3 6.4 %collective-permute-start.3 = (bf16[256,256]{1,0:T(8,128)(2,1)S(1)}, bf16[256,256]{1,0:T(8,128)(2,1)S(1)}, u32[]{:S(2)}, u32[]{:S(2)}) collective-permute-start(bf16[256,256]{1,0:T(8,128)(2,1)S(1)} %collective-permute-done.1.refs_2_), channel_id=1, source_target_pairs={{0,1},{1,0},{2,3},{3,2},{4,5},{5,4},{6,7},{7,6},{8,9},{9,8},{10,11... | collective-permute-start | bytes 393224 | tf_op jit(solution)/shard_map/ppermute | solution.py:57
  22.9 8.3 %copy-start.28 = (bf16[256,256]{1,0:T(8,128)(2,1)}, bf16[256,256]{1,0:T(8,128)(2,1)S(1)}, u32[]{:S(2)}) copy-start(bf16[256,256]{1,0:T(8,128)(2,1)S(1)} %collective-permute-done.2.refs_3_) | copy-start | bytes 393220
  23.0 6.1 %collective-permute-start.4 = (bf16[256,256]{1,0:T(8,128)(2,1)S(1)}, bf16[256,256]{1,0:T(8,128)(2,1)S(1)}, u32[]{:S(2)}, u32[]{:S(2)}) collective-permute-start(bf16[256,256]{1,0:T(8,128)(2,1)S(1)} %collective-permute-done.2.refs_3_), channel_id=1, source_target_pairs={{0,1},{1,0},{2,3},{3,2},{4,5},{5,4},{6,7},{7,6},{8,9},{9,8},{10,11... | collective-permute-start | bytes 393224 | tf_op jit(solution)/shard_map/ppermute | solution.py:57
  27.6 3.6 %copy-start.29 = (bf16[256,256]{1,0:T(8,128)(2,1)}, bf16[256,256]{1,0:T(8,128)(2,1)S(1)}, u32[]{:S(2)}) copy-start(bf16[256,256]{1,0:T(8,128)(2,1)S(1)} %collective-permute-done.3.refs_4_) | copy-start | bytes 393220
  29.0 2.2 %copy-start.30 = (bf16[256,256]{1,0:T(8,128)(2,1)}, bf16[256,256]{1,0:T(8,128)(2,1)S(1)}, u32[]{:S(2)}) copy-start(bf16[256,256]{1,0:T(8,128)(2,1)S(1)} %collective-permute-done.4.refs_5_) | copy-start | bytes 393220
  29.1 2.2 %copy-start.26 = (bf16[512,256]{1,0:T(8,128)(2,1)}, bf16[512,256]{1,0:T(8,128)(2,1)S(1)}, u32[]{:S(2)}) copy-start(bf16[512,256]{1,0:T(8,128)(2,1)S(1)} %collective-permute-done.refs_1_) | copy-start | bytes 786436
  31.2 19.8 %copy-start.25 = (bf16[2,512,128]{2,1,0:T(8,128)(2,1)S(1)}, bf16[2,512,128]{2,1,0:T(8,128)(2,1)}, u32[]{:S(2)}) copy-start(bf16[2,512,128]{2,1,0:T(8,128)(2,1)} %get-tuple-element.62.query_marks) | copy-start | bytes 786436
  35.0 10.6 %collective-permute-start.10 = (bf16[528,256]{1,0:T(8,128)(2,1)}, bf16[528,256]{1,0:T(8,128)(2,1)S(1)}, u32[]{:S(2)}, u32[]{:S(2)}) collective-permute-start(bf16[528,256]{1,0:T(8,128)(2,1)} %get-tuple-element.88.refs_0_), channel_id=1, source_target_pairs={{0,24},{4,28},{8,16},{12,20},{16,8},{20,12},{24,0},{28,4},{1,25},{... | collective-permute-start | bytes 811016 | tf_op jit(solution)/shard_map/ppermute | solution.py:254
  36.6 12.5 %collective-permute-start.6 = (bf16[528,256]{1,0:T(8,128)(2,1)}, bf16[528,256]{1,0:T(8,128)(2,1)S(1)}, u32[]{:S(2)}, u32[]{:S(2)}) collective-permute-start(bf16[528,256]{1,0:T(8,128)(2,1)} %get-tuple-element.88.refs_0_), channel_id=1, source_target_pairs={{0,8},{4,12},{8,0},{12,4},{16,24},{20,28},{24,16},{28,20},{1,9},{5... | collective-permute-start | bytes 811016 | tf_op jit(solution)/shard_map/ppermute | solution.py:254
  38.1 11.1 %collective-permute-start.8 = (bf16[528,256]{1,0:T(8,128)(2,1)}, bf16[528,256]{1,0:T(8,128)(2,1)S(1)}, u32[]{:S(2)}, u32[]{:S(2)}) collective-permute-start(bf16[528,256]{1,0:T(8,128)(2,1)} %get-tuple-element.88.refs_0_), channel_id=1, source_target_pairs={{0,16},{4,20},{8,24},{12,28},{16,0},{20,4},{24,8},{28,12},{1,17},{... | collective-permute-start | bytes 811016 | tf_op jit(solution)/shard_map/ppermute | solution.py:254
  38.6 11.1 %collective-permute-start.5 = (bf16[528,256]{1,0:T(8,128)(2,1)}, bf16[528,256]{1,0:T(8,128)(2,1)S(1)}, u32[]{:S(2)}, u32[]{:S(2)}) collective-permute-start(bf16[528,256]{1,0:T(8,128)(2,1)} %get-tuple-element.88.refs_0_), channel_id=1, source_target_pairs={{0,4},{4,0},{8,12},{12,8},{16,20},{20,16},{24,28},{28,24},{1,5},{5... | collective-permute-start | bytes 811016 | tf_op jit(solution)/shard_map/ppermute | solution.py:254
  45.6 12.1 %copy-start.7 = (bf16[528,256]{1,0:T(8,128)(2,1)}, bf16[528,256]{1,0:T(8,128)(2,1)S(1)}, u32[]{:S(2)}) copy-start(bf16[528,256]{1,0:T(8,128)(2,1)S(1)} %collective-permute-done.10.refs_6_) | copy-start | bytes 811012
  45.6 4.0 %collective-permute-start.11 = (bf16[528,256]{1,0:T(8,128)(2,1)S(1)}, bf16[528,256]{1,0:T(8,128)(2,1)S(1)}, u32[]{:S(2)}, u32[]{:S(2)}) collective-permute-start(bf16[528,256]{1,0:T(8,128)(2,1)S(1)} %collective-permute-done.10.refs_6_), channel_id=1, source_target_pairs={{0,4},{4,0},{8,12},{12,8},{16,20},{20,16},{24,28},{28,24},{1,5},{5... | collective-permute-start | bytes 811016 | tf_op jit(solution)/shard_map/ppermute | solution.py:254
  49.1 8.7 %copy-start.9 = (bf16[528,256]{1,0:T(8,128)(2,1)}, bf16[528,256]{1,0:T(8,128)(2,1)S(1)}, u32[]{:S(2)}) copy-start(bf16[528,256]{1,0:T(8,128)(2,1)S(1)} %collective-permute-done.6.refs_2_) | copy-start | bytes 811012
  49.1 1.5 %collective-permute-start.7 = (bf16[528,256]{1,0:T(8,128)(2,1)S(1)}, bf16[528,256]{1,0:T(8,128)(2,1)S(1)}, u32[]{:S(2)}, u32[]{:S(2)}) collective-permute-start(bf16[528,256]{1,0:T(8,128)(2,1)S(1)} %collective-permute-done.6.refs_2_), channel_id=1, source_target_pairs={{0,4},{4,0},{8,12},{12,8},{16,20},{20,16},{24,28},{28,24},{1,5},{5... | collective-permute-start | bytes 811016 | tf_op jit(solution)/shard_map/ppermute | solution.py:254
  49.1 8.7 %copy-start.11 = (bf16[528,256]{1,0:T(8,128)(2,1)}, bf16[528,256]{1,0:T(8,128)(2,1)S(1)}, u32[]{:S(2)}) copy-start(bf16[528,256]{1,0:T(8,128)(2,1)S(1)} %collective-permute-done.8.refs_4_) | copy-start | bytes 811012
  49.1 1.9 %collective-permute-start.9 = (bf16[528,256]{1,0:T(8,128)(2,1)S(1)}, bf16[528,256]{1,0:T(8,128)(2,1)S(1)}, u32[]{:S(2)}, u32[]{:S(2)}) collective-permute-start(bf16[528,256]{1,0:T(8,128)(2,1)S(1)} %collective-permute-done.8.refs_4_), channel_id=1, source_target_pairs={{0,4},{4,0},{8,12},{12,8},{16,20},{20,16},{24,28},{28,24},{1,5},{5... | collective-permute-start | bytes 811016 | tf_op jit(solution)/shard_map/ppermute | solution.py:254
  49.6 8.2 %copy-start.13 = (bf16[528,256]{1,0:T(8,128)(2,1)}, bf16[528,256]{1,0:T(8,128)(2,1)S(1)}, u32[]{:S(2)}) copy-start(bf16[528,256]{1,0:T(8,128)(2,1)S(1)} %collective-permute-done.5.refs_1_) | copy-start | bytes 811012
  49.6 8.2 %copy-start.15 = (bf16[528,256]{1,0:T(8,128)(2,1)}, bf16[528,256]{1,0:T(8,128)(2,1)S(1)}, u32[]{:S(2)}) copy-start(bf16[528,256]{1,0:T(8,128)(2,1)S(1)} %collective-permute-done.11.refs_7_) | copy-start | bytes 811012
  50.7 7.2 %copy-start.17 = (bf16[528,256]{1,0:T(8,128)(2,1)}, bf16[528,256]{1,0:T(8,128)(2,1)S(1)}, u32[]{:S(2)}) copy-start(bf16[528,256]{1,0:T(8,128)(2,1)S(1)} %collective-permute-done.7.refs_3_) | copy-start | bytes 811012
  51.0 6.8 %copy-start.19 = (bf16[528,256]{1,0:T(8,128)(2,1)}, bf16[528,256]{1,0:T(8,128)(2,1)S(1)}, u32[]{:S(2)}) copy-start(bf16[528,256]{1,0:T(8,128)(2,1)S(1)} %collective-permute-done.9.refs_5_) | copy-start | bytes 811012
  53.0 10.4 %copy-start = (bf16[1024,1024]{1,0:T(8,128)(2,1)S(1)}, bf16[1024,1024]{1,0:T(8,128)(2,1)}, u32[]{:S(2)}) copy-start(bf16[1024,1024]{1,0:T(8,128)(2,1)} %refs_3_) | copy-start | bytes 6291460
  53.0 10.4 %copy-start.4 = (bf16[512,1024]{1,0:T(8,128)(2,1)S(1)}, bf16[512,1024]{1,0:T(8,128)(2,1)}, u32[]{:S(2)}) copy-start(bf16[512,1024]{1,0:T(8,128)(2,1)} %get-tuple-element.66.refs_0_) | copy-start | bytes 3145732
  53.0 10.4 %copy-start.21 = (bf16[1024]{0:T(1024)(128)(2,1)S(1)}, bf16[1024]{0:T(1024)(128)(2,1)}, u32[]{:S(2)}) copy-start(bf16[1024]{0:T(1024)(128)(2,1)} %refs_1_) | copy-start | bytes 6148
  57.8 10.7 %collective-permute-start.12 = (bf16[512,128]{1,0:T(8,128)(2,1)S(1)}, bf16[512,128]{1,0:T(8,128)(2,1)S(1)}, u32[]{:S(2)}, u32[]{:S(2)}) collective-permute-start(bf16[512,128]{1,0:T(8,128)(2,1)S(1)} %attend.1.refs_0_), channel_id=1, source_target_pairs={{0,1},{1,2},{2,3},{3,0},{4,5},{5,6},{6,7},{7,4},{8,9},{9,10},{10,1... | collective-permute-start | bytes 393224 | tf_op jit(solution)/shard_map/ppermute | solution.py:75
  59.3 11.4 %collective-permute-start.13 = (bf16[512,128]{1,0:T(8,128)(2,1)S(1)}, bf16[512,128]{1,0:T(8,128)(2,1)S(1)}, u32[]{:S(2)}, u32[]{:S(2)}) collective-permute-start(bf16[512,128]{1,0:T(8,128)(2,1)S(1)} %attend.1.refs_0_), channel_id=1, source_target_pairs={{0,2},{1,3},{2,0},{3,1},{4,6},{5,7},{6,4},{7,5},{8,10},{9,11},{10,... | collective-permute-start | bytes 393224 | tf_op jit(solution)/shard_map/ppermute | solution.py:75
  63.0 8.1 %collective-permute-start.14 = (bf16[512,128]{1,0:T(8,128)(2,1)S(1)}, bf16[512,128]{1,0:T(8,128)(2,1)}, u32[]{:S(2)}, u32[]{:S(2)}) collective-permute-start(bf16[512,128]{1,0:T(8,128)(2,1)S(1)} %attend.1.refs_0_), channel_id=1, source_target_pairs={{0,3},{1,0},{2,1},{3,2},{4,7},{5,4},{6,5},{7,6},{8,11},{9,8},{10,9... | collective-permute-start | bytes 393224 | tf_op jit(solution)/shard_map/ppermute | solution.py:75
  63.4 1.6 %copy-start.1 = (bf16[1024,1024]{1,0:T(8,128)(2,1)S(1)}, bf16[1024,1024]{1,0:T(8,128)(2,1)}, u32[]{:S(2)}) copy-start(bf16[1024,1024]{1,0:T(8,128)(2,1)} %refs_4_) | copy-start | bytes 6291460
  74.2 9.6 %collective-permute-start.18 = (bf16[256,256]{1,0:T(8,128)(2,1)S(1)}, bf16[256,256]{1,0:T(8,128)(2,1)S(1)}, u32[]{:S(2)}, u32[]{:S(2)}) collective-permute-start(bf16[256,256]{1,0:T(8,128)(2,1)S(1)} %get-tuple-element.87), channel_id=1, source_target_pairs={{0,1},{1,0},{2,3},{3,2},{4,5},{5,4},{6,7},{7,6},{8,9},{9,8},{10,11... | collective-permute-start | bytes 393224 | tf_op jit(solution)/shard_map/ppermute | solution.py:57
  80.6 9.1 %collective-permute-start.16 = (bf16[256,256]{1,0:T(8,128)(2,1)S(1)}, bf16[256,256]{1,0:T(8,128)(2,1)S(1)}, u32[]{:S(2)}, u32[]{:S(2)}) collective-permute-start(bf16[256,256]{1,0:T(8,128)(2,1)S(1)} %get-tuple-element.85), channel_id=1, source_target_pairs={{0,1},{1,0},{2,3},{3,2},{4,5},{5,4},{6,7},{7,6},{8,9},{9,8},{10,11... | collective-permute-start | bytes 393224 | tf_op jit(solution)/shard_map/ppermute | solution.py:57
  80.7 9.1 %copy-start.6 = (bf16[528,256]{1,0:T(8,128)(2,1)S(1)}, bf16[528,256]{1,0:T(8,128)(2,1)}, u32[]{:S(2)}) copy-start(bf16[528,256]{1,0:T(8,128)(2,1)} %get-tuple-element.88.refs_0_) | copy-start | bytes 811012
  80.7 9.1 %copy-start.8 = (bf16[528,256]{1,0:T(8,128)(2,1)S(1)}, bf16[528,256]{1,0:T(8,128)(2,1)}, u32[]{:S(2)}) copy-start(bf16[528,256]{1,0:T(8,128)(2,1)} %copy-done.7) | copy-start | bytes 811012
  80.7 9.1 %copy-start.10 = (bf16[528,256]{1,0:T(8,128)(2,1)S(1)}, bf16[528,256]{1,0:T(8,128)(2,1)}, u32[]{:S(2)}) copy-start(bf16[528,256]{1,0:T(8,128)(2,1)} %copy-done.9) | copy-start | bytes 811012
  80.7 9.1 %copy-start.12 = (bf16[528,256]{1,0:T(8,128)(2,1)S(1)}, bf16[528,256]{1,0:T(8,128)(2,1)}, u32[]{:S(2)}) copy-start(bf16[528,256]{1,0:T(8,128)(2,1)} %copy-done.11) | copy-start | bytes 811012
  80.7 9.1 %copy-start.14 = (bf16[528,256]{1,0:T(8,128)(2,1)S(1)}, bf16[528,256]{1,0:T(8,128)(2,1)}, u32[]{:S(2)}) copy-start(bf16[528,256]{1,0:T(8,128)(2,1)} %copy-done.13) | copy-start | bytes 811012
  80.7 9.1 %copy-start.16 = (bf16[528,256]{1,0:T(8,128)(2,1)S(1)}, bf16[528,256]{1,0:T(8,128)(2,1)}, u32[]{:S(2)}) copy-start(bf16[528,256]{1,0:T(8,128)(2,1)} %copy-done.15) | copy-start | bytes 811012
  80.7 9.1 %copy-start.18 = (bf16[528,256]{1,0:T(8,128)(2,1)S(1)}, bf16[528,256]{1,0:T(8,128)(2,1)}, u32[]{:S(2)}) copy-start(bf16[528,256]{1,0:T(8,128)(2,1)} %copy-done.17) | copy-start | bytes 811012
  80.7 9.1 %copy-start.20 = (bf16[528,256]{1,0:T(8,128)(2,1)S(1)}, bf16[528,256]{1,0:T(8,128)(2,1)}, u32[]{:S(2)}) copy-start(bf16[528,256]{1,0:T(8,128)(2,1)} %copy-done.19) | copy-start | bytes 811012
  80.8 9.1 %copy-start.23 = (s32[72]{0:T(128)S(1)}, s32[72]{0:T(128)}, u32[]{:S(2)}) copy-start(s32[72]{0:T(128)} %page_table.1) | copy-start | bytes 868
  81.8 13.9 %collective-permute-start.15 = (bf16[512,256]{1,0:T(8,128)(2,1)S(1)}, bf16[512,256]{1,0:T(8,128)(2,1)S(1)}, u32[]{:S(2)}, u32[]{:S(2)}) collective-permute-start(bf16[512,256]{1,0:T(8,128)(2,1)S(1)} %get-tuple-element.83), channel_id=1, source_target_pairs={{0,1},{1,0},{2,3},{3,2},{4,5},{5,4},{6,7},{7,6},{8,9},{9,8},{10,11... | collective-permute-start | bytes 786440 | tf_op jit(solution)/shard_map/ppermute | solution.py:57
  83.9 11.9 %collective-permute-start.19 = (bf16[256,256]{1,0:T(8,128)(2,1)S(1)}, bf16[256,256]{1,0:T(8,128)(2,1)S(1)}, u32[]{:S(2)}, u32[]{:S(2)}) collective-permute-start(bf16[256,256]{1,0:T(8,128)(2,1)S(1)} %add_up.4), channel_id=1, source_target_pairs={{0,2},{1,3},{2,0},{3,1},{4,6},{5,7},{6,4},{7,5},{8,10},{9,11},{10,... | collective-permute-start | bytes 393224 | tf_op jit(solution)/shard_map/ppermute | solution.py:57
  89.7 8.5 %collective-permute-start.17 = (bf16[256,256]{1,0:T(8,128)(2,1)S(1)}, bf16[256,256]{1,0:T(8,128)(2,1)S(1)}, u32[]{:S(2)}, u32[]{:S(2)}) collective-permute-start(bf16[256,256]{1,0:T(8,128)(2,1)S(1)} %add_up.3), channel_id=1, source_target_pairs={{0,2},{1,3},{2,0},{3,1},{4,6},{5,7},{6,4},{7,5},{8,10},{9,11},{10,... | collective-permute-start | bytes 393224 | tf_op jit(solution)/shard_map/ppermute | solution.py:57
  (4 other events, 4.8 us)
Sparse Core Ops, SparseCore 0:
  29.2 30.1 all-gather.1

commit v7 on v5

--- a/solution.py
+++ b/solution.py
@@ -122,9 +122,9 @@
     return round_up(BIAS_PARTS * VARS + requests, 16)
 
 
-def tables_kernel(count, lengths, bias, frequency, positions, variate, *refs):
-    cosine, sine, extra, marks = refs[count : count + 4]
-    loads = start_loads(refs[:count], refs[count + 4 : -1], refs[-1])
+def tables_kernel(
+    lengths, bias, frequency, positions, variate, cosine, sine, extra, marks
+):
     rows = positions.shape[1]
     width = cosine.shape[1]
     angles = frequency[...] * positions[...].astype(jnp.float32)
@@ -160,28 +160,25 @@
         column = jnp.where(other, HIDDEN_SCORE, column)
         rest = jnp.zeros((LANES - shape[0], rows), jnp.float32)
         marks[h] = jnp.transpose(jnp.concatenate([column, rest], axis=0)).astype(jnp.bfloat16)
-    finish_loads(loads)
-
-
-def tables(lengths, bias, positions, variate, width, arrays):
+
+
+def tables(lengths, bias, positions, variate, width):
     rows = positions.shape[0]
     half = HD // 2
     heads = width // HD
     frequency = 10000.0 ** (-np.arange(half, dtype=np.float32) / np.float32(half))
     extra = round_up(rows // (2 * width), 16)
     return pl.pallas_call(
-        functools.partial(tables_kernel, len(arrays)),
+        tables_kernel,
         out_shape=[
             jax.ShapeDtypeStruct((rows, width), jnp.float32),
             jax.ShapeDtypeStruct((rows, width), jnp.float32),
             jax.ShapeDtypeStruct((extra, 2 * width), jnp.bfloat16),
             jax.ShapeDtypeStruct((heads, rows, LANES), jnp.bfloat16),
-        ]
-        + [jax.ShapeDtypeStruct(array.shape, array.dtype) for array in arrays],
-        in_specs=[SMEM, SMEM, VMEM, VMEM, VMEM] + [ANY] * len(arrays),
-        out_specs=[VMEM] * (4 + len(arrays)),
-        scratch_shapes=[pltpu.SemaphoreType.DMA((len(arrays),))],
-        compiler_params=params(6),
+        ],
+        in_specs=[SMEM, SMEM, VMEM, VMEM, VMEM],
+        out_specs=[VMEM] * 4,
+        compiler_params=params(4),
         cost_estimate=cost(rows * 1024, 1 << 20, rows * 64),
         name="tables",
     )(
@@ -190,7 +187,6 @@
         jnp.asarray(frequency.astype(np.float32).reshape(half, 1)),
         positions.reshape(1, rows),
         variate.reshape(1, rows),
-        *arrays,
     )
 
 
@@ -246,7 +242,7 @@
         in_specs=[VMEM] * (len(pieces) + 7),
         out_specs=[HBM, VMEM, VMEM],
         scratch_shapes=[pltpu.VMEM((rows, features), jnp.bfloat16), pltpu.SemaphoreType.DMA],
-        compiler_params=params(6),
+        compiler_params=params(5),
         cost_estimate=cost(6 * rows * features * width, 4 << 20),
         name="project",
     )(*pieces, gain, w_query, w_key, w_value, cosine, sine, extra)
@@ -529,13 +525,16 @@
     )(*arrays)
 
 
-def hidden_kernel(places, count, on_line, *refs):
-    pieces = refs[:count]
-    tokens, gain, w_out, w_gate, w_up, w_down = refs[count : count + 6]
-    outs, attended = refs[count + 6 : -1], refs[-1]
+def hidden_kernel(places, *refs):
+    pieces, w_out_pieces = refs[:places], refs[places : 2 * places]
+    tokens, gain, w_gate, w_up, w_down = refs[2 * places : 2 * places + 5]
+    outs, attended, w_out = refs[2 * places + 5 : -2], refs[-2], refs[-1]
     hidden, kept = outs[:2]
     place = lax.axis_index("tp")
-    assemble(pieces, place, places, attended)
+    each = pieces[0].shape[1]
+    for i in range(places):
+        attended[:, i * each : (i + 1) * each] = pieces[i][...]
+        w_out[i * each : (i + 1) * each, :] = w_out_pieces[i][...]
     rows, features = tokens.shape
     width = kept.shape[1]
     step = min(rows, 256)
@@ -552,37 +551,34 @@
         gate = dot_f32(normed, w_gate[...])
         up = dot_f32(normed, w_up[...])
         hidden[part, :] = (jax.nn.silu(gate) * up).astype(jnp.bfloat16)
-    if not on_line:
+    if len(outs) == 2:
         return
-
     weights = w_down[:, pl.ds(pl.multiple_of((place ^ 3) * width, width), width)]
     through = dot_f32(hidden[...], weights).astype(jnp.bfloat16)
     outs[2][...] = through[: rows // 2]
     outs[3][...] = through[rows // 2 :]
 
 
-def hidden_of(pieces, tokens, gain, w_out, w_gate, w_up, w_down):
+def hidden_of(pieces, w_out_pieces, tokens, gain, w_gate, w_up, w_down):
     rows, features = tokens.shape
     places = lax.axis_size("tp")
     width = features // places
     units = w_gate.shape[1]
-    on_line = places == 4
-    shapes = [
-        jax.ShapeDtypeStruct((rows, units), jnp.bfloat16),
-        jax.ShapeDtypeStruct((rows, width), jnp.bfloat16),
-    ]
-    if on_line:
-        shapes += [jax.ShapeDtypeStruct((rows // 2, width), jnp.bfloat16)] * 2
+    inner = places * pieces[0].shape[1]
+    shapes = [(rows, units), (rows, width)] + [(rows // 2, width)] * (2 * (places == 4))
     return pl.pallas_call(
-        functools.partial(hidden_kernel, places, len(pieces), on_line),
-        out_shape=shapes,
-        in_specs=[VMEM] * (len(pieces) + 6),
+        functools.partial(hidden_kernel, places),
+        out_shape=[jax.ShapeDtypeStruct(shape, jnp.bfloat16) for shape in shapes],
+        in_specs=[VMEM] * (2 * places + 5),
         out_specs=[VMEM] * len(shapes),
-        scratch_shapes=[pltpu.VMEM((rows, w_out.shape[0]), jnp.bfloat16)],
+        scratch_shapes=[
+            pltpu.VMEM((rows, inner), jnp.bfloat16),
+            pltpu.VMEM((inner, features), jnp.bfloat16),
+        ],
         compiler_params=params(12),
         cost_estimate=cost(6 * rows * features * units, 10 << 20),
         name="hidden",
-    )(*pieces, tokens, gain, w_out, w_gate, w_up, w_down)
+    )(*pieces, *w_out_pieces, tokens, gain, w_gate, w_up, w_down)
 
 
 def down_kernel(hidden, kept, w_down, far_top, far_low, near, own):
@@ -642,8 +638,9 @@
     )(*terms)
 
 
-def feed_forward(pieces, tokens, gain, w_out, w_gate, w_up, w_down):
-    hidden, kept, *through = hidden_of(pieces, tokens, gain, w_out, w_gate, w_up, w_down)
+def feed_forward(pieces, w_out_pieces, *arrays):
+    hidden, kept, *through = hidden_of(pieces, w_out_pieces, *arrays)
+    w_down = arrays[-1]
     if lax.axis_size("tp") != 4:
         share = lax.psum_scatter(
             dot_f32(hidden, w_down).astype(jnp.bfloat16), "tp", scatter_dimension=1, tiled=True
@@ -679,21 +676,20 @@
     heads = width // HD
     reach = lax.axis_size("seq") // 2
 
-    weights = (tokens, gain_attn, w_query, w_key, w_value)
-    cosine, sine, extra, marks, *weights = tables(
-        lengths, var_bias, positions, variate, width, weights
+    cosine, sine, extra, marks = tables(lengths, var_bias, positions, variate, width)
+    pieces = gather_pieces(tokens, 2, extra)
+    token_rows, queries, pairs = project(
+        pieces, gain_attn, w_query, w_key, w_value, cosine, sine, extra
     )
-    pieces = gather_pieces(tokens, 2, extra)
-    pieces, w_out = lax.optimization_barrier((pieces, w_out))
-    w_out_all = lax.all_gather(w_out, "tp", axis=0, tiled=True)
-    pieces[0] = weights[0]
-    token_rows, queries, pairs = project(pieces, *weights[1:], cosine, sine, extra)
+    w_out, _ = lax.optimization_barrier((w_out, pairs))
     row_pieces = seq_pieces(pairs)
+    w_out_pieces = gather_pieces(w_out, 1)
     attended = attend(lengths, queries, marks, row_pieces, heads, reach)
-    attended_pieces = gather_pieces(attended, 1)
-    large = (token_rows, gain_ffn, w_out_all, w_gate, w_up, w_down)
+    large = (token_rows, gain_ffn, w_gate, w_up, w_down)
     large = lax.optimization_barrier((large, attended))[0]
-    mixed, joined = feed_forward(attended_pieces, *fetch(large))
+    large = fetch(large)
+    attended_pieces = gather_pieces(attended, 1, large[1])
+    mixed, joined = feed_forward(attended_pieces, w_out_pieces, *large)
     row_pieces, _ = lax.optimization_barrier((row_pieces, joined))
     cache = fill_cache(lengths, page_table, row_pieces, rows)
     return (mixed, cache)

time: 107 us -> 108 us (level)
  waiting for transfers between devices: 34.5 us -> 52.6 us
  between operations: 14.4 us -> 0.82 us
  local copies, waits for them, and re-layouts: 17.5 us -> 8.96 us
  starting transfers between devices: 20.2 us -> 27 us
  Pallas kernels: 18.2 us -> 16.9 us
    ppermute x13 -> x16, waiting for transfers between devices: 23.4 us -> 42.6 us  [tp_xor(): lax.ppermute(value, 'tp', [(i, i ^ mask) for i in range(lax.axis_size('tp...]
    unnamed x76 -> x34, local copies, waits for them, and re-layouts: 16.5 us -> 7.93 us
    ppermute x13 -> x16, starting transfers between devices: 16.1 us -> 23 us  [tp_xor(): lax.ppermute(value, 'tp', [(i, i ^ mask) for i in range(lax.axis_size('tp...]
    pallas_call x2, Pallas kernels: 6.09 us -> 4.81 us  [the longest x1 3.73 us: hidden_of(): pl.pallas_call(functools.partial(hidden_kernel, places), out_shape=[jax.S...]
    ppermute x7, waiting for transfers between devices: 11.2 us -> 10 us  [seq_xor(): lax.ppermute(value, 'seq', [(i, i ^ mask) for i in range(lax.axis_size('s...]
  transfers between devices with their start and end apart: 21 -> 23, of which waited for: 11 -> 15; matrix products, arithmetic and copies ran while one was open for 0% -> 0% of each run, Pallas kernels for 12% -> 10%
where the time goes in v7:
time: 108 us; the launch traced here: 106 us
  waiting for transfers between devices  52.6 us (49%)
  starting transfers between devices  27 us (25%)
  Pallas kernels  16.9 us (16%)
  local copies, waits for them, and re-layouts  8.96 us (8%)
    ppermute x16, waiting for transfers between devices, tp_xor(): lax.ppermute(value, 'tp', [(i, i ^ mask) for i in range(lax.axis_size('tp...  42.6 us
    ppermute x16, starting transfers between devices, tp_xor(): lax.ppermute(value, 'tp', [(i, i ^ mask) for i in range(lax.axis_size('tp...  23 us
    ppermute x7, waiting for transfers between devices, seq_xor(): lax.ppermute(value, 'seq', [(i, i ^ mask) for i in range(lax.axis_size('s...  10 us
    unnamed x34, local copies, waits for them, and re-layouts  7.93 us
    pallas_call x1, Pallas kernels, fill_cache(): pl.pallas_call(functools.partial(cache_kernel, len(pieces), 2 * PAGE), ou...  4.69 us
    ppermute x7, starting transfers between devices, seq_xor(): lax.ppermute(value, 'seq', [(i, i ^ mask) for i in range(lax.axis_size('s...  3.99 us
    pallas_call x1, Pallas kernels, hidden_of(): pl.pallas_call(functools.partial(hidden_kernel, places), out_shape=[jax.S...  3.73 us
    pallas_call x1, Pallas kernels, attend(): pl.pallas_call(functools.partial(attend_kernel, len(pieces), heads, reach...  3.6 us
  transfers between devices with their start and end apart: 23, of which 15 were waited for; matrix products, arithmetic and copies ran while one was open for 0% of the time, Pallas kernels for 10%

profile of v7, /device:TPU:2, one launch (start us, length us, event | category | flops | bytes accessed | tf_op | source)
XLA Modules:
  0.0 106.3 jit_solution(66694784311507636)
XLA Ops:
  0.7 1.0 fusion
  1.7 2.7 %collective-permute-start.1 = (bf16[256,256]{1,0:T(8,128)(2,1)S(1)}, bf16[256,256]{1,0:T(8,128)(2,1)S(1)}, u32[]{:S(2)}, u32[]{:S(2)}) collective-permute-start(bf16[256,256]{1,0:T(8,128)(2,1)S(1)} %get-tuple-element.42), channel_id=1, source_target_pairs={{0,2},{1,3},{2,0},{3,1},{4,6},{5,7},{6,4},{7,5},{8,10},{9,11},{10,... | collective-permute-start | bytes 393224 | tf_op jit(solution)/shard_map/ppermute | solution.py:57
  4.7 1.6 %collective-permute-start = (bf16[512,256]{1,0:T(8,128)(2,1)}, bf16[512,256]{1,0:T(8,128)(2,1)S(1)}, u32[]{:S(2)}, u32[]{:S(2)}) collective-permute-start(bf16[512,256]{1,0:T(8,128)(2,1)} %refs_0_), channel_id=1, source_target_pairs={{0,1},{1,0},{2,3},{3,2},{4,5},{5,4},{6,7},{7,6},{8,9},{9,8},{10,11... | collective-permute-start | bytes 786440 | tf_op jit(solution)/shard_map/ppermute | solution.py:57
  6.3 0.7 copy-done.9
  6.9 0.7 copy-done.13
  7.6 0.7 copy-done.14
  8.3 0.7 copy-done.15
  9.0 0.7 copy-done.16
  9.7 1.1 %tables.1 = (f32[512,128]{1,0:T(8,128)S(1)}, f32[512,128]{1,0:T(8,128)S(1)}, bf16[16,256]{1,0:T(8,128)(2,1)S(1)}, bf16[2,512,128]{2,1,0:T(8,128)(2,1)S(1)}) custom-call(s32[4]{0:T(128)S(1)} %copy-done.9, f32[2,2]{1,0:T(2,128)S(1)} %copy-done.15, f32[32,1]{1,0:T(8,128)S(1)} %copy-done.16, s32[1,512]{1,0:T(1,128)S(1)} %bitcast.2, s32[1,512]{1,0:T(1,128)S(1)} %bitcast.3), custom_call_target="tpu_custom_call" | custom-call | flops 524288 | bytes 1048576 | tf_op jit(solution)/shard_map/tables/pallas_call | solution.py:171
  10.8 4.0 %collective-permute-done.1.refs_2_ = bf16[256,256]{1,0:T(8,128)(2,1)S(1)} collective-permute-done((bf16[256,256]{1,0:T(8,128)(2,1)S(1)}, bf16[256,256]{1,0:T(8,128)(2,1)S(1)}, u32[]{:S(2)}, u32[]{:S(2)}) %collective-permute-start.1) | collective-permute-done | bytes 131104 | tf_op jit(solution)/shard_map/ppermute | solution.py:57
  14.7 1.7 %collective-permute-done.2.refs_3_ = bf16[256,256]{1,0:T(8,128)(2,1)S(1)} collective-permute-done((bf16[256,256]{1,0:T(8,128)(2,1)S(1)}, bf16[256,256]{1,0:T(8,128)(2,1)S(1)}, u32[]{:S(2)}, u32[]{:S(2)}) %collective-permute-start.2) | collective-permute-done | bytes 131104 | tf_op jit(solution)/shard_map/ppermute | solution.py:57
  16.4 0.6 collective-permute-start.4
  17.0 1.4 %collective-permute-start.3 = (bf16[256,256]{1,0:T(8,128)(2,1)S(1)}, bf16[256,256]{1,0:T(8,128)(2,1)S(1)}, u32[]{:S(2)}, u32[]{:S(2)}) collective-permute-start(bf16[256,256]{1,0:T(8,128)(2,1)S(1)} %collective-permute-done.1.refs_2_), channel_id=1, source_target_pairs={{0,1},{1,0},{2,3},{3,2},{4,5},{5,4},{6,7},{7,6},{8,9},{9,8},{10,11... | collective-permute-start | bytes 393224 | tf_op jit(solution)/shard_map/ppermute | solution.py:57
  18.4 3.7 %collective-permute-done.4.refs_5_ = bf16[256,256]{1,0:T(8,128)(2,1)S(1)} collective-permute-done((bf16[256,256]{1,0:T(8,128)(2,1)S(1)}, bf16[256,256]{1,0:T(8,128)(2,1)S(1)}, u32[]{:S(2)}, u32[]{:S(2)}) %collective-permute-start.4) | collective-permute-done | bytes 131104 | tf_op jit(solution)/shard_map/ppermute | solution.py:57
  22.2 1.4 %collective-permute-done.3.refs_4_ = bf16[256,256]{1,0:T(8,128)(2,1)S(1)} collective-permute-done((bf16[256,256]{1,0:T(8,128)(2,1)S(1)}, bf16[256,256]{1,0:T(8,128)(2,1)S(1)}, u32[]{:S(2)}, u32[]{:S(2)}) %collective-permute-start.3) | collective-permute-done | bytes 131104 | tf_op jit(solution)/shard_map/ppermute | solution.py:57
  23.6 0.9 copy-done.3
  24.5 0.9 copy-done.4
  25.5 0.9 copy-done.5
  26.4 0.9 copy-done.6
  27.4 0.7 copy-done.7
  28.1 1.4 %project.1 = (bf16[512,1024]{1,0:T(8,128)(2,1)S(1)}, bf16[512,128]{1,0:T(8,128)(2,1)S(1)}, bf16[528,256]{1,0:T(8,128)(2,1)S(1)}) custom-call(bf16[512,256]{1,0:T(8,128)(2,1)S(1)} %copy-done.3, bf16[512,256]{1,0:T(8,128)(2,1)S(1)} %collective-permute-done.refs_1_, bf16[256,256]{1,0:T(8,128)(2,1)S(1)} %collective-permute-done.1.refs_2_, ...), custom_call_target="tpu_custom_call" | custom-call | flops 402653184 | bytes 4194304 | tf_op jit(solution)/shard_map/project/pallas_call | solution.py:235
  29.5 1.5 %collective-permute-start.10 = (bf16[528,256]{1,0:T(8,128)(2,1)S(1)}, bf16[528,256]{1,0:T(8,128)(2,1)S(1)}, u32[]{:S(2)}, u32[]{:S(2)}) collective-permute-start(bf16[528,256]{1,0:T(8,128)(2,1)S(1)} %get-tuple-element.72.refs_0_), channel_id=1, source_target_pairs={{0,24},{4,28},{8,16},{12,20},{16,8},{20,12},{24,0},{28,4},{1,25},{... | collective-permute-start | bytes 811016 | tf_op jit(solution)/shard_map/ppermute | solution.py:252
  31.1 0.7 collective-permute-start.8
  31.8 1.3 %collective-permute-start.6 = (bf16[528,256]{1,0:T(8,128)(2,1)S(1)}, bf16[528,256]{1,0:T(8,128)(2,1)S(1)}, u32[]{:S(2)}, u32[]{:S(2)}) collective-permute-start(bf16[528,256]{1,0:T(8,128)(2,1)S(1)} %get-tuple-element.72.refs_0_), channel_id=1, source_target_pairs={{0,8},{4,12},{8,0},{12,4},{16,24},{20,28},{24,16},{28,20},{1,9},{5... | collective-permute-start | bytes 811016 | tf_op jit(solution)/shard_map/ppermute | solution.py:252
  33.1 6.8 %collective-permute-done.10.refs_6_ = bf16[528,256]{1,0:T(8,128)(2,1)S(1)} collective-permute-done((bf16[528,256]{1,0:T(8,128)(2,1)S(1)}, bf16[528,256]{1,0:T(8,128)(2,1)S(1)}, u32[]{:S(2)}, u32[]{:S(2)}) %collective-permute-start.10) | collective-permute-done | bytes 270368 | tf_op jit(solution)/shard_map/ppermute | solution.py:252
  39.9 3.1 %collective-permute-done.8.refs_4_ = bf16[528,256]{1,0:T(8,128)(2,1)S(1)} collective-permute-done((bf16[528,256]{1,0:T(8,128)(2,1)S(1)}, bf16[528,256]{1,0:T(8,128)(2,1)S(1)}, u32[]{:S(2)}, u32[]{:S(2)}) %collective-permute-start.8) | collective-permute-done | bytes 270368 | tf_op jit(solution)/shard_map/ppermute | solution.py:252
  43.1 0.4 collective-permute-start.7
  43.5 4.4 %collective-permute-start.16 = (bf16[128,1024]{1,0:T(8,128)(2,1)S(1)}, bf16[128,1024]{1,0:T(8,128)(2,1)S(1)}, u32[]{:S(2)}, u32[]{:S(2)}) collective-permute-start(bf16[128,1024]{1,0:T(8,128)(2,1)S(1)} %copy-done.12), channel_id=1, source_target_pairs={{0,2},{1,3},{2,0},{3,1},{4,6},{5,7},{6,4},{7,5},{8,10},{9,11},{10,... | collective-permute-start | bytes 786440 | tf_op jit(solution)/shard_map/ppermute | solution.py:57
  48.0 3.6 %attend.1.refs_0_ = bf16[512,128]{1,0:T(8,128)(2,1)S(1)} custom-call(s32[4]{0:T(128)S(1)} %copy-done.10, bf16[512,128]{1,0:T(8,128)(2,1)S(1)} %get-tuple-element.48.queries, bf16[2,512,128]{2,1,0:T(8,128)(2,1)S(1)} %get-tuple-element.49.query_marks, bf16[528,256]{1,0:T(8,128)(2,1)S(1)} %get-tuple-element.72.refs_0_, ...), custom_call_target="tpu_custom_call" | custom-call | flops 2684354560 | bytes 4194304 | tf_op jit(solution)/shard_map/attend/pallas_call | solution.py:399
  51.6 1.4 %collective-permute-start.13 = (bf16[512,128]{1,0:T(8,128)(2,1)S(1)}, bf16[512,128]{1,0:T(8,128)(2,1)S(1)}, u32[]{:S(2)}, u32[]{:S(2)}) collective-permute-start(bf16[512,128]{1,0:T(8,128)(2,1)S(1)} %attend.1.refs_0_), channel_id=1, source_target_pairs={{0,2},{1,3},{2,0},{3,1},{4,6},{5,7},{6,4},{7,5},{8,10},{9,11},{10,... | collective-permute-start | bytes 393224 | tf_op jit(solution)/shard_map/ppermute | solution.py:57
  53.0 1.5 %collective-permute-start.15 = (bf16[128,1024]{1,0:T(8,128)(2,1)S(1)}, bf16[128,1024]{1,0:T(8,128)(2,1)S(1)}, u32[]{:S(2)}, u32[]{:S(2)}) collective-permute-start(bf16[128,1024]{1,0:T(8,128)(2,1)S(1)} %copy-done.12), channel_id=1, source_target_pairs={{0,1},{1,0},{2,3},{3,2},{4,5},{5,4},{6,7},{7,6},{8,9},{9,8},{10,11... | collective-permute-start | bytes 786440 | tf_op jit(solution)/shard_map/ppermute | solution.py:57
  54.5 9.1 %collective-permute-done.16.refs_6_ = bf16[128,1024]{1,0:T(8,128)(2,1)S(1)} collective-permute-done((bf16[128,1024]{1,0:T(8,128)(2,1)S(1)}, bf16[128,1024]{1,0:T(8,128)(2,1)S(1)}, u32[]{:S(2)}, u32[]{:S(2)}) %collective-permute-start.16) | collective-permute-done | bytes 262176 | tf_op jit(solution)/shard_map/ppermute | solution.py:57
  63.8 1.8 %collective-permute-start.12 = (bf16[512,128]{1,0:T(8,128)(2,1)S(1)}, bf16[512,128]{1,0:T(8,128)(2,1)S(1)}, u32[]{:S(2)}, u32[]{:S(2)}) collective-permute-start(bf16[512,128]{1,0:T(8,128)(2,1)S(1)} %attend.1.refs_0_), channel_id=1, source_target_pairs={{0,1},{1,0},{2,3},{3,2},{4,5},{5,4},{6,7},{7,6},{8,9},{9,8},{10,11... | collective-permute-start | bytes 393224 | tf_op jit(solution)/shard_map/ppermute | solution.py:57
  65.6 0.5 fetch.1
  66.4 2.1 %collective-permute-done.15.refs_5_ = bf16[128,1024]{1,0:T(8,128)(2,1)S(1)} collective-permute-done((bf16[128,1024]{1,0:T(8,128)(2,1)S(1)}, bf16[128,1024]{1,0:T(8,128)(2,1)S(1)}, u32[]{:S(2)}, u32[]{:S(2)}) %collective-permute-start.15) | collective-permute-done | bytes 262176 | tf_op jit(solution)/shard_map/ppermute | solution.py:57
  68.5 5.6 %collective-permute-done.17.refs_7_ = bf16[128,1024]{1,0:T(8,128)(2,1)S(1)} collective-permute-done((bf16[128,1024]{1,0:T(8,128)(2,1)S(1)}, bf16[128,1024]{1,0:T(8,128)(2,1)S(1)}, u32[]{:S(2)}, u32[]{:S(2)}) %collective-permute-start.17) | collective-permute-done | bytes 262176 | tf_op jit(solution)/shard_map/ppermute | solution.py:57
  74.1 2.8 %collective-permute-done.12.refs_1_ = bf16[512,128]{1,0:T(8,128)(2,1)S(1)} collective-permute-done((bf16[512,128]{1,0:T(8,128)(2,1)S(1)}, bf16[512,128]{1,0:T(8,128)(2,1)S(1)}, u32[]{:S(2)}, u32[]{:S(2)}) %collective-permute-start.12) | collective-permute-done | bytes 131104 | tf_op jit(solution)/shard_map/ppermute | solution.py:57
  76.9 2.8 %collective-permute-done.14.refs_3_ = bf16[512,128]{1,0:T(8,128)(2,1)S(1)} collective-permute-done((bf16[512,128]{1,0:T(8,128)(2,1)S(1)}, bf16[512,128]{1,0:T(8,128)(2,1)S(1)}, u32[]{:S(2)}, u32[]{:S(2)}) %collective-permute-start.14) | collective-permute-done | bytes 131104 | tf_op jit(solution)/shard_map/ppermute | solution.py:57
  79.7 3.7 %hidden.1 = (bf16[512,1024]{1,0:T(8,128)(2,1)S(1)}, bf16[512,256]{1,0:T(8,128)(2,1)S(1)}, bf16[256,256]{1,0:T(8,128)(2,1)S(1)}, bf16[256,256]{1,0:T(8,128)(2,1)S(1)}) custom-call(bf16[512,128]{1,0:T(8,128)(2,1)S(1)} %attend.1.refs_0_, bf16[512,128]{1,0:T(8,128)(2,1)S(1)} %collective-permute-done.12.refs_1_, ...), custom_call_target="tpu_custom_call" | custom-call | flops 3221225472 | bytes 10485760 | tf_op jit(solution)/shard_map/hidden/pallas_call | solution.py:569
  83.6 2.0 %collective-permute-start.21 = (bf16[256,256]{1,0:T(8,128)(2,1)S(1)}, bf16[256,256]{1,0:T(8,128)(2,1)S(1)}, u32[]{:S(2)}, u32[]{:S(2)}) collective-permute-start(bf16[256,256]{1,0:T(8,128)(2,1)S(1)} %get-tuple-element.71), channel_id=1, source_target_pairs={{0,1},{1,0},{2,3},{3,2},{4,5},{5,4},{6,7},{7,6},{8,9},{9,8},{10,11... | collective-permute-start | bytes 393224 | tf_op jit(solution)/shard_map/ppermute | solution.py:57
  85.6 1.0 down_blocks.1
  86.7 3.2 %collective-permute-done.19.refs_1_ = bf16[256,256]{1,0:T(8,128)(2,1)S(1)} collective-permute-done((bf16[256,256]{1,0:T(8,128)(2,1)S(1)}, bf16[256,256]{1,0:T(8,128)(2,1)S(1)}, u32[]{:S(2)}, u32[]{:S(2)}) %collective-permute-start.19) | collective-permute-done | bytes 131104 | tf_op jit(solution)/shard_map/ppermute | solution.py:57
  89.9 2.4 %collective-permute-start.20 = (bf16[256,256]{1,0:T(8,128)(2,1)S(1)}, bf16[256,256]{1,0:T(8,128)(2,1)S(1)}, u32[]{:S(2)}, u32[]{:S(2)}) collective-permute-start(bf16[256,256]{1,0:T(8,128)(2,1)S(1)} %add_up.3), channel_id=1, source_target_pairs={{0,2},{1,3},{2,0},{3,1},{4,6},{5,7},{6,4},{7,5},{8,10},{9,11},{10,... | collective-permute-start | bytes 393224 | tf_op jit(solution)/shard_map/ppermute | solution.py:57
  92.4 1.7 %collective-permute-done.21.refs_1_ = bf16[256,256]{1,0:T(8,128)(2,1)S(1)} collective-permute-done((bf16[256,256]{1,0:T(8,128)(2,1)S(1)}, bf16[256,256]{1,0:T(8,128)(2,1)S(1)}, u32[]{:S(2)}, u32[]{:S(2)}) %collective-permute-start.21) | collective-permute-done | bytes 131104 | tf_op jit(solution)/shard_map/ppermute | solution.py:57
  94.1 2.1 %collective-permute-start.22 = (bf16[256,256]{1,0:T(8,128)(2,1)S(1)}, bf16[256,256]{1,0:T(8,128)(2,1)S(1)}, u32[]{:S(2)}, u32[]{:S(2)}) collective-permute-start(bf16[256,256]{1,0:T(8,128)(2,1)S(1)} %add_up.4), channel_id=1, source_target_pairs={{0,2},{1,3},{2,0},{3,1},{4,6},{5,7},{6,4},{7,5},{8,10},{9,11},{10,... | collective-permute-start | bytes 393224 | tf_op jit(solution)/shard_map/ppermute | solution.py:57
  96.3 4.7 %fill_cache.1 = bf16[576,2,128]{2,1,0:T(2,128)(2,1)} custom-call(s32[4]{0:T(128)S(1)} %copy-done.10, s32[72]{0:T(128)S(1)} %copy-done.11, bf16[528,256]{1,0:T(8,128)(2,1)S(1)} %get-tuple-element.72.refs_0_, bf16[528,256]{1,0:T(8,128)(2,1)S(1)} %collective-permute-done.5.refs_1_, bf16[528,256]{1,0:T(8,128)(2,1)S(1)} %collective-permute-done.6.refs_2_, ...), custom_call_target="tpu_custom_call" | custom-call | flops 75497472 | bytes 3145728 | tf_op jit(solution)/shard_map/fill_cache/pallas_call | solution.py:495
  101.0 4.6 %collective-permute-done.22.refs_3_ = bf16[256,256]{1,0:T(8,128)(2,1)S(1)} collective-permute-done((bf16[256,256]{1,0:T(8,128)(2,1)S(1)}, bf16[256,256]{1,0:T(8,128)(2,1)S(1)}, u32[]{:S(2)}, u32[]{:S(2)}) %collective-permute-start.22) | collective-permute-done | bytes 131104 | tf_op jit(solution)/shard_map/ppermute | solution.py:57
  105.5 0.8 add_up.5
  (43 shorter events, 1.3 us)
Async XLA Ops:
  0.6 47.3 %copy-start.10 = (s32[4]{0:T(128)S(1)}, s32[4]{0:T(128)}, u32[]{:S(2)}) copy-start(s32[4]{0:T(128)} %lengths.5) | copy-start | bytes 52
  0.6 42.9 %copy-start.12 = (bf16[128,1024]{1,0:T(8,128)(2,1)S(1)}, bf16[128,1024]{1,0:T(8,128)(2,1)}, u32[]{:S(2)}) copy-start(bf16[128,1024]{1,0:T(8,128)(2,1)} %refs_4_.1) | copy-start | bytes 786436
  1.7 13.0 %collective-permute-start.1 = (bf16[256,256]{1,0:T(8,128)(2,1)S(1)}, bf16[256,256]{1,0:T(8,128)(2,1)S(1)}, u32[]{:S(2)}, u32[]{:S(2)}) collective-permute-start(bf16[256,256]{1,0:T(8,128)(2,1)S(1)} %get-tuple-element.42), channel_id=1, source_target_pairs={{0,2},{1,3},{2,0},{3,1},{4,6},{5,7},{6,4},{7,5},{8,10},{9,11},{10,... | collective-permute-start | bytes 393224 | tf_op jit(solution)/shard_map/ppermute | solution.py:57
  4.3 12.1 %collective-permute-start.2 = (bf16[256,256]{1,0:T(8,128)(2,1)S(1)}, bf16[256,256]{1,0:T(8,128)(2,1)S(1)}, u32[]{:S(2)}, u32[]{:S(2)}) collective-permute-start(bf16[256,256]{1,0:T(8,128)(2,1)S(1)} %get-tuple-element.45), channel_id=1, source_target_pairs={{0,2},{1,3},{2,0},{3,1},{4,6},{5,7},{6,4},{7,5},{8,10},{9,11},{10,... | collective-permute-start | bytes 393224 | tf_op jit(solution)/shard_map/ppermute | solution.py:57
  4.7 17.5 %collective-permute-start = (bf16[512,256]{1,0:T(8,128)(2,1)}, bf16[512,256]{1,0:T(8,128)(2,1)S(1)}, u32[]{:S(2)}, u32[]{:S(2)}) collective-permute-start(bf16[512,256]{1,0:T(8,128)(2,1)} %refs_0_), channel_id=1, source_target_pairs={{0,1},{1,0},{2,3},{3,2},{4,5},{5,4},{6,7},{7,6},{8,9},{9,8},{10,11... | collective-permute-start | bytes 786440 | tf_op jit(solution)/shard_map/ppermute | solution.py:57
  6.3 0.7 copy-start.9
  6.9 0.7 copy-start.13
  7.6 0.7 copy-start.14
  8.3 0.7 copy-start.15
  9.0 0.7 copy-start.16
  16.4 5.7 %collective-permute-start.4 = (bf16[256,256]{1,0:T(8,128)(2,1)S(1)}, bf16[256,256]{1,0:T(8,128)(2,1)S(1)}, u32[]{:S(2)}, u32[]{:S(2)}) collective-permute-start(bf16[256,256]{1,0:T(8,128)(2,1)S(1)} %collective-permute-done.2.refs_3_), channel_id=1, source_target_pairs={{0,1},{1,0},{2,3},{3,2},{4,5},{5,4},{6,7},{7,6},{8,9},{9,8},{10,11... | collective-permute-start | bytes 393224 | tf_op jit(solution)/shard_map/ppermute | solution.py:57
  17.0 6.5 %collective-permute-start.3 = (bf16[256,256]{1,0:T(8,128)(2,1)S(1)}, bf16[256,256]{1,0:T(8,128)(2,1)S(1)}, u32[]{:S(2)}, u32[]{:S(2)}) collective-permute-start(bf16[256,256]{1,0:T(8,128)(2,1)S(1)} %collective-permute-done.1.refs_2_), channel_id=1, source_target_pairs={{0,1},{1,0},{2,3},{3,2},{4,5},{5,4},{6,7},{7,6},{8,9},{9,8},{10,11... | collective-permute-start | bytes 393224 | tf_op jit(solution)/shard_map/ppermute | solution.py:57
  23.6 1.0 copy-start.3
  24.5 0.9 copy-start.4
  25.5 0.9 copy-start.5
  26.4 0.9 copy-start.6
  27.4 0.7 copy-start.7
  29.5 10.4 %collective-permute-start.10 = (bf16[528,256]{1,0:T(8,128)(2,1)S(1)}, bf16[528,256]{1,0:T(8,128)(2,1)S(1)}, u32[]{:S(2)}, u32[]{:S(2)}) collective-permute-start(bf16[528,256]{1,0:T(8,128)(2,1)S(1)} %get-tuple-element.72.refs_0_), channel_id=1, source_target_pairs={{0,24},{4,28},{8,16},{12,20},{16,8},{20,12},{24,0},{28,4},{1,25},{... | collective-permute-start | bytes 811016 | tf_op jit(solution)/shard_map/ppermute | solution.py:252
  31.1 12.0 %collective-permute-start.8 = (bf16[528,256]{1,0:T(8,128)(2,1)S(1)}, bf16[528,256]{1,0:T(8,128)(2,1)S(1)}, u32[]{:S(2)}, u32[]{:S(2)}) collective-permute-start(bf16[528,256]{1,0:T(8,128)(2,1)S(1)} %get-tuple-element.72.refs_0_), channel_id=1, source_target_pairs={{0,16},{4,20},{8,24},{12,28},{16,0},{20,4},{24,8},{28,12},{1,17},{... | collective-permute-start | bytes 811016 | tf_op jit(solution)/shard_map/ppermute | solution.py:252
  31.8 11.3 %collective-permute-start.6 = (bf16[528,256]{1,0:T(8,128)(2,1)S(1)}, bf16[528,256]{1,0:T(8,128)(2,1)S(1)}, u32[]{:S(2)}, u32[]{:S(2)}) collective-permute-start(bf16[528,256]{1,0:T(8,128)(2,1)S(1)} %get-tuple-element.72.refs_0_), channel_id=1, source_target_pairs={{0,8},{4,12},{8,0},{12,4},{16,24},{20,28},{24,16},{28,20},{1,9},{5... | collective-permute-start | bytes 811016 | tf_op jit(solution)/shard_map/ppermute | solution.py:252
  33.1 14.8 %collective-permute-start.5 = (bf16[528,256]{1,0:T(8,128)(2,1)S(1)}, bf16[528,256]{1,0:T(8,128)(2,1)S(1)}, u32[]{:S(2)}, u32[]{:S(2)}) collective-permute-start(bf16[528,256]{1,0:T(8,128)(2,1)S(1)} %get-tuple-element.72.refs_0_), channel_id=1, source_target_pairs={{0,4},{4,0},{8,12},{12,8},{16,20},{20,16},{24,28},{28,24},{1,5},{5... | collective-permute-start | bytes 811016 | tf_op jit(solution)/shard_map/ppermute | solution.py:252
  39.9 8.0 %collective-permute-start.11 = (bf16[528,256]{1,0:T(8,128)(2,1)S(1)}, bf16[528,256]{1,0:T(8,128)(2,1)S(1)}, u32[]{:S(2)}, u32[]{:S(2)}) collective-permute-start(bf16[528,256]{1,0:T(8,128)(2,1)S(1)} %collective-permute-done.10.refs_6_), channel_id=1, source_target_pairs={{0,4},{4,0},{8,12},{12,8},{16,20},{20,16},{24,28},{28,24},{1,5},{5... | collective-permute-start | bytes 811016 | tf_op jit(solution)/shard_map/ppermute | solution.py:252
  43.0 4.9 %collective-permute-start.9 = (bf16[528,256]{1,0:T(8,128)(2,1)S(1)}, bf16[528,256]{1,0:T(8,128)(2,1)S(1)}, u32[]{:S(2)}, u32[]{:S(2)}) collective-permute-start(bf16[528,256]{1,0:T(8,128)(2,1)S(1)} %collective-permute-done.8.refs_4_), channel_id=1, source_target_pairs={{0,4},{4,0},{8,12},{12,8},{16,20},{20,16},{24,28},{28,24},{1,5},{5... | collective-permute-start | bytes 811016 | tf_op jit(solution)/shard_map/ppermute | solution.py:252
  43.1 4.8 %collective-permute-start.7 = (bf16[528,256]{1,0:T(8,128)(2,1)S(1)}, bf16[528,256]{1,0:T(8,128)(2,1)S(1)}, u32[]{:S(2)}, u32[]{:S(2)}) collective-permute-start(bf16[528,256]{1,0:T(8,128)(2,1)S(1)} %collective-permute-done.6.refs_2_), channel_id=1, source_target_pairs={{0,4},{4,0},{8,12},{12,8},{16,20},{20,16},{24,28},{28,24},{1,5},{5... | collective-permute-start | bytes 811016 | tf_op jit(solution)/shard_map/ppermute | solution.py:252
  43.5 20.0 %collective-permute-start.16 = (bf16[128,1024]{1,0:T(8,128)(2,1)S(1)}, bf16[128,1024]{1,0:T(8,128)(2,1)S(1)}, u32[]{:S(2)}, u32[]{:S(2)}) collective-permute-start(bf16[128,1024]{1,0:T(8,128)(2,1)S(1)} %copy-done.12), channel_id=1, source_target_pairs={{0,2},{1,3},{2,0},{3,1},{4,6},{5,7},{6,4},{7,5},{8,10},{9,11},{10,... | collective-permute-start | bytes 786440 | tf_op jit(solution)/shard_map/ppermute | solution.py:57
  47.9 17.6 %copy-start = (bf16[1024,1024]{1,0:T(8,128)(2,1)S(1)}, bf16[1024,1024]{1,0:T(8,128)(2,1)}, u32[]{:S(2)}) copy-start(bf16[1024,1024]{1,0:T(8,128)(2,1)} %refs_2_) | copy-start | bytes 6291460
  47.9 17.6 %copy-start.1 = (bf16[1024,1024]{1,0:T(8,128)(2,1)S(1)}, bf16[1024,1024]{1,0:T(8,128)(2,1)}, u32[]{:S(2)}) copy-start(bf16[1024,1024]{1,0:T(8,128)(2,1)} %refs_3_) | copy-start | bytes 6291460
  48.0 17.6 %copy-start.2 = (bf16[1024,1024]{1,0:T(8,128)(2,1)S(1)}, bf16[1024,1024]{1,0:T(8,128)(2,1)}, u32[]{:S(2)}) copy-start(bf16[1024,1024]{1,0:T(8,128)(2,1)} %refs_4_) | copy-start | bytes 6291460
  48.0 17.6 %copy-start.8 = (bf16[1024]{0:T(1024)(128)(2,1)S(1)}, bf16[1024]{0:T(1024)(128)(2,1)}, u32[]{:S(2)}) copy-start(bf16[1024]{0:T(1024)(128)(2,1)} %refs_1_) | copy-start | bytes 6148
  51.6 14.5 %collective-permute-start.13 = (bf16[512,128]{1,0:T(8,128)(2,1)S(1)}, bf16[512,128]{1,0:T(8,128)(2,1)S(1)}, u32[]{:S(2)}, u32[]{:S(2)}) collective-permute-start(bf16[512,128]{1,0:T(8,128)(2,1)S(1)} %attend.1.refs_0_), channel_id=1, source_target_pairs={{0,2},{1,3},{2,0},{3,1},{4,6},{5,7},{6,4},{7,5},{8,10},{9,11},{10,... | collective-permute-start | bytes 393224 | tf_op jit(solution)/shard_map/ppermute | solution.py:57
  53.0 15.5 %collective-permute-start.15 = (bf16[128,1024]{1,0:T(8,128)(2,1)S(1)}, bf16[128,1024]{1,0:T(8,128)(2,1)S(1)}, u32[]{:S(2)}, u32[]{:S(2)}) collective-permute-start(bf16[128,1024]{1,0:T(8,128)(2,1)S(1)} %copy-done.12), channel_id=1, source_target_pairs={{0,1},{1,0},{2,3},{3,2},{4,5},{5,4},{6,7},{7,6},{8,9},{9,8},{10,11... | collective-permute-start | bytes 786440 | tf_op jit(solution)/shard_map/ppermute | solution.py:57
  63.5 10.6 %collective-permute-start.17 = (bf16[128,1024]{1,0:T(8,128)(2,1)S(1)}, bf16[128,1024]{1,0:T(8,128)(2,1)S(1)}, u32[]{:S(2)}, u32[]{:S(2)}) collective-permute-start(bf16[128,1024]{1,0:T(8,128)(2,1)S(1)} %collective-permute-done.16.refs_6_), channel_id=1, source_target_pairs={{0,1},{1,0},{2,3},{3,2},{4,5},{5,4},{6,7},{7,6},{8,9},{9,8},{10,11... | collective-permute-start | bytes 786440 | tf_op jit(solution)/shard_map/ppermute | solution.py:57
  63.8 13.2 %collective-permute-start.12 = (bf16[512,128]{1,0:T(8,128)(2,1)S(1)}, bf16[512,128]{1,0:T(8,128)(2,1)S(1)}, u32[]{:S(2)}, u32[]{:S(2)}) collective-permute-start(bf16[512,128]{1,0:T(8,128)(2,1)S(1)} %attend.1.refs_0_), channel_id=1, source_target_pairs={{0,1},{1,0},{2,3},{3,2},{4,5},{5,4},{6,7},{7,6},{8,9},{9,8},{10,11... | collective-permute-start | bytes 393224 | tf_op jit(solution)/shard_map/ppermute | solution.py:57
  66.1 13.6 %collective-permute-start.14 = (bf16[512,128]{1,0:T(8,128)(2,1)S(1)}, bf16[512,128]{1,0:T(8,128)(2,1)S(1)}, u32[]{:S(2)}, u32[]{:S(2)}) collective-permute-start(bf16[512,128]{1,0:T(8,128)(2,1)S(1)} %collective-permute-done.13.refs_2_), channel_id=1, source_target_pairs={{0,1},{1,0},{2,3},{3,2},{4,5},{5,4},{6,7},{7,6},{8,9},{9,8},{10,11... | collective-permute-start | bytes 393224 | tf_op jit(solution)/shard_map/ppermute | solution.py:57
  83.5 6.4 %collective-permute-start.19 = (bf16[256,256]{1,0:T(8,128)(2,1)S(1)}, bf16[256,256]{1,0:T(8,128)(2,1)S(1)}, u32[]{:S(2)}, u32[]{:S(2)}) collective-permute-start(bf16[256,256]{1,0:T(8,128)(2,1)S(1)} %get-tuple-element.69), channel_id=1, source_target_pairs={{0,1},{1,0},{2,3},{3,2},{4,5},{5,4},{6,7},{7,6},{8,9},{9,8},{10,11... | collective-permute-start | bytes 393224 | tf_op jit(solution)/shard_map/ppermute | solution.py:57
  83.6 10.5 %collective-permute-start.21 = (bf16[256,256]{1,0:T(8,128)(2,1)S(1)}, bf16[256,256]{1,0:T(8,128)(2,1)S(1)}, u32[]{:S(2)}, u32[]{:S(2)}) collective-permute-start(bf16[256,256]{1,0:T(8,128)(2,1)S(1)} %get-tuple-element.71), channel_id=1, source_target_pairs={{0,1},{1,0},{2,3},{3,2},{4,5},{5,4},{6,7},{7,6},{8,9},{9,8},{10,11... | collective-permute-start | bytes 393224 | tf_op jit(solution)/shard_map/ppermute | solution.py:57
  85.6 10.7 %copy-start.11 = (s32[72]{0:T(128)S(1)}, s32[72]{0:T(128)}, u32[]{:S(2)}) copy-start(s32[72]{0:T(128)} %page_table.1) | copy-start | bytes 868
  86.6 19.0 %collective-permute-start.18 = (bf16[512,256]{1,0:T(8,128)(2,1)S(1)}, bf16[512,256]{1,0:T(8,128)(2,1)S(1)}, u32[]{:S(2)}, u32[]{:S(2)}) collective-permute-start(bf16[512,256]{1,0:T(8,128)(2,1)S(1)} %get-tuple-element.67), channel_id=1, source_target_pairs={{0,1},{1,0},{2,3},{3,2},{4,5},{5,4},{6,7},{7,6},{8,9},{9,8},{10,11... | collective-permute-start | bytes 786440 | tf_op jit(solution)/shard_map/ppermute | solution.py:57
  89.9 11.0 %collective-permute-start.20 = (bf16[256,256]{1,0:T(8,128)(2,1)S(1)}, bf16[256,256]{1,0:T(8,128)(2,1)S(1)}, u32[]{:S(2)}, u32[]{:S(2)}) collective-permute-start(bf16[256,256]{1,0:T(8,128)(2,1)S(1)} %add_up.3), channel_id=1, source_target_pairs={{0,2},{1,3},{2,0},{3,1},{4,6},{5,7},{6,4},{7,5},{8,10},{9,11},{10,... | collective-permute-start | bytes 393224 | tf_op jit(solution)/shard_map/ppermute | solution.py:57
  94.1 11.4 %collective-permute-start.22 = (bf16[256,256]{1,0:T(8,128)(2,1)S(1)}, bf16[256,256]{1,0:T(8,128)(2,1)S(1)}, u32[]{:S(2)}, u32[]{:S(2)}) collective-permute-start(bf16[256,256]{1,0:T(8,128)(2,1)S(1)} %add_up.4), channel_id=1, source_target_pairs={{0,2},{1,3},{2,0},{3,1},{4,6},{5,7},{6,4},{7,5},{8,10},{9,11},{10,... | collective-permute-start | bytes 393224 | tf_op jit(solution)/shard_map/ppermute | solution.py:57

commit v8 on v7

--- a/solution.py
+++ b/solution.py
@@ -122,9 +122,14 @@
     return round_up(BIAS_PARTS * VARS + requests, 16)
 
 
-def tables_kernel(
-    lengths, bias, frequency, positions, variate, cosine, sine, extra, marks
-):
+def tables_kernel(count, lengths, bias, frequency, positions, variate, *refs):
+    cosine, sine, extra, marks = refs[count : count + 4]
+    sources, targets, sems = list(refs[:count]), refs[count + 4 : -1], refs[-1]
+    if targets[-1].shape != sources[-1].shape:
+        half = targets[-1].shape[1]
+        columns = pl.ds(pl.multiple_of(lax.rem(lax.axis_index("seq"), 2) * half, half), half)
+        sources[-1] = sources[-1].at[:, columns]
+    loads = start_loads(sources, targets, sems)
     rows = positions.shape[1]
     width = cosine.shape[1]
     angles = frequency[...] * positions[...].astype(jnp.float32)
@@ -160,25 +165,31 @@
         column = jnp.where(other, HIDDEN_SCORE, column)
         rest = jnp.zeros((LANES - shape[0], rows), jnp.float32)
         marks[h] = jnp.transpose(jnp.concatenate([column, rest], axis=0)).astype(jnp.bfloat16)
-
-
-def tables(lengths, bias, positions, variate, width):
+    finish_loads(loads)
+
+
+def tables(lengths, bias, positions, variate, width, arrays, halve):
     rows = positions.shape[0]
     half = HD // 2
     heads = width // HD
     frequency = 10000.0 ** (-np.arange(half, dtype=np.float32) / np.float32(half))
     extra = round_up(rows // (2 * width), 16)
+    kept = [array.shape for array in arrays]
+    if halve:
+        kept[-1] = (kept[-1][0], kept[-1][1] // 2)
     return pl.pallas_call(
-        tables_kernel,
+        functools.partial(tables_kernel, len(arrays)),
         out_shape=[
             jax.ShapeDtypeStruct((rows, width), jnp.float32),
             jax.ShapeDtypeStruct((rows, width), jnp.float32),
             jax.ShapeDtypeStruct((extra, 2 * width), jnp.bfloat16),
             jax.ShapeDtypeStruct((heads, rows, LANES), jnp.bfloat16),
-        ],
-        in_specs=[SMEM, SMEM, VMEM, VMEM, VMEM],
-        out_specs=[VMEM] * 4,
-        compiler_params=params(4),
+        ]
+        + [jax.ShapeDtypeStruct(shape, array.dtype) for shape, array in zip(kept, arrays)],
+        in_specs=[SMEM, SMEM, VMEM, VMEM, VMEM] + [ANY] * len(arrays),
+        out_specs=[VMEM] * (4 + len(arrays)),
+        scratch_shapes=[pltpu.SemaphoreType.DMA((len(arrays),))],
+        compiler_params=params(6),
         cost_estimate=cost(rows * 1024, 1 << 20, rows * 64),
         name="tables",
     )(
@@ -187,6 +198,7 @@
         jnp.asarray(frequency.astype(np.float32).reshape(half, 1)),
         positions.reshape(1, rows),
         variate.reshape(1, rows),
+        *arrays,
     )
 
 
@@ -525,16 +537,24 @@
     )(*arrays)
 
 
-def hidden_kernel(places, *refs):
-    pieces, w_out_pieces = refs[:places], refs[places : 2 * places]
-    tokens, gain, w_gate, w_up, w_down = refs[2 * places : 2 * places + 5]
-    outs, attended, w_out = refs[2 * places + 5 : -2], refs[-2], refs[-1]
+def hidden_kernel(counts, *refs):
+    places = len(counts)
+    pieces, refs = refs[:places], refs[places:]
+    w_out_pieces, refs = refs[: sum(counts)], refs[sum(counts) :]
+    tokens, gain, w_gate, w_up, w_down = refs[:5]
+    outs, attended, w_out = refs[5:-2], refs[-2], refs[-1]
     hidden, kept = outs[:2]
     place = lax.axis_index("tp")
+    core = lax.rem(lax.axis_index("seq"), 2)
     each = pieces[0].shape[1]
-    for i in range(places):
+    at = 0
+    for i, count in enumerate(counts):
         attended[:, i * each : (i + 1) * each] = pieces[i][...]
-        w_out[i * each : (i + 1) * each, :] = w_out_pieces[i][...]
+        part = w_out.shape[1] // count
+        for j in range(count):
+            columns = pl.ds(pl.multiple_of((core ^ j) * part, part), part) if count > 1 else slice(None)
+            w_out[i * each : (i + 1) * each, columns] = w_out_pieces[at][...]
+            at += 1
     rows, features = tokens.shape
     width = kept.shape[1]
     step = min(rows, 256)
@@ -566,10 +586,12 @@
     units = w_gate.shape[1]
     inner = places * pieces[0].shape[1]
     shapes = [(rows, units), (rows, width)] + [(rows // 2, width)] * (2 * (places == 4))
+    counts = [len(piece) for piece in w_out_pieces]
+    w_out_pieces = [part for piece in w_out_pieces for part in piece]
     return pl.pallas_call(
-        functools.partial(hidden_kernel, places),
+        functools.partial(hidden_kernel, counts),
         out_shape=[jax.ShapeDtypeStruct(shape, jnp.bfloat16) for shape in shapes],
-        in_specs=[VMEM] * (2 * places + 5),
+        in_specs=[VMEM] * (places + len(w_out_pieces) + 5),
         out_specs=[VMEM] * len(shapes),
         scratch_shapes=[
             pltpu.VMEM((rows, inner), jnp.bfloat16),
@@ -676,18 +698,32 @@
     heads = width // HD
     reach = lax.axis_size("seq") // 2
 
-    cosine, sine, extra, marks = tables(lengths, var_bias, positions, variate, width)
+    halve = lax.axis_size("tp") == 4 and lax.axis_size("seq") == 8
+    cosine, sine, extra, marks, *weights, w_out_part = tables(
+        lengths,
+        var_bias,
+        positions,
+        variate,
+        width,
+        (tokens, gain_attn, w_query, w_key, w_value, w_out),
+        halve,
+    )
     pieces = gather_pieces(tokens, 2, extra)
-    token_rows, queries, pairs = project(
-        pieces, gain_attn, w_query, w_key, w_value, cosine, sine, extra
-    )
-    w_out, _ = lax.optimization_barrier((w_out, pairs))
+    pieces[0] = weights[0]
+    token_rows, queries, pairs = project(pieces, *weights[1:], cosine, sine, extra)
+    w_out_part, _ = lax.optimization_barrier((w_out_part, pairs))
     row_pieces = seq_pieces(pairs)
-    w_out_pieces = gather_pieces(w_out, 1)
+    w_out_pieces = [(piece,) for piece in gather_pieces(w_out_part, 1)]
+    if halve:
+        twins = [(piece, seq_xor(piece, 1)) for (piece,) in w_out_pieces[1:]]
+        w_out_pieces = w_out_pieces[:1] + twins
+    marks, w_out_pieces = lax.optimization_barrier((marks, w_out_pieces))
     attended = attend(lengths, queries, marks, row_pieces, heads, reach)
-    large = (token_rows, gain_ffn, w_gate, w_up, w_down)
+    large = (w_out, token_rows, gain_ffn, w_gate, w_up, w_down)
     large = lax.optimization_barrier((large, attended))[0]
-    large = fetch(large)
+    w_out, *large = fetch(large)
+    if halve:
+        w_out_pieces[0] = (w_out,)
     attended_pieces = gather_pieces(attended, 1, large[1])
     mixed, joined = feed_forward(attended_pieces, w_out_pieces, *large)
     row_pieces, _ = lax.optimization_barrier((row_pieces, joined))

time: 108 us -> 93.2 us (0.86); the launches traced: 106 us -> 92.7 us
  waiting for transfers between devices: 52.6 us -> 31.1 us
  starting transfers between devices: 27 us -> 32.6 us
  Pallas kernels: 16.9 us -> 18.4 us
    ppermute x16, waiting for transfers between devices: 42.6 us -> 28.1 us  [tp_xor(): lax.ppermute(value, 'tp', [(i, i ^ mask) for i in range(lax.axis_size('tp...]
    ppermute x7 -> x10, waiting for transfers between devices: 10 us -> 3.02 us  [seq_xor(): lax.ppermute(value, 'seq', [(i, i ^ mask) for i in range(lax.axis_size('s...]
    ppermute x16, starting transfers between devices: 23 us -> 27.8 us  [tp_xor(): lax.ppermute(value, 'tp', [(i, i ^ mask) for i in range(lax.axis_size('tp...]
    pallas_call x1, Pallas kernels: 3.6 us -> 4.73 us  [attend(): pl.pallas_call(functools.partial(attend_kernel, len(pieces), heads, reach...]
    unnamed x34 -> x36, local copies, waits for them, and re-layouts: 7.93 us -> 8.88 us
    ppermute x7 -> x10, starting transfers between devices: 3.99 us -> 4.78 us  [seq_xor(): lax.ppermute(value, 'seq', [(i, i ^ mask) for i in range(lax.axis_size('s...]
  transfers between devices with their start and end apart: 23 -> 26, of which waited for: 15 -> 12; matrix products, arithmetic and copies ran while one was open for 0% -> 0% of each run, Pallas kernels for 10% -> 8%
where the time goes in v8:
time: 93.2 us; the launch traced here: 92.7 us
  starting transfers between devices  32.6 us (35%)
  waiting for transfers between devices  31.1 us (33%)
  Pallas kernels  18.4 us (20%)
  local copies, waits for them, and re-layouts  9.87 us (11%)
    ppermute x16, waiting for transfers between devices, tp_xor(): lax.ppermute(value, 'tp', [(i, i ^ mask) for i in range(lax.axis_size('tp...  28.1 us
    ppermute x16, starting transfers between devices, tp_xor(): lax.ppermute(value, 'tp', [(i, i ^ mask) for i in range(lax.axis_size('tp...  27.8 us
    unnamed x36, local copies, waits for them, and re-layouts  8.88 us
    ppermute x10, starting transfers between devices, seq_xor(): lax.ppermute(value, 'seq', [(i, i ^ mask) for i in range(lax.axis_size('s...  4.78 us
    pallas_call x1, Pallas kernels, attend(): pl.pallas_call(functools.partial(attend_kernel, len(pieces), heads, reach...  4.73 us
    pallas_call x1, Pallas kernels, fill_cache(): pl.pallas_call(functools.partial(cache_kernel, len(pieces), 2 * PAGE), ou...  4.69 us
    pallas_call x1, Pallas kernels, hidden_of(): pl.pallas_call(functools.partial(hidden_kernel, counts), out_shape=[jax.S...  3.82 us
    ppermute x10, waiting for transfers between devices, seq_xor(): lax.ppermute(value, 'seq', [(i, i ^ mask) for i in range(lax.axis_size('s...  3.02 us
  transfers between devices with their start and end apart: 26, of which 12 were waited for; matrix products, arithmetic and copies ran while one was open for 0% of the time, Pallas kernels for 8%

profile of v8, /device:TPU:2, one launch (start us, length us, event | category | flops | bytes accessed | tf_op | source)
XLA Modules:
  0.0 92.7 jit_solution(14005789651158473854)
XLA Ops:
  0.6 1.0 %fusion = (bf16[256,256]{1,0:T(8,128)(2,1)S(1)}, bf16[256,256]{1,0:T(8,128)(2,1)S(1)}) fusion(bf16[512,256]{1,0:T(8,128)(2,1)} %refs_0_.1), kind=kLoop, calls=%fused_computation | loop fusion | bytes 524288 | tf_op jit(solution)/shard_map/slice | solution.py:64
  1.6 2.7 %collective-permute-start.1 = (bf16[256,256]{1,0:T(8,128)(2,1)S(1)}, bf16[256,256]{1,0:T(8,128)(2,1)S(1)}, u32[]{:S(2)}, u32[]{:S(2)}) collective-permute-start(bf16[256,256]{1,0:T(8,128)(2,1)S(1)} %get-tuple-element.58), channel_id=1, source_target_pairs={{0,2},{1,3},{2,0},{3,1},{4,6},{5,7},{6,4},{7,5},{8,10},{9,11},{10,... | collective-permute-start | bytes 393224 | tf_op jit(solution)/shard_map/ppermute | solution.py:57
  4.6 1.6 %collective-permute-start = (bf16[512,256]{1,0:T(8,128)(2,1)}, bf16[512,256]{1,0:T(8,128)(2,1)S(1)}, u32[]{:S(2)}, u32[]{:S(2)}) collective-permute-start(bf16[512,256]{1,0:T(8,128)(2,1)} %refs_0_.1), channel_id=1, source_target_pairs={{0,1},{1,0},{2,3},{3,2},{4,5},{5,4},{6,7},{7,6},{8,9},{9,8},{10,11... | collective-permute-start | bytes 786440 | tf_op jit(solution)/shard_map/ppermute | solution.py:57
  6.2 0.9 %copy-done.3 = bf16[128,1024]{1,0:T(8,128)(2,1)S(1)} copy-done((bf16[128,1024]{1,0:T(8,128)(2,1)S(1)}, bf16[128,1024]{1,0:T(8,128)(2,1)}, u32[]{:S(2)}) %copy-start.3) | copy-done | bytes 262168
  7.2 0.9 %copy-done.5 = bf16[512,256]{1,0:T(8,128)(2,1)S(1)} copy-done((bf16[512,256]{1,0:T(8,128)(2,1)S(1)}, bf16[512,256]{1,0:T(8,128)(2,1)}, u32[]{:S(2)}) %copy-start.5) | copy-done | bytes 262168
  8.1 0.9 %copy-done.6 = bf16[1024,128]{1,0:T(8,128)(2,1)S(1)} copy-done((bf16[1024,128]{1,0:T(8,128)(2,1)S(1)}, bf16[1024,128]{1,0:T(8,128)(2,1)}, u32[]{:S(2)}) %copy-start.6) | copy-done | bytes 262168
  9.1 0.9 %copy-done.7 = bf16[1024,128]{1,0:T(8,128)(2,1)S(1)} copy-done((bf16[1024,128]{1,0:T(8,128)(2,1)S(1)}, bf16[1024,128]{1,0:T(8,128)(2,1)}, u32[]{:S(2)}) %copy-start.7) | copy-done | bytes 262168
  10.0 0.9 %copy-done.8 = bf16[1024,128]{1,0:T(8,128)(2,1)S(1)} copy-done((bf16[1024,128]{1,0:T(8,128)(2,1)S(1)}, bf16[1024,128]{1,0:T(8,128)(2,1)}, u32[]{:S(2)}) %copy-start.8) | copy-done | bytes 262168
  11.0 0.7 copy-done.9
  11.7 0.7 copy-done.10
  12.4 0.7 copy-done.11
  13.0 0.7 copy-done.12
  13.7 0.7 copy-done.14
  14.4 0.7 copy-done.16
  15.1 1.3 %tables.1 = (f32[512,128]{1,0:T(8,128)S(1)}, f32[512,128]{1,0:T(8,128)S(1)}, bf16[16,256]{1,0:T(8,128)(2,1)S(1)}, bf16[2,512,128]{2,1,0:T(8,128)(2,1)S(1)}, bf16...) custom-call(s32[4]{0:T(128)S(1)} %copy-done.14, ...), custom_call_target="tpu_custom_call" | custom-call | flops 524288 | bytes 1048576 | tf_op jit(solution)/shard_map/tables/pallas_call | solution.py:180
  17.0 1.5 %collective-permute-start.3 = (bf16[256,256]{1,0:T(8,128)(2,1)S(1)}, bf16[256,256]{1,0:T(8,128)(2,1)S(1)}, u32[]{:S(2)}, u32[]{:S(2)}) collective-permute-start(bf16[256,256]{1,0:T(8,128)(2,1)S(1)} %collective-permute-done.1.refs_2_), channel_id=1, source_target_pairs={{0,1},{1,0},{2,3},{3,2},{4,5},{5,4},{6,7},{7,6},{8,9},{9,8},{10,11... | collective-permute-start | bytes 393224 | tf_op jit(solution)/shard_map/ppermute | solution.py:57
  18.4 3.8 %collective-permute-done.4.refs_5_ = bf16[256,256]{1,0:T(8,128)(2,1)S(1)} collective-permute-done((bf16[256,256]{1,0:T(8,128)(2,1)S(1)}, bf16[256,256]{1,0:T(8,128)(2,1)S(1)}, u32[]{:S(2)}, u32[]{:S(2)}) %collective-permute-start.4) | collective-permute-done | bytes 131104 | tf_op jit(solution)/shard_map/ppermute | solution.py:57
  22.2 1.4 %collective-permute-done.3.refs_4_ = bf16[256,256]{1,0:T(8,128)(2,1)S(1)} collective-permute-done((bf16[256,256]{1,0:T(8,128)(2,1)S(1)}, bf16[256,256]{1,0:T(8,128)(2,1)S(1)}, u32[]{:S(2)}, u32[]{:S(2)}) %collective-permute-start.3) | collective-permute-done | bytes 131104 | tf_op jit(solution)/shard_map/ppermute | solution.py:57
  23.6 1.4 %project.1 = (bf16[512,1024]{1,0:T(8,128)(2,1)S(1)}, bf16[512,128]{1,0:T(8,128)(2,1)S(1)}, bf16[528,256]{1,0:T(8,128)(2,1)S(1)}) custom-call(bf16[512,256]{1,0:T(8,128)(2,1)S(1)} %get-tuple-element.56.refs_0_, bf16[512,256]{1,0:T(8,128)(2,1)S(1)} %collective-permute-done.refs_1_, bf16[256,256]{1,0:T(8,128)(2,1)S(1)} %collective-permute-done.1.refs_2_, ...), custom_call_target="tpu_custom_call" | custom-call | flops 402653184 | bytes 4194304 | tf_op jit(solution)/shard_map/project/pallas_call | solution.py:247
  25.1 1.6 %collective-permute-start.16 = (bf16[528,256]{1,0:T(8,128)(2,1)S(1)}, bf16[528,256]{1,0:T(8,128)(2,1)S(1)}, u32[]{:S(2)}, u32[]{:S(2)}) collective-permute-start(bf16[528,256]{1,0:T(8,128)(2,1)S(1)} %get-tuple-element.102.refs_0_), channel_id=1, source_target_pairs={{0,24},{4,28},{8,16},{12,20},{16,8},{20,12},{24,0},{28,4},{1,25},{... | collective-permute-start | bytes 811016 | tf_op jit(solution)/shard_map/ppermute | solution.py:264
  26.6 0.6 collective-permute-start.14
  27.2 1.4 %collective-permute-start.12 = (bf16[528,256]{1,0:T(8,128)(2,1)S(1)}, bf16[528,256]{1,0:T(8,128)(2,1)S(1)}, u32[]{:S(2)}, u32[]{:S(2)}) collective-permute-start(bf16[528,256]{1,0:T(8,128)(2,1)S(1)} %get-tuple-element.102.refs_0_), channel_id=1, source_target_pairs={{0,8},{4,12},{8,0},{12,4},{16,24},{20,28},{24,16},{28,20},{1,9},{5... | collective-permute-start | bytes 811016 | tf_op jit(solution)/shard_map/ppermute | solution.py:264
  28.6 3.2 %collective-permute-start.7 = (bf16[128,512]{1,0:T(8,128)(2,1)S(1)}, bf16[128,512]{1,0:T(8,128)(2,1)S(1)}, u32[]{:S(2)}, u32[]{:S(2)}) collective-permute-start(bf16[128,512]{1,0:T(8,128)(2,1)S(1)} %get-tuple-element.72), channel_id=1, source_target_pairs={{0,2},{1,3},{2,0},{3,1},{4,6},{5,7},{6,4},{7,5},{8,10},{9,11},{10,... | collective-permute-start | bytes 393224 | tf_op jit(solution)/shard_map/ppermute | solution.py:57
  31.8 1.7 %collective-permute-start.5 = (bf16[128,512]{1,0:T(8,128)(2,1)S(1)}, bf16[128,512]{1,0:T(8,128)(2,1)S(1)}, u32[]{:S(2)}, u32[]{:S(2)}) collective-permute-start(bf16[128,512]{1,0:T(8,128)(2,1)S(1)} %get-tuple-element.72), channel_id=1, source_target_pairs={{0,1},{1,0},{2,3},{3,2},{4,5},{5,4},{6,7},{7,6},{8,9},{9,8},{10,11... | collective-permute-start | bytes 393224 | tf_op jit(solution)/shard_map/ppermute | solution.py:57
  33.6 1.7 %collective-permute-done.7.refs_7_ = bf16[128,512]{1,0:T(8,128)(2,1)S(1)} collective-permute-done((bf16[128,512]{1,0:T(8,128)(2,1)S(1)}, bf16[128,512]{1,0:T(8,128)(2,1)S(1)}, u32[]{:S(2)}, u32[]{:S(2)}) %collective-permute-start.7) | collective-permute-done | bytes 131104 | tf_op jit(solution)/shard_map/ppermute | solution.py:57
  35.3 2.0 %collective-permute-start.9 = (bf16[128,512]{1,0:T(8,128)(2,1)S(1)}, bf16[128,512]{1,0:T(8,128)(2,1)S(1)}, u32[]{:S(2)}, u32[]{:S(2)}) collective-permute-start(bf16[128,512]{1,0:T(8,128)(2,1)S(1)} %collective-permute-done.7.refs_7_), channel_id=1, source_target_pairs={{0,1},{1,0},{2,3},{3,2},{4,5},{5,4},{6,7},{7,6},{8,9},{9,8},{10,11... | collective-permute-start | bytes 393224 | tf_op jit(solution)/shard_map/ppermute | solution.py:57
  37.3 0.7 collective-permute-done.5.refs_5_
  38.0 2.3 %collective-permute-done.9.refs_9_ = bf16[128,512]{1,0:T(8,128)(2,1)S(1)} collective-permute-done((bf16[128,512]{1,0:T(8,128)(2,1)S(1)}, bf16[128,512]{1,0:T(8,128)(2,1)S(1)}, u32[]{:S(2)}, u32[]{:S(2)}) %collective-permute-start.9) | collective-permute-done | bytes 131104 | tf_op jit(solution)/shard_map/ppermute | solution.py:57
  41.4 1.8 %collective-permute-done.6.refs_6_ = bf16[128,512]{1,0:T(8,128)(2,1)S(1)} collective-permute-done((bf16[128,512]{1,0:T(8,128)(2,1)S(1)}, bf16[128,512]{1,0:T(8,128)(2,1)S(1)}, u32[]{:S(2)}, u32[]{:S(2)}) %collective-permute-start.6) | collective-permute-done | bytes 131104 | tf_op jit(solution)/shard_map/ppermute | solution.py:264
  43.3 1.2 %collective-permute-done.10.refs_10_ = bf16[128,512]{1,0:T(8,128)(2,1)S(1)} collective-permute-done((bf16[128,512]{1,0:T(8,128)(2,1)S(1)}, bf16[128,512]{1,0:T(8,128)(2,1)S(1)}, u32[]{:S(2)}, u32[]{:S(2)}) %collective-permute-start.10) | collective-permute-done | bytes 131104 | tf_op jit(solution)/shard_map/ppermute | solution.py:264
  44.6 4.7 %attend.1.refs_0_ = bf16[512,128]{1,0:T(8,128)(2,1)S(1)} custom-call(s32[4]{0:T(128)S(1)} %copy-done.15, bf16[512,128]{1,0:T(8,128)(2,1)S(1)} %get-tuple-element.68.queries, bf16[2,512,128]{2,1,0:T(8,128)(2,1)S(1)} %get-tuple-element.73.query_marks, bf16[528,256]{1,0:T(8,128)(2,1)S(1)} %get-tuple-element.102.refs_0_, ...), custom_call_target="tpu_custom_call" | custom-call | flops 2684354560 | bytes 4194304 | tf_op jit(solution)/shard_map/attend/pallas_call | solution.py:411
  49.4 3.5 %collective-permute-start.19 = (bf16[512,128]{1,0:T(8,128)(2,1)S(1)}, bf16[512,128]{1,0:T(8,128)(2,1)S(1)}, u32[]{:S(2)}, u32[]{:S(2)}) collective-permute-start(bf16[512,128]{1,0:T(8,128)(2,1)S(1)} %attend.1.refs_0_), channel_id=1, source_target_pairs={{0,2},{1,3},{2,0},{3,1},{4,6},{5,7},{6,4},{7,5},{8,10},{9,11},{10,... | collective-permute-start | bytes 393224 | tf_op jit(solution)/shard_map/ppermute | solution.py:57
  52.8 2.0 %collective-permute-start.18 = (bf16[512,128]{1,0:T(8,128)(2,1)S(1)}, bf16[512,128]{1,0:T(8,128)(2,1)S(1)}, u32[]{:S(2)}, u32[]{:S(2)}) collective-permute-start(bf16[512,128]{1,0:T(8,128)(2,1)S(1)} %attend.1.refs_0_), channel_id=1, source_target_pairs={{0,1},{1,0},{2,3},{3,2},{4,5},{5,4},{6,7},{7,6},{8,9},{9,8},{10,11... | collective-permute-start | bytes 393224 | tf_op jit(solution)/shard_map/ppermute | solution.py:57
  55.5 4.1 %collective-permute-done.19.refs_2_ = bf16[512,128]{1,0:T(8,128)(2,1)S(1)} collective-permute-done((bf16[512,128]{1,0:T(8,128)(2,1)S(1)}, bf16[512,128]{1,0:T(8,128)(2,1)S(1)}, u32[]{:S(2)}, u32[]{:S(2)}) %collective-permute-start.19) | collective-permute-done | bytes 131104 | tf_op jit(solution)/shard_map/ppermute | solution.py:57
  59.6 1.4 %collective-permute-start.20 = (bf16[512,128]{1,0:T(8,128)(2,1)S(1)}, bf16[512,128]{1,0:T(8,128)(2,1)S(1)}, u32[]{:S(2)}, u32[]{:S(2)}) collective-permute-start(bf16[512,128]{1,0:T(8,128)(2,1)S(1)} %collective-permute-done.19.refs_2_), channel_id=1, source_target_pairs={{0,1},{1,0},{2,3},{3,2},{4,5},{5,4},{6,7},{7,6},{8,9},{9,8},{10,11... | collective-permute-start | bytes 393224 | tf_op jit(solution)/shard_map/ppermute | solution.py:57
  61.0 4.4 %collective-permute-done.20.refs_3_ = bf16[512,128]{1,0:T(8,128)(2,1)S(1)} collective-permute-done((bf16[512,128]{1,0:T(8,128)(2,1)S(1)}, bf16[512,128]{1,0:T(8,128)(2,1)S(1)}, u32[]{:S(2)}, u32[]{:S(2)}) %collective-permute-start.20) | collective-permute-done | bytes 131104 | tf_op jit(solution)/shard_map/ppermute | solution.py:57
  65.3 3.8 %hidden.1 = (bf16[512,1024]{1,0:T(8,128)(2,1)S(1)}, bf16[512,256]{1,0:T(8,128)(2,1)S(1)}, bf16[256,256]{1,0:T(8,128)(2,1)S(1)}, bf16[256,256]{1,0:T(8,128)(2,1)S(1)}) custom-call(bf16[512,128]{1,0:T(8,128)(2,1)S(1)} %attend.1.refs_0_, bf16[512,128]{1,0:T(8,128)(2,1)S(1)} %collective-permute-done.18.refs_1_, ...), custom_call_target="tpu_custom_call" | custom-call | flops 3221225472 | bytes 10485760 | tf_op jit(solution)/shard_map/hidden/pallas_call | solution.py:591
  69.2 1.3 %collective-permute-start.22 = (bf16[256,256]{1,0:T(8,128)(2,1)S(1)}, bf16[256,256]{1,0:T(8,128)(2,1)S(1)}, u32[]{:S(2)}, u32[]{:S(2)}) collective-permute-start(bf16[256,256]{1,0:T(8,128)(2,1)S(1)} %get-tuple-element.99), channel_id=1, source_target_pairs={{0,1},{1,0},{2,3},{3,2},{4,5},{5,4},{6,7},{7,6},{8,9},{9,8},{10,11... | collective-permute-start | bytes 393224 | tf_op jit(solution)/shard_map/ppermute | solution.py:57
  70.4 0.8 collective-permute-start.24
  71.3 1.0 %down_blocks.1 = (f32[256,256]{1,0:T(8,128)S(1)}, f32[256,256]{1,0:T(8,128)S(1)}, bf16[512,256]{1,0:T(8,128)(2,1)S(1)}, f32[512,256]{1,0:T(8,128)S(1)}) custom-call(bf16[512,1024]{1,0:T(8,128)(2,1)S(1)} %get-tuple-element.94.hidden, bf16[512,256]{1,0:T(8,128)(2,1)S(1)} %get-tuple-element.95.kept, bf16[1024,1024]{1,0:T(8,128)(2,1)S(1)} %get-tuple-element.93.refs_15_.w_down), custom_call_target="tpu_custom_call" | custom-call | flops 805306368 | bytes 5242880 | tf_op jit(solution)/shard_map/down_blocks/pallas_call | solution.py:625
  72.3 1.3 %collective-permute-start.21 = (bf16[512,256]{1,0:T(8,128)(2,1)S(1)}, bf16[512,256]{1,0:T(8,128)(2,1)S(1)}, u32[]{:S(2)}, u32[]{:S(2)}) collective-permute-start(bf16[512,256]{1,0:T(8,128)(2,1)S(1)} %get-tuple-element.97), channel_id=1, source_target_pairs={{0,1},{1,0},{2,3},{3,2},{4,5},{5,4},{6,7},{7,6},{8,9},{9,8},{10,11... | collective-permute-start | bytes 786440 | tf_op jit(solution)/shard_map/ppermute | solution.py:57
  73.5 2.1 %collective-permute-done.22.refs_1_ = bf16[256,256]{1,0:T(8,128)(2,1)S(1)} collective-permute-done((bf16[256,256]{1,0:T(8,128)(2,1)S(1)}, bf16[256,256]{1,0:T(8,128)(2,1)S(1)}, u32[]{:S(2)}, u32[]{:S(2)}) %collective-permute-start.22) | collective-permute-done | bytes 131104 | tf_op jit(solution)/shard_map/ppermute | solution.py:57
  75.7 2.9 %collective-permute-start.23 = (bf16[256,256]{1,0:T(8,128)(2,1)S(1)}, bf16[256,256]{1,0:T(8,128)(2,1)S(1)}, u32[]{:S(2)}, u32[]{:S(2)}) collective-permute-start(bf16[256,256]{1,0:T(8,128)(2,1)S(1)} %add_up.3), channel_id=1, source_target_pairs={{0,2},{1,3},{2,0},{3,1},{4,6},{5,7},{6,4},{7,5},{8,10},{9,11},{10,... | collective-permute-start | bytes 393224 | tf_op jit(solution)/shard_map/ppermute | solution.py:57
  78.5 4.1 %collective-permute-done.24.refs_1_ = bf16[256,256]{1,0:T(8,128)(2,1)S(1)} collective-permute-done((bf16[256,256]{1,0:T(8,128)(2,1)S(1)}, bf16[256,256]{1,0:T(8,128)(2,1)S(1)}, u32[]{:S(2)}, u32[]{:S(2)}) %collective-permute-start.24) | collective-permute-done | bytes 131104 | tf_op jit(solution)/shard_map/ppermute | solution.py:57
  82.7 1.0 %collective-permute-start.25 = (bf16[256,256]{1,0:T(8,128)(2,1)S(1)}, bf16[256,256]{1,0:T(8,128)(2,1)S(1)}, u32[]{:S(2)}, u32[]{:S(2)}) collective-permute-start(bf16[256,256]{1,0:T(8,128)(2,1)S(1)} %add_up.4), channel_id=1, source_target_pairs={{0,2},{1,3},{2,0},{3,1},{4,6},{5,7},{6,4},{7,5},{8,10},{9,11},{10,... | collective-permute-start | bytes 393224 | tf_op jit(solution)/shard_map/ppermute | solution.py:57
  83.7 4.7 %fill_cache.1 = bf16[576,2,128]{2,1,0:T(2,128)(2,1)} custom-call(s32[4]{0:T(128)S(1)} %copy-done.15, s32[72]{0:T(128)S(1)} %copy-done.17, bf16[528,256]{1,0:T(8,128)(2,1)S(1)} %get-tuple-element.102.refs_0_, bf16[528,256]{1,0:T(8,128)(2,1)S(1)} %collective-permute-done.11.refs_1_, bf16[528,256]{1,0:T(8,128)(2,1)S(1)} %collective-permute-done.12.refs_2_, ...), custom_call_target="tpu_custom_call" | custom-call | flops 75497472 | bytes 3145728 | tf_op jit(solution)/shard_map/fill_cache/pallas_call | solution.py:507
  88.4 3.5 %collective-permute-done.25.refs_3_ = bf16[256,256]{1,0:T(8,128)(2,1)S(1)} collective-permute-done((bf16[256,256]{1,0:T(8,128)(2,1)S(1)}, bf16[256,256]{1,0:T(8,128)(2,1)S(1)}, u32[]{:S(2)}, u32[]{:S(2)}) %collective-permute-start.25) | collective-permute-done | bytes 131104 | tf_op jit(solution)/shard_map/ppermute | solution.py:57
  91.9 0.8 add_up.5
  (51 shorter events, 2.9 us)
Async XLA Ops:
  0.6 43.9 %copy-start.15 = (s32[4]{0:T(128)S(1)}, s32[4]{0:T(128)}, u32[]{:S(2)}) copy-start(s32[4]{0:T(128)} %lengths.5) | copy-start | bytes 52
  1.6 14.7 %collective-permute-start.1 = (bf16[256,256]{1,0:T(8,128)(2,1)S(1)}, bf16[256,256]{1,0:T(8,128)(2,1)S(1)}, u32[]{:S(2)}, u32[]{:S(2)}) collective-permute-start(bf16[256,256]{1,0:T(8,128)(2,1)S(1)} %get-tuple-element.58), channel_id=1, source_target_pairs={{0,2},{1,3},{2,0},{3,1},{4,6},{5,7},{6,4},{7,5},{8,10},{9,11},{10,... | collective-permute-start | bytes 393224 | tf_op jit(solution)/shard_map/ppermute | solution.py:57
  4.3 12.1 %collective-permute-start.2 = (bf16[256,256]{1,0:T(8,128)(2,1)S(1)}, bf16[256,256]{1,0:T(8,128)(2,1)S(1)}, u32[]{:S(2)}, u32[]{:S(2)}) collective-permute-start(bf16[256,256]{1,0:T(8,128)(2,1)S(1)} %get-tuple-element.61), channel_id=1, source_target_pairs={{0,2},{1,3},{2,0},{3,1},{4,6},{5,7},{6,4},{7,5},{8,10},{9,11},{10,... | collective-permute-start | bytes 393224 | tf_op jit(solution)/shard_map/ppermute | solution.py:57
  4.6 17.6 %collective-permute-start = (bf16[512,256]{1,0:T(8,128)(2,1)}, bf16[512,256]{1,0:T(8,128)(2,1)S(1)}, u32[]{:S(2)}, u32[]{:S(2)}) collective-permute-start(bf16[512,256]{1,0:T(8,128)(2,1)} %refs_0_.1), channel_id=1, source_target_pairs={{0,1},{1,0},{2,3},{3,2},{4,5},{5,4},{6,7},{7,6},{8,9},{9,8},{10,11... | collective-permute-start | bytes 786440 | tf_op jit(solution)/shard_map/ppermute | solution.py:57
  6.2 0.9 %copy-start.3 = (bf16[128,1024]{1,0:T(8,128)(2,1)S(1)}, bf16[128,1024]{1,0:T(8,128)(2,1)}, u32[]{:S(2)}) copy-start(bf16[128,1024]{1,0:T(8,128)(2,1)} %refs_0_.2) | copy-start | bytes 786436
  7.2 0.9 %copy-start.5 = (bf16[512,256]{1,0:T(8,128)(2,1)S(1)}, bf16[512,256]{1,0:T(8,128)(2,1)}, u32[]{:S(2)}) copy-start(bf16[512,256]{1,0:T(8,128)(2,1)} %refs_0_.1) | copy-start | bytes 786436
  8.1 0.9 %copy-start.6 = (bf16[1024,128]{1,0:T(8,128)(2,1)S(1)}, bf16[1024,128]{1,0:T(8,128)(2,1)}, u32[]{:S(2)}) copy-start(bf16[1024,128]{1,0:T(8,128)(2,1)} %refs_2_.1) | copy-start | bytes 786436
  9.1 0.9 %copy-start.7 = (bf16[1024,128]{1,0:T(8,128)(2,1)S(1)}, bf16[1024,128]{1,0:T(8,128)(2,1)}, u32[]{:S(2)}) copy-start(bf16[1024,128]{1,0:T(8,128)(2,1)} %refs_3_.1) | copy-start | bytes 786436
  10.0 0.9 %copy-start.8 = (bf16[1024,128]{1,0:T(8,128)(2,1)S(1)}, bf16[1024,128]{1,0:T(8,128)(2,1)}, u32[]{:S(2)}) copy-start(bf16[1024,128]{1,0:T(8,128)(2,1)} %refs_4_.1) | copy-start | bytes 786436
  11.0 0.7 copy-start.9
  11.7 0.7 copy-start.10
  12.4 0.7 copy-start.11
  13.0 0.7 copy-start.12
  13.7 0.7 copy-start.14
  14.4 0.7 copy-start.16
  16.4 5.9 %collective-permute-start.4 = (bf16[256,256]{1,0:T(8,128)(2,1)S(1)}, bf16[256,256]{1,0:T(8,128)(2,1)S(1)}, u32[]{:S(2)}, u32[]{:S(2)}) collective-permute-start(bf16[256,256]{1,0:T(8,128)(2,1)S(1)} %collective-permute-done.2.refs_3_), channel_id=1, source_target_pairs={{0,1},{1,0},{2,3},{3,2},{4,5},{5,4},{6,7},{7,6},{8,9},{9,8},{10,11... | collective-permute-start | bytes 393224 | tf_op jit(solution)/shard_map/ppermute | solution.py:57
  17.0 6.7 %collective-permute-start.3 = (bf16[256,256]{1,0:T(8,128)(2,1)S(1)}, bf16[256,256]{1,0:T(8,128)(2,1)S(1)}, u32[]{:S(2)}, u32[]{:S(2)}) collective-permute-start(bf16[256,256]{1,0:T(8,128)(2,1)S(1)} %collective-permute-done.1.refs_2_), channel_id=1, source_target_pairs={{0,1},{1,0},{2,3},{3,2},{4,5},{5,4},{6,7},{7,6},{8,9},{9,8},{10,11... | collective-permute-start | bytes 393224 | tf_op jit(solution)/shard_map/ppermute | solution.py:57
  25.1 15.2 %collective-permute-start.16 = (bf16[528,256]{1,0:T(8,128)(2,1)S(1)}, bf16[528,256]{1,0:T(8,128)(2,1)S(1)}, u32[]{:S(2)}, u32[]{:S(2)}) collective-permute-start(bf16[528,256]{1,0:T(8,128)(2,1)S(1)} %get-tuple-element.102.refs_0_), channel_id=1, source_target_pairs={{0,24},{4,28},{8,16},{12,20},{16,8},{20,12},{24,0},{28,4},{1,25},{... | collective-permute-start | bytes 811016 | tf_op jit(solution)/shard_map/ppermute | solution.py:264
  26.6 14.2 %collective-permute-start.14 = (bf16[528,256]{1,0:T(8,128)(2,1)S(1)}, bf16[528,256]{1,0:T(8,128)(2,1)S(1)}, u32[]{:S(2)}, u32[]{:S(2)}) collective-permute-start(bf16[528,256]{1,0:T(8,128)(2,1)S(1)} %get-tuple-element.102.refs_0_), channel_id=1, source_target_pairs={{0,16},{4,20},{8,24},{12,28},{16,0},{20,4},{24,8},{28,12},{1,17},{... | collective-permute-start | bytes 811016 | tf_op jit(solution)/shard_map/ppermute | solution.py:264
  27.2 13.6 %collective-permute-start.12 = (bf16[528,256]{1,0:T(8,128)(2,1)S(1)}, bf16[528,256]{1,0:T(8,128)(2,1)S(1)}, u32[]{:S(2)}, u32[]{:S(2)}) collective-permute-start(bf16[528,256]{1,0:T(8,128)(2,1)S(1)} %get-tuple-element.102.refs_0_), channel_id=1, source_target_pairs={{0,8},{4,12},{8,0},{12,4},{16,24},{20,28},{24,16},{28,20},{1,9},{5... | collective-permute-start | bytes 811016 | tf_op jit(solution)/shard_map/ppermute | solution.py:264
  28.6 6.7 %collective-permute-start.7 = (bf16[128,512]{1,0:T(8,128)(2,1)S(1)}, bf16[128,512]{1,0:T(8,128)(2,1)S(1)}, u32[]{:S(2)}, u32[]{:S(2)}) collective-permute-start(bf16[128,512]{1,0:T(8,128)(2,1)S(1)} %get-tuple-element.72), channel_id=1, source_target_pairs={{0,2},{1,3},{2,0},{3,1},{4,6},{5,7},{6,4},{7,5},{8,10},{9,11},{10,... | collective-permute-start | bytes 393224 | tf_op jit(solution)/shard_map/ppermute | solution.py:57
  31.8 6.2 %collective-permute-start.5 = (bf16[128,512]{1,0:T(8,128)(2,1)S(1)}, bf16[128,512]{1,0:T(8,128)(2,1)S(1)}, u32[]{:S(2)}, u32[]{:S(2)}) collective-permute-start(bf16[128,512]{1,0:T(8,128)(2,1)S(1)} %get-tuple-element.72), channel_id=1, source_target_pairs={{0,1},{1,0},{2,3},{3,2},{4,5},{5,4},{6,7},{7,6},{8,9},{9,8},{10,11... | collective-permute-start | bytes 393224 | tf_op jit(solution)/shard_map/ppermute | solution.py:57
  35.3 5.0 %collective-permute-start.9 = (bf16[128,512]{1,0:T(8,128)(2,1)S(1)}, bf16[128,512]{1,0:T(8,128)(2,1)S(1)}, u32[]{:S(2)}, u32[]{:S(2)}) collective-permute-start(bf16[128,512]{1,0:T(8,128)(2,1)S(1)} %collective-permute-done.7.refs_7_), channel_id=1, source_target_pairs={{0,1},{1,0},{2,3},{3,2},{4,5},{5,4},{6,7},{7,6},{8,9},{9,8},{10,11... | collective-permute-start | bytes 393224 | tf_op jit(solution)/shard_map/ppermute | solution.py:57
  38.0 3.3 %collective-permute-start.8 = (bf16[128,512]{1,0:T(8,128)(2,1)S(1)}, bf16[128,512]{1,0:T(8,128)(2,1)S(1)}, u32[]{:S(2)}, u32[]{:S(2)}) collective-permute-start(bf16[128,512]{1,0:T(8,128)(2,1)S(1)} %collective-permute-done.7.refs_7_), channel_id=1, source_target_pairs={{0,4},{4,0},{8,12},{12,8},{16,20},{20,16},{24,28},{28,24},{1,5},{5... | collective-permute-start | bytes 393224 | tf_op jit(solution)/shard_map/ppermute | solution.py:264
  40.3 4.2 %collective-permute-start.11 = (bf16[528,256]{1,0:T(8,128)(2,1)S(1)}, bf16[528,256]{1,0:T(8,128)(2,1)S(1)}, u32[]{:S(2)}, u32[]{:S(2)}) collective-permute-start(bf16[528,256]{1,0:T(8,128)(2,1)S(1)} %get-tuple-element.102.refs_0_), channel_id=1, source_target_pairs={{0,4},{4,0},{8,12},{12,8},{16,20},{20,16},{24,28},{28,24},{1,5},{5... | collective-permute-start | bytes 811016 | tf_op jit(solution)/shard_map/ppermute | solution.py:264
  40.3 4.2 %collective-permute-start.17 = (bf16[528,256]{1,0:T(8,128)(2,1)S(1)}, bf16[528,256]{1,0:T(8,128)(2,1)S(1)}, u32[]{:S(2)}, u32[]{:S(2)}) collective-permute-start(bf16[528,256]{1,0:T(8,128)(2,1)S(1)} %collective-permute-done.16.refs_6_), channel_id=1, source_target_pairs={{0,4},{4,0},{8,12},{12,8},{16,20},{20,16},{24,28},{28,24},{1,5},{5... | collective-permute-start | bytes 811016 | tf_op jit(solution)/shard_map/ppermute | solution.py:264
  40.8 3.7 %collective-permute-start.15 = (bf16[528,256]{1,0:T(8,128)(2,1)S(1)}, bf16[528,256]{1,0:T(8,128)(2,1)S(1)}, u32[]{:S(2)}, u32[]{:S(2)}) collective-permute-start(bf16[528,256]{1,0:T(8,128)(2,1)S(1)} %collective-permute-done.14.refs_4_), channel_id=1, source_target_pairs={{0,4},{4,0},{8,12},{12,8},{16,20},{20,16},{24,28},{28,24},{1,5},{5... | collective-permute-start | bytes 811016 | tf_op jit(solution)/shard_map/ppermute | solution.py:264
  40.9 3.7 %collective-permute-start.13 = (bf16[528,256]{1,0:T(8,128)(2,1)S(1)}, bf16[528,256]{1,0:T(8,128)(2,1)S(1)}, u32[]{:S(2)}, u32[]{:S(2)}) collective-permute-start(bf16[528,256]{1,0:T(8,128)(2,1)S(1)} %collective-permute-done.12.refs_2_), channel_id=1, source_target_pairs={{0,4},{4,0},{8,12},{12,8},{16,20},{20,16},{24,28},{28,24},{1,5},{5... | collective-permute-start | bytes 811016 | tf_op jit(solution)/shard_map/ppermute | solution.py:264
  41.3 1.9 %collective-permute-start.6 = (bf16[128,512]{1,0:T(8,128)(2,1)S(1)}, bf16[128,512]{1,0:T(8,128)(2,1)S(1)}, u32[]{:S(2)}, u32[]{:S(2)}) collective-permute-start(bf16[128,512]{1,0:T(8,128)(2,1)S(1)} %collective-permute-done.5.refs_5_), channel_id=1, source_target_pairs={{0,4},{4,0},{8,12},{12,8},{16,20},{20,16},{24,28},{28,24},{1,5},{5... | collective-permute-start | bytes 393224 | tf_op jit(solution)/shard_map/ppermute | solution.py:264
  43.2 1.3 %collective-permute-start.10 = (bf16[128,512]{1,0:T(8,128)(2,1)S(1)}, bf16[128,512]{1,0:T(8,128)(2,1)S(1)}, u32[]{:S(2)}, u32[]{:S(2)}) collective-permute-start(bf16[128,512]{1,0:T(8,128)(2,1)S(1)} %collective-permute-done.9.refs_9_), channel_id=1, source_target_pairs={{0,4},{4,0},{8,12},{12,8},{16,20},{20,16},{24,28},{28,24},{1,5},{5... | collective-permute-start | bytes 393224 | tf_op jit(solution)/shard_map/ppermute | solution.py:264
  44.6 10.3 %copy-start = (bf16[1024,1024]{1,0:T(8,128)(2,1)S(1)}, bf16[1024,1024]{1,0:T(8,128)(2,1)}, u32[]{:S(2)}) copy-start(bf16[1024,1024]{1,0:T(8,128)(2,1)} %refs_3_.2) | copy-start | bytes 6291460
  44.6 10.3 %copy-start.1 = (bf16[1024,1024]{1,0:T(8,128)(2,1)S(1)}, bf16[1024,1024]{1,0:T(8,128)(2,1)}, u32[]{:S(2)}) copy-start(bf16[1024,1024]{1,0:T(8,128)(2,1)} %refs_4_.2) | copy-start | bytes 6291460
  44.6 10.3 %copy-start.2 = (bf16[1024,1024]{1,0:T(8,128)(2,1)S(1)}, bf16[1024,1024]{1,0:T(8,128)(2,1)}, u32[]{:S(2)}) copy-start(bf16[1024,1024]{1,0:T(8,128)(2,1)} %refs_5_.2) | copy-start | bytes 6291460
  44.6 10.3 %copy-start.4 = (bf16[128,1024]{1,0:T(8,128)(2,1)S(1)}, bf16[128,1024]{1,0:T(8,128)(2,1)}, u32[]{:S(2)}) copy-start(bf16[128,1024]{1,0:T(8,128)(2,1)} %refs_0_.2) | copy-start | bytes 786436
  44.6 10.3 %copy-start.13 = (bf16[1024]{0:T(1024)(128)(2,1)S(1)}, bf16[1024]{0:T(1024)(128)(2,1)}, u32[]{:S(2)}) copy-start(bf16[1024]{0:T(1024)(128)(2,1)} %refs_2_.2) | copy-start | bytes 6148
  49.4 10.2 %collective-permute-start.19 = (bf16[512,128]{1,0:T(8,128)(2,1)S(1)}, bf16[512,128]{1,0:T(8,128)(2,1)S(1)}, u32[]{:S(2)}, u32[]{:S(2)}) collective-permute-start(bf16[512,128]{1,0:T(8,128)(2,1)S(1)} %attend.1.refs_0_), channel_id=1, source_target_pairs={{0,2},{1,3},{2,0},{3,1},{4,6},{5,7},{6,4},{7,5},{8,10},{9,11},{10,... | collective-permute-start | bytes 393224 | tf_op jit(solution)/shard_map/ppermute | solution.py:57
  52.8 8.1 %collective-permute-start.18 = (bf16[512,128]{1,0:T(8,128)(2,1)S(1)}, bf16[512,128]{1,0:T(8,128)(2,1)S(1)}, u32[]{:S(2)}, u32[]{:S(2)}) collective-permute-start(bf16[512,128]{1,0:T(8,128)(2,1)S(1)} %attend.1.refs_0_), channel_id=1, source_target_pairs={{0,1},{1,0},{2,3},{3,2},{4,5},{5,4},{6,7},{7,6},{8,9},{9,8},{10,11... | collective-permute-start | bytes 393224 | tf_op jit(solution)/shard_map/ppermute | solution.py:57
  59.6 5.8 %collective-permute-start.20 = (bf16[512,128]{1,0:T(8,128)(2,1)S(1)}, bf16[512,128]{1,0:T(8,128)(2,1)S(1)}, u32[]{:S(2)}, u32[]{:S(2)}) collective-permute-start(bf16[512,128]{1,0:T(8,128)(2,1)S(1)} %collective-permute-done.19.refs_2_), channel_id=1, source_target_pairs={{0,1},{1,0},{2,3},{3,2},{4,5},{5,4},{6,7},{7,6},{8,9},{9,8},{10,11... | collective-permute-start | bytes 393224 | tf_op jit(solution)/shard_map/ppermute | solution.py:57
  69.2 6.5 %collective-permute-start.22 = (bf16[256,256]{1,0:T(8,128)(2,1)S(1)}, bf16[256,256]{1,0:T(8,128)(2,1)S(1)}, u32[]{:S(2)}, u32[]{:S(2)}) collective-permute-start(bf16[256,256]{1,0:T(8,128)(2,1)S(1)} %get-tuple-element.99), channel_id=1, source_target_pairs={{0,1},{1,0},{2,3},{3,2},{4,5},{5,4},{6,7},{7,6},{8,9},{9,8},{10,11... | collective-permute-start | bytes 393224 | tf_op jit(solution)/shard_map/ppermute | solution.py:57
  70.4 12.2 %collective-permute-start.24 = (bf16[256,256]{1,0:T(8,128)(2,1)S(1)}, bf16[256,256]{1,0:T(8,128)(2,1)S(1)}, u32[]{:S(2)}, u32[]{:S(2)}) collective-permute-start(bf16[256,256]{1,0:T(8,128)(2,1)S(1)} %get-tuple-element.101), channel_id=1, source_target_pairs={{0,1},{1,0},{2,3},{3,2},{4,5},{5,4},{6,7},{7,6},{8,9},{9,8},{10,11... | collective-permute-start | bytes 393224 | tf_op jit(solution)/shard_map/ppermute | solution.py:57
  71.3 12.5 %copy-start.17 = (s32[72]{0:T(128)S(1)}, s32[72]{0:T(128)}, u32[]{:S(2)}) copy-start(s32[72]{0:T(128)} %page_table.1) | copy-start | bytes 868
  72.3 19.6 %collective-permute-start.21 = (bf16[512,256]{1,0:T(8,128)(2,1)S(1)}, bf16[512,256]{1,0:T(8,128)(2,1)S(1)}, u32[]{:S(2)}, u32[]{:S(2)}) collective-permute-start(bf16[512,256]{1,0:T(8,128)(2,1)S(1)} %get-tuple-element.97), channel_id=1, source_target_pairs={{0,1},{1,0},{2,3},{3,2},{4,5},{5,4},{6,7},{7,6},{8,9},{9,8},{10,11... | collective-permute-start | bytes 786440 | tf_op jit(solution)/shard_map/ppermute | solution.py:57
  75.7 12.7 %collective-permute-start.23 = (bf16[256,256]{1,0:T(8,128)(2,1)S(1)}, bf16[256,256]{1,0:T(8,128)(2,1)S(1)}, u32[]{:S(2)}, u32[]{:S(2)}) collective-permute-start(bf16[256,256]{1,0:T(8,128)(2,1)S(1)} %add_up.3), channel_id=1, source_target_pairs={{0,2},{1,3},{2,0},{3,1},{4,6},{5,7},{6,4},{7,5},{8,10},{9,11},{10,... | collective-permute-start | bytes 393224 | tf_op jit(solution)/shard_map/ppermute | solution.py:57
  82.7 9.2 %collective-permute-start.25 = (bf16[256,256]{1,0:T(8,128)(2,1)S(1)}, bf16[256,256]{1,0:T(8,128)(2,1)S(1)}, u32[]{:S(2)}, u32[]{:S(2)}) collective-permute-start(bf16[256,256]{1,0:T(8,128)(2,1)S(1)} %add_up.4), channel_id=1, source_target_pairs={{0,2},{1,3},{2,0},{3,1},{4,6},{5,7},{6,4},{7,5},{8,10},{9,11},{10,... | collective-permute-start | bytes 393224 | tf_op jit(solution)/shard_map/ppermute | solution.py:57

commit v9 on v8

--- a/solution.py
+++ b/solution.py
@@ -1,8 +1,8 @@
 import functools
+import math
 
 import jax
 import jax.numpy as jnp
-import numpy as np
 from jax import lax
 from jax.experimental import pallas as pl
 from jax.experimental.pallas import tpu as pltpu
@@ -57,49 +57,36 @@
     return lax.ppermute(value, "tp", [(i, i ^ mask) for i in range(lax.axis_size("tp"))])
 
 
-def pair_gather(shard, parts, first=None):
-    step = shard.shape[0] // parts
-    split = [shard]
-    if parts > 1:
-        split = [shard[i * step : (i + 1) * step] for i in range(parts)]
-        split, shard = lax.optimization_barrier((split, shard))
+def pair_gather(shard, split, before=()):
     far = [tp_xor(part, 2) for part in split]
     near = tp_xor(shard, 1)
-    if first is not None:
-        far[0], _ = lax.optimization_barrier((far[0], first))
-    return [shard, near] + far + [tp_xor(part, 1) for part in far]
+    for i, value in enumerate(before):
+        far[i], _ = lax.optimization_barrier((far[i], value))
+    return [[shard], [near], far, [tp_xor(part, 1) for part in far]]
 
 
 def turn_gather(shard):
     count = lax.axis_size("tp")
     pairs = [[(i, (i + turn) % count) for i in range(count)] for turn in range(1, count)]
-    return [shard] + [lax.ppermute(shard, "tp", each) for each in pairs]
-
-
-def gather_pieces(shard, parts, first=None):
+    return [[shard]] + [[lax.ppermute(shard, "tp", each)] for each in pairs]
+
+
+def gather_pieces(shard, split, before=()):
     if lax.axis_size("tp") == 4:
-        return pair_gather(shard, parts, first)
+        return pair_gather(shard, split, before)
     return turn_gather(shard)
 
 
-def assemble(pieces, place, count, target):
-    width = pieces[0].shape[1]
-
-    def put(block, value, first=0):
-        columns = pl.ds(pl.multiple_of(block * width, width), width)
-        target[pl.ds(first, value.shape[0]), columns] = value
-
-    if count != 4:
-        for turn, piece in enumerate(pieces):
-            put(lax.rem(place + count - turn, count), piece[...])
-        return
-    put(place, pieces[0][...])
-    put(place ^ 1, pieces[1][...])
-    parts = (len(pieces) - 2) // 2
-    for i in range(parts):
-        first = i * (target.shape[0] // parts)
-        put(place ^ 2, pieces[2 + i][...], first)
-        put(place ^ 3, pieces[2 + parts + i][...], first)
+def piece_place(i, place, count):
+    return place ^ i if count == 4 else lax.rem(place + count - i, count)
+
+
+def nested(counts, refs):
+    groups, at = [], 0
+    for count in counts:
+        groups.append(refs[at : at + count])
+        at += count
+    return groups, refs[at:]
 
 
 def request_bounds(lengths):
@@ -122,17 +109,19 @@
     return round_up(BIAS_PARTS * VARS + requests, 16)
 
 
-def tables_kernel(count, lengths, bias, frequency, positions, variate, *refs):
+def tables_kernel(count, lengths, bias, positions, variate, *refs):
     cosine, sine, extra, marks = refs[count : count + 4]
     sources, targets, sems = list(refs[:count]), refs[count + 4 : -1], refs[-1]
     if targets[-1].shape != sources[-1].shape:
-        half = targets[-1].shape[1]
-        columns = pl.ds(pl.multiple_of(lax.rem(lax.axis_index("seq"), 2) * half, half), half)
+        part = targets[-1].shape[1]
+        columns = pl.ds(pl.multiple_of(lax.rem(lax.axis_index("seq"), 2) * part, part), part)
         sources[-1] = sources[-1].at[:, columns]
     loads = start_loads(sources, targets, sems)
     rows = positions.shape[1]
     width = cosine.shape[1]
-    angles = frequency[...] * positions[...].astype(jnp.float32)
+    half = HD // 2
+    step = lax.broadcasted_iota(jnp.int32, (half, rows), 0).astype(jnp.float32) / half
+    angles = jnp.exp(-math.log(10000.0) * step) * positions[...].astype(jnp.float32)
     cos_rows, sin_rows = jnp.cos(angles), jnp.sin(angles)
     copies = width // HD
     cosine[...] = jnp.transpose(jnp.concatenate([cos_rows, cos_rows] * copies, axis=0))
@@ -170,9 +159,7 @@
 
 def tables(lengths, bias, positions, variate, width, arrays, halve):
     rows = positions.shape[0]
-    half = HD // 2
     heads = width // HD
-    frequency = 10000.0 ** (-np.arange(half, dtype=np.float32) / np.float32(half))
     extra = round_up(rows // (2 * width), 16)
     kept = [array.shape for array in arrays]
     if halve:
@@ -186,7 +173,7 @@
             jax.ShapeDtypeStruct((heads, rows, LANES), jnp.bfloat16),
         ]
         + [jax.ShapeDtypeStruct(shape, array.dtype) for shape, array in zip(kept, arrays)],
-        in_specs=[SMEM, SMEM, VMEM, VMEM, VMEM] + [ANY] * len(arrays),
+        in_specs=[SMEM, SMEM, VMEM, VMEM] + [ANY] * len(arrays),
         out_specs=[VMEM] * (4 + len(arrays)),
         scratch_shapes=[pltpu.SemaphoreType.DMA((len(arrays),))],
         compiler_params=params(6),
@@ -195,7 +182,6 @@
     )(
         lengths,
         bias,
-        jnp.asarray(frequency.astype(np.float32).reshape(half, 1)),
         positions.reshape(1, rows),
         variate.reshape(1, rows),
         *arrays,
@@ -216,12 +202,18 @@
     return (values * scale * gain).astype(jnp.bfloat16)
 
 
-def project_kernel(places, count, *refs):
-    pieces = refs[:count]
-    gain, w_q, w_k, w_v, cosine, sine, extra, tokens_out, queries, pairs = refs[count:-2]
-    tokens, sem = refs[-2:]
+def project_kernel(counts, *refs):
+    pieces, refs = nested(counts, refs)
+    gain, w_q, w_k, w_v, cosine, sine, extra, tokens_out, queries, pairs, tokens, sem = refs
     pairs[tokens.shape[0] :, :] = extra[...]
-    assemble(pieces, lax.axis_index("tp"), places, tokens)
+    place = lax.axis_index("tp")
+    part_width = pieces[0][0].shape[1]
+    for i, piece in enumerate(pieces):
+        block = piece_place(i, place, len(counts))
+        columns = pl.ds(pl.multiple_of(block * part_width, part_width), part_width)
+        step = tokens.shape[0] // len(piece)
+        for j, part in enumerate(piece):
+            tokens[j * step : (j + 1) * step, columns] = part[...]
     keep = pltpu.make_async_copy(tokens, tokens_out, sem)
     keep.start()
     rows = tokens.shape[0]
@@ -241,11 +233,13 @@
 
 
 def project(pieces, gain, w_query, w_key, w_value, cosine, sine, extra):
-    rows, part = pieces[0].shape
+    rows = pieces[0][0].shape[0]
+    counts = [len(piece) for piece in pieces]
+    pieces = [part for piece in pieces for part in piece]
     width = w_query.shape[1]
     features = w_query.shape[0]
     return pl.pallas_call(
-        functools.partial(project_kernel, lax.axis_size("tp"), len(pieces)),
+        functools.partial(project_kernel, counts),
         out_shape=[
             jax.ShapeDtypeStruct((rows, features), jnp.bfloat16),
             jax.ShapeDtypeStruct((rows, width), jnp.bfloat16),
@@ -288,7 +282,8 @@
 
 def attend_kernel(count, heads, reach, lengths, queries, query_marks, *refs):
     pieces = refs[:count]
-    out, q_buf, k_buf, v_buf, extra_buf, scores, peak, total, sems = refs[count:]
+    outs, scratch = refs[count:-8], refs[-8:]
+    q_buf, k_buf, v_buf, extra_buf, scores, peak, total, sems = scratch
     me = lax.axis_index("seq")
     rows = queries.shape[0]
     _, ends = request_bounds(lengths)
@@ -402,7 +397,11 @@
     result = total[0, :, :width] / total[0, :, width:]
     for h in range(1, heads):
         result = jnp.where(lane // HD == h, total[h, :, :width] / total[h, :, width:], result)
-    out[...] = result.astype(jnp.bfloat16)
+    result = result.astype(jnp.bfloat16)
+    outs[0][...] = result
+    for i, out in enumerate(outs[1:]):
+        step = out.shape[0]
+        out[...] = result[i * step : (i + 1) * step]
 
 
 def attend(lengths, queries, query_marks, pieces, heads, reach):
@@ -410,9 +409,12 @@
     slots = reach + 1
     return pl.pallas_call(
         functools.partial(attend_kernel, len(pieces), heads, reach),
-        out_shape=jax.ShapeDtypeStruct((rows, width), jnp.bfloat16),
+        out_shape=[
+            jax.ShapeDtypeStruct((each, width), jnp.bfloat16)
+            for each in (rows, rows // 2, rows // 2)
+        ],
         in_specs=[SMEM, VMEM, VMEM] + [ANY] * len(pieces),
-        out_specs=VMEM,
+        out_specs=[VMEM] * 3,
         scratch_shapes=[
             pltpu.VMEM((heads * rows, width + LANES), jnp.bfloat16),
             pltpu.VMEM((slots, rows, width + LANES), jnp.bfloat16),
@@ -537,24 +539,27 @@
     )(*arrays)
 
 
-def hidden_kernel(counts, *refs):
-    places = len(counts)
-    pieces, refs = refs[:places], refs[places:]
-    w_out_pieces, refs = refs[: sum(counts)], refs[sum(counts) :]
+def hidden_kernel(counts, w_counts, *refs):
+    pieces, refs = nested(counts, refs)
+    w_out_pieces, refs = nested(w_counts, refs)
     tokens, gain, w_gate, w_up, w_down = refs[:5]
     outs, attended, w_out = refs[5:-2], refs[-2], refs[-1]
     hidden, kept = outs[:2]
+    places = len(counts)
     place = lax.axis_index("tp")
     core = lax.rem(lax.axis_index("seq"), 2)
-    each = pieces[0].shape[1]
-    at = 0
-    for i, count in enumerate(counts):
-        attended[:, i * each : (i + 1) * each] = pieces[i][...]
-        part = w_out.shape[1] // count
-        for j in range(count):
-            columns = pl.ds(pl.multiple_of((core ^ j) * part, part), part) if count > 1 else slice(None)
-            w_out[i * each : (i + 1) * each, columns] = w_out_pieces[at][...]
-            at += 1
+    each = pieces[0][0].shape[1]
+    for i in range(places):
+        inner = slice(i * each, (i + 1) * each)
+        step = attended.shape[0] // counts[i]
+        for j, part in enumerate(pieces[i]):
+            attended[j * step : (j + 1) * step, inner] = part[...]
+        if w_counts[i] == 1:
+            w_out[inner, :] = w_out_pieces[i][0][...]
+            continue
+        step = w_out.shape[1] // w_counts[i]
+        for j, part in enumerate(w_out_pieces[i]):
+            w_out[inner, pl.ds(pl.multiple_of((core ^ j) * step, step), step)] = part[...]
     rows, features = tokens.shape
     width = kept.shape[1]
     step = min(rows, 256)
@@ -584,14 +589,14 @@
     places = lax.axis_size("tp")
     width = features // places
     units = w_gate.shape[1]
-    inner = places * pieces[0].shape[1]
+    inner = places * pieces[0][0].shape[1]
     shapes = [(rows, units), (rows, width)] + [(rows // 2, width)] * (2 * (places == 4))
-    counts = [len(piece) for piece in w_out_pieces]
-    w_out_pieces = [part for piece in w_out_pieces for part in piece]
+    counts = [[len(piece) for piece in group] for group in (pieces, w_out_pieces)]
+    parts = [part for group in (pieces, w_out_pieces) for piece in group for part in piece]
     return pl.pallas_call(
-        functools.partial(hidden_kernel, counts),
+        functools.partial(hidden_kernel, *counts),
         out_shape=[jax.ShapeDtypeStruct(shape, jnp.bfloat16) for shape in shapes],
-        in_specs=[VMEM] * (places + len(w_out_pieces) + 5),
+        in_specs=[VMEM] * (len(parts) + 5),
         out_specs=[VMEM] * len(shapes),
         scratch_shapes=[
             pltpu.VMEM((rows, inner), jnp.bfloat16),
@@ -600,7 +605,7 @@
         compiler_params=params(12),
         cost_estimate=cost(6 * rows * features * units, 10 << 20),
         name="hidden",
-    )(*pieces, *w_out_pieces, tokens, gain, w_gate, w_up, w_down)
+    )(*parts, tokens, gain, w_gate, w_up, w_down)
 
 
 def down_kernel(hidden, kept, w_down, far_top, far_low, near, own):
@@ -699,32 +704,29 @@
     reach = lax.axis_size("seq") // 2
 
     halve = lax.axis_size("tp") == 4 and lax.axis_size("seq") == 8
-    cosine, sine, extra, marks, *weights, w_out_part = tables(
-        lengths,
-        var_bias,
-        positions,
-        variate,
-        width,
-        (tokens, gain_attn, w_query, w_key, w_value, w_out),
-        halve,
+    cosine, sine, extra, marks, w_query, w_key, w_out_part = tables(
+        lengths, var_bias, positions, variate, width, (w_query, w_key, w_out), halve
     )
-    pieces = gather_pieces(tokens, 2, extra)
-    pieces[0] = weights[0]
-    token_rows, queries, pairs = project(pieces, *weights[1:], cosine, sine, extra)
+    own_tokens, gain_attn, w_value = fetch((tokens, gain_attn, w_value))
+    step = rows // 2
+    halves = lax.optimization_barrier((tokens[:step], tokens[step:], tokens))
+    pieces = gather_pieces(halves[2], halves[:2], (extra, gain_attn))
+    pieces[0] = [own_tokens]
+    token_rows, queries, pairs = project(
+        pieces, gain_attn, w_query, w_key, w_value, cosine, sine, extra
+    )
     w_out_part, _ = lax.optimization_barrier((w_out_part, pairs))
     row_pieces = seq_pieces(pairs)
-    w_out_pieces = [(piece,) for piece in gather_pieces(w_out_part, 1)]
-    if halve:
-        twins = [(piece, seq_xor(piece, 1)) for (piece,) in w_out_pieces[1:]]
-        w_out_pieces = w_out_pieces[:1] + twins
+    w_out_pieces = gather_pieces(w_out_part, [w_out_part])
     marks, w_out_pieces = lax.optimization_barrier((marks, w_out_pieces))
-    attended = attend(lengths, queries, marks, row_pieces, heads, reach)
+    attended, *halves = attend(lengths, queries, marks, row_pieces, heads, reach)
     large = (w_out, token_rows, gain_ffn, w_gate, w_up, w_down)
-    large = lax.optimization_barrier((large, attended))[0]
+    large, w_out_pieces = lax.optimization_barrier((large, w_out_pieces, attended))[:2]
     w_out, *large = fetch(large)
     if halve:
-        w_out_pieces[0] = (w_out,)
-    attended_pieces = gather_pieces(attended, 1, large[1])
+        twins = [[piece, seq_xor(piece, 1)] for (piece,) in w_out_pieces[1:]]
+        w_out_pieces = [[w_out]] + twins
+    attended_pieces = gather_pieces(attended, halves, large[1:2])
     mixed, joined = feed_forward(attended_pieces, w_out_pieces, *large)
     row_pieces, _ = lax.optimization_barrier((row_pieces, joined))
     cache = fill_cache(lengths, page_table, row_pieces, rows)

time: 93.2 us -> 95 us (1.019)
  starting transfers between devices: 32.6 us -> 36.5 us
    ppermute x16 -> x18, waiting for transfers between devices: 28.1 us -> 23.1 us  [tp_xor(): lax.ppermute(value, 'tp', [(i, i ^ mask) for i in range(lax.axis_size('tp...]
    ppermute x16 -> x18, starting transfers between devices: 27.8 us -> 32 us  [tp_xor(): lax.ppermute(value, 'tp', [(i, i ^ mask) for i in range(lax.axis_size('tp...]
    ppermute x10, waiting for transfers between devices: 3.02 us -> 7.23 us  [seq_xor(): lax.ppermute(value, 'seq', [(i, i ^ mask) for i in range(lax.axis_size('s...]
    unnamed x36 -> x34, local copies, waits for them, and re-layouts: 8.88 us -> 8.19 us
  transfers between devices with their start and end apart: 26 -> 28, of which waited for: 12 -> 16; matrix products, arithmetic and copies ran while one was open for 0% -> 0% of each run, Pallas kernels for 8% -> 8%
where the time goes in v9:
time: 95 us; the launch traced here: 95.2 us
  starting transfers between devices  36.5 us (38%)
  waiting for transfers between devices  30.4 us (32%)
  Pallas kernels  18.3 us (19%)
  local copies, waits for them, and re-layouts  9.19 us (10%)
    ppermute x18, starting transfers between devices, tp_xor(): lax.ppermute(value, 'tp', [(i, i ^ mask) for i in range(lax.axis_size('tp...  32 us
    ppermute x18, waiting for transfers between devices, tp_xor(): lax.ppermute(value, 'tp', [(i, i ^ mask) for i in range(lax.axis_size('tp...  23.1 us
    unnamed x34, local copies, waits for them, and re-layouts  8.19 us
    ppermute x10, waiting for transfers between devices, seq_xor(): lax.ppermute(value, 'seq', [(i, i ^ mask) for i in range(lax.axis_size('s...  7.23 us
    pallas_call x1, Pallas kernels, attend(): pl.pallas_call(functools.partial(attend_kernel, len(pieces), heads, reach...  4.74 us
    pallas_call x1, Pallas kernels, fill_cache(): pl.pallas_call(functools.partial(cache_kernel, len(pieces), 2 * PAGE), ou...  4.69 us
    ppermute x10, starting transfers between devices, seq_xor(): lax.ppermute(value, 'seq', [(i, i ^ mask) for i in range(lax.axis_size('s...  4.48 us
    pallas_call x1, Pallas kernels, hidden_of(): pl.pallas_call(functools.partial(hidden_kernel, *counts), out_shape=[jax....  3.82 us
  transfers between devices with their start and end apart: 28, of which 16 were waited for; matrix products, arithmetic and copies ran while one was open for 0% of the time, Pallas kernels for 8%

profile of v9, /device:TPU:2, one launch (start us, length us, event | category | flops | bytes accessed | tf_op | source)
XLA Modules:
  0.0 95.2 jit_solution(14337811009360830573)
XLA Ops:
  0.6 1.0 %fusion = (bf16[256,256]{1,0:T(8,128)(2,1)S(1)}, bf16[256,256]{1,0:T(8,128)(2,1)S(1)}) fusion(bf16[512,256]{1,0:T(8,128)(2,1)} %refs_0_.2), kind=kLoop, calls=%fused_computation | loop fusion | bytes 524288 | tf_op jit(solution)/shard_map/slice | solution.py:712
  1.6 2.7 %collective-permute-start.2 = (bf16[256,256]{1,0:T(8,128)(2,1)S(1)}, bf16[256,256]{1,0:T(8,128)(2,1)S(1)}, u32[]{:S(2)}, u32[]{:S(2)}) collective-permute-start(bf16[256,256]{1,0:T(8,128)(2,1)S(1)} %get-tuple-element.65), channel_id=1, source_target_pairs={{0,2},{1,3},{2,0},{3,1},{4,6},{5,7},{6,4},{7,5},{8,10},{9,11},{10,... | collective-permute-start | bytes 393224 | tf_op jit(solution)/shard_map/ppermute | solution.py:57
  4.6 1.6 %collective-permute-start = (bf16[512,256]{1,0:T(8,128)(2,1)}, bf16[512,256]{1,0:T(8,128)(2,1)S(1)}, u32[]{:S(2)}, u32[]{:S(2)}) collective-permute-start(bf16[512,256]{1,0:T(8,128)(2,1)} %refs_0_.2), channel_id=1, source_target_pairs={{0,1},{1,0},{2,3},{3,2},{4,5},{5,4},{6,7},{7,6},{8,9},{9,8},{10,11... | collective-permute-start | bytes 786440 | tf_op jit(solution)/shard_map/ppermute | solution.py:57
  6.2 1.0 %copy-done.5 = bf16[512,256]{1,0:T(8,128)(2,1)S(1)} copy-done((bf16[512,256]{1,0:T(8,128)(2,1)S(1)}, bf16[512,256]{1,0:T(8,128)(2,1)}, u32[]{:S(2)}) %copy-start.5) | copy-done | bytes 262168
  7.2 0.9 copy-done.6
  8.1 0.7 copy-done.9
  8.9 0.9 copy-done.3
  9.9 0.9 copy-done.7
  10.8 0.9 copy-done.8
  11.8 0.7 copy-done.10
  12.4 0.7 copy-done.11
  13.1 0.7 copy-done.13
  13.8 0.7 copy-done.15
  14.4 1.1 %tables.1 = (f32[512,128]{1,0:T(8,128)S(1)}, f32[512,128]{1,0:T(8,128)S(1)}, bf16[16,256]{1,0:T(8,128)(2,1)S(1)}, bf16[2,512,128]{2,1,0:T(8,128)(2,1)S(1)}, bf16...) custom-call(s32[4]{0:T(128)S(1)} %copy-done.13, f32[2,2]{1,0:T(2,128)S(1)} %copy-done.15, ...), custom_call_target="tpu_custom_call" | custom-call | flops 524288 | bytes 1048576 | tf_op jit(solution)/shard_map/tables/pallas_call | solution.py:167
  15.6 0.5 collective-permute-start.4
  16.4 1.3 %collective-permute-start.3 = (bf16[256,256]{1,0:T(8,128)(2,1)S(1)}, bf16[256,256]{1,0:T(8,128)(2,1)S(1)}, u32[]{:S(2)}, u32[]{:S(2)}) collective-permute-start(bf16[256,256]{1,0:T(8,128)(2,1)S(1)} %collective-permute-done.1.refs_2_), channel_id=1, source_target_pairs={{0,1},{1,0},{2,3},{3,2},{4,5},{5,4},{6,7},{7,6},{8,9},{9,8},{10,11... | collective-permute-start | bytes 393224 | tf_op jit(solution)/shard_map/ppermute | solution.py:57
  17.7 3.8 %collective-permute-done.4.refs_5_ = bf16[256,256]{1,0:T(8,128)(2,1)S(1)} collective-permute-done((bf16[256,256]{1,0:T(8,128)(2,1)S(1)}, bf16[256,256]{1,0:T(8,128)(2,1)S(1)}, u32[]{:S(2)}, u32[]{:S(2)}) %collective-permute-start.4) | collective-permute-done | bytes 131104 | tf_op jit(solution)/shard_map/ppermute | solution.py:57
  21.5 1.4 %collective-permute-done.3.refs_4_ = bf16[256,256]{1,0:T(8,128)(2,1)S(1)} collective-permute-done((bf16[256,256]{1,0:T(8,128)(2,1)S(1)}, bf16[256,256]{1,0:T(8,128)(2,1)S(1)}, u32[]{:S(2)}, u32[]{:S(2)}) %collective-permute-start.3) | collective-permute-done | bytes 131104 | tf_op jit(solution)/shard_map/ppermute | solution.py:57
  22.9 1.4 %project.1 = (bf16[512,1024]{1,0:T(8,128)(2,1)S(1)}, bf16[512,128]{1,0:T(8,128)(2,1)S(1)}, bf16[528,256]{1,0:T(8,128)(2,1)S(1)}) custom-call(bf16[512,256]{1,0:T(8,128)(2,1)S(1)} %get-tuple-element.60.refs_0_, bf16[512,256]{1,0:T(8,128)(2,1)S(1)} %collective-permute-done.refs_1_, bf16[256,256]{1,0:T(8,128)(2,1)S(1)} %collective-permute-done.1.refs_2_, ...), custom_call_target="tpu_custom_call" | custom-call | flops 402653184 | bytes 4194304 | tf_op jit(solution)/shard_map/project/pallas_call | solution.py:241
  24.3 1.6 %collective-permute-start.13 = (bf16[528,256]{1,0:T(8,128)(2,1)S(1)}, bf16[528,256]{1,0:T(8,128)(2,1)S(1)}, u32[]{:S(2)}, u32[]{:S(2)}) collective-permute-start(bf16[528,256]{1,0:T(8,128)(2,1)S(1)} %get-tuple-element.110.refs_0_), channel_id=1, source_target_pairs={{0,24},{4,28},{8,16},{12,20},{16,8},{20,12},{24,0},{28,4},{1,25},{... | collective-permute-start | bytes 811016 | tf_op jit(solution)/shard_map/ppermute | solution.py:258
  26.4 1.5 %collective-permute-start.9 = (bf16[528,256]{1,0:T(8,128)(2,1)S(1)}, bf16[528,256]{1,0:T(8,128)(2,1)S(1)}, u32[]{:S(2)}, u32[]{:S(2)}) collective-permute-start(bf16[528,256]{1,0:T(8,128)(2,1)S(1)} %get-tuple-element.110.refs_0_), channel_id=1, source_target_pairs={{0,8},{4,12},{8,0},{12,4},{16,24},{20,28},{24,16},{28,20},{1,9},{5... | collective-permute-start | bytes 811016 | tf_op jit(solution)/shard_map/ppermute | solution.py:258
  27.9 2.6 %collective-permute-start.6 = (bf16[128,512]{1,0:T(8,128)(2,1)S(1)}, bf16[128,512]{1,0:T(8,128)(2,1)S(1)}, u32[]{:S(2)}, u32[]{:S(2)}) collective-permute-start(bf16[128,512]{1,0:T(8,128)(2,1)S(1)} %get-tuple-element.77), channel_id=1, source_target_pairs={{0,2},{1,3},{2,0},{3,1},{4,6},{5,7},{6,4},{7,5},{8,10},{9,11},{10,... | collective-permute-start | bytes 393224 | tf_op jit(solution)/shard_map/ppermute | solution.py:57
  30.5 4.3 %collective-permute-done.13.refs_6_ = bf16[528,256]{1,0:T(8,128)(2,1)S(1)} collective-permute-done((bf16[528,256]{1,0:T(8,128)(2,1)S(1)}, bf16[528,256]{1,0:T(8,128)(2,1)S(1)}, u32[]{:S(2)}, u32[]{:S(2)}) %collective-permute-start.13) | collective-permute-done | bytes 270368 | tf_op jit(solution)/shard_map/ppermute | solution.py:258
  34.7 2.8 %collective-permute-done.11.refs_4_ = bf16[528,256]{1,0:T(8,128)(2,1)S(1)} collective-permute-done((bf16[528,256]{1,0:T(8,128)(2,1)S(1)}, bf16[528,256]{1,0:T(8,128)(2,1)S(1)}, u32[]{:S(2)}, u32[]{:S(2)}) %collective-permute-start.11) | collective-permute-done | bytes 270368 | tf_op jit(solution)/shard_map/ppermute | solution.py:258
  38.1 1.4 %collective-permute-start.5 = (bf16[128,512]{1,0:T(8,128)(2,1)S(1)}, bf16[128,512]{1,0:T(8,128)(2,1)S(1)}, u32[]{:S(2)}, u32[]{:S(2)}) collective-permute-start(bf16[128,512]{1,0:T(8,128)(2,1)S(1)} %get-tuple-element.77), channel_id=1, source_target_pairs={{0,1},{1,0},{2,3},{3,2},{4,5},{5,4},{6,7},{7,6},{8,9},{9,8},{10,11... | collective-permute-start | bytes 393224 | tf_op jit(solution)/shard_map/ppermute | solution.py:57
  39.5 4.1 %collective-permute-done.5.refs_7_ = bf16[128,512]{1,0:T(8,128)(2,1)S(1)} collective-permute-done((bf16[128,512]{1,0:T(8,128)(2,1)S(1)}, bf16[128,512]{1,0:T(8,128)(2,1)S(1)}, u32[]{:S(2)}, u32[]{:S(2)}) %collective-permute-start.5) | collective-permute-done | bytes 131104 | tf_op jit(solution)/shard_map/ppermute | solution.py:57
  43.6 1.4 %collective-permute-start.7 = (bf16[128,512]{1,0:T(8,128)(2,1)S(1)}, bf16[128,512]{1,0:T(8,128)(2,1)S(1)}, u32[]{:S(2)}, u32[]{:S(2)}) collective-permute-start(bf16[128,512]{1,0:T(8,128)(2,1)S(1)} %collective-permute-done.6.refs_9_), channel_id=1, source_target_pairs={{0,1},{1,0},{2,3},{3,2},{4,5},{5,4},{6,7},{7,6},{8,9},{9,8},{10,11... | collective-permute-start | bytes 393224 | tf_op jit(solution)/shard_map/ppermute | solution.py:57
  45.0 3.5 %collective-permute-done.7.refs_11_ = bf16[128,512]{1,0:T(8,128)(2,1)S(1)} collective-permute-done((bf16[128,512]{1,0:T(8,128)(2,1)S(1)}, bf16[128,512]{1,0:T(8,128)(2,1)S(1)}, u32[]{:S(2)}, u32[]{:S(2)}) %collective-permute-start.7) | collective-permute-done | bytes 131104 | tf_op jit(solution)/shard_map/ppermute | solution.py:57
  48.7 4.7 %attend.1 = (bf16[512,128]{1,0:T(8,128)(2,1)S(1)}, bf16[256,128]{1,0:T(8,128)(2,1)S(1)}, bf16[256,128]{1,0:T(8,128)(2,1)S(1)}) custom-call(s32[4]{0:T(128)S(1)} %copy-done.14, bf16[512,128]{1,0:T(8,128)(2,1)S(1)} %get-tuple-element.73.queries, bf16[2,512,128]{2,1,0:T(8,128)(2,1)S(1)} %get-tuple-element.78.query_marks, ...), custom_call_target="tpu_custom_call" | custom-call | flops 2684354560 | bytes 4194304 | tf_op jit(solution)/shard_map/attend/pallas_call | solution.py:410
  53.4 3.5 %collective-permute-start.16 = (bf16[256,128]{1,0:T(8,128)(2,1)S(1)}, bf16[256,128]{1,0:T(8,128)(2,1)S(1)}, u32[]{:S(2)}, u32[]{:S(2)}) collective-permute-start(bf16[256,128]{1,0:T(8,128)(2,1)S(1)} %get-tuple-element.80), channel_id=1, source_target_pairs={{0,2},{1,3},{2,0},{3,1},{4,6},{5,7},{6,4},{7,5},{8,10},{9,11},{10,... | collective-permute-start | bytes 196616 | tf_op jit(solution)/shard_map/ppermute | solution.py:57
  57.6 2.0 %collective-permute-done.16.refs_2_ = bf16[256,128]{1,0:T(8,128)(2,1)S(1)} collective-permute-done((bf16[256,128]{1,0:T(8,128)(2,1)S(1)}, bf16[256,128]{1,0:T(8,128)(2,1)S(1)}, u32[]{:S(2)}, u32[]{:S(2)}) %collective-permute-start.16) | collective-permute-done | bytes 65568 | tf_op jit(solution)/shard_map/ppermute | solution.py:57
  59.6 3.3 %collective-permute-start.15 = (bf16[512,128]{1,0:T(8,128)(2,1)S(1)}, bf16[512,128]{1,0:T(8,128)(2,1)S(1)}, u32[]{:S(2)}, u32[]{:S(2)}) collective-permute-start(bf16[512,128]{1,0:T(8,128)(2,1)S(1)} %get-tuple-element.79.refs_0_), channel_id=1, source_target_pairs={{0,1},{1,0},{2,3},{3,2},{4,5},{5,4},{6,7},{7,6},{8,9},{9,8},{10,11... | collective-permute-start | bytes 393224 | tf_op jit(solution)/shard_map/ppermute | solution.py:57
  62.9 0.6 fetch.3
  64.2 1.6 %collective-permute-start.18 = (bf16[256,128]{1,0:T(8,128)(2,1)S(1)}, bf16[256,128]{1,0:T(8,128)(2,1)S(1)}, u32[]{:S(2)}, u32[]{:S(2)}) collective-permute-start(bf16[256,128]{1,0:T(8,128)(2,1)S(1)} %collective-permute-done.16.refs_2_), channel_id=1, source_target_pairs={{0,1},{1,0},{2,3},{3,2},{4,5},{5,4},{6,7},{7,6},{8,9},{9,8},{10,11... | collective-permute-start | bytes 196616 | tf_op jit(solution)/shard_map/ppermute | solution.py:57
  65.8 1.0 %collective-permute-done.15.refs_1_ = bf16[512,128]{1,0:T(8,128)(2,1)S(1)} collective-permute-done((bf16[512,128]{1,0:T(8,128)(2,1)S(1)}, bf16[512,128]{1,0:T(8,128)(2,1)S(1)}, u32[]{:S(2)}, u32[]{:S(2)}) %collective-permute-start.15) | collective-permute-done | bytes 131104 | tf_op jit(solution)/shard_map/ppermute | solution.py:57
  66.8 1.3 %collective-permute-done.19.refs_5_ = bf16[256,128]{1,0:T(8,128)(2,1)S(1)} collective-permute-done((bf16[256,128]{1,0:T(8,128)(2,1)S(1)}, bf16[256,128]{1,0:T(8,128)(2,1)S(1)}, u32[]{:S(2)}, u32[]{:S(2)}) %collective-permute-start.19) | collective-permute-done | bytes 65568 | tf_op jit(solution)/shard_map/ppermute | solution.py:57
  68.0 0.7 collective-permute-done.18.refs_4_
  68.7 3.8 %hidden.1 = (bf16[512,1024]{1,0:T(8,128)(2,1)S(1)}, bf16[512,256]{1,0:T(8,128)(2,1)S(1)}, bf16[256,256]{1,0:T(8,128)(2,1)S(1)}, bf16[256,256]{1,0:T(8,128)(2,1)S(1)}) custom-call(bf16[512,128]{1,0:T(8,128)(2,1)S(1)} %get-tuple-element.79.refs_0_, bf16[512,128]{1,0:T(8,128)(2,1)S(1)} %collective-permute-done.15.refs_1_, ...), custom_call_target="tpu_custom_call" | custom-call | flops 3221225472 | bytes 10485760 | tf_op jit(solution)/shard_map/hidden/pallas_call | solution.py:596
  72.6 2.0 %collective-permute-start.24 = (bf16[256,256]{1,0:T(8,128)(2,1)S(1)}, bf16[256,256]{1,0:T(8,128)(2,1)S(1)}, u32[]{:S(2)}, u32[]{:S(2)}) collective-permute-start(bf16[256,256]{1,0:T(8,128)(2,1)S(1)} %get-tuple-element.107), channel_id=1, source_target_pairs={{0,1},{1,0},{2,3},{3,2},{4,5},{5,4},{6,7},{7,6},{8,9},{9,8},{10,11... | collective-permute-start | bytes 393224 | tf_op jit(solution)/shard_map/ppermute | solution.py:57
  74.7 1.0 %down_blocks.1 = (f32[256,256]{1,0:T(8,128)S(1)}, f32[256,256]{1,0:T(8,128)S(1)}, bf16[512,256]{1,0:T(8,128)(2,1)S(1)}, f32[512,256]{1,0:T(8,128)S(1)}) custom-call(bf16[512,1024]{1,0:T(8,128)(2,1)S(1)} %get-tuple-element.102.hidden, bf16[512,256]{1,0:T(8,128)(2,1)S(1)} %get-tuple-element.103.kept, bf16[1024,1024]{1,0:T(8,128)(2,1)S(1)} %get-tuple-element.101.refs_17_.w_down), custom_call_target="tpu_custom_call" | custom-call | flops 805306368 | bytes 5242880 | tf_op jit(solution)/shard_map/down_blocks/pallas_call | solution.py:630
  75.7 2.0 %collective-permute-start.23 = (bf16[512,256]{1,0:T(8,128)(2,1)S(1)}, bf16[512,256]{1,0:T(8,128)(2,1)S(1)}, u32[]{:S(2)}, u32[]{:S(2)}) collective-permute-start(bf16[512,256]{1,0:T(8,128)(2,1)S(1)} %get-tuple-element.105), channel_id=1, source_target_pairs={{0,1},{1,0},{2,3},{3,2},{4,5},{5,4},{6,7},{7,6},{8,9},{9,8},{10,11... | collective-permute-start | bytes 786440 | tf_op jit(solution)/shard_map/ppermute | solution.py:57
  77.6 1.3 %collective-permute-done.24.refs_1_ = bf16[256,256]{1,0:T(8,128)(2,1)S(1)} collective-permute-done((bf16[256,256]{1,0:T(8,128)(2,1)S(1)}, bf16[256,256]{1,0:T(8,128)(2,1)S(1)}, u32[]{:S(2)}, u32[]{:S(2)}) %collective-permute-start.24) | collective-permute-done | bytes 131104 | tf_op jit(solution)/shard_map/ppermute | solution.py:57
  79.0 5.1 %collective-permute-start.25 = (bf16[256,256]{1,0:T(8,128)(2,1)S(1)}, bf16[256,256]{1,0:T(8,128)(2,1)S(1)}, u32[]{:S(2)}, u32[]{:S(2)}) collective-permute-start(bf16[256,256]{1,0:T(8,128)(2,1)S(1)} %add_up.3), channel_id=1, source_target_pairs={{0,2},{1,3},{2,0},{3,1},{4,6},{5,7},{6,4},{7,5},{8,10},{9,11},{10,... | collective-permute-start | bytes 393224 | tf_op jit(solution)/shard_map/ppermute | solution.py:57
  84.1 0.5 collective-permute-done.26.refs_1_
  84.6 2.1 %collective-permute-start.27 = (bf16[256,256]{1,0:T(8,128)(2,1)S(1)}, bf16[256,256]{1,0:T(8,128)(2,1)S(1)}, u32[]{:S(2)}, u32[]{:S(2)}) collective-permute-start(bf16[256,256]{1,0:T(8,128)(2,1)S(1)} %add_up.4), channel_id=1, source_target_pairs={{0,2},{1,3},{2,0},{3,1},{4,6},{5,7},{6,4},{7,5},{8,10},{9,11},{10,... | collective-permute-start | bytes 393224 | tf_op jit(solution)/shard_map/ppermute | solution.py:57
  86.7 4.7 %fill_cache.1 = bf16[576,2,128]{2,1,0:T(2,128)(2,1)} custom-call(s32[4]{0:T(128)S(1)} %copy-done.14, s32[72]{0:T(128)S(1)} %copy-done.16, bf16[528,256]{1,0:T(8,128)(2,1)S(1)} %get-tuple-element.110.refs_0_, bf16[528,256]{1,0:T(8,128)(2,1)S(1)} %collective-permute-done.8.refs_1_, bf16[528,256]{1,0:T(8,128)(2,1)S(1)} %collective-permute-done.9.refs_2_, ...), custom_call_target="tpu_custom_call" | custom-call | flops 75497472 | bytes 3145728 | tf_op jit(solution)/shard_map/fill_cache/pallas_call | solution.py:509
  91.4 3.0 %collective-permute-done.27.refs_3_ = bf16[256,256]{1,0:T(8,128)(2,1)S(1)} collective-permute-done((bf16[256,256]{1,0:T(8,128)(2,1)S(1)}, bf16[256,256]{1,0:T(8,128)(2,1)S(1)}, u32[]{:S(2)}, u32[]{:S(2)}) %collective-permute-start.27) | collective-permute-done | bytes 131104 | tf_op jit(solution)/shard_map/ppermute | solution.py:57
  94.4 0.8 add_up.5
  (54 shorter events, 3.3 us)
Async XLA Ops:
  0.6 48.0 %copy-start.14 = (s32[4]{0:T(128)S(1)}, s32[4]{0:T(128)}, u32[]{:S(2)}) copy-start(s32[4]{0:T(128)} %lengths.5) | copy-start | bytes 52
  1.6 14.0 %collective-permute-start.2 = (bf16[256,256]{1,0:T(8,128)(2,1)S(1)}, bf16[256,256]{1,0:T(8,128)(2,1)S(1)}, u32[]{:S(2)}, u32[]{:S(2)}) collective-permute-start(bf16[256,256]{1,0:T(8,128)(2,1)S(1)} %get-tuple-element.65), channel_id=1, source_target_pairs={{0,2},{1,3},{2,0},{3,1},{4,6},{5,7},{6,4},{7,5},{8,10},{9,11},{10,... | collective-permute-start | bytes 393224 | tf_op jit(solution)/shard_map/ppermute | solution.py:57
  4.3 12.1 %collective-permute-start.1 = (bf16[256,256]{1,0:T(8,128)(2,1)S(1)}, bf16[256,256]{1,0:T(8,128)(2,1)S(1)}, u32[]{:S(2)}, u32[]{:S(2)}) collective-permute-start(bf16[256,256]{1,0:T(8,128)(2,1)S(1)} %get-tuple-element.62), channel_id=1, source_target_pairs={{0,2},{1,3},{2,0},{3,1},{4,6},{5,7},{6,4},{7,5},{8,10},{9,11},{10,... | collective-permute-start | bytes 393224 | tf_op jit(solution)/shard_map/ppermute | solution.py:57
  4.6 13.1 %collective-permute-start = (bf16[512,256]{1,0:T(8,128)(2,1)}, bf16[512,256]{1,0:T(8,128)(2,1)S(1)}, u32[]{:S(2)}, u32[]{:S(2)}) collective-permute-start(bf16[512,256]{1,0:T(8,128)(2,1)} %refs_0_.2), channel_id=1, source_target_pairs={{0,1},{1,0},{2,3},{3,2},{4,5},{5,4},{6,7},{7,6},{8,9},{9,8},{10,11... | collective-permute-start | bytes 786440 | tf_op jit(solution)/shard_map/ppermute | solution.py:57
  6.2 1.0 %copy-start.5 = (bf16[512,256]{1,0:T(8,128)(2,1)S(1)}, bf16[512,256]{1,0:T(8,128)(2,1)}, u32[]{:S(2)}) copy-start(bf16[512,256]{1,0:T(8,128)(2,1)} %refs_0_.2) | copy-start | bytes 786436
  7.2 0.9 copy-start.6
  8.1 0.7 copy-start.9
  8.9 1.0 %copy-start.3 = (bf16[128,1024]{1,0:T(8,128)(2,1)S(1)}, bf16[128,1024]{1,0:T(8,128)(2,1)}, u32[]{:S(2)}) copy-start(bf16[128,1024]{1,0:T(8,128)(2,1)} %refs_0_.4) | copy-start | bytes 786436
  9.8 0.9 copy-start.7
  10.8 0.9 copy-start.8
  11.8 0.7 copy-start.10
  12.4 0.7 copy-start.11
  13.1 0.7 copy-start.13
  13.8 0.7 copy-start.15
  15.6 5.9 %collective-permute-start.4 = (bf16[256,256]{1,0:T(8,128)(2,1)S(1)}, bf16[256,256]{1,0:T(8,128)(2,1)S(1)}, u32[]{:S(2)}, u32[]{:S(2)}) collective-permute-start(bf16[256,256]{1,0:T(8,128)(2,1)S(1)} %collective-permute-done.2.refs_3_), channel_id=1, source_target_pairs={{0,1},{1,0},{2,3},{3,2},{4,5},{5,4},{6,7},{7,6},{8,9},{9,8},{10,11... | collective-permute-start | bytes 393224 | tf_op jit(solution)/shard_map/ppermute | solution.py:57
  16.4 6.5 %collective-permute-start.3 = (bf16[256,256]{1,0:T(8,128)(2,1)S(1)}, bf16[256,256]{1,0:T(8,128)(2,1)S(1)}, u32[]{:S(2)}, u32[]{:S(2)}) collective-permute-start(bf16[256,256]{1,0:T(8,128)(2,1)S(1)} %collective-permute-done.1.refs_2_), channel_id=1, source_target_pairs={{0,1},{1,0},{2,3},{3,2},{4,5},{5,4},{6,7},{7,6},{8,9},{9,8},{10,11... | collective-permute-start | bytes 393224 | tf_op jit(solution)/shard_map/ppermute | solution.py:57
  24.3 10.4 %collective-permute-start.13 = (bf16[528,256]{1,0:T(8,128)(2,1)S(1)}, bf16[528,256]{1,0:T(8,128)(2,1)S(1)}, u32[]{:S(2)}, u32[]{:S(2)}) collective-permute-start(bf16[528,256]{1,0:T(8,128)(2,1)S(1)} %get-tuple-element.110.refs_0_), channel_id=1, source_target_pairs={{0,24},{4,28},{8,16},{12,20},{16,8},{20,12},{24,0},{28,4},{1,25},{... | collective-permute-start | bytes 811016 | tf_op jit(solution)/shard_map/ppermute | solution.py:258
  25.9 11.7 %collective-permute-start.11 = (bf16[528,256]{1,0:T(8,128)(2,1)S(1)}, bf16[528,256]{1,0:T(8,128)(2,1)S(1)}, u32[]{:S(2)}, u32[]{:S(2)}) collective-permute-start(bf16[528,256]{1,0:T(8,128)(2,1)S(1)} %get-tuple-element.110.refs_0_), channel_id=1, source_target_pairs={{0,16},{4,20},{8,24},{12,28},{16,0},{20,4},{24,8},{28,12},{1,17},{... | collective-permute-start | bytes 811016 | tf_op jit(solution)/shard_map/ppermute | solution.py:258
  26.4 11.3 %collective-permute-start.9 = (bf16[528,256]{1,0:T(8,128)(2,1)S(1)}, bf16[528,256]{1,0:T(8,128)(2,1)S(1)}, u32[]{:S(2)}, u32[]{:S(2)}) collective-permute-start(bf16[528,256]{1,0:T(8,128)(2,1)S(1)} %get-tuple-element.110.refs_0_), channel_id=1, source_target_pairs={{0,8},{4,12},{8,0},{12,4},{16,24},{20,28},{24,16},{28,20},{1,9},{5... | collective-permute-start | bytes 811016 | tf_op jit(solution)/shard_map/ppermute | solution.py:258
  27.9 10.2 %collective-permute-start.6 = (bf16[128,512]{1,0:T(8,128)(2,1)S(1)}, bf16[128,512]{1,0:T(8,128)(2,1)S(1)}, u32[]{:S(2)}, u32[]{:S(2)}) collective-permute-start(bf16[128,512]{1,0:T(8,128)(2,1)S(1)} %get-tuple-element.77), channel_id=1, source_target_pairs={{0,2},{1,3},{2,0},{3,1},{4,6},{5,7},{6,4},{7,5},{8,10},{9,11},{10,... | collective-permute-start | bytes 393224 | tf_op jit(solution)/shard_map/ppermute | solution.py:57
  30.5 18.1 %collective-permute-start.8 = (bf16[528,256]{1,0:T(8,128)(2,1)S(1)}, bf16[528,256]{1,0:T(8,128)(2,1)S(1)}, u32[]{:S(2)}, u32[]{:S(2)}) collective-permute-start(bf16[528,256]{1,0:T(8,128)(2,1)S(1)} %get-tuple-element.110.refs_0_), channel_id=1, source_target_pairs={{0,4},{4,0},{8,12},{12,8},{16,20},{20,16},{24,28},{28,24},{1,5},{5... | collective-permute-start | bytes 811016 | tf_op jit(solution)/shard_map/ppermute | solution.py:258
  34.7 13.8 %collective-permute-start.14 = (bf16[528,256]{1,0:T(8,128)(2,1)S(1)}, bf16[528,256]{1,0:T(8,128)(2,1)S(1)}, u32[]{:S(2)}, u32[]{:S(2)}) collective-permute-start(bf16[528,256]{1,0:T(8,128)(2,1)S(1)} %collective-permute-done.13.refs_6_), channel_id=1, source_target_pairs={{0,4},{4,0},{8,12},{12,8},{16,20},{20,16},{24,28},{28,24},{1,5},{5... | collective-permute-start | bytes 811016 | tf_op jit(solution)/shard_map/ppermute | solution.py:258
  37.6 11.0 %collective-permute-start.12 = (bf16[528,256]{1,0:T(8,128)(2,1)S(1)}, bf16[528,256]{1,0:T(8,128)(2,1)S(1)}, u32[]{:S(2)}, u32[]{:S(2)}) collective-permute-start(bf16[528,256]{1,0:T(8,128)(2,1)S(1)} %collective-permute-done.11.refs_4_), channel_id=1, source_target_pairs={{0,4},{4,0},{8,12},{12,8},{16,20},{20,16},{24,28},{28,24},{1,5},{5... | collective-permute-start | bytes 811016 | tf_op jit(solution)/shard_map/ppermute | solution.py:258
  37.7 10.9 %collective-permute-start.10 = (bf16[528,256]{1,0:T(8,128)(2,1)S(1)}, bf16[528,256]{1,0:T(8,128)(2,1)S(1)}, u32[]{:S(2)}, u32[]{:S(2)}) collective-permute-start(bf16[528,256]{1,0:T(8,128)(2,1)S(1)} %collective-permute-done.9.refs_2_), channel_id=1, source_target_pairs={{0,4},{4,0},{8,12},{12,8},{16,20},{20,16},{24,28},{28,24},{1,5},{5... | collective-permute-start | bytes 811016 | tf_op jit(solution)/shard_map/ppermute | solution.py:258
  38.1 5.5 %collective-permute-start.5 = (bf16[128,512]{1,0:T(8,128)(2,1)S(1)}, bf16[128,512]{1,0:T(8,128)(2,1)S(1)}, u32[]{:S(2)}, u32[]{:S(2)}) collective-permute-start(bf16[128,512]{1,0:T(8,128)(2,1)S(1)} %get-tuple-element.77), channel_id=1, source_target_pairs={{0,1},{1,0},{2,3},{3,2},{4,5},{5,4},{6,7},{7,6},{8,9},{9,8},{10,11... | collective-permute-start | bytes 393224 | tf_op jit(solution)/shard_map/ppermute | solution.py:57
  43.6 5.0 %collective-permute-start.7 = (bf16[128,512]{1,0:T(8,128)(2,1)S(1)}, bf16[128,512]{1,0:T(8,128)(2,1)S(1)}, u32[]{:S(2)}, u32[]{:S(2)}) collective-permute-start(bf16[128,512]{1,0:T(8,128)(2,1)S(1)} %collective-permute-done.6.refs_9_), channel_id=1, source_target_pairs={{0,1},{1,0},{2,3},{3,2},{4,5},{5,4},{6,7},{7,6},{8,9},{9,8},{10,11... | collective-permute-start | bytes 393224 | tf_op jit(solution)/shard_map/ppermute | solution.py:57
  48.6 14.3 %copy-start = (bf16[1024,1024]{1,0:T(8,128)(2,1)S(1)}, bf16[1024,1024]{1,0:T(8,128)(2,1)}, u32[]{:S(2)}) copy-start(bf16[1024,1024]{1,0:T(8,128)(2,1)} %refs_3_) | copy-start | bytes 6291460
  48.6 14.3 %copy-start.1 = (bf16[1024,1024]{1,0:T(8,128)(2,1)S(1)}, bf16[1024,1024]{1,0:T(8,128)(2,1)}, u32[]{:S(2)}) copy-start(bf16[1024,1024]{1,0:T(8,128)(2,1)} %refs_4_) | copy-start | bytes 6291460
  48.6 14.3 %copy-start.2 = (bf16[1024,1024]{1,0:T(8,128)(2,1)S(1)}, bf16[1024,1024]{1,0:T(8,128)(2,1)}, u32[]{:S(2)}) copy-start(bf16[1024,1024]{1,0:T(8,128)(2,1)} %refs_5_) | copy-start | bytes 6291460
  48.6 14.2 %copy-start.4 = (bf16[128,1024]{1,0:T(8,128)(2,1)S(1)}, bf16[128,1024]{1,0:T(8,128)(2,1)}, u32[]{:S(2)}) copy-start(bf16[128,1024]{1,0:T(8,128)(2,1)} %refs_0_.4) | copy-start | bytes 786436
  48.6 14.2 %copy-start.12 = (bf16[1024]{0:T(1024)(128)(2,1)S(1)}, bf16[1024]{0:T(1024)(128)(2,1)}, u32[]{:S(2)}) copy-start(bf16[1024]{0:T(1024)(128)(2,1)} %refs_2_.4) | copy-start | bytes 6148
  53.4 6.2 %collective-permute-start.16 = (bf16[256,128]{1,0:T(8,128)(2,1)S(1)}, bf16[256,128]{1,0:T(8,128)(2,1)S(1)}, u32[]{:S(2)}, u32[]{:S(2)}) collective-permute-start(bf16[256,128]{1,0:T(8,128)(2,1)S(1)} %get-tuple-element.80), channel_id=1, source_target_pairs={{0,2},{1,3},{2,0},{3,1},{4,6},{5,7},{6,4},{7,5},{8,10},{9,11},{10,... | collective-permute-start | bytes 196616 | tf_op jit(solution)/shard_map/ppermute | solution.py:57
  56.9 7.3 %collective-permute-start.20 = (bf16[128,512]{1,0:T(8,128)(2,1)S(1)}, bf16[128,512]{1,0:T(8,128)(2,1)S(1)}, u32[]{:S(2)}, u32[]{:S(2)}) collective-permute-start(bf16[128,512]{1,0:T(8,128)(2,1)S(1)} %collective-permute-done.5.refs_7_), channel_id=1, source_target_pairs={{0,4},{4,0},{8,12},{12,8},{16,20},{20,16},{24,28},{28,24},{1,5},{5... | collective-permute-start | bytes 393224 | tf_op jit(solution)/shard_map/ppermute | solution.py:258
  56.9 6.9 %collective-permute-start.17 = (bf16[256,128]{1,0:T(8,128)(2,1)S(1)}, bf16[256,128]{1,0:T(8,128)(2,1)S(1)}, u32[]{:S(2)}, u32[]{:S(2)}) collective-permute-start(bf16[256,128]{1,0:T(8,128)(2,1)S(1)} %get-tuple-element.93), channel_id=1, source_target_pairs={{0,2},{1,3},{2,0},{3,1},{4,6},{5,7},{6,4},{7,5},{8,10},{9,11},{10,... | collective-permute-start | bytes 196616 | tf_op jit(solution)/shard_map/ppermute | solution.py:57
  57.1 8.7 %collective-permute-start.21 = (bf16[128,512]{1,0:T(8,128)(2,1)S(1)}, bf16[128,512]{1,0:T(8,128)(2,1)S(1)}, u32[]{:S(2)}, u32[]{:S(2)}) collective-permute-start(bf16[128,512]{1,0:T(8,128)(2,1)S(1)} %collective-permute-done.6.refs_9_), channel_id=1, source_target_pairs={{0,4},{4,0},{8,12},{12,8},{16,20},{20,16},{24,28},{28,24},{1,5},{5... | collective-permute-start | bytes 393224 | tf_op jit(solution)/shard_map/ppermute | solution.py:258
  57.4 8.4 %collective-permute-start.22 = (bf16[128,512]{1,0:T(8,128)(2,1)S(1)}, bf16[128,512]{1,0:T(8,128)(2,1)S(1)}, u32[]{:S(2)}, u32[]{:S(2)}) collective-permute-start(bf16[128,512]{1,0:T(8,128)(2,1)S(1)} %collective-permute-done.7.refs_11_), channel_id=1, source_target_pairs={{0,4},{4,0},{8,12},{12,8},{16,20},{20,16},{24,28},{28,24},{1,5},{5... | collective-permute-start | bytes 393224 | tf_op jit(solution)/shard_map/ppermute | solution.py:258
  59.6 7.2 %collective-permute-start.15 = (bf16[512,128]{1,0:T(8,128)(2,1)S(1)}, bf16[512,128]{1,0:T(8,128)(2,1)S(1)}, u32[]{:S(2)}, u32[]{:S(2)}) collective-permute-start(bf16[512,128]{1,0:T(8,128)(2,1)S(1)} %get-tuple-element.79.refs_0_), channel_id=1, source_target_pairs={{0,1},{1,0},{2,3},{3,2},{4,5},{5,4},{6,7},{7,6},{8,9},{9,8},{10,11... | collective-permute-start | bytes 393224 | tf_op jit(solution)/shard_map/ppermute | solution.py:57
  63.8 4.3 %collective-permute-start.19 = (bf16[256,128]{1,0:T(8,128)(2,1)S(1)}, bf16[256,128]{1,0:T(8,128)(2,1)S(1)}, u32[]{:S(2)}, u32[]{:S(2)}) collective-permute-start(bf16[256,128]{1,0:T(8,128)(2,1)S(1)} %collective-permute-done.17.refs_3_), channel_id=1, source_target_pairs={{0,1},{1,0},{2,3},{3,2},{4,5},{5,4},{6,7},{7,6},{8,9},{9,8},{10,11... | collective-permute-start | bytes 196616 | tf_op jit(solution)/shard_map/ppermute | solution.py:57
  64.2 4.6 %collective-permute-start.18 = (bf16[256,128]{1,0:T(8,128)(2,1)S(1)}, bf16[256,128]{1,0:T(8,128)(2,1)S(1)}, u32[]{:S(2)}, u32[]{:S(2)}) collective-permute-start(bf16[256,128]{1,0:T(8,128)(2,1)S(1)} %collective-permute-done.16.refs_2_), channel_id=1, source_target_pairs={{0,1},{1,0},{2,3},{3,2},{4,5},{5,4},{6,7},{7,6},{8,9},{9,8},{10,11... | collective-permute-start | bytes 196616 | tf_op jit(solution)/shard_map/ppermute | solution.py:57
  72.6 6.4 %collective-permute-start.24 = (bf16[256,256]{1,0:T(8,128)(2,1)S(1)}, bf16[256,256]{1,0:T(8,128)(2,1)S(1)}, u32[]{:S(2)}, u32[]{:S(2)}) collective-permute-start(bf16[256,256]{1,0:T(8,128)(2,1)S(1)} %get-tuple-element.107), channel_id=1, source_target_pairs={{0,1},{1,0},{2,3},{3,2},{4,5},{5,4},{6,7},{7,6},{8,9},{9,8},{10,11... | collective-permute-start | bytes 393224 | tf_op jit(solution)/shard_map/ppermute | solution.py:57
  74.5 10.0 %collective-permute-start.26 = (bf16[256,256]{1,0:T(8,128)(2,1)S(1)}, bf16[256,256]{1,0:T(8,128)(2,1)S(1)}, u32[]{:S(2)}, u32[]{:S(2)}) collective-permute-start(bf16[256,256]{1,0:T(8,128)(2,1)S(1)} %get-tuple-element.109), channel_id=1, source_target_pairs={{0,1},{1,0},{2,3},{3,2},{4,5},{5,4},{6,7},{7,6},{8,9},{9,8},{10,11... | collective-permute-start | bytes 393224 | tf_op jit(solution)/shard_map/ppermute | solution.py:57
  74.7 12.0 %copy-start.16 = (s32[72]{0:T(128)S(1)}, s32[72]{0:T(128)}, u32[]{:S(2)}) copy-start(s32[72]{0:T(128)} %page_table.1) | copy-start | bytes 868
  75.7 18.7 %collective-permute-start.23 = (bf16[512,256]{1,0:T(8,128)(2,1)S(1)}, bf16[512,256]{1,0:T(8,128)(2,1)S(1)}, u32[]{:S(2)}, u32[]{:S(2)}) collective-permute-start(bf16[512,256]{1,0:T(8,128)(2,1)S(1)} %get-tuple-element.105), channel_id=1, source_target_pairs={{0,1},{1,0},{2,3},{3,2},{4,5},{5,4},{6,7},{7,6},{8,9},{9,8},{10,11... | collective-permute-start | bytes 786440 | tf_op jit(solution)/shard_map/ppermute | solution.py:57
  79.0 12.4 %collective-permute-start.25 = (bf16[256,256]{1,0:T(8,128)(2,1)S(1)}, bf16[256,256]{1,0:T(8,128)(2,1)S(1)}, u32[]{:S(2)}, u32[]{:S(2)}) collective-permute-start(bf16[256,256]{1,0:T(8,128)(2,1)S(1)} %add_up.3), channel_id=1, source_target_pairs={{0,2},{1,3},{2,0},{3,1},{4,6},{5,7},{6,4},{7,5},{8,10},{9,11},{10,... | collective-permute-start | bytes 393224 | tf_op jit(solution)/shard_map/ppermute | solution.py:57
  84.6 9.8 %collective-permute-start.27 = (bf16[256,256]{1,0:T(8,128)(2,1)S(1)}, bf16[256,256]{1,0:T(8,128)(2,1)S(1)}, u32[]{:S(2)}, u32[]{:S(2)}) collective-permute-start(bf16[256,256]{1,0:T(8,128)(2,1)S(1)} %add_up.4), channel_id=1, source_target_pairs={{0,2},{1,3},{2,0},{3,1},{4,6},{5,7},{6,4},{7,5},{8,10},{9,11},{10,... | collective-permute-start | bytes 393224 | tf_op jit(solution)/shard_map/ppermute | solution.py:57

commit v10 on v9

--- a/solution.py
+++ b/solution.py
@@ -57,9 +57,11 @@
     return lax.ppermute(value, "tp", [(i, i ^ mask) for i in range(lax.axis_size("tp"))])
 
 
-def pair_gather(shard, split, before=()):
+def pair_gather(shard, split, before=(), near_first=False):
     far = [tp_xor(part, 2) for part in split]
     near = tp_xor(shard, 1)
+    if near_first:
+        far[0], _ = lax.optimization_barrier((far[0], near))
     for i, value in enumerate(before):
         far[i], _ = lax.optimization_barrier((far[i], value))
     return [[shard], [near], far, [tp_xor(part, 1) for part in far]]
@@ -71,9 +73,9 @@
     return [[shard]] + [[lax.ppermute(shard, "tp", each)] for each in pairs]
 
 
-def gather_pieces(shard, split, before=()):
+def gather_pieces(shard, split, before=(), near_first=False):
     if lax.axis_size("tp") == 4:
-        return pair_gather(shard, split, before)
+        return pair_gather(shard, split, before, near_first)
     return turn_gather(shard)
 
 
@@ -258,12 +260,13 @@
     return lax.ppermute(value, "seq", [(i, i ^ mask) for i in range(lax.axis_size("seq"))])
 
 
-def seq_pieces(pairs):
+def seq_pieces(pairs, before):
     if lax.axis_size("seq") == 8:
         diagonal = seq_xor(pairs, 6)
         across = seq_xor(pairs, 2)
         down = seq_xor(pairs, 4)
         twin = seq_xor(pairs, 1)
+        (across, down, diagonal), _ = lax.optimization_barrier(((across, down, diagonal), before))
         across_twin = seq_xor(across, 1)
         down_twin = seq_xor(down, 1)
         diagonal_twin = seq_xor(diagonal, 1)
@@ -716,17 +719,20 @@
         pieces, gain_attn, w_query, w_key, w_value, cosine, sine, extra
     )
     w_out_part, _ = lax.optimization_barrier((w_out_part, pairs))
-    row_pieces = seq_pieces(pairs)
-    w_out_pieces = gather_pieces(w_out_part, [w_out_part])
+    w_out_pieces = gather_pieces(w_out_part, [w_out_part], (), True)
+    if halve:
+        twins = [[piece, seq_xor(piece, 1)] for (piece,) in w_out_pieces[1:-1]]
+        w_out_pieces = w_out_pieces[:1] + twins + w_out_pieces[-1:]
+    row_pieces = seq_pieces(pairs, w_out_pieces[1:-1])
     marks, w_out_pieces = lax.optimization_barrier((marks, w_out_pieces))
     attended, *halves = attend(lengths, queries, marks, row_pieces, heads, reach)
     large = (w_out, token_rows, gain_ffn, w_gate, w_up, w_down)
-    large, w_out_pieces = lax.optimization_barrier((large, w_out_pieces, attended))[:2]
+    large, last = lax.optimization_barrier((large, w_out_pieces[-1], attended))[:2]
     w_out, *large = fetch(large)
     if halve:
-        twins = [[piece, seq_xor(piece, 1)] for (piece,) in w_out_pieces[1:]]
-        w_out_pieces = [[w_out]] + twins
-    attended_pieces = gather_pieces(attended, halves, large[1:2])
+        w_out_pieces[0] = [w_out]
+        w_out_pieces[-1] = [last[0], seq_xor(last[0], 1)]
+    attended_pieces = gather_pieces(attended, halves, large[1:2], True)
     mixed, joined = feed_forward(attended_pieces, w_out_pieces, *large)
     row_pieces, _ = lax.optimization_barrier((row_pieces, joined))
     cache = fill_cache(lengths, page_table, row_pieces, rows)

time: 95 us -> 93 us (0.979); the launches traced: 95.2 us -> 92.1 us
  starting transfers between devices: 36.5 us -> 29.1 us
  waiting for transfers between devices: 30.4 us -> 34.7 us
    ppermute x18, waiting for transfers between devices: 23.1 us -> 33.3 us  [tp_xor(): lax.ppermute(value, 'tp', [(i, i ^ mask) for i in range(lax.axis_size('tp...]
    ppermute x18, starting transfers between devices: 32 us -> 24.1 us  [tp_xor(): lax.ppermute(value, 'tp', [(i, i ^ mask) for i in range(lax.axis_size('tp...]
    ppermute x10, waiting for transfers between devices: 7.23 us -> 1.4 us  [seq_xor(): lax.ppermute(value, 'seq', [(i, i ^ mask) for i in range(lax.axis_size('s...]
  transfers between devices with their start and end apart: 28 -> 28, of which waited for: 16 -> 15; matrix products, arithmetic and copies ran while one was open for 0% -> 0% of each run, Pallas kernels for 8% -> 8%
where the time goes in v10:
time: 93 us; the launch traced here: 92.1 us
  waiting for transfers between devices  34.7 us (37%)
  starting transfers between devices  29.1 us (31%)
  Pallas kernels  18.3 us (20%)
  local copies, waits for them, and re-layouts  9.19 us (10%)
    ppermute x18, waiting for transfers between devices, tp_xor(): lax.ppermute(value, 'tp', [(i, i ^ mask) for i in range(lax.axis_size('tp...  33.3 us
    ppermute x18, starting transfers between devices, tp_xor(): lax.ppermute(value, 'tp', [(i, i ^ mask) for i in range(lax.axis_size('tp...  24.1 us
    unnamed x34, local copies, waits for them, and re-layouts  8.19 us
    ppermute x10, starting transfers between devices, seq_xor(): lax.ppermute(value, 'seq', [(i, i ^ mask) for i in range(lax.axis_size('s...  5.02 us
    pallas_call x1, Pallas kernels, attend(): pl.pallas_call(functools.partial(attend_kernel, len(pieces), heads, reach...  4.73 us
    pallas_call x1, Pallas kernels, fill_cache(): pl.pallas_call(functools.partial(cache_kernel, len(pieces), 2 * PAGE), ou...  4.69 us
    pallas_call x1, Pallas kernels, hidden_of(): pl.pallas_call(functools.partial(hidden_kernel, *counts), out_shape=[jax....  3.82 us
  transfers between devices with their start and end apart: 28, of which 15 were waited for; matrix products, arithmetic and copies ran while one was open for 0% of the time, Pallas kernels for 8%

profile of v10, /device:TPU:2, one launch (start us, length us, event | category | flops | bytes accessed | tf_op | source)
XLA Modules:
  0.0 92.1 jit_solution(7791510584085850106)
XLA Ops:
  0.6 1.0 %fusion = (bf16[256,256]{1,0:T(8,128)(2,1)S(1)}, bf16[256,256]{1,0:T(8,128)(2,1)S(1)}) fusion(bf16[512,256]{1,0:T(8,128)(2,1)} %refs_0_.2), kind=kLoop, calls=%fused_computation | loop fusion | bytes 524288 | tf_op jit(solution)/shard_map/slice | solution.py:715
  1.6 2.7 %collective-permute-start.2 = (bf16[256,256]{1,0:T(8,128)(2,1)S(1)}, bf16[256,256]{1,0:T(8,128)(2,1)S(1)}, u32[]{:S(2)}, u32[]{:S(2)}) collective-permute-start(bf16[256,256]{1,0:T(8,128)(2,1)S(1)} %get-tuple-element.70), channel_id=1, source_target_pairs={{0,2},{1,3},{2,0},{3,1},{4,6},{5,7},{6,4},{7,5},{8,10},{9,11},{10,... | collective-permute-start | bytes 393224 | tf_op jit(solution)/shard_map/ppermute | solution.py:57
  4.6 1.6 %collective-permute-start = (bf16[512,256]{1,0:T(8,128)(2,1)}, bf16[512,256]{1,0:T(8,128)(2,1)S(1)}, u32[]{:S(2)}, u32[]{:S(2)}) collective-permute-start(bf16[512,256]{1,0:T(8,128)(2,1)} %refs_0_.2), channel_id=1, source_target_pairs={{0,1},{1,0},{2,3},{3,2},{4,5},{5,4},{6,7},{7,6},{8,9},{9,8},{10,11... | collective-permute-start | bytes 786440 | tf_op jit(solution)/shard_map/ppermute | solution.py:57
  6.2 1.0 %copy-done.5 = bf16[512,256]{1,0:T(8,128)(2,1)S(1)} copy-done((bf16[512,256]{1,0:T(8,128)(2,1)S(1)}, bf16[512,256]{1,0:T(8,128)(2,1)}, u32[]{:S(2)}) %copy-start.5) | copy-done | bytes 262168
  7.2 0.9 %copy-done.6 = bf16[1024,128]{1,0:T(8,128)(2,1)S(1)} copy-done((bf16[1024,128]{1,0:T(8,128)(2,1)S(1)}, bf16[1024,128]{1,0:T(8,128)(2,1)}, u32[]{:S(2)}) %copy-start.6) | copy-done | bytes 262168
  8.1 0.7 copy-done.9
  8.9 0.9 %copy-done.3 = bf16[128,1024]{1,0:T(8,128)(2,1)S(1)} copy-done((bf16[128,1024]{1,0:T(8,128)(2,1)S(1)}, bf16[128,1024]{1,0:T(8,128)(2,1)}, u32[]{:S(2)}) %copy-start.3) | copy-done | bytes 262168
  9.9 0.9 %copy-done.7 = bf16[1024,128]{1,0:T(8,128)(2,1)S(1)} copy-done((bf16[1024,128]{1,0:T(8,128)(2,1)S(1)}, bf16[1024,128]{1,0:T(8,128)(2,1)}, u32[]{:S(2)}) %copy-start.7) | copy-done | bytes 262168
  10.8 0.9 %copy-done.8 = bf16[1024,128]{1,0:T(8,128)(2,1)S(1)} copy-done((bf16[1024,128]{1,0:T(8,128)(2,1)S(1)}, bf16[1024,128]{1,0:T(8,128)(2,1)}, u32[]{:S(2)}) %copy-start.8) | copy-done | bytes 262168
  11.8 0.7 copy-done.10
  12.4 0.7 copy-done.11
  13.1 0.7 copy-done.13
  13.8 0.7 copy-done.15
  14.4 1.1 %tables.1 = (f32[512,128]{1,0:T(8,128)S(1)}, f32[512,128]{1,0:T(8,128)S(1)}, bf16[16,256]{1,0:T(8,128)(2,1)S(1)}, bf16[2,512,128]{2,1,0:T(8,128)(2,1)S(1)}, bf16...) custom-call(s32[4]{0:T(128)S(1)} %copy-done.13, f32[2,2]{1,0:T(2,128)S(1)} %copy-done.15, ...), custom_call_target="tpu_custom_call" | custom-call | flops 524288 | bytes 1048576 | tf_op jit(solution)/shard_map/tables/pallas_call | solution.py:169
  15.6 0.5 collective-permute-start.4
  16.4 1.3 %collective-permute-start.3 = (bf16[256,256]{1,0:T(8,128)(2,1)S(1)}, bf16[256,256]{1,0:T(8,128)(2,1)S(1)}, u32[]{:S(2)}, u32[]{:S(2)}) collective-permute-start(bf16[256,256]{1,0:T(8,128)(2,1)S(1)} %collective-permute-done.1.refs_2_), channel_id=1, source_target_pairs={{0,1},{1,0},{2,3},{3,2},{4,5},{5,4},{6,7},{7,6},{8,9},{9,8},{10,11... | collective-permute-start | bytes 393224 | tf_op jit(solution)/shard_map/ppermute | solution.py:57
  17.7 3.8 %collective-permute-done.4.refs_5_ = bf16[256,256]{1,0:T(8,128)(2,1)S(1)} collective-permute-done((bf16[256,256]{1,0:T(8,128)(2,1)S(1)}, bf16[256,256]{1,0:T(8,128)(2,1)S(1)}, u32[]{:S(2)}, u32[]{:S(2)}) %collective-permute-start.4) | collective-permute-done | bytes 131104 | tf_op jit(solution)/shard_map/ppermute | solution.py:57
  21.5 1.4 %collective-permute-done.3.refs_4_ = bf16[256,256]{1,0:T(8,128)(2,1)S(1)} collective-permute-done((bf16[256,256]{1,0:T(8,128)(2,1)S(1)}, bf16[256,256]{1,0:T(8,128)(2,1)S(1)}, u32[]{:S(2)}, u32[]{:S(2)}) %collective-permute-start.3) | collective-permute-done | bytes 131104 | tf_op jit(solution)/shard_map/ppermute | solution.py:57
  22.9 1.4 %project.1 = (bf16[512,1024]{1,0:T(8,128)(2,1)S(1)}, bf16[512,128]{1,0:T(8,128)(2,1)S(1)}, bf16[528,256]{1,0:T(8,128)(2,1)S(1)}) custom-call(bf16[512,256]{1,0:T(8,128)(2,1)S(1)} %get-tuple-element.65.refs_0_, bf16[512,256]{1,0:T(8,128)(2,1)S(1)} %collective-permute-done.refs_1_, bf16[256,256]{1,0:T(8,128)(2,1)S(1)} %collective-permute-done.1.refs_2_, ...), custom_call_target="tpu_custom_call" | custom-call | flops 402653184 | bytes 4194304 | tf_op jit(solution)/shard_map/project/pallas_call | solution.py:243
  24.3 1.6 %collective-permute-start.13 = (bf16[528,256]{1,0:T(8,128)(2,1)S(1)}, bf16[528,256]{1,0:T(8,128)(2,1)S(1)}, u32[]{:S(2)}, u32[]{:S(2)}) collective-permute-start(bf16[528,256]{1,0:T(8,128)(2,1)S(1)} %get-tuple-element.120.refs_0_), channel_id=1, source_target_pairs={{0,24},{4,28},{8,16},{12,20},{16,8},{20,12},{24,0},{28,4},{1,25},{... | collective-permute-start | bytes 811016 | tf_op jit(solution)/shard_map/ppermute | solution.py:260
  25.9 0.5 collective-permute-start.12
  26.4 1.5 %collective-permute-start.11 = (bf16[528,256]{1,0:T(8,128)(2,1)S(1)}, bf16[528,256]{1,0:T(8,128)(2,1)S(1)}, u32[]{:S(2)}, u32[]{:S(2)}) collective-permute-start(bf16[528,256]{1,0:T(8,128)(2,1)S(1)} %get-tuple-element.120.refs_0_), channel_id=1, source_target_pairs={{0,8},{4,12},{8,0},{12,4},{16,24},{20,28},{24,16},{28,20},{1,9},{5... | collective-permute-start | bytes 811016 | tf_op jit(solution)/shard_map/ppermute | solution.py:260
  27.9 2.6 %collective-permute-start.7 = (bf16[128,512]{1,0:T(8,128)(2,1)S(1)}, bf16[128,512]{1,0:T(8,128)(2,1)S(1)}, u32[]{:S(2)}, u32[]{:S(2)}) collective-permute-start(bf16[128,512]{1,0:T(8,128)(2,1)S(1)} %get-tuple-element.82), channel_id=1, source_target_pairs={{0,2},{1,3},{2,0},{3,1},{4,6},{5,7},{6,4},{7,5},{8,10},{9,11},{10,... | collective-permute-start | bytes 393224 | tf_op jit(solution)/shard_map/ppermute | solution.py:57
  30.5 2.2 %collective-permute-start.5 = (bf16[128,512]{1,0:T(8,128)(2,1)S(1)}, bf16[128,512]{1,0:T(8,128)(2,1)S(1)}, u32[]{:S(2)}, u32[]{:S(2)}) collective-permute-start(bf16[128,512]{1,0:T(8,128)(2,1)S(1)} %get-tuple-element.82), channel_id=1, source_target_pairs={{0,1},{1,0},{2,3},{3,2},{4,5},{5,4},{6,7},{7,6},{8,9},{9,8},{10,11... | collective-permute-start | bytes 393224 | tf_op jit(solution)/shard_map/ppermute | solution.py:57
  32.6 2.7 %collective-permute-done.7.refs_9_ = bf16[128,512]{1,0:T(8,128)(2,1)S(1)} collective-permute-done((bf16[128,512]{1,0:T(8,128)(2,1)S(1)}, bf16[128,512]{1,0:T(8,128)(2,1)S(1)}, u32[]{:S(2)}, u32[]{:S(2)}) %collective-permute-start.7) | collective-permute-done | bytes 131104 | tf_op jit(solution)/shard_map/ppermute | solution.py:57
  35.6 0.5 collective-permute-start.6
  36.1 0.8 collective-permute-done.8.refs_10_
  37.7 0.5 collective-permute-start.15
  38.2 1.8 %collective-permute-start.9 = (bf16[128,512]{1,0:T(8,128)(2,1)S(1)}, bf16[128,512]{1,0:T(8,128)(2,1)S(1)}, u32[]{:S(2)}, u32[]{:S(2)}) collective-permute-start(bf16[128,512]{1,0:T(8,128)(2,1)S(1)} %collective-permute-done.7.refs_9_), channel_id=1, source_target_pairs={{0,1},{1,0},{2,3},{3,2},{4,5},{5,4},{6,7},{7,6},{8,9},{9,8},{10,11... | collective-permute-start | bytes 393224 | tf_op jit(solution)/shard_map/ppermute | solution.py:57
  40.0 4.1 %collective-permute-done.9.refs_11_ = bf16[128,512]{1,0:T(8,128)(2,1)S(1)} collective-permute-done((bf16[128,512]{1,0:T(8,128)(2,1)S(1)}, bf16[128,512]{1,0:T(8,128)(2,1)S(1)}, u32[]{:S(2)}, u32[]{:S(2)}) %collective-permute-start.9) | collective-permute-done | bytes 131104 | tf_op jit(solution)/shard_map/ppermute | solution.py:57
  44.2 4.7 %attend.1 = (bf16[512,128]{1,0:T(8,128)(2,1)S(1)}, bf16[256,128]{1,0:T(8,128)(2,1)S(1)}, bf16[256,128]{1,0:T(8,128)(2,1)S(1)}) custom-call(s32[4]{0:T(128)S(1)} %copy-done.14, bf16[512,128]{1,0:T(8,128)(2,1)S(1)} %get-tuple-element.78.queries, bf16[2,512,128]{2,1,0:T(8,128)(2,1)S(1)} %get-tuple-element.84.query_marks, ...), custom_call_target="tpu_custom_call" | custom-call | flops 2684354560 | bytes 4194304 | tf_op jit(solution)/shard_map/attend/pallas_call | solution.py:413
  48.9 1.6 %collective-permute-start.17 = (bf16[512,128]{1,0:T(8,128)(2,1)S(1)}, bf16[512,128]{1,0:T(8,128)(2,1)S(1)}, u32[]{:S(2)}, u32[]{:S(2)}) collective-permute-start(bf16[512,128]{1,0:T(8,128)(2,1)S(1)} %get-tuple-element.88.refs_0_), channel_id=1, source_target_pairs={{0,1},{1,0},{2,3},{3,2},{4,5},{5,4},{6,7},{7,6},{8,9},{9,8},{10,11... | collective-permute-start | bytes 393224 | tf_op jit(solution)/shard_map/ppermute | solution.py:57
  50.5 3.7 %collective-permute-start.18 = (bf16[256,128]{1,0:T(8,128)(2,1)S(1)}, bf16[256,128]{1,0:T(8,128)(2,1)S(1)}, u32[]{:S(2)}, u32[]{:S(2)}) collective-permute-start(bf16[256,128]{1,0:T(8,128)(2,1)S(1)} %get-tuple-element.89), channel_id=1, source_target_pairs={{0,2},{1,3},{2,0},{3,1},{4,6},{5,7},{6,4},{7,5},{8,10},{9,11},{10,... | collective-permute-start | bytes 196616 | tf_op jit(solution)/shard_map/ppermute | solution.py:57
  54.6 0.6 fetch.3
  55.1 7.1 %collective-permute-done.19.refs_3_ = bf16[256,128]{1,0:T(8,128)(2,1)S(1)} collective-permute-done((bf16[256,128]{1,0:T(8,128)(2,1)S(1)}, bf16[256,128]{1,0:T(8,128)(2,1)S(1)}, u32[]{:S(2)}, u32[]{:S(2)}) %collective-permute-start.19) | collective-permute-done | bytes 65568 | tf_op jit(solution)/shard_map/ppermute | solution.py:57
  62.2 2.0 %collective-permute-start.20 = (bf16[256,128]{1,0:T(8,128)(2,1)S(1)}, bf16[256,128]{1,0:T(8,128)(2,1)S(1)}, u32[]{:S(2)}, u32[]{:S(2)}) collective-permute-start(bf16[256,128]{1,0:T(8,128)(2,1)S(1)} %collective-permute-done.18.refs_2_), channel_id=1, source_target_pairs={{0,1},{1,0},{2,3},{3,2},{4,5},{5,4},{6,7},{7,6},{8,9},{9,8},{10,11... | collective-permute-start | bytes 196616 | tf_op jit(solution)/shard_map/ppermute | solution.py:57
  64.2 2.4 %collective-permute-done.21.refs_5_ = bf16[256,128]{1,0:T(8,128)(2,1)S(1)} collective-permute-done((bf16[256,128]{1,0:T(8,128)(2,1)S(1)}, bf16[256,128]{1,0:T(8,128)(2,1)S(1)}, u32[]{:S(2)}, u32[]{:S(2)}) %collective-permute-start.21) | collective-permute-done | bytes 65568 | tf_op jit(solution)/shard_map/ppermute | solution.py:57
  66.7 0.7 collective-permute-done.20.refs_4_
  67.4 3.8 %hidden.1 = (bf16[512,1024]{1,0:T(8,128)(2,1)S(1)}, bf16[512,256]{1,0:T(8,128)(2,1)S(1)}, bf16[256,256]{1,0:T(8,128)(2,1)S(1)}, bf16[256,256]{1,0:T(8,128)(2,1)S(1)}) custom-call(bf16[512,128]{1,0:T(8,128)(2,1)S(1)} %get-tuple-element.88.refs_0_, bf16[512,128]{1,0:T(8,128)(2,1)S(1)} %collective-permute-done.17.refs_1_, ...), custom_call_target="tpu_custom_call" | custom-call | flops 3221225472 | bytes 10485760 | tf_op jit(solution)/shard_map/hidden/pallas_call | solution.py:599
  71.2 1.2 %collective-permute-start.24 = (bf16[256,256]{1,0:T(8,128)(2,1)S(1)}, bf16[256,256]{1,0:T(8,128)(2,1)S(1)}, u32[]{:S(2)}, u32[]{:S(2)}) collective-permute-start(bf16[256,256]{1,0:T(8,128)(2,1)S(1)} %get-tuple-element.117), channel_id=1, source_target_pairs={{0,1},{1,0},{2,3},{3,2},{4,5},{5,4},{6,7},{7,6},{8,9},{9,8},{10,11... | collective-permute-start | bytes 393224 | tf_op jit(solution)/shard_map/ppermute | solution.py:57
  72.4 0.9 %collective-permute-start.26 = (bf16[256,256]{1,0:T(8,128)(2,1)S(1)}, bf16[256,256]{1,0:T(8,128)(2,1)S(1)}, u32[]{:S(2)}, u32[]{:S(2)}) collective-permute-start(bf16[256,256]{1,0:T(8,128)(2,1)S(1)} %get-tuple-element.119), channel_id=1, source_target_pairs={{0,1},{1,0},{2,3},{3,2},{4,5},{5,4},{6,7},{7,6},{8,9},{9,8},{10,11... | collective-permute-start | bytes 393224 | tf_op jit(solution)/shard_map/ppermute | solution.py:57
  73.3 1.0 %down_blocks.1 = (f32[256,256]{1,0:T(8,128)S(1)}, f32[256,256]{1,0:T(8,128)S(1)}, bf16[512,256]{1,0:T(8,128)(2,1)S(1)}, f32[512,256]{1,0:T(8,128)S(1)}) custom-call(bf16[512,1024]{1,0:T(8,128)(2,1)S(1)} %get-tuple-element.112.hidden, bf16[512,256]{1,0:T(8,128)(2,1)S(1)} %get-tuple-element.113.kept, bf16[1024,1024]{1,0:T(8,128)(2,1)S(1)} %get-tuple-element.111.refs_17_.w_down), custom_call_target="tpu_custom_call" | custom-call | flops 805306368 | bytes 5242880 | tf_op jit(solution)/shard_map/down_blocks/pallas_call | solution.py:633
  74.3 1.2 %collective-permute-start.23 = (bf16[512,256]{1,0:T(8,128)(2,1)S(1)}, bf16[512,256]{1,0:T(8,128)(2,1)S(1)}, u32[]{:S(2)}, u32[]{:S(2)}) collective-permute-start(bf16[512,256]{1,0:T(8,128)(2,1)S(1)} %get-tuple-element.115), channel_id=1, source_target_pairs={{0,1},{1,0},{2,3},{3,2},{4,5},{5,4},{6,7},{7,6},{8,9},{9,8},{10,11... | collective-permute-start | bytes 786440 | tf_op jit(solution)/shard_map/ppermute | solution.py:57
  75.5 3.6 %collective-permute-done.24.refs_1_ = bf16[256,256]{1,0:T(8,128)(2,1)S(1)} collective-permute-done((bf16[256,256]{1,0:T(8,128)(2,1)S(1)}, bf16[256,256]{1,0:T(8,128)(2,1)S(1)}, u32[]{:S(2)}, u32[]{:S(2)}) %collective-permute-start.24) | collective-permute-done | bytes 131104 | tf_op jit(solution)/shard_map/ppermute | solution.py:57
  79.2 4.1 %collective-permute-done.26.refs_1_ = bf16[256,256]{1,0:T(8,128)(2,1)S(1)} collective-permute-done((bf16[256,256]{1,0:T(8,128)(2,1)S(1)}, bf16[256,256]{1,0:T(8,128)(2,1)S(1)}, u32[]{:S(2)}, u32[]{:S(2)}) %collective-permute-start.26) | collective-permute-done | bytes 131104 | tf_op jit(solution)/shard_map/ppermute | solution.py:57
  83.8 4.7 %fill_cache.1 = bf16[576,2,128]{2,1,0:T(2,128)(2,1)} custom-call(s32[4]{0:T(128)S(1)} %copy-done.14, s32[72]{0:T(128)S(1)} %copy-done.16, bf16[528,256]{1,0:T(8,128)(2,1)S(1)} %get-tuple-element.120.refs_0_, bf16[528,256]{1,0:T(8,128)(2,1)S(1)} %collective-permute-done.10.refs_1_, bf16[528,256]{1,0:T(8,128)(2,1)S(1)} %collective-permute-done.11.refs_2_, ...), custom_call_target="tpu_custom_call" | custom-call | flops 75497472 | bytes 3145728 | tf_op jit(solution)/shard_map/fill_cache/pallas_call | solution.py:512
  88.5 2.8 %collective-permute-done.27.refs_3_ = bf16[256,256]{1,0:T(8,128)(2,1)S(1)} collective-permute-done((bf16[256,256]{1,0:T(8,128)(2,1)S(1)}, bf16[256,256]{1,0:T(8,128)(2,1)S(1)}, u32[]{:S(2)}, u32[]{:S(2)}) %collective-permute-start.27) | collective-permute-done | bytes 131104 | tf_op jit(solution)/shard_map/ppermute | solution.py:57
  91.3 0.8 add_up.5
  (54 shorter events, 2.7 us)
Async XLA Ops:
  0.6 43.5 %copy-start.14 = (s32[4]{0:T(128)S(1)}, s32[4]{0:T(128)}, u32[]{:S(2)}) copy-start(s32[4]{0:T(128)} %lengths.5) | copy-start | bytes 52
  1.6 14.0 %collective-permute-start.2 = (bf16[256,256]{1,0:T(8,128)(2,1)S(1)}, bf16[256,256]{1,0:T(8,128)(2,1)S(1)}, u32[]{:S(2)}, u32[]{:S(2)}) collective-permute-start(bf16[256,256]{1,0:T(8,128)(2,1)S(1)} %get-tuple-element.70), channel_id=1, source_target_pairs={{0,2},{1,3},{2,0},{3,1},{4,6},{5,7},{6,4},{7,5},{8,10},{9,11},{10,... | collective-permute-start | bytes 393224 | tf_op jit(solution)/shard_map/ppermute | solution.py:57
  4.3 12.1 %collective-permute-start.1 = (bf16[256,256]{1,0:T(8,128)(2,1)S(1)}, bf16[256,256]{1,0:T(8,128)(2,1)S(1)}, u32[]{:S(2)}, u32[]{:S(2)}) collective-permute-start(bf16[256,256]{1,0:T(8,128)(2,1)S(1)} %get-tuple-element.67), channel_id=1, source_target_pairs={{0,2},{1,3},{2,0},{3,1},{4,6},{5,7},{6,4},{7,5},{8,10},{9,11},{10,... | collective-permute-start | bytes 393224 | tf_op jit(solution)/shard_map/ppermute | solution.py:57
  4.6 13.1 %collective-permute-start = (bf16[512,256]{1,0:T(8,128)(2,1)}, bf16[512,256]{1,0:T(8,128)(2,1)S(1)}, u32[]{:S(2)}, u32[]{:S(2)}) collective-permute-start(bf16[512,256]{1,0:T(8,128)(2,1)} %refs_0_.2), channel_id=1, source_target_pairs={{0,1},{1,0},{2,3},{3,2},{4,5},{5,4},{6,7},{7,6},{8,9},{9,8},{10,11... | collective-permute-start | bytes 786440 | tf_op jit(solution)/shard_map/ppermute | solution.py:57
  6.2 1.0 %copy-start.5 = (bf16[512,256]{1,0:T(8,128)(2,1)S(1)}, bf16[512,256]{1,0:T(8,128)(2,1)}, u32[]{:S(2)}) copy-start(bf16[512,256]{1,0:T(8,128)(2,1)} %refs_0_.2) | copy-start | bytes 786436
  7.2 0.9 %copy-start.6 = (bf16[1024,128]{1,0:T(8,128)(2,1)S(1)}, bf16[1024,128]{1,0:T(8,128)(2,1)}, u32[]{:S(2)}) copy-start(bf16[1024,128]{1,0:T(8,128)(2,1)} %refs_2_.2) | copy-start | bytes 786436
  8.1 0.7 copy-start.9
  8.9 1.0 %copy-start.3 = (bf16[128,1024]{1,0:T(8,128)(2,1)S(1)}, bf16[128,1024]{1,0:T(8,128)(2,1)}, u32[]{:S(2)}) copy-start(bf16[128,1024]{1,0:T(8,128)(2,1)} %refs_0_.4) | copy-start | bytes 786436
  9.8 0.9 %copy-start.7 = (bf16[1024,128]{1,0:T(8,128)(2,1)S(1)}, bf16[1024,128]{1,0:T(8,128)(2,1)}, u32[]{:S(2)}) copy-start(bf16[1024,128]{1,0:T(8,128)(2,1)} %refs_0_.3) | copy-start | bytes 786436
  10.8 0.9 %copy-start.8 = (bf16[1024,128]{1,0:T(8,128)(2,1)S(1)}, bf16[1024,128]{1,0:T(8,128)(2,1)}, u32[]{:S(2)}) copy-start(bf16[1024,128]{1,0:T(8,128)(2,1)} %refs_1_.3) | copy-start | bytes 786436
  11.8 0.7 copy-start.10
  12.4 0.7 copy-start.11
  13.1 0.7 copy-start.13
  13.8 0.7 copy-start.15
  15.6 5.9 %collective-permute-start.4 = (bf16[256,256]{1,0:T(8,128)(2,1)S(1)}, bf16[256,256]{1,0:T(8,128)(2,1)S(1)}, u32[]{:S(2)}, u32[]{:S(2)}) collective-permute-start(bf16[256,256]{1,0:T(8,128)(2,1)S(1)} %collective-permute-done.2.refs_3_), channel_id=1, source_target_pairs={{0,1},{1,0},{2,3},{3,2},{4,5},{5,4},{6,7},{7,6},{8,9},{9,8},{10,11... | collective-permute-start | bytes 393224 | tf_op jit(solution)/shard_map/ppermute | solution.py:57
  16.4 6.5 %collective-permute-start.3 = (bf16[256,256]{1,0:T(8,128)(2,1)S(1)}, bf16[256,256]{1,0:T(8,128)(2,1)S(1)}, u32[]{:S(2)}, u32[]{:S(2)}) collective-permute-start(bf16[256,256]{1,0:T(8,128)(2,1)S(1)} %collective-permute-done.1.refs_2_), channel_id=1, source_target_pairs={{0,1},{1,0},{2,3},{3,2},{4,5},{5,4},{6,7},{7,6},{8,9},{9,8},{10,11... | collective-permute-start | bytes 393224 | tf_op jit(solution)/shard_map/ppermute | solution.py:57
  24.3 12.8 %collective-permute-start.13 = (bf16[528,256]{1,0:T(8,128)(2,1)S(1)}, bf16[528,256]{1,0:T(8,128)(2,1)S(1)}, u32[]{:S(2)}, u32[]{:S(2)}) collective-permute-start(bf16[528,256]{1,0:T(8,128)(2,1)S(1)} %get-tuple-element.120.refs_0_), channel_id=1, source_target_pairs={{0,24},{4,28},{8,16},{12,20},{16,8},{20,12},{24,0},{28,4},{1,25},{... | collective-permute-start | bytes 811016 | tf_op jit(solution)/shard_map/ppermute | solution.py:260
  25.9 11.7 %collective-permute-start.12 = (bf16[528,256]{1,0:T(8,128)(2,1)S(1)}, bf16[528,256]{1,0:T(8,128)(2,1)S(1)}, u32[]{:S(2)}, u32[]{:S(2)}) collective-permute-start(bf16[528,256]{1,0:T(8,128)(2,1)S(1)} %get-tuple-element.120.refs_0_), channel_id=1, source_target_pairs={{0,16},{4,20},{8,24},{12,28},{16,0},{20,4},{24,8},{28,12},{1,17},{... | collective-permute-start | bytes 811016 | tf_op jit(solution)/shard_map/ppermute | solution.py:260
  26.4 11.3 %collective-permute-start.11 = (bf16[528,256]{1,0:T(8,128)(2,1)S(1)}, bf16[528,256]{1,0:T(8,128)(2,1)S(1)}, u32[]{:S(2)}, u32[]{:S(2)}) collective-permute-start(bf16[528,256]{1,0:T(8,128)(2,1)S(1)} %get-tuple-element.120.refs_0_), channel_id=1, source_target_pairs={{0,8},{4,12},{8,0},{12,4},{16,24},{20,28},{24,16},{28,20},{1,9},{5... | collective-permute-start | bytes 811016 | tf_op jit(solution)/shard_map/ppermute | solution.py:260
  27.9 7.4 %collective-permute-start.7 = (bf16[128,512]{1,0:T(8,128)(2,1)S(1)}, bf16[128,512]{1,0:T(8,128)(2,1)S(1)}, u32[]{:S(2)}, u32[]{:S(2)}) collective-permute-start(bf16[128,512]{1,0:T(8,128)(2,1)S(1)} %get-tuple-element.82), channel_id=1, source_target_pairs={{0,2},{1,3},{2,0},{3,1},{4,6},{5,7},{6,4},{7,5},{8,10},{9,11},{10,... | collective-permute-start | bytes 393224 | tf_op jit(solution)/shard_map/ppermute | solution.py:57
  30.5 5.2 %collective-permute-start.5 = (bf16[128,512]{1,0:T(8,128)(2,1)S(1)}, bf16[128,512]{1,0:T(8,128)(2,1)S(1)}, u32[]{:S(2)}, u32[]{:S(2)}) collective-permute-start(bf16[128,512]{1,0:T(8,128)(2,1)S(1)} %get-tuple-element.82), channel_id=1, source_target_pairs={{0,1},{1,0},{2,3},{3,2},{4,5},{5,4},{6,7},{7,6},{8,9},{9,8},{10,11... | collective-permute-start | bytes 393224 | tf_op jit(solution)/shard_map/ppermute | solution.py:57
  35.6 1.3 %collective-permute-start.8 = (bf16[128,512]{1,0:T(8,128)(2,1)S(1)}, bf16[128,512]{1,0:T(8,128)(2,1)S(1)}, u32[]{:S(2)}, u32[]{:S(2)}) collective-permute-start(bf16[128,512]{1,0:T(8,128)(2,1)S(1)} %collective-permute-done.7.refs_9_), channel_id=1, source_target_pairs={{0,4},{4,0},{8,12},{12,8},{16,20},{20,16},{24,28},{28,24},{1,5},{5... | collective-permute-start | bytes 393224 | tf_op jit(solution)/shard_map/ppermute | solution.py:260
  35.6 1.5 %collective-permute-start.6 = (bf16[128,512]{1,0:T(8,128)(2,1)S(1)}, bf16[128,512]{1,0:T(8,128)(2,1)S(1)}, u32[]{:S(2)}, u32[]{:S(2)}) collective-permute-start(bf16[128,512]{1,0:T(8,128)(2,1)S(1)} %collective-permute-done.5.refs_7_), channel_id=1, source_target_pairs={{0,4},{4,0},{8,12},{12,8},{16,20},{20,16},{24,28},{28,24},{1,5},{5... | collective-permute-start | bytes 393224 | tf_op jit(solution)/shard_map/ppermute | solution.py:260
  37.0 7.1 %collective-permute-start.10 = (bf16[528,256]{1,0:T(8,128)(2,1)S(1)}, bf16[528,256]{1,0:T(8,128)(2,1)S(1)}, u32[]{:S(2)}, u32[]{:S(2)}) collective-permute-start(bf16[528,256]{1,0:T(8,128)(2,1)S(1)} %get-tuple-element.120.refs_0_), channel_id=1, source_target_pairs={{0,4},{4,0},{8,12},{12,8},{16,20},{20,16},{24,28},{28,24},{1,5},{5... | collective-permute-start | bytes 811016 | tf_op jit(solution)/shard_map/ppermute | solution.py:260
  37.7 6.4 %collective-permute-start.14 = (bf16[528,256]{1,0:T(8,128)(2,1)S(1)}, bf16[528,256]{1,0:T(8,128)(2,1)S(1)}, u32[]{:S(2)}, u32[]{:S(2)}) collective-permute-start(bf16[528,256]{1,0:T(8,128)(2,1)S(1)} %collective-permute-done.11.refs_2_), channel_id=1, source_target_pairs={{0,4},{4,0},{8,12},{12,8},{16,20},{20,16},{24,28},{28,24},{1,5},{5... | collective-permute-start | bytes 811016 | tf_op jit(solution)/shard_map/ppermute | solution.py:260
  37.7 6.4 %collective-permute-start.15 = (bf16[528,256]{1,0:T(8,128)(2,1)S(1)}, bf16[528,256]{1,0:T(8,128)(2,1)S(1)}, u32[]{:S(2)}, u32[]{:S(2)}) collective-permute-start(bf16[528,256]{1,0:T(8,128)(2,1)S(1)} %collective-permute-done.12.refs_4_), channel_id=1, source_target_pairs={{0,4},{4,0},{8,12},{12,8},{16,20},{20,16},{24,28},{28,24},{1,5},{5... | collective-permute-start | bytes 811016 | tf_op jit(solution)/shard_map/ppermute | solution.py:260
  38.2 5.9 %collective-permute-start.16 = (bf16[528,256]{1,0:T(8,128)(2,1)S(1)}, bf16[528,256]{1,0:T(8,128)(2,1)S(1)}, u32[]{:S(2)}, u32[]{:S(2)}) collective-permute-start(bf16[528,256]{1,0:T(8,128)(2,1)S(1)} %collective-permute-done.13.refs_6_), channel_id=1, source_target_pairs={{0,4},{4,0},{8,12},{12,8},{16,20},{20,16},{24,28},{28,24},{1,5},{5... | collective-permute-start | bytes 811016 | tf_op jit(solution)/shard_map/ppermute | solution.py:260
  38.2 5.9 %collective-permute-start.9 = (bf16[128,512]{1,0:T(8,128)(2,1)S(1)}, bf16[128,512]{1,0:T(8,128)(2,1)S(1)}, u32[]{:S(2)}, u32[]{:S(2)}) collective-permute-start(bf16[128,512]{1,0:T(8,128)(2,1)S(1)} %collective-permute-done.7.refs_9_), channel_id=1, source_target_pairs={{0,1},{1,0},{2,3},{3,2},{4,5},{5,4},{6,7},{7,6},{8,9},{9,8},{10,11... | collective-permute-start | bytes 393224 | tf_op jit(solution)/shard_map/ppermute | solution.py:57
  44.1 10.4 %copy-start = (bf16[1024,1024]{1,0:T(8,128)(2,1)S(1)}, bf16[1024,1024]{1,0:T(8,128)(2,1)}, u32[]{:S(2)}) copy-start(bf16[1024,1024]{1,0:T(8,128)(2,1)} %refs_3_) | copy-start | bytes 6291460
  44.1 10.4 %copy-start.1 = (bf16[1024,1024]{1,0:T(8,128)(2,1)S(1)}, bf16[1024,1024]{1,0:T(8,128)(2,1)}, u32[]{:S(2)}) copy-start(bf16[1024,1024]{1,0:T(8,128)(2,1)} %refs_4_) | copy-start | bytes 6291460
  44.2 10.4 %copy-start.2 = (bf16[1024,1024]{1,0:T(8,128)(2,1)S(1)}, bf16[1024,1024]{1,0:T(8,128)(2,1)}, u32[]{:S(2)}) copy-start(bf16[1024,1024]{1,0:T(8,128)(2,1)} %refs_5_) | copy-start | bytes 6291460
  44.2 10.4 %copy-start.4 = (bf16[128,1024]{1,0:T(8,128)(2,1)S(1)}, bf16[128,1024]{1,0:T(8,128)(2,1)}, u32[]{:S(2)}) copy-start(bf16[128,1024]{1,0:T(8,128)(2,1)} %refs_0_.4) | copy-start | bytes 786436
  44.2 10.4 %copy-start.12 = (bf16[1024]{0:T(1024)(128)(2,1)S(1)}, bf16[1024]{0:T(1024)(128)(2,1)}, u32[]{:S(2)}) copy-start(bf16[1024]{0:T(1024)(128)(2,1)} %refs_2_.4) | copy-start | bytes 6148
  48.9 13.3 %collective-permute-start.17 = (bf16[512,128]{1,0:T(8,128)(2,1)S(1)}, bf16[512,128]{1,0:T(8,128)(2,1)S(1)}, u32[]{:S(2)}, u32[]{:S(2)}) collective-permute-start(bf16[512,128]{1,0:T(8,128)(2,1)S(1)} %get-tuple-element.88.refs_0_), channel_id=1, source_target_pairs={{0,1},{1,0},{2,3},{3,2},{4,5},{5,4},{6,7},{7,6},{8,9},{9,8},{10,11... | collective-permute-start | bytes 393224 | tf_op jit(solution)/shard_map/ppermute | solution.py:57
  50.5 11.7 %collective-permute-start.18 = (bf16[256,128]{1,0:T(8,128)(2,1)S(1)}, bf16[256,128]{1,0:T(8,128)(2,1)S(1)}, u32[]{:S(2)}, u32[]{:S(2)}) collective-permute-start(bf16[256,128]{1,0:T(8,128)(2,1)S(1)} %get-tuple-element.89), channel_id=1, source_target_pairs={{0,2},{1,3},{2,0},{3,1},{4,6},{5,7},{6,4},{7,5},{8,10},{9,11},{10,... | collective-permute-start | bytes 196616 | tf_op jit(solution)/shard_map/ppermute | solution.py:57
  54.2 8.0 %collective-permute-start.19 = (bf16[256,128]{1,0:T(8,128)(2,1)S(1)}, bf16[256,128]{1,0:T(8,128)(2,1)S(1)}, u32[]{:S(2)}, u32[]{:S(2)}) collective-permute-start(bf16[256,128]{1,0:T(8,128)(2,1)S(1)} %get-tuple-element.101), channel_id=1, source_target_pairs={{0,2},{1,3},{2,0},{3,1},{4,6},{5,7},{6,4},{7,5},{8,10},{9,11},{10,... | collective-permute-start | bytes 196616 | tf_op jit(solution)/shard_map/ppermute | solution.py:57
  54.2 10.0 %collective-permute-start.22 = (bf16[128,512]{1,0:T(8,128)(2,1)S(1)}, bf16[128,512]{1,0:T(8,128)(2,1)S(1)}, u32[]{:S(2)}, u32[]{:S(2)}) collective-permute-start(bf16[128,512]{1,0:T(8,128)(2,1)S(1)} %collective-permute-done.9.refs_11_), channel_id=1, source_target_pairs={{0,4},{4,0},{8,12},{12,8},{16,20},{20,16},{24,28},{28,24},{1,5},{5... | collective-permute-start | bytes 393224 | tf_op jit(solution)/shard_map/ppermute | solution.py:260
  62.2 4.5 %collective-permute-start.21 = (bf16[256,128]{1,0:T(8,128)(2,1)S(1)}, bf16[256,128]{1,0:T(8,128)(2,1)S(1)}, u32[]{:S(2)}, u32[]{:S(2)}) collective-permute-start(bf16[256,128]{1,0:T(8,128)(2,1)S(1)} %collective-permute-done.19.refs_3_), channel_id=1, source_target_pairs={{0,1},{1,0},{2,3},{3,2},{4,5},{5,4},{6,7},{7,6},{8,9},{9,8},{10,11... | collective-permute-start | bytes 196616 | tf_op jit(solution)/shard_map/ppermute | solution.py:57
  62.2 5.2 %collective-permute-start.20 = (bf16[256,128]{1,0:T(8,128)(2,1)S(1)}, bf16[256,128]{1,0:T(8,128)(2,1)S(1)}, u32[]{:S(2)}, u32[]{:S(2)}) collective-permute-start(bf16[256,128]{1,0:T(8,128)(2,1)S(1)} %collective-permute-done.18.refs_2_), channel_id=1, source_target_pairs={{0,1},{1,0},{2,3},{3,2},{4,5},{5,4},{6,7},{7,6},{8,9},{9,8},{10,11... | collective-permute-start | bytes 196616 | tf_op jit(solution)/shard_map/ppermute | solution.py:57
  71.2 7.9 %collective-permute-start.24 = (bf16[256,256]{1,0:T(8,128)(2,1)S(1)}, bf16[256,256]{1,0:T(8,128)(2,1)S(1)}, u32[]{:S(2)}, u32[]{:S(2)}) collective-permute-start(bf16[256,256]{1,0:T(8,128)(2,1)S(1)} %get-tuple-element.117), channel_id=1, source_target_pairs={{0,1},{1,0},{2,3},{3,2},{4,5},{5,4},{6,7},{7,6},{8,9},{9,8},{10,11... | collective-permute-start | bytes 393224 | tf_op jit(solution)/shard_map/ppermute | solution.py:57
  72.4 11.0 %collective-permute-start.26 = (bf16[256,256]{1,0:T(8,128)(2,1)S(1)}, bf16[256,256]{1,0:T(8,128)(2,1)S(1)}, u32[]{:S(2)}, u32[]{:S(2)}) collective-permute-start(bf16[256,256]{1,0:T(8,128)(2,1)S(1)} %get-tuple-element.119), channel_id=1, source_target_pairs={{0,1},{1,0},{2,3},{3,2},{4,5},{5,4},{6,7},{7,6},{8,9},{9,8},{10,11... | collective-permute-start | bytes 393224 | tf_op jit(solution)/shard_map/ppermute | solution.py:57
  73.3 10.5 %copy-start.16 = (s32[72]{0:T(128)S(1)}, s32[72]{0:T(128)}, u32[]{:S(2)}) copy-start(s32[72]{0:T(128)} %page_table.1) | copy-start | bytes 868
  74.3 17.0 %collective-permute-start.23 = (bf16[512,256]{1,0:T(8,128)(2,1)S(1)}, bf16[512,256]{1,0:T(8,128)(2,1)S(1)}, u32[]{:S(2)}, u32[]{:S(2)}) collective-permute-start(bf16[512,256]{1,0:T(8,128)(2,1)S(1)} %get-tuple-element.115), channel_id=1, source_target_pairs={{0,1},{1,0},{2,3},{3,2},{4,5},{5,4},{6,7},{7,6},{8,9},{9,8},{10,11... | collective-permute-start | bytes 786440 | tf_op jit(solution)/shard_map/ppermute | solution.py:57
  79.1 9.4 %collective-permute-start.25 = (bf16[256,256]{1,0:T(8,128)(2,1)S(1)}, bf16[256,256]{1,0:T(8,128)(2,1)S(1)}, u32[]{:S(2)}, u32[]{:S(2)}) collective-permute-start(bf16[256,256]{1,0:T(8,128)(2,1)S(1)} %add_up.3), channel_id=1, source_target_pairs={{0,2},{1,3},{2,0},{3,1},{4,6},{5,7},{6,4},{7,5},{8,10},{9,11},{10,... | collective-permute-start | bytes 393224 | tf_op jit(solution)/shard_map/ppermute | solution.py:57
  83.4 8.0 %collective-permute-start.27 = (bf16[256,256]{1,0:T(8,128)(2,1)S(1)}, bf16[256,256]{1,0:T(8,128)(2,1)S(1)}, u32[]{:S(2)}, u32[]{:S(2)}) collective-permute-start(bf16[256,256]{1,0:T(8,128)(2,1)S(1)} %add_up.4), channel_id=1, source_target_pairs={{0,2},{1,3},{2,0},{3,1},{4,6},{5,7},{6,4},{7,5},{8,10},{9,11},{10,... | collective-permute-start | bytes 393224 | tf_op jit(solution)/shard_map/ppermute | solution.py:57

commit v11 on v10

--- a/solution.py
+++ b/solution.py
@@ -71,6 +71,13 @@
     count = lax.axis_size("tp")
     pairs = [[(i, (i + turn) % count) for i in range(count)] for turn in range(1, count)]
     return [[shard]] + [[lax.ppermute(shard, "tp", each)] for each in pairs]
+
+
+def direct_gather(shard):
+    if lax.axis_size("tp") != 4:
+        return turn_gather(shard)
+    moved = {mask: tp_xor(shard, mask) for mask in (3, 2, 1)}
+    return [[shard]] + [[moved[mask]] for mask in (1, 2, 3)]
 
 
 def gather_pieces(shard, split, before=(), near_first=False):
@@ -285,8 +292,7 @@
 
 def attend_kernel(count, heads, reach, lengths, queries, query_marks, *refs):
     pieces = refs[:count]
-    outs, scratch = refs[count:-8], refs[-8:]
-    q_buf, k_buf, v_buf, extra_buf, scores, peak, total, sems = scratch
+    out, q_buf, k_buf, v_buf, extra_buf, scores, peak, total, sems = refs[count:]
     me = lax.axis_index("seq")
     rows = queries.shape[0]
     _, ends = request_bounds(lengths)
@@ -400,11 +406,7 @@
     result = total[0, :, :width] / total[0, :, width:]
     for h in range(1, heads):
         result = jnp.where(lane // HD == h, total[h, :, :width] / total[h, :, width:], result)
-    result = result.astype(jnp.bfloat16)
-    outs[0][...] = result
-    for i, out in enumerate(outs[1:]):
-        step = out.shape[0]
-        out[...] = result[i * step : (i + 1) * step]
+    out[...] = result.astype(jnp.bfloat16)
 
 
 def attend(lengths, queries, query_marks, pieces, heads, reach):
@@ -412,12 +414,9 @@
     slots = reach + 1
     return pl.pallas_call(
         functools.partial(attend_kernel, len(pieces), heads, reach),
-        out_shape=[
-            jax.ShapeDtypeStruct((each, width), jnp.bfloat16)
-            for each in (rows, rows // 2, rows // 2)
-        ],
+        out_shape=jax.ShapeDtypeStruct((rows, width), jnp.bfloat16),
         in_specs=[SMEM, VMEM, VMEM] + [ANY] * len(pieces),
-        out_specs=[VMEM] * 3,
+        out_specs=VMEM,
         scratch_shapes=[
             pltpu.VMEM((heads * rows, width + LANES), jnp.bfloat16),
             pltpu.VMEM((slots, rows, width + LANES), jnp.bfloat16),
@@ -723,16 +722,16 @@
     if halve:
         twins = [[piece, seq_xor(piece, 1)] for (piece,) in w_out_pieces[1:-1]]
         w_out_pieces = w_out_pieces[:1] + twins + w_out_pieces[-1:]
-    row_pieces = seq_pieces(pairs, w_out_pieces[1:-1])
+    row_pieces = seq_pieces(pairs, w_out_pieces[1:])
     marks, w_out_pieces = lax.optimization_barrier((marks, w_out_pieces))
-    attended, *halves = attend(lengths, queries, marks, row_pieces, heads, reach)
+    attended = attend(lengths, queries, marks, row_pieces, heads, reach)
     large = (w_out, token_rows, gain_ffn, w_gate, w_up, w_down)
     large, last = lax.optimization_barrier((large, w_out_pieces[-1], attended))[:2]
     w_out, *large = fetch(large)
     if halve:
         w_out_pieces[0] = [w_out]
         w_out_pieces[-1] = [last[0], seq_xor(last[0], 1)]
-    attended_pieces = gather_pieces(attended, halves, large[1:2], True)
+    attended_pieces = direct_gather(attended)
     mixed, joined = feed_forward(attended_pieces, w_out_pieces, *large)
     row_pieces, _ = lax.optimization_barrier((row_pieces, joined))
     cache = fill_cache(lengths, page_table, row_pieces, rows)

time: 93 us -> 88.6 us (0.953)
  starting transfers between devices: 29.1 us -> 24.3 us
  Pallas kernels: 18.3 us -> 17.2 us
  waiting for transfers between devices: 34.7 us -> 35.8 us
    ppermute x10, waiting for transfers between devices: 1.4 us -> 6.03 us  [seq_xor(): lax.ppermute(value, 'seq', [(i, i ^ mask) for i in range(lax.axis_size('s...]
    ppermute x18 -> x16, starting transfers between devices: 24.1 us -> 19.6 us  [tp_xor(): lax.ppermute(value, 'tp', [(i, i ^ mask) for i in range(lax.axis_size('tp...]
    ppermute x18 -> x16, waiting for transfers between devices: 33.3 us -> 29.8 us  [tp_xor(): lax.ppermute(value, 'tp', [(i, i ^ mask) for i in range(lax.axis_size('tp...]
    pallas_call x1, Pallas kernels: 4.73 us -> 3.6 us  [attend(): pl.pallas_call(functools.partial(attend_kernel, len(pieces), heads, reach...]
  transfers between devices with their start and end apart: 28 -> 26, of which waited for: 15 -> 16; matrix products, arithmetic and copies ran while one was open for 0% -> 0% of each run, Pallas kernels for 8% -> 9%
where the time goes in v11:
time: 88.6 us; the launch traced here: 87.3 us
  waiting for transfers between devices  35.8 us (40%)
  starting transfers between devices  24.3 us (27%)
  Pallas kernels  17.2 us (19%)
  local copies, waits for them, and re-layouts  9.18 us (10%)
    ppermute x16, waiting for transfers between devices, tp_xor(): lax.ppermute(value, 'tp', [(i, i ^ mask) for i in range(lax.axis_size('tp...  29.8 us
    ppermute x16, starting transfers between devices, tp_xor(): lax.ppermute(value, 'tp', [(i, i ^ mask) for i in range(lax.axis_size('tp...  19.6 us
    unnamed x34, local copies, waits for them, and re-layouts  8.19 us
    ppermute x10, waiting for transfers between devices, seq_xor(): lax.ppermute(value, 'seq', [(i, i ^ mask) for i in range(lax.axis_size('s...  6.03 us
    ppermute x10, starting transfers between devices, seq_xor(): lax.ppermute(value, 'seq', [(i, i ^ mask) for i in range(lax.axis_size('s...  4.71 us
    pallas_call x1, Pallas kernels, fill_cache(): pl.pallas_call(functools.partial(cache_kernel, len(pieces), 2 * PAGE), ou...  4.69 us
    pallas_call x1, Pallas kernels, hidden_of(): pl.pallas_call(functools.partial(hidden_kernel, *counts), out_shape=[jax....  3.82 us
    pallas_call x1, Pallas kernels, attend(): pl.pallas_call(functools.partial(attend_kernel, len(pieces), heads, reach...  3.6 us
  transfers between devices with their start and end apart: 26, of which 16 were waited for; matrix products, arithmetic and copies ran while one was open for 0% of the time, Pallas kernels for 9%

profile of v11, /device:TPU:2, one launch (start us, length us, event | category | flops | bytes accessed | tf_op | source)
XLA Modules:
  0.0 87.3 jit_solution(5336309175850678779)
XLA Ops:
  0.6 1.0 %fusion = (bf16[256,256]{1,0:T(8,128)(2,1)S(1)}, bf16[256,256]{1,0:T(8,128)(2,1)S(1)}) fusion(bf16[512,256]{1,0:T(8,128)(2,1)} %refs_0_.2), kind=kLoop, calls=%fused_computation | loop fusion | bytes 524288 | tf_op jit(solution)/shard_map/slice | solution.py:714
  1.6 2.7 %collective-permute-start.2 = (bf16[256,256]{1,0:T(8,128)(2,1)S(1)}, bf16[256,256]{1,0:T(8,128)(2,1)S(1)}, u32[]{:S(2)}, u32[]{:S(2)}) collective-permute-start(bf16[256,256]{1,0:T(8,128)(2,1)S(1)} %get-tuple-element.65), channel_id=1, source_target_pairs={{0,2},{1,3},{2,0},{3,1},{4,6},{5,7},{6,4},{7,5},{8,10},{9,11},{10,... | collective-permute-start | bytes 393224 | tf_op jit(solution)/shard_map/ppermute | solution.py:57
  4.6 1.6 %collective-permute-start = (bf16[512,256]{1,0:T(8,128)(2,1)}, bf16[512,256]{1,0:T(8,128)(2,1)S(1)}, u32[]{:S(2)}, u32[]{:S(2)}) collective-permute-start(bf16[512,256]{1,0:T(8,128)(2,1)} %refs_0_.2), channel_id=1, source_target_pairs={{0,1},{1,0},{2,3},{3,2},{4,5},{5,4},{6,7},{7,6},{8,9},{9,8},{10,11... | collective-permute-start | bytes 786440 | tf_op jit(solution)/shard_map/ppermute | solution.py:57
  6.2 1.0 %copy-done.5 = bf16[512,256]{1,0:T(8,128)(2,1)S(1)} copy-done((bf16[512,256]{1,0:T(8,128)(2,1)S(1)}, bf16[512,256]{1,0:T(8,128)(2,1)}, u32[]{:S(2)}) %copy-start.5) | copy-done | bytes 262168
  7.2 0.9 %copy-done.6 = bf16[1024,128]{1,0:T(8,128)(2,1)S(1)} copy-done((bf16[1024,128]{1,0:T(8,128)(2,1)S(1)}, bf16[1024,128]{1,0:T(8,128)(2,1)}, u32[]{:S(2)}) %copy-start.6) | copy-done | bytes 262168
  8.1 0.7 copy-done.9
  8.9 0.9 %copy-done.3 = bf16[128,1024]{1,0:T(8,128)(2,1)S(1)} copy-done((bf16[128,1024]{1,0:T(8,128)(2,1)S(1)}, bf16[128,1024]{1,0:T(8,128)(2,1)}, u32[]{:S(2)}) %copy-start.3) | copy-done | bytes 262168
  9.9 0.9 %copy-done.7 = bf16[1024,128]{1,0:T(8,128)(2,1)S(1)} copy-done((bf16[1024,128]{1,0:T(8,128)(2,1)S(1)}, bf16[1024,128]{1,0:T(8,128)(2,1)}, u32[]{:S(2)}) %copy-start.7) | copy-done | bytes 262168
  10.8 0.9 %copy-done.8 = bf16[1024,128]{1,0:T(8,128)(2,1)S(1)} copy-done((bf16[1024,128]{1,0:T(8,128)(2,1)S(1)}, bf16[1024,128]{1,0:T(8,128)(2,1)}, u32[]{:S(2)}) %copy-start.8) | copy-done | bytes 262168
  11.8 0.7 copy-done.10
  12.4 0.7 copy-done.11
  13.1 0.7 copy-done.13
  13.8 0.7 copy-done.15
  14.4 1.1 %tables.1 = (f32[512,128]{1,0:T(8,128)S(1)}, f32[512,128]{1,0:T(8,128)S(1)}, bf16[16,256]{1,0:T(8,128)(2,1)S(1)}, bf16[2,512,128]{2,1,0:T(8,128)(2,1)S(1)}, bf16...) custom-call(s32[4]{0:T(128)S(1)} %copy-done.13, f32[2,2]{1,0:T(2,128)S(1)} %copy-done.15, ...), custom_call_target="tpu_custom_call" | custom-call | flops 524288 | bytes 1048576 | tf_op jit(solution)/shard_map/tables/pallas_call | solution.py:176
  15.6 0.5 collective-permute-start.4
  16.4 1.3 %collective-permute-start.3 = (bf16[256,256]{1,0:T(8,128)(2,1)S(1)}, bf16[256,256]{1,0:T(8,128)(2,1)S(1)}, u32[]{:S(2)}, u32[]{:S(2)}) collective-permute-start(bf16[256,256]{1,0:T(8,128)(2,1)S(1)} %collective-permute-done.1.refs_2_), channel_id=1, source_target_pairs={{0,1},{1,0},{2,3},{3,2},{4,5},{5,4},{6,7},{7,6},{8,9},{9,8},{10,11... | collective-permute-start | bytes 393224 | tf_op jit(solution)/shard_map/ppermute | solution.py:57
  17.7 3.8 %collective-permute-done.4.refs_5_ = bf16[256,256]{1,0:T(8,128)(2,1)S(1)} collective-permute-done((bf16[256,256]{1,0:T(8,128)(2,1)S(1)}, bf16[256,256]{1,0:T(8,128)(2,1)S(1)}, u32[]{:S(2)}, u32[]{:S(2)}) %collective-permute-start.4) | collective-permute-done | bytes 131104 | tf_op jit(solution)/shard_map/ppermute | solution.py:57
  21.5 1.4 %collective-permute-done.3.refs_4_ = bf16[256,256]{1,0:T(8,128)(2,1)S(1)} collective-permute-done((bf16[256,256]{1,0:T(8,128)(2,1)S(1)}, bf16[256,256]{1,0:T(8,128)(2,1)S(1)}, u32[]{:S(2)}, u32[]{:S(2)}) %collective-permute-start.3) | collective-permute-done | bytes 131104 | tf_op jit(solution)/shard_map/ppermute | solution.py:57
  22.9 1.4 %project.1 = (bf16[512,1024]{1,0:T(8,128)(2,1)S(1)}, bf16[512,128]{1,0:T(8,128)(2,1)S(1)}, bf16[528,256]{1,0:T(8,128)(2,1)S(1)}) custom-call(bf16[512,256]{1,0:T(8,128)(2,1)S(1)} %get-tuple-element.60.refs_0_, bf16[512,256]{1,0:T(8,128)(2,1)S(1)} %collective-permute-done.refs_1_, bf16[256,256]{1,0:T(8,128)(2,1)S(1)} %collective-permute-done.1.refs_2_, ...), custom_call_target="tpu_custom_call" | custom-call | flops 402653184 | bytes 4194304 | tf_op jit(solution)/shard_map/project/pallas_call | solution.py:250
  24.3 2.6 %collective-permute-start.7 = (bf16[128,512]{1,0:T(8,128)(2,1)S(1)}, bf16[128,512]{1,0:T(8,128)(2,1)S(1)}, u32[]{:S(2)}, u32[]{:S(2)}) collective-permute-start(bf16[128,512]{1,0:T(8,128)(2,1)S(1)} %get-tuple-element.77), channel_id=1, source_target_pairs={{0,2},{1,3},{2,0},{3,1},{4,6},{5,7},{6,4},{7,5},{8,10},{9,11},{10,... | collective-permute-start | bytes 393224 | tf_op jit(solution)/shard_map/ppermute | solution.py:57
  27.0 2.2 %collective-permute-start.5 = (bf16[128,512]{1,0:T(8,128)(2,1)S(1)}, bf16[128,512]{1,0:T(8,128)(2,1)S(1)}, u32[]{:S(2)}, u32[]{:S(2)}) collective-permute-start(bf16[128,512]{1,0:T(8,128)(2,1)S(1)} %get-tuple-element.77), channel_id=1, source_target_pairs={{0,1},{1,0},{2,3},{3,2},{4,5},{5,4},{6,7},{7,6},{8,9},{9,8},{10,11... | collective-permute-start | bytes 393224 | tf_op jit(solution)/shard_map/ppermute | solution.py:57
  29.1 1.5 %collective-permute-start.13 = (bf16[528,256]{1,0:T(8,128)(2,1)S(1)}, bf16[528,256]{1,0:T(8,128)(2,1)S(1)}, u32[]{:S(2)}, u32[]{:S(2)}) collective-permute-start(bf16[528,256]{1,0:T(8,128)(2,1)S(1)} %get-tuple-element.110.refs_0_), channel_id=1, source_target_pairs={{0,24},{4,28},{8,16},{12,20},{16,8},{20,12},{24,0},{28,4},{1,25},{... | collective-permute-start | bytes 811016 | tf_op jit(solution)/shard_map/ppermute | solution.py:267
  30.6 0.5 collective-permute-start.12
  31.1 1.5 %collective-permute-start.11 = (bf16[528,256]{1,0:T(8,128)(2,1)S(1)}, bf16[528,256]{1,0:T(8,128)(2,1)S(1)}, u32[]{:S(2)}, u32[]{:S(2)}) collective-permute-start(bf16[528,256]{1,0:T(8,128)(2,1)S(1)} %get-tuple-element.110.refs_0_), channel_id=1, source_target_pairs={{0,8},{4,12},{8,0},{12,4},{16,24},{20,28},{24,16},{28,20},{1,9},{5... | collective-permute-start | bytes 811016 | tf_op jit(solution)/shard_map/ppermute | solution.py:267
  32.6 1.6 %collective-permute-start.9 = (bf16[128,512]{1,0:T(8,128)(2,1)S(1)}, bf16[128,512]{1,0:T(8,128)(2,1)S(1)}, u32[]{:S(2)}, u32[]{:S(2)}) collective-permute-start(bf16[128,512]{1,0:T(8,128)(2,1)S(1)} %collective-permute-done.7.refs_7_), channel_id=1, source_target_pairs={{0,1},{1,0},{2,3},{3,2},{4,5},{5,4},{6,7},{7,6},{8,9},{9,8},{10,11... | collective-permute-start | bytes 393224 | tf_op jit(solution)/shard_map/ppermute | solution.py:57
  34.2 3.4 %collective-permute-done.9.refs_9_ = bf16[128,512]{1,0:T(8,128)(2,1)S(1)} collective-permute-done((bf16[128,512]{1,0:T(8,128)(2,1)S(1)}, bf16[128,512]{1,0:T(8,128)(2,1)S(1)}, u32[]{:S(2)}, u32[]{:S(2)}) %collective-permute-start.9) | collective-permute-done | bytes 131104 | tf_op jit(solution)/shard_map/ppermute | solution.py:57
  37.6 0.5 collective-permute-start.10
  38.1 0.8 collective-permute-done.6.refs_6_
  38.9 0.4 collective-permute-done.13.refs_6_
  39.4 2.8 %collective-permute-done.12.refs_4_ = bf16[528,256]{1,0:T(8,128)(2,1)S(1)} collective-permute-done((bf16[528,256]{1,0:T(8,128)(2,1)S(1)}, bf16[528,256]{1,0:T(8,128)(2,1)S(1)}, u32[]{:S(2)}, u32[]{:S(2)}) %collective-permute-start.12) | collective-permute-done | bytes 270368 | tf_op jit(solution)/shard_map/ppermute | solution.py:267
  42.3 0.5 collective-permute-start.15
  42.8 1.0 %collective-permute-done.14.refs_3_ = bf16[528,256]{1,0:T(8,128)(2,1)S(1)} collective-permute-done((bf16[528,256]{1,0:T(8,128)(2,1)S(1)}, bf16[528,256]{1,0:T(8,128)(2,1)S(1)}, u32[]{:S(2)}, u32[]{:S(2)}) %collective-permute-start.14) | collective-permute-done | bytes 270368 | tf_op jit(solution)/shard_map/ppermute | solution.py:267
  43.9 0.4 collective-permute-done.15.refs_5_
  44.3 0.4 collective-permute-done.16.refs_7_
  44.7 3.6 %attend.1.refs_0_ = bf16[512,128]{1,0:T(8,128)(2,1)S(1)} custom-call(s32[4]{0:T(128)S(1)} %copy-done.14, bf16[512,128]{1,0:T(8,128)(2,1)S(1)} %get-tuple-element.73.queries, bf16[2,512,128]{2,1,0:T(8,128)(2,1)S(1)} %get-tuple-element.79.query_marks, bf16[528,256]{1,0:T(8,128)(2,1)S(1)} %get-tuple-element.110.refs_0_, ...), custom_call_target="tpu_custom_call" | custom-call | flops 2684354560 | bytes 4194304 | tf_op jit(solution)/shard_map/attend/pallas_call | solution.py:415
  48.7 1.6 %collective-permute-start.18 = (bf16[512,128]{1,0:T(8,128)(2,1)S(1)}, bf16[512,128]{1,0:T(8,128)(2,1)S(1)}, u32[]{:S(2)}, u32[]{:S(2)}) collective-permute-start(bf16[512,128]{1,0:T(8,128)(2,1)S(1)} %attend.1.refs_0_), channel_id=1, source_target_pairs={{0,2},{1,3},{2,0},{3,1},{4,6},{5,7},{6,4},{7,5},{8,10},{9,11},{10,... | collective-permute-start | bytes 393224 | tf_op jit(solution)/shard_map/ppermute | solution.py:57
  50.2 2.6 %collective-permute-start.17 = (bf16[512,128]{1,0:T(8,128)(2,1)S(1)}, bf16[512,128]{1,0:T(8,128)(2,1)S(1)}, u32[]{:S(2)}, u32[]{:S(2)}) collective-permute-start(bf16[512,128]{1,0:T(8,128)(2,1)S(1)} %attend.1.refs_0_), channel_id=1, source_target_pairs={{0,1},{1,0},{2,3},{3,2},{4,5},{5,4},{6,7},{7,6},{8,9},{9,8},{10,11... | collective-permute-start | bytes 393224 | tf_op jit(solution)/shard_map/ppermute | solution.py:57
  52.9 0.6 fetch.3
  53.5 3.2 %collective-permute-done.19.refs_3_ = bf16[512,128]{1,0:T(8,128)(2,1)S(1)} collective-permute-done((bf16[512,128]{1,0:T(8,128)(2,1)S(1)}, bf16[512,128]{1,0:T(8,128)(2,1)S(1)}, u32[]{:S(2)}, u32[]{:S(2)}) %collective-permute-start.19) | collective-permute-done | bytes 131104 | tf_op jit(solution)/shard_map/ppermute | solution.py:57
  56.8 5.7 %collective-permute-done.18.refs_2_ = bf16[512,128]{1,0:T(8,128)(2,1)S(1)} collective-permute-done((bf16[512,128]{1,0:T(8,128)(2,1)S(1)}, bf16[512,128]{1,0:T(8,128)(2,1)S(1)}, u32[]{:S(2)}, u32[]{:S(2)}) %collective-permute-start.18) | collective-permute-done | bytes 131104 | tf_op jit(solution)/shard_map/ppermute | solution.py:57
  62.4 3.8 %hidden.1 = (bf16[512,1024]{1,0:T(8,128)(2,1)S(1)}, bf16[512,256]{1,0:T(8,128)(2,1)S(1)}, bf16[256,256]{1,0:T(8,128)(2,1)S(1)}, bf16[256,256]{1,0:T(8,128)(2,1)S(1)}) custom-call(bf16[512,128]{1,0:T(8,128)(2,1)S(1)} %attend.1.refs_0_, bf16[512,128]{1,0:T(8,128)(2,1)S(1)} %collective-permute-done.17.refs_1_, ...), custom_call_target="tpu_custom_call" | custom-call | flops 3221225472 | bytes 10485760 | tf_op jit(solution)/shard_map/hidden/pallas_call | solution.py:598
  66.3 2.0 %collective-permute-start.24 = (bf16[256,256]{1,0:T(8,128)(2,1)S(1)}, bf16[256,256]{1,0:T(8,128)(2,1)S(1)}, u32[]{:S(2)}, u32[]{:S(2)}) collective-permute-start(bf16[256,256]{1,0:T(8,128)(2,1)S(1)} %get-tuple-element.109), channel_id=1, source_target_pairs={{0,1},{1,0},{2,3},{3,2},{4,5},{5,4},{6,7},{7,6},{8,9},{9,8},{10,11... | collective-permute-start | bytes 393224 | tf_op jit(solution)/shard_map/ppermute | solution.py:57
  68.3 1.0 %down_blocks.1 = (f32[256,256]{1,0:T(8,128)S(1)}, f32[256,256]{1,0:T(8,128)S(1)}, bf16[512,256]{1,0:T(8,128)(2,1)S(1)}, f32[512,256]{1,0:T(8,128)S(1)}) custom-call(bf16[512,1024]{1,0:T(8,128)(2,1)S(1)} %get-tuple-element.102.hidden, bf16[512,256]{1,0:T(8,128)(2,1)S(1)} %get-tuple-element.103.kept, bf16[1024,1024]{1,0:T(8,128)(2,1)S(1)} %get-tuple-element.101.refs_15_.w_down), custom_call_target="tpu_custom_call" | custom-call | flops 805306368 | bytes 5242880 | tf_op jit(solution)/shard_map/down_blocks/pallas_call | solution.py:632
  69.5 3.2 %collective-permute-done.22.refs_1_ = bf16[256,256]{1,0:T(8,128)(2,1)S(1)} collective-permute-done((bf16[256,256]{1,0:T(8,128)(2,1)S(1)}, bf16[256,256]{1,0:T(8,128)(2,1)S(1)}, u32[]{:S(2)}, u32[]{:S(2)}) %collective-permute-start.22) | collective-permute-done | bytes 131104 | tf_op jit(solution)/shard_map/ppermute | solution.py:57
  72.9 6.6 %collective-permute-done.24.refs_1_ = bf16[256,256]{1,0:T(8,128)(2,1)S(1)} collective-permute-done((bf16[256,256]{1,0:T(8,128)(2,1)S(1)}, bf16[256,256]{1,0:T(8,128)(2,1)S(1)}, u32[]{:S(2)}, u32[]{:S(2)}) %collective-permute-start.24) | collective-permute-done | bytes 131104 | tf_op jit(solution)/shard_map/ppermute | solution.py:57
  79.6 4.7 %fill_cache.1 = bf16[576,2,128]{2,1,0:T(2,128)(2,1)} custom-call(s32[4]{0:T(128)S(1)} %copy-done.14, s32[72]{0:T(128)S(1)} %copy-done.16, bf16[528,256]{1,0:T(8,128)(2,1)S(1)} %get-tuple-element.110.refs_0_, bf16[528,256]{1,0:T(8,128)(2,1)S(1)} %collective-permute-done.10.refs_1_, bf16[528,256]{1,0:T(8,128)(2,1)S(1)} %collective-permute-done.11.refs_2_, ...), custom_call_target="tpu_custom_call" | custom-call | flops 75497472 | bytes 3145728 | tf_op jit(solution)/shard_map/fill_cache/pallas_call | solution.py:511
  84.3 2.2 %collective-permute-done.25.refs_3_ = bf16[256,256]{1,0:T(8,128)(2,1)S(1)} collective-permute-done((bf16[256,256]{1,0:T(8,128)(2,1)S(1)}, bf16[256,256]{1,0:T(8,128)(2,1)S(1)}, u32[]{:S(2)}, u32[]{:S(2)}) %collective-permute-start.25) | collective-permute-done | bytes 131104 | tf_op jit(solution)/shard_map/ppermute | solution.py:57
  86.5 0.8 add_up.5
  (50 shorter events, 1.7 us)
Async XLA Ops:
  0.6 44.0 %copy-start.14 = (s32[4]{0:T(128)S(1)}, s32[4]{0:T(128)}, u32[]{:S(2)}) copy-start(s32[4]{0:T(128)} %lengths.5) | copy-start | bytes 52
  1.6 14.0 %collective-permute-start.2 = (bf16[256,256]{1,0:T(8,128)(2,1)S(1)}, bf16[256,256]{1,0:T(8,128)(2,1)S(1)}, u32[]{:S(2)}, u32[]{:S(2)}) collective-permute-start(bf16[256,256]{1,0:T(8,128)(2,1)S(1)} %get-tuple-element.65), channel_id=1, source_target_pairs={{0,2},{1,3},{2,0},{3,1},{4,6},{5,7},{6,4},{7,5},{8,10},{9,11},{10,... | collective-permute-start | bytes 393224 | tf_op jit(solution)/shard_map/ppermute | solution.py:57
  4.3 12.1 %collective-permute-start.1 = (bf16[256,256]{1,0:T(8,128)(2,1)S(1)}, bf16[256,256]{1,0:T(8,128)(2,1)S(1)}, u32[]{:S(2)}, u32[]{:S(2)}) collective-permute-start(bf16[256,256]{1,0:T(8,128)(2,1)S(1)} %get-tuple-element.62), channel_id=1, source_target_pairs={{0,2},{1,3},{2,0},{3,1},{4,6},{5,7},{6,4},{7,5},{8,10},{9,11},{10,... | collective-permute-start | bytes 393224 | tf_op jit(solution)/shard_map/ppermute | solution.py:57
  4.6 13.1 %collective-permute-start = (bf16[512,256]{1,0:T(8,128)(2,1)}, bf16[512,256]{1,0:T(8,128)(2,1)S(1)}, u32[]{:S(2)}, u32[]{:S(2)}) collective-permute-start(bf16[512,256]{1,0:T(8,128)(2,1)} %refs_0_.2), channel_id=1, source_target_pairs={{0,1},{1,0},{2,3},{3,2},{4,5},{5,4},{6,7},{7,6},{8,9},{9,8},{10,11... | collective-permute-start | bytes 786440 | tf_op jit(solution)/shard_map/ppermute | solution.py:57
  6.2 1.0 %copy-start.5 = (bf16[512,256]{1,0:T(8,128)(2,1)S(1)}, bf16[512,256]{1,0:T(8,128)(2,1)}, u32[]{:S(2)}) copy-start(bf16[512,256]{1,0:T(8,128)(2,1)} %refs_0_.2) | copy-start | bytes 786436
  7.2 0.9 %copy-start.6 = (bf16[1024,128]{1,0:T(8,128)(2,1)S(1)}, bf16[1024,128]{1,0:T(8,128)(2,1)}, u32[]{:S(2)}) copy-start(bf16[1024,128]{1,0:T(8,128)(2,1)} %refs_2_.2) | copy-start | bytes 786436
  8.1 0.7 copy-start.9
  8.9 1.0 %copy-start.3 = (bf16[128,1024]{1,0:T(8,128)(2,1)S(1)}, bf16[128,1024]{1,0:T(8,128)(2,1)}, u32[]{:S(2)}) copy-start(bf16[128,1024]{1,0:T(8,128)(2,1)} %refs_0_.4) | copy-start | bytes 786436
  9.8 0.9 %copy-start.7 = (bf16[1024,128]{1,0:T(8,128)(2,1)S(1)}, bf16[1024,128]{1,0:T(8,128)(2,1)}, u32[]{:S(2)}) copy-start(bf16[1024,128]{1,0:T(8,128)(2,1)} %refs_0_.3) | copy-start | bytes 786436
  10.8 0.9 %copy-start.8 = (bf16[1024,128]{1,0:T(8,128)(2,1)S(1)}, bf16[1024,128]{1,0:T(8,128)(2,1)}, u32[]{:S(2)}) copy-start(bf16[1024,128]{1,0:T(8,128)(2,1)} %refs_1_.3) | copy-start | bytes 786436
  11.8 0.7 copy-start.10
  12.4 0.7 copy-start.11
  13.1 0.7 copy-start.13
  13.8 0.7 copy-start.15
  15.6 5.9 %collective-permute-start.4 = (bf16[256,256]{1,0:T(8,128)(2,1)S(1)}, bf16[256,256]{1,0:T(8,128)(2,1)S(1)}, u32[]{:S(2)}, u32[]{:S(2)}) collective-permute-start(bf16[256,256]{1,0:T(8,128)(2,1)S(1)} %collective-permute-done.2.refs_3_), channel_id=1, source_target_pairs={{0,1},{1,0},{2,3},{3,2},{4,5},{5,4},{6,7},{7,6},{8,9},{9,8},{10,11... | collective-permute-start | bytes 393224 | tf_op jit(solution)/shard_map/ppermute | solution.py:57
  16.4 6.5 %collective-permute-start.3 = (bf16[256,256]{1,0:T(8,128)(2,1)S(1)}, bf16[256,256]{1,0:T(8,128)(2,1)S(1)}, u32[]{:S(2)}, u32[]{:S(2)}) collective-permute-start(bf16[256,256]{1,0:T(8,128)(2,1)S(1)} %collective-permute-done.1.refs_2_), channel_id=1, source_target_pairs={{0,1},{1,0},{2,3},{3,2},{4,5},{5,4},{6,7},{7,6},{8,9},{9,8},{10,11... | collective-permute-start | bytes 393224 | tf_op jit(solution)/shard_map/ppermute | solution.py:57
  24.3 8.3 %collective-permute-start.7 = (bf16[128,512]{1,0:T(8,128)(2,1)S(1)}, bf16[128,512]{1,0:T(8,128)(2,1)S(1)}, u32[]{:S(2)}, u32[]{:S(2)}) collective-permute-start(bf16[128,512]{1,0:T(8,128)(2,1)S(1)} %get-tuple-element.77), channel_id=1, source_target_pairs={{0,2},{1,3},{2,0},{3,1},{4,6},{5,7},{6,4},{7,5},{8,10},{9,11},{10,... | collective-permute-start | bytes 393224 | tf_op jit(solution)/shard_map/ppermute | solution.py:57
  27.0 5.7 %collective-permute-start.5 = (bf16[128,512]{1,0:T(8,128)(2,1)S(1)}, bf16[128,512]{1,0:T(8,128)(2,1)S(1)}, u32[]{:S(2)}, u32[]{:S(2)}) collective-permute-start(bf16[128,512]{1,0:T(8,128)(2,1)S(1)} %get-tuple-element.77), channel_id=1, source_target_pairs={{0,1},{1,0},{2,3},{3,2},{4,5},{5,4},{6,7},{7,6},{8,9},{9,8},{10,11... | collective-permute-start | bytes 393224 | tf_op jit(solution)/shard_map/ppermute | solution.py:57
  29.1 10.3 %collective-permute-start.13 = (bf16[528,256]{1,0:T(8,128)(2,1)S(1)}, bf16[528,256]{1,0:T(8,128)(2,1)S(1)}, u32[]{:S(2)}, u32[]{:S(2)}) collective-permute-start(bf16[528,256]{1,0:T(8,128)(2,1)S(1)} %get-tuple-element.110.refs_0_), channel_id=1, source_target_pairs={{0,24},{4,28},{8,16},{12,20},{16,8},{20,12},{24,0},{28,4},{1,25},{... | collective-permute-start | bytes 811016 | tf_op jit(solution)/shard_map/ppermute | solution.py:267
  30.6 11.6 %collective-permute-start.12 = (bf16[528,256]{1,0:T(8,128)(2,1)S(1)}, bf16[528,256]{1,0:T(8,128)(2,1)S(1)}, u32[]{:S(2)}, u32[]{:S(2)}) collective-permute-start(bf16[528,256]{1,0:T(8,128)(2,1)S(1)} %get-tuple-element.110.refs_0_), channel_id=1, source_target_pairs={{0,16},{4,20},{8,24},{12,28},{16,0},{20,4},{24,8},{28,12},{1,17},{... | collective-permute-start | bytes 811016 | tf_op jit(solution)/shard_map/ppermute | solution.py:267
  31.1 11.2 %collective-permute-start.11 = (bf16[528,256]{1,0:T(8,128)(2,1)S(1)}, bf16[528,256]{1,0:T(8,128)(2,1)S(1)}, u32[]{:S(2)}, u32[]{:S(2)}) collective-permute-start(bf16[528,256]{1,0:T(8,128)(2,1)S(1)} %get-tuple-element.110.refs_0_), channel_id=1, source_target_pairs={{0,8},{4,12},{8,0},{12,4},{16,24},{20,28},{24,16},{28,20},{1,9},{5... | collective-permute-start | bytes 811016 | tf_op jit(solution)/shard_map/ppermute | solution.py:267
  32.6 5.0 %collective-permute-start.9 = (bf16[128,512]{1,0:T(8,128)(2,1)S(1)}, bf16[128,512]{1,0:T(8,128)(2,1)S(1)}, u32[]{:S(2)}, u32[]{:S(2)}) collective-permute-start(bf16[128,512]{1,0:T(8,128)(2,1)S(1)} %collective-permute-done.7.refs_7_), channel_id=1, source_target_pairs={{0,1},{1,0},{2,3},{3,2},{4,5},{5,4},{6,7},{7,6},{8,9},{9,8},{10,11... | collective-permute-start | bytes 393224 | tf_op jit(solution)/shard_map/ppermute | solution.py:57
  34.2 3.4 %collective-permute-start.8 = (bf16[128,512]{1,0:T(8,128)(2,1)S(1)}, bf16[128,512]{1,0:T(8,128)(2,1)S(1)}, u32[]{:S(2)}, u32[]{:S(2)}) collective-permute-start(bf16[128,512]{1,0:T(8,128)(2,1)S(1)} %collective-permute-done.7.refs_7_), channel_id=1, source_target_pairs={{0,4},{4,0},{8,12},{12,8},{16,20},{20,16},{24,28},{28,24},{1,5},{5... | collective-permute-start | bytes 393224 | tf_op jit(solution)/shard_map/ppermute | solution.py:267
  37.6 1.3 %collective-permute-start.6 = (bf16[128,512]{1,0:T(8,128)(2,1)S(1)}, bf16[128,512]{1,0:T(8,128)(2,1)S(1)}, u32[]{:S(2)}, u32[]{:S(2)}) collective-permute-start(bf16[128,512]{1,0:T(8,128)(2,1)S(1)} %collective-permute-done.5.refs_5_), channel_id=1, source_target_pairs={{0,4},{4,0},{8,12},{12,8},{16,20},{20,16},{24,28},{28,24},{1,5},{5... | collective-permute-start | bytes 393224 | tf_op jit(solution)/shard_map/ppermute | solution.py:267
  37.6 5.2 %collective-permute-start.10 = (bf16[528,256]{1,0:T(8,128)(2,1)S(1)}, bf16[528,256]{1,0:T(8,128)(2,1)S(1)}, u32[]{:S(2)}, u32[]{:S(2)}) collective-permute-start(bf16[528,256]{1,0:T(8,128)(2,1)S(1)} %get-tuple-element.110.refs_0_), channel_id=1, source_target_pairs={{0,4},{4,0},{8,12},{12,8},{16,20},{20,16},{24,28},{28,24},{1,5},{5... | collective-permute-start | bytes 811016 | tf_op jit(solution)/shard_map/ppermute | solution.py:267
  42.3 1.5 %collective-permute-start.14 = (bf16[528,256]{1,0:T(8,128)(2,1)S(1)}, bf16[528,256]{1,0:T(8,128)(2,1)S(1)}, u32[]{:S(2)}, u32[]{:S(2)}) collective-permute-start(bf16[528,256]{1,0:T(8,128)(2,1)S(1)} %collective-permute-done.11.refs_2_), channel_id=1, source_target_pairs={{0,4},{4,0},{8,12},{12,8},{16,20},{20,16},{24,28},{28,24},{1,5},{5... | collective-permute-start | bytes 811016 | tf_op jit(solution)/shard_map/ppermute | solution.py:267
  42.3 1.9 %collective-permute-start.15 = (bf16[528,256]{1,0:T(8,128)(2,1)S(1)}, bf16[528,256]{1,0:T(8,128)(2,1)S(1)}, u32[]{:S(2)}, u32[]{:S(2)}) collective-permute-start(bf16[528,256]{1,0:T(8,128)(2,1)S(1)} %collective-permute-done.12.refs_4_), channel_id=1, source_target_pairs={{0,4},{4,0},{8,12},{12,8},{16,20},{20,16},{24,28},{28,24},{1,5},{5... | collective-permute-start | bytes 811016 | tf_op jit(solution)/shard_map/ppermute | solution.py:267
  42.8 1.8 %collective-permute-start.16 = (bf16[528,256]{1,0:T(8,128)(2,1)S(1)}, bf16[528,256]{1,0:T(8,128)(2,1)S(1)}, u32[]{:S(2)}, u32[]{:S(2)}) collective-permute-start(bf16[528,256]{1,0:T(8,128)(2,1)S(1)} %collective-permute-done.13.refs_6_), channel_id=1, source_target_pairs={{0,4},{4,0},{8,12},{12,8},{16,20},{20,16},{24,28},{28,24},{1,5},{5... | collective-permute-start | bytes 811016 | tf_op jit(solution)/shard_map/ppermute | solution.py:267
  44.6 8.2 %copy-start = (bf16[1024,1024]{1,0:T(8,128)(2,1)S(1)}, bf16[1024,1024]{1,0:T(8,128)(2,1)}, u32[]{:S(2)}) copy-start(bf16[1024,1024]{1,0:T(8,128)(2,1)} %refs_3_) | copy-start | bytes 6291460
  44.6 8.2 %copy-start.1 = (bf16[1024,1024]{1,0:T(8,128)(2,1)S(1)}, bf16[1024,1024]{1,0:T(8,128)(2,1)}, u32[]{:S(2)}) copy-start(bf16[1024,1024]{1,0:T(8,128)(2,1)} %refs_4_) | copy-start | bytes 6291460
  44.6 8.3 %copy-start.2 = (bf16[1024,1024]{1,0:T(8,128)(2,1)S(1)}, bf16[1024,1024]{1,0:T(8,128)(2,1)}, u32[]{:S(2)}) copy-start(bf16[1024,1024]{1,0:T(8,128)(2,1)} %refs_5_) | copy-start | bytes 6291460
  44.7 8.2 %copy-start.4 = (bf16[128,1024]{1,0:T(8,128)(2,1)S(1)}, bf16[128,1024]{1,0:T(8,128)(2,1)}, u32[]{:S(2)}) copy-start(bf16[128,1024]{1,0:T(8,128)(2,1)} %refs_0_.4) | copy-start | bytes 786436
  44.7 8.2 %copy-start.12 = (bf16[1024]{0:T(1024)(128)(2,1)S(1)}, bf16[1024]{0:T(1024)(128)(2,1)}, u32[]{:S(2)}) copy-start(bf16[1024]{0:T(1024)(128)(2,1)} %refs_2_.4) | copy-start | bytes 6148
  48.3 5.2 %collective-permute-start.20 = (bf16[128,512]{1,0:T(8,128)(2,1)S(1)}, bf16[128,512]{1,0:T(8,128)(2,1)S(1)}, u32[]{:S(2)}, u32[]{:S(2)}) collective-permute-start(bf16[128,512]{1,0:T(8,128)(2,1)S(1)} %collective-permute-done.9.refs_9_), channel_id=1, source_target_pairs={{0,4},{4,0},{8,12},{12,8},{16,20},{20,16},{24,28},{28,24},{1,5},{5... | collective-permute-start | bytes 393224 | tf_op jit(solution)/shard_map/ppermute | solution.py:267
  48.5 8.3 %collective-permute-start.19 = (bf16[512,128]{1,0:T(8,128)(2,1)S(1)}, bf16[512,128]{1,0:T(8,128)(2,1)S(1)}, u32[]{:S(2)}, u32[]{:S(2)}) collective-permute-start(bf16[512,128]{1,0:T(8,128)(2,1)S(1)} %attend.1.refs_0_), channel_id=1, source_target_pairs={{0,3},{1,2},{2,1},{3,0},{4,7},{5,6},{6,5},{7,4},{8,11},{9,10},{10,... | collective-permute-start | bytes 393224 | tf_op jit(solution)/shard_map/ppermute | solution.py:57
  48.7 13.8 %collective-permute-start.18 = (bf16[512,128]{1,0:T(8,128)(2,1)S(1)}, bf16[512,128]{1,0:T(8,128)(2,1)S(1)}, u32[]{:S(2)}, u32[]{:S(2)}) collective-permute-start(bf16[512,128]{1,0:T(8,128)(2,1)S(1)} %attend.1.refs_0_), channel_id=1, source_target_pairs={{0,2},{1,3},{2,0},{3,1},{4,6},{5,7},{6,4},{7,5},{8,10},{9,11},{10,... | collective-permute-start | bytes 393224 | tf_op jit(solution)/shard_map/ppermute | solution.py:57
  50.2 12.2 %collective-permute-start.17 = (bf16[512,128]{1,0:T(8,128)(2,1)S(1)}, bf16[512,128]{1,0:T(8,128)(2,1)S(1)}, u32[]{:S(2)}, u32[]{:S(2)}) collective-permute-start(bf16[512,128]{1,0:T(8,128)(2,1)S(1)} %attend.1.refs_0_), channel_id=1, source_target_pairs={{0,1},{1,0},{2,3},{3,2},{4,5},{5,4},{6,7},{7,6},{8,9},{9,8},{10,11... | collective-permute-start | bytes 393224 | tf_op jit(solution)/shard_map/ppermute | solution.py:57
  66.2 6.5 %collective-permute-start.22 = (bf16[256,256]{1,0:T(8,128)(2,1)S(1)}, bf16[256,256]{1,0:T(8,128)(2,1)S(1)}, u32[]{:S(2)}, u32[]{:S(2)}) collective-permute-start(bf16[256,256]{1,0:T(8,128)(2,1)S(1)} %get-tuple-element.107), channel_id=1, source_target_pairs={{0,1},{1,0},{2,3},{3,2},{4,5},{5,4},{6,7},{7,6},{8,9},{9,8},{10,11... | collective-permute-start | bytes 393224 | tf_op jit(solution)/shard_map/ppermute | solution.py:57
  66.3 13.2 %collective-permute-start.24 = (bf16[256,256]{1,0:T(8,128)(2,1)S(1)}, bf16[256,256]{1,0:T(8,128)(2,1)S(1)}, u32[]{:S(2)}, u32[]{:S(2)}) collective-permute-start(bf16[256,256]{1,0:T(8,128)(2,1)S(1)} %get-tuple-element.109), channel_id=1, source_target_pairs={{0,1},{1,0},{2,3},{3,2},{4,5},{5,4},{6,7},{7,6},{8,9},{9,8},{10,11... | collective-permute-start | bytes 393224 | tf_op jit(solution)/shard_map/ppermute | solution.py:57
  68.3 11.3 %copy-start.16 = (s32[72]{0:T(128)S(1)}, s32[72]{0:T(128)}, u32[]{:S(2)}) copy-start(s32[72]{0:T(128)} %page_table.1) | copy-start | bytes 868
  69.3 17.2 %collective-permute-start.21 = (bf16[512,256]{1,0:T(8,128)(2,1)S(1)}, bf16[512,256]{1,0:T(8,128)(2,1)S(1)}, u32[]{:S(2)}, u32[]{:S(2)}) collective-permute-start(bf16[512,256]{1,0:T(8,128)(2,1)S(1)} %get-tuple-element.105), channel_id=1, source_target_pairs={{0,1},{1,0},{2,3},{3,2},{4,5},{5,4},{6,7},{7,6},{8,9},{9,8},{10,11... | collective-permute-start | bytes 786440 | tf_op jit(solution)/shard_map/ppermute | solution.py:57
  72.8 11.6 %collective-permute-start.23 = (bf16[256,256]{1,0:T(8,128)(2,1)S(1)}, bf16[256,256]{1,0:T(8,128)(2,1)S(1)}, u32[]{:S(2)}, u32[]{:S(2)}) collective-permute-start(bf16[256,256]{1,0:T(8,128)(2,1)S(1)} %add_up.3), channel_id=1, source_target_pairs={{0,2},{1,3},{2,0},{3,1},{4,6},{5,7},{6,4},{7,5},{8,10},{9,11},{10,... | collective-permute-start | bytes 393224 | tf_op jit(solution)/shard_map/ppermute | solution.py:57
  79.5 7.0 %collective-permute-start.25 = (bf16[256,256]{1,0:T(8,128)(2,1)S(1)}, bf16[256,256]{1,0:T(8,128)(2,1)S(1)}, u32[]{:S(2)}, u32[]{:S(2)}) collective-permute-start(bf16[256,256]{1,0:T(8,128)(2,1)S(1)} %add_up.4), channel_id=1, source_target_pairs={{0,2},{1,3},{2,0},{3,1},{4,6},{5,7},{6,4},{7,5},{8,10},{9,11},{10,... | collective-permute-start | bytes 393224 | tf_op jit(solution)/shard_map/ppermute | solution.py:57

commit v12 on v11

--- a/solution.py
+++ b/solution.py
@@ -63,6 +63,7 @@
     if near_first:
         far[0], _ = lax.optimization_barrier((far[0], near))
     for i, value in enumerate(before):
+        value = value(far) if callable(value) else value
         far[i], _ = lax.optimization_barrier((far[i], value))
     return [[shard], [near], far, [tp_xor(part, 1) for part in far]]
 
@@ -709,11 +710,19 @@
     cosine, sine, extra, marks, w_query, w_key, w_out_part = tables(
         lengths, var_bias, positions, variate, width, (w_query, w_key, w_out), halve
     )
-    own_tokens, gain_attn, w_value = fetch((tokens, gain_attn, w_value))
+    loaded = []
+
+    def load(far):
+        operands = lax.optimization_barrier(((tokens, gain_attn, w_value), far[0]))[0]
+        loaded.extend(fetch(operands))
+        return loaded[1]
+
     step = rows // 2
     halves = lax.optimization_barrier((tokens[:step], tokens[step:], tokens))
-    pieces = gather_pieces(halves[2], halves[:2], (extra, gain_attn))
-    pieces[0] = [own_tokens]
+    pieces = gather_pieces(halves[2], halves[:2], (extra, load))
+    if loaded:
+        own_tokens, gain_attn, w_value = loaded
+        pieces[0] = [own_tokens]
     token_rows, queries, pairs = project(
         pieces, gain_attn, w_query, w_key, w_value, cosine, sine, extra
     )

time: 88.6 us -> 89.7 us (1.012)
  Pallas kernels: 17.2 us -> 18.3 us
    pallas_call x1, Pallas kernels: 3.6 us -> 4.72 us  [attend(): pl.pallas_call(functools.partial(attend_kernel, len(pieces), heads, reach...]
where the time goes in v12:
time: 89.7 us; the launch traced here: 88.6 us
  waiting for transfers between devices  35.3 us (39%)
  starting transfers between devices  24.9 us (28%)
  Pallas kernels  18.3 us (20%)
  local copies, waits for them, and re-layouts  9.15 us (10%)
    ppermute x16, waiting for transfers between devices, tp_xor(): lax.ppermute(value, 'tp', [(i, i ^ mask) for i in range(lax.axis_size('tp...  29.3 us
    ppermute x16, starting transfers between devices, tp_xor(): lax.ppermute(value, 'tp', [(i, i ^ mask) for i in range(lax.axis_size('tp...  20.3 us
    unnamed x34, local copies, waits for them, and re-layouts  8.16 us
    ppermute x10, waiting for transfers between devices, seq_xor(): lax.ppermute(value, 'seq', [(i, i ^ mask) for i in range(lax.axis_size('s...  6.03 us
    pallas_call x1, Pallas kernels, attend(): pl.pallas_call(functools.partial(attend_kernel, len(pieces), heads, reach...  4.72 us
    pallas_call x1, Pallas kernels, fill_cache(): pl.pallas_call(functools.partial(cache_kernel, len(pieces), 2 * PAGE), ou...  4.7 us
    ppermute x10, starting transfers between devices, seq_xor(): lax.ppermute(value, 'seq', [(i, i ^ mask) for i in range(lax.axis_size('s...  4.59 us
    pallas_call x1, Pallas kernels, hidden_of(): pl.pallas_call(functools.partial(hidden_kernel, *counts), out_shape=[jax....  3.83 us
  transfers between devices with their start and end apart: 26, of which 16 were waited for; matrix products, arithmetic and copies ran while one was open for 0% of the time, Pallas kernels for 9%

profile of v12, /device:TPU:2, one launch (start us, length us, event | category | flops | bytes accessed | tf_op | source)
XLA Modules:
  0.0 88.6 jit_solution(8848496657200990405)
XLA Ops:
  0.6 1.0 %fusion = (bf16[256,256]{1,0:T(8,128)(2,1)S(1)}, bf16[256,256]{1,0:T(8,128)(2,1)S(1)}) fusion(bf16[512,256]{1,0:T(8,128)(2,1)} %refs_0_.2), kind=kLoop, calls=%fused_computation | loop fusion | bytes 524288 | tf_op jit(solution)/shard_map/slice | solution.py:721
  1.6 2.7 %collective-permute-start = (bf16[256,256]{1,0:T(8,128)(2,1)S(1)}, bf16[256,256]{1,0:T(8,128)(2,1)S(1)}, u32[]{:S(2)}, u32[]{:S(2)}) collective-permute-start(bf16[256,256]{1,0:T(8,128)(2,1)S(1)} %get-tuple-element.63), channel_id=1, source_target_pairs={{0,2},{1,3},{2,0},{3,1},{4,6},{5,7},{6,4},{7,5},{8,10},{9,11},{10,... | collective-permute-start | bytes 393224 | tf_op jit(solution)/shard_map/ppermute | solution.py:57
  4.6 1.6 %collective-permute-start.1 = (bf16[512,256]{1,0:T(8,128)(2,1)}, bf16[512,256]{1,0:T(8,128)(2,1)S(1)}, u32[]{:S(2)}, u32[]{:S(2)}) collective-permute-start(bf16[512,256]{1,0:T(8,128)(2,1)} %refs_0_.2), channel_id=1, source_target_pairs={{0,1},{1,0},{2,3},{3,2},{4,5},{5,4},{6,7},{7,6},{8,9},{9,8},{10,11... | collective-permute-start | bytes 786440 | tf_op jit(solution)/shard_map/ppermute | solution.py:57
  6.2 0.9 %copy-done.3 = bf16[128,1024]{1,0:T(8,128)(2,1)S(1)} copy-done((bf16[128,1024]{1,0:T(8,128)(2,1)S(1)}, bf16[128,1024]{1,0:T(8,128)(2,1)}, u32[]{:S(2)}) %copy-start.3) | copy-done | bytes 262168
  7.2 0.9 %copy-done.6 = bf16[1024,128]{1,0:T(8,128)(2,1)S(1)} copy-done((bf16[1024,128]{1,0:T(8,128)(2,1)S(1)}, bf16[1024,128]{1,0:T(8,128)(2,1)}, u32[]{:S(2)}) %copy-start.6) | copy-done | bytes 262168
  8.1 0.9 %copy-done.7 = bf16[1024,128]{1,0:T(8,128)(2,1)S(1)} copy-done((bf16[1024,128]{1,0:T(8,128)(2,1)S(1)}, bf16[1024,128]{1,0:T(8,128)(2,1)}, u32[]{:S(2)}) %copy-start.7) | copy-done | bytes 262168
  9.1 0.7 copy-done.9
  9.7 0.7 copy-done.10
  10.4 0.7 copy-done.13
  11.1 0.7 copy-done.15
  11.8 1.1 %tables.1 = (f32[512,128]{1,0:T(8,128)S(1)}, f32[512,128]{1,0:T(8,128)S(1)}, bf16[16,256]{1,0:T(8,128)(2,1)S(1)}, bf16[2,512,128]{2,1,0:T(8,128)(2,1)S(1)}, bf16...) custom-call(s32[4]{0:T(128)S(1)} %copy-done.13, f32[2,2]{1,0:T(2,128)S(1)} %copy-done.15, ...), custom_call_target="tpu_custom_call" | custom-call | flops 524288 | bytes 1048576 | tf_op jit(solution)/shard_map/tables/pallas_call | solution.py:177
  12.9 1.8 %collective-permute-done.refs_2_ = bf16[256,256]{1,0:T(8,128)(2,1)S(1)} collective-permute-done((bf16[256,256]{1,0:T(8,128)(2,1)S(1)}, bf16[256,256]{1,0:T(8,128)(2,1)S(1)}, u32[]{:S(2)}, u32[]{:S(2)}) %collective-permute-start) | collective-permute-done | bytes 131104 | tf_op jit(solution)/shard_map/ppermute | solution.py:57
  14.7 0.9 %copy-done.5 = bf16[512,256]{1,0:T(8,128)(2,1)S(1)} copy-done((bf16[512,256]{1,0:T(8,128)(2,1)S(1)}, bf16[512,256]{1,0:T(8,128)(2,1)}, u32[]{:S(2)}) %copy-start.5) | copy-done | bytes 262168
  15.6 0.9 %copy-done.8 = bf16[1024,128]{1,0:T(8,128)(2,1)S(1)} copy-done((bf16[1024,128]{1,0:T(8,128)(2,1)S(1)}, bf16[1024,128]{1,0:T(8,128)(2,1)}, u32[]{:S(2)}) %copy-start.8) | copy-done | bytes 262168
  16.6 0.7 copy-done.11
  17.4 2.1 %collective-permute-start.4 = (bf16[256,256]{1,0:T(8,128)(2,1)S(1)}, bf16[256,256]{1,0:T(8,128)(2,1)S(1)}, u32[]{:S(2)}, u32[]{:S(2)}) collective-permute-start(bf16[256,256]{1,0:T(8,128)(2,1)S(1)} %collective-permute-done.2.refs_3_), channel_id=1, source_target_pairs={{0,1},{1,0},{2,3},{3,2},{4,5},{5,4},{6,7},{7,6},{8,9},{9,8},{10,11... | collective-permute-start | bytes 393224 | tf_op jit(solution)/shard_map/ppermute | solution.py:57
  19.4 0.6 collective-permute-done.3.refs_4_
  20.1 2.4 %collective-permute-done.4.refs_5_ = bf16[256,256]{1,0:T(8,128)(2,1)S(1)} collective-permute-done((bf16[256,256]{1,0:T(8,128)(2,1)S(1)}, bf16[256,256]{1,0:T(8,128)(2,1)S(1)}, u32[]{:S(2)}, u32[]{:S(2)}) %collective-permute-start.4) | collective-permute-done | bytes 131104 | tf_op jit(solution)/shard_map/ppermute | solution.py:57
  22.5 1.4 %project.1 = (bf16[512,1024]{1,0:T(8,128)(2,1)S(1)}, bf16[512,128]{1,0:T(8,128)(2,1)S(1)}, bf16[528,256]{1,0:T(8,128)(2,1)S(1)}) custom-call(bf16[512,256]{1,0:T(8,128)(2,1)S(1)} %get-tuple-element.69.refs_0_, bf16[512,256]{1,0:T(8,128)(2,1)S(1)} %collective-permute-done.1.refs_1_, bf16[256,256]{1,0:T(8,128)(2,1)S(1)} %collective-permute-done.refs_2_, ...), custom_call_target="tpu_custom_call" | custom-call | flops 402653184 | bytes 4194304 | tf_op jit(solution)/shard_map/project/pallas_call | solution.py:251
  23.9 3.0 %collective-permute-start.7 = (bf16[128,512]{1,0:T(8,128)(2,1)S(1)}, bf16[128,512]{1,0:T(8,128)(2,1)S(1)}, u32[]{:S(2)}, u32[]{:S(2)}) collective-permute-start(bf16[128,512]{1,0:T(8,128)(2,1)S(1)} %get-tuple-element.83), channel_id=1, source_target_pairs={{0,2},{1,3},{2,0},{3,1},{4,6},{5,7},{6,4},{7,5},{8,10},{9,11},{10,... | collective-permute-start | bytes 393224 | tf_op jit(solution)/shard_map/ppermute | solution.py:57
  26.9 2.2 %collective-permute-start.5 = (bf16[128,512]{1,0:T(8,128)(2,1)S(1)}, bf16[128,512]{1,0:T(8,128)(2,1)S(1)}, u32[]{:S(2)}, u32[]{:S(2)}) collective-permute-start(bf16[128,512]{1,0:T(8,128)(2,1)S(1)} %get-tuple-element.83), channel_id=1, source_target_pairs={{0,1},{1,0},{2,3},{3,2},{4,5},{5,4},{6,7},{7,6},{8,9},{9,8},{10,11... | collective-permute-start | bytes 393224 | tf_op jit(solution)/shard_map/ppermute | solution.py:57
  29.1 1.5 %collective-permute-start.13 = (bf16[528,256]{1,0:T(8,128)(2,1)S(1)}, bf16[528,256]{1,0:T(8,128)(2,1)S(1)}, u32[]{:S(2)}, u32[]{:S(2)}) collective-permute-start(bf16[528,256]{1,0:T(8,128)(2,1)S(1)} %get-tuple-element.116.refs_0_), channel_id=1, source_target_pairs={{0,24},{4,28},{8,16},{12,20},{16,8},{20,12},{24,0},{28,4},{1,25},{... | collective-permute-start | bytes 811016 | tf_op jit(solution)/shard_map/ppermute | solution.py:268
  30.6 0.5 collective-permute-start.12
  31.1 1.5 %collective-permute-start.11 = (bf16[528,256]{1,0:T(8,128)(2,1)S(1)}, bf16[528,256]{1,0:T(8,128)(2,1)S(1)}, u32[]{:S(2)}, u32[]{:S(2)}) collective-permute-start(bf16[528,256]{1,0:T(8,128)(2,1)S(1)} %get-tuple-element.116.refs_0_), channel_id=1, source_target_pairs={{0,8},{4,12},{8,0},{12,4},{16,24},{20,28},{24,16},{28,20},{1,9},{5... | collective-permute-start | bytes 811016 | tf_op jit(solution)/shard_map/ppermute | solution.py:268
  32.6 1.6 %collective-permute-start.9 = (bf16[128,512]{1,0:T(8,128)(2,1)S(1)}, bf16[128,512]{1,0:T(8,128)(2,1)S(1)}, u32[]{:S(2)}, u32[]{:S(2)}) collective-permute-start(bf16[128,512]{1,0:T(8,128)(2,1)S(1)} %collective-permute-done.7.refs_7_), channel_id=1, source_target_pairs={{0,1},{1,0},{2,3},{3,2},{4,5},{5,4},{6,7},{7,6},{8,9},{9,8},{10,11... | collective-permute-start | bytes 393224 | tf_op jit(solution)/shard_map/ppermute | solution.py:57
  34.2 3.4 %collective-permute-done.9.refs_9_ = bf16[128,512]{1,0:T(8,128)(2,1)S(1)} collective-permute-done((bf16[128,512]{1,0:T(8,128)(2,1)S(1)}, bf16[128,512]{1,0:T(8,128)(2,1)S(1)}, u32[]{:S(2)}, u32[]{:S(2)}) %collective-permute-start.9) | collective-permute-done | bytes 131104 | tf_op jit(solution)/shard_map/ppermute | solution.py:57
  37.6 0.5 collective-permute-start.10
  38.1 0.8 collective-permute-done.6.refs_6_
  38.9 0.4 collective-permute-done.13.refs_6_
  39.4 2.8 %collective-permute-done.12.refs_4_ = bf16[528,256]{1,0:T(8,128)(2,1)S(1)} collective-permute-done((bf16[528,256]{1,0:T(8,128)(2,1)S(1)}, bf16[528,256]{1,0:T(8,128)(2,1)S(1)}, u32[]{:S(2)}, u32[]{:S(2)}) %collective-permute-start.12) | collective-permute-done | bytes 270368 | tf_op jit(solution)/shard_map/ppermute | solution.py:268
  42.3 0.5 collective-permute-start.15
  42.8 1.0 %collective-permute-done.14.refs_3_ = bf16[528,256]{1,0:T(8,128)(2,1)S(1)} collective-permute-done((bf16[528,256]{1,0:T(8,128)(2,1)S(1)}, bf16[528,256]{1,0:T(8,128)(2,1)S(1)}, u32[]{:S(2)}, u32[]{:S(2)}) %collective-permute-start.14) | collective-permute-done | bytes 270368 | tf_op jit(solution)/shard_map/ppermute | solution.py:268
  43.9 0.4 collective-permute-done.15.refs_5_
  44.3 0.4 collective-permute-done.16.refs_7_
  44.7 4.7 %attend.1.refs_0_ = bf16[512,128]{1,0:T(8,128)(2,1)S(1)} custom-call(s32[4]{0:T(128)S(1)} %copy-done.14, bf16[512,128]{1,0:T(8,128)(2,1)S(1)} %get-tuple-element.79.queries, bf16[2,512,128]{2,1,0:T(8,128)(2,1)S(1)} %get-tuple-element.85.query_marks, bf16[528,256]{1,0:T(8,128)(2,1)S(1)} %get-tuple-element.116.refs_0_, ...), custom_call_target="tpu_custom_call" | custom-call | flops 2684354560 | bytes 4194304 | tf_op jit(solution)/shard_map/attend/pallas_call | solution.py:416
  49.7 1.6 %collective-permute-start.18 = (bf16[512,128]{1,0:T(8,128)(2,1)S(1)}, bf16[512,128]{1,0:T(8,128)(2,1)S(1)}, u32[]{:S(2)}, u32[]{:S(2)}) collective-permute-start(bf16[512,128]{1,0:T(8,128)(2,1)S(1)} %attend.1.refs_0_), channel_id=1, source_target_pairs={{0,2},{1,3},{2,0},{3,1},{4,6},{5,7},{6,4},{7,5},{8,10},{9,11},{10,... | collective-permute-start | bytes 393224 | tf_op jit(solution)/shard_map/ppermute | solution.py:57
  51.3 2.6 %collective-permute-start.17 = (bf16[512,128]{1,0:T(8,128)(2,1)S(1)}, bf16[512,128]{1,0:T(8,128)(2,1)S(1)}, u32[]{:S(2)}, u32[]{:S(2)}) collective-permute-start(bf16[512,128]{1,0:T(8,128)(2,1)S(1)} %attend.1.refs_0_), channel_id=1, source_target_pairs={{0,1},{1,0},{2,3},{3,2},{4,5},{5,4},{6,7},{7,6},{8,9},{9,8},{10,11... | collective-permute-start | bytes 393224 | tf_op jit(solution)/shard_map/ppermute | solution.py:57
  54.0 0.6 fetch.3
  54.6 3.2 %collective-permute-done.19.refs_3_ = bf16[512,128]{1,0:T(8,128)(2,1)S(1)} collective-permute-done((bf16[512,128]{1,0:T(8,128)(2,1)S(1)}, bf16[512,128]{1,0:T(8,128)(2,1)S(1)}, u32[]{:S(2)}, u32[]{:S(2)}) %collective-permute-start.19) | collective-permute-done | bytes 131104 | tf_op jit(solution)/shard_map/ppermute | solution.py:57
  57.8 5.8 %collective-permute-done.18.refs_2_ = bf16[512,128]{1,0:T(8,128)(2,1)S(1)} collective-permute-done((bf16[512,128]{1,0:T(8,128)(2,1)S(1)}, bf16[512,128]{1,0:T(8,128)(2,1)S(1)}, u32[]{:S(2)}, u32[]{:S(2)}) %collective-permute-start.18) | collective-permute-done | bytes 131104 | tf_op jit(solution)/shard_map/ppermute | solution.py:57
  63.6 3.8 %hidden.1 = (bf16[512,1024]{1,0:T(8,128)(2,1)S(1)}, bf16[512,256]{1,0:T(8,128)(2,1)S(1)}, bf16[256,256]{1,0:T(8,128)(2,1)S(1)}, bf16[256,256]{1,0:T(8,128)(2,1)S(1)}) custom-call(bf16[512,128]{1,0:T(8,128)(2,1)S(1)} %attend.1.refs_0_, bf16[512,128]{1,0:T(8,128)(2,1)S(1)} %collective-permute-done.17.refs_1_, ...), custom_call_target="tpu_custom_call" | custom-call | flops 3221225472 | bytes 10485760 | tf_op jit(solution)/shard_map/hidden/pallas_call | solution.py:599
  67.5 2.0 %collective-permute-start.24 = (bf16[256,256]{1,0:T(8,128)(2,1)S(1)}, bf16[256,256]{1,0:T(8,128)(2,1)S(1)}, u32[]{:S(2)}, u32[]{:S(2)}) collective-permute-start(bf16[256,256]{1,0:T(8,128)(2,1)S(1)} %get-tuple-element.115), channel_id=1, source_target_pairs={{0,1},{1,0},{2,3},{3,2},{4,5},{5,4},{6,7},{7,6},{8,9},{9,8},{10,11... | collective-permute-start | bytes 393224 | tf_op jit(solution)/shard_map/ppermute | solution.py:57
  69.5 1.0 %down_blocks.1 = (f32[256,256]{1,0:T(8,128)S(1)}, f32[256,256]{1,0:T(8,128)S(1)}, bf16[512,256]{1,0:T(8,128)(2,1)S(1)}, f32[512,256]{1,0:T(8,128)S(1)}) custom-call(bf16[512,1024]{1,0:T(8,128)(2,1)S(1)} %get-tuple-element.108.hidden, bf16[512,256]{1,0:T(8,128)(2,1)S(1)} %get-tuple-element.109.kept, bf16[1024,1024]{1,0:T(8,128)(2,1)S(1)} %get-tuple-element.107.refs_15_.w_down), custom_call_target="tpu_custom_call" | custom-call | flops 805306368 | bytes 5242880 | tf_op jit(solution)/shard_map/down_blocks/pallas_call | solution.py:633
  70.6 3.2 %collective-permute-done.22.refs_1_ = bf16[256,256]{1,0:T(8,128)(2,1)S(1)} collective-permute-done((bf16[256,256]{1,0:T(8,128)(2,1)S(1)}, bf16[256,256]{1,0:T(8,128)(2,1)S(1)}, u32[]{:S(2)}, u32[]{:S(2)}) %collective-permute-start.22) | collective-permute-done | bytes 131104 | tf_op jit(solution)/shard_map/ppermute | solution.py:57
  74.0 6.4 %collective-permute-done.24.refs_1_ = bf16[256,256]{1,0:T(8,128)(2,1)S(1)} collective-permute-done((bf16[256,256]{1,0:T(8,128)(2,1)S(1)}, bf16[256,256]{1,0:T(8,128)(2,1)S(1)}, u32[]{:S(2)}, u32[]{:S(2)}) %collective-permute-start.24) | collective-permute-done | bytes 131104 | tf_op jit(solution)/shard_map/ppermute | solution.py:57
  80.5 4.7 %fill_cache.1 = bf16[576,2,128]{2,1,0:T(2,128)(2,1)} custom-call(s32[4]{0:T(128)S(1)} %copy-done.14, s32[72]{0:T(128)S(1)} %copy-done.16, bf16[528,256]{1,0:T(8,128)(2,1)S(1)} %get-tuple-element.116.refs_0_, bf16[528,256]{1,0:T(8,128)(2,1)S(1)} %collective-permute-done.10.refs_1_, bf16[528,256]{1,0:T(8,128)(2,1)S(1)} %collective-permute-done.11.refs_2_, ...), custom_call_target="tpu_custom_call" | custom-call | flops 75497472 | bytes 3145728 | tf_op jit(solution)/shard_map/fill_cache/pallas_call | solution.py:512
  85.3 2.5 %collective-permute-done.25.refs_3_ = bf16[256,256]{1,0:T(8,128)(2,1)S(1)} collective-permute-done((bf16[256,256]{1,0:T(8,128)(2,1)S(1)}, bf16[256,256]{1,0:T(8,128)(2,1)S(1)}, u32[]{:S(2)}, u32[]{:S(2)}) %collective-permute-start.25) | collective-permute-done | bytes 131104 | tf_op jit(solution)/shard_map/ppermute | solution.py:57
  87.8 0.8 add_up.5
  (50 shorter events, 1.3 us)
Async XLA Ops:
  0.6 44.0 %copy-start.14 = (s32[4]{0:T(128)S(1)}, s32[4]{0:T(128)}, u32[]{:S(2)}) copy-start(s32[4]{0:T(128)} %lengths.5) | copy-start | bytes 52
  1.6 13.0 %collective-permute-start = (bf16[256,256]{1,0:T(8,128)(2,1)S(1)}, bf16[256,256]{1,0:T(8,128)(2,1)S(1)}, u32[]{:S(2)}, u32[]{:S(2)}) collective-permute-start(bf16[256,256]{1,0:T(8,128)(2,1)S(1)} %get-tuple-element.63), channel_id=1, source_target_pairs={{0,2},{1,3},{2,0},{3,1},{4,6},{5,7},{6,4},{7,5},{8,10},{9,11},{10,... | collective-permute-start | bytes 393224 | tf_op jit(solution)/shard_map/ppermute | solution.py:57
  4.3 13.1 %collective-permute-start.2 = (bf16[256,256]{1,0:T(8,128)(2,1)S(1)}, bf16[256,256]{1,0:T(8,128)(2,1)S(1)}, u32[]{:S(2)}, u32[]{:S(2)}) collective-permute-start(bf16[256,256]{1,0:T(8,128)(2,1)S(1)} %get-tuple-element.71), channel_id=1, source_target_pairs={{0,2},{1,3},{2,0},{3,1},{4,6},{5,7},{6,4},{7,5},{8,10},{9,11},{10,... | collective-permute-start | bytes 393224 | tf_op jit(solution)/shard_map/ppermute | solution.py:57
  4.6 14.8 %collective-permute-start.1 = (bf16[512,256]{1,0:T(8,128)(2,1)}, bf16[512,256]{1,0:T(8,128)(2,1)S(1)}, u32[]{:S(2)}, u32[]{:S(2)}) collective-permute-start(bf16[512,256]{1,0:T(8,128)(2,1)} %refs_0_.2), channel_id=1, source_target_pairs={{0,1},{1,0},{2,3},{3,2},{4,5},{5,4},{6,7},{7,6},{8,9},{9,8},{10,11... | collective-permute-start | bytes 786440 | tf_op jit(solution)/shard_map/ppermute | solution.py:57
  6.2 0.9 %copy-start.3 = (bf16[128,1024]{1,0:T(8,128)(2,1)S(1)}, bf16[128,1024]{1,0:T(8,128)(2,1)}, u32[]{:S(2)}) copy-start(bf16[128,1024]{1,0:T(8,128)(2,1)} %refs_0_.3) | copy-start | bytes 786436
  7.2 0.9 %copy-start.6 = (bf16[1024,128]{1,0:T(8,128)(2,1)S(1)}, bf16[1024,128]{1,0:T(8,128)(2,1)}, u32[]{:S(2)}) copy-start(bf16[1024,128]{1,0:T(8,128)(2,1)} %refs_0_.1) | copy-start | bytes 786436
  8.1 0.9 %copy-start.7 = (bf16[1024,128]{1,0:T(8,128)(2,1)S(1)}, bf16[1024,128]{1,0:T(8,128)(2,1)}, u32[]{:S(2)}) copy-start(bf16[1024,128]{1,0:T(8,128)(2,1)} %refs_1_.1) | copy-start | bytes 786436
  9.1 0.7 copy-start.9
  9.7 0.7 copy-start.10
  10.4 0.7 copy-start.13
  11.1 0.7 copy-start.15
  14.7 5.4 %collective-permute-start.3 = (bf16[256,256]{1,0:T(8,128)(2,1)S(1)}, bf16[256,256]{1,0:T(8,128)(2,1)S(1)}, u32[]{:S(2)}, u32[]{:S(2)}) collective-permute-start(bf16[256,256]{1,0:T(8,128)(2,1)S(1)} %collective-permute-done.refs_2_), channel_id=1, source_target_pairs={{0,1},{1,0},{2,3},{3,2},{4,5},{5,4},{6,7},{7,6},{8,9},{9,8},{10,11... | collective-permute-start | bytes 393224 | tf_op jit(solution)/shard_map/ppermute | solution.py:57
  14.7 1.0 %copy-start.5 = (bf16[512,256]{1,0:T(8,128)(2,1)S(1)}, bf16[512,256]{1,0:T(8,128)(2,1)}, u32[]{:S(2)}) copy-start(bf16[512,256]{1,0:T(8,128)(2,1)} %refs_0_.2) | copy-start | bytes 786436
  15.6 0.9 %copy-start.8 = (bf16[1024,128]{1,0:T(8,128)(2,1)S(1)}, bf16[1024,128]{1,0:T(8,128)(2,1)}, u32[]{:S(2)}) copy-start(bf16[1024,128]{1,0:T(8,128)(2,1)} %refs_2_.2) | copy-start | bytes 786436
  16.6 0.7 copy-start.11
  17.4 5.1 %collective-permute-start.4 = (bf16[256,256]{1,0:T(8,128)(2,1)S(1)}, bf16[256,256]{1,0:T(8,128)(2,1)S(1)}, u32[]{:S(2)}, u32[]{:S(2)}) collective-permute-start(bf16[256,256]{1,0:T(8,128)(2,1)S(1)} %collective-permute-done.2.refs_3_), channel_id=1, source_target_pairs={{0,1},{1,0},{2,3},{3,2},{4,5},{5,4},{6,7},{7,6},{8,9},{9,8},{10,11... | collective-permute-start | bytes 393224 | tf_op jit(solution)/shard_map/ppermute | solution.py:57
  23.9 8.7 %collective-permute-start.7 = (bf16[128,512]{1,0:T(8,128)(2,1)S(1)}, bf16[128,512]{1,0:T(8,128)(2,1)S(1)}, u32[]{:S(2)}, u32[]{:S(2)}) collective-permute-start(bf16[128,512]{1,0:T(8,128)(2,1)S(1)} %get-tuple-element.83), channel_id=1, source_target_pairs={{0,2},{1,3},{2,0},{3,1},{4,6},{5,7},{6,4},{7,5},{8,10},{9,11},{10,... | collective-permute-start | bytes 393224 | tf_op jit(solution)/shard_map/ppermute | solution.py:57
  26.9 5.7 %collective-permute-start.5 = (bf16[128,512]{1,0:T(8,128)(2,1)S(1)}, bf16[128,512]{1,0:T(8,128)(2,1)S(1)}, u32[]{:S(2)}, u32[]{:S(2)}) collective-permute-start(bf16[128,512]{1,0:T(8,128)(2,1)S(1)} %get-tuple-element.83), channel_id=1, source_target_pairs={{0,1},{1,0},{2,3},{3,2},{4,5},{5,4},{6,7},{7,6},{8,9},{9,8},{10,11... | collective-permute-start | bytes 393224 | tf_op jit(solution)/shard_map/ppermute | solution.py:57
  29.1 10.3 %collective-permute-start.13 = (bf16[528,256]{1,0:T(8,128)(2,1)S(1)}, bf16[528,256]{1,0:T(8,128)(2,1)S(1)}, u32[]{:S(2)}, u32[]{:S(2)}) collective-permute-start(bf16[528,256]{1,0:T(8,128)(2,1)S(1)} %get-tuple-element.116.refs_0_), channel_id=1, source_target_pairs={{0,24},{4,28},{8,16},{12,20},{16,8},{20,12},{24,0},{28,4},{1,25},{... | collective-permute-start | bytes 811016 | tf_op jit(solution)/shard_map/ppermute | solution.py:268
  30.6 11.6 %collective-permute-start.12 = (bf16[528,256]{1,0:T(8,128)(2,1)S(1)}, bf16[528,256]{1,0:T(8,128)(2,1)S(1)}, u32[]{:S(2)}, u32[]{:S(2)}) collective-permute-start(bf16[528,256]{1,0:T(8,128)(2,1)S(1)} %get-tuple-element.116.refs_0_), channel_id=1, source_target_pairs={{0,16},{4,20},{8,24},{12,28},{16,0},{20,4},{24,8},{28,12},{1,17},{... | collective-permute-start | bytes 811016 | tf_op jit(solution)/shard_map/ppermute | solution.py:268
  31.1 11.2 %collective-permute-start.11 = (bf16[528,256]{1,0:T(8,128)(2,1)S(1)}, bf16[528,256]{1,0:T(8,128)(2,1)S(1)}, u32[]{:S(2)}, u32[]{:S(2)}) collective-permute-start(bf16[528,256]{1,0:T(8,128)(2,1)S(1)} %get-tuple-element.116.refs_0_), channel_id=1, source_target_pairs={{0,8},{4,12},{8,0},{12,4},{16,24},{20,28},{24,16},{28,20},{1,9},{5... | collective-permute-start | bytes 811016 | tf_op jit(solution)/shard_map/ppermute | solution.py:268
  32.6 5.0 %collective-permute-start.9 = (bf16[128,512]{1,0:T(8,128)(2,1)S(1)}, bf16[128,512]{1,0:T(8,128)(2,1)S(1)}, u32[]{:S(2)}, u32[]{:S(2)}) collective-permute-start(bf16[128,512]{1,0:T(8,128)(2,1)S(1)} %collective-permute-done.7.refs_7_), channel_id=1, source_target_pairs={{0,1},{1,0},{2,3},{3,2},{4,5},{5,4},{6,7},{7,6},{8,9},{9,8},{10,11... | collective-permute-start | bytes 393224 | tf_op jit(solution)/shard_map/ppermute | solution.py:57
  34.2 3.4 %collective-permute-start.8 = (bf16[128,512]{1,0:T(8,128)(2,1)S(1)}, bf16[128,512]{1,0:T(8,128)(2,1)S(1)}, u32[]{:S(2)}, u32[]{:S(2)}) collective-permute-start(bf16[128,512]{1,0:T(8,128)(2,1)S(1)} %collective-permute-done.7.refs_7_), channel_id=1, source_target_pairs={{0,4},{4,0},{8,12},{12,8},{16,20},{20,16},{24,28},{28,24},{1,5},{5... | collective-permute-start | bytes 393224 | tf_op jit(solution)/shard_map/ppermute | solution.py:268
  37.6 1.3 %collective-permute-start.6 = (bf16[128,512]{1,0:T(8,128)(2,1)S(1)}, bf16[128,512]{1,0:T(8,128)(2,1)S(1)}, u32[]{:S(2)}, u32[]{:S(2)}) collective-permute-start(bf16[128,512]{1,0:T(8,128)(2,1)S(1)} %collective-permute-done.5.refs_5_), channel_id=1, source_target_pairs={{0,4},{4,0},{8,12},{12,8},{16,20},{20,16},{24,28},{28,24},{1,5},{5... | collective-permute-start | bytes 393224 | tf_op jit(solution)/shard_map/ppermute | solution.py:268
  37.6 5.2 %collective-permute-start.10 = (bf16[528,256]{1,0:T(8,128)(2,1)S(1)}, bf16[528,256]{1,0:T(8,128)(2,1)S(1)}, u32[]{:S(2)}, u32[]{:S(2)}) collective-permute-start(bf16[528,256]{1,0:T(8,128)(2,1)S(1)} %get-tuple-element.116.refs_0_), channel_id=1, source_target_pairs={{0,4},{4,0},{8,12},{12,8},{16,20},{20,16},{24,28},{28,24},{1,5},{5... | collective-permute-start | bytes 811016 | tf_op jit(solution)/shard_map/ppermute | solution.py:268
  42.3 1.5 %collective-permute-start.14 = (bf16[528,256]{1,0:T(8,128)(2,1)S(1)}, bf16[528,256]{1,0:T(8,128)(2,1)S(1)}, u32[]{:S(2)}, u32[]{:S(2)}) collective-permute-start(bf16[528,256]{1,0:T(8,128)(2,1)S(1)} %collective-permute-done.11.refs_2_), channel_id=1, source_target_pairs={{0,4},{4,0},{8,12},{12,8},{16,20},{20,16},{24,28},{28,24},{1,5},{5... | collective-permute-start | bytes 811016 | tf_op jit(solution)/shard_map/ppermute | solution.py:268
  42.3 1.9 %collective-permute-start.15 = (bf16[528,256]{1,0:T(8,128)(2,1)S(1)}, bf16[528,256]{1,0:T(8,128)(2,1)S(1)}, u32[]{:S(2)}, u32[]{:S(2)}) collective-permute-start(bf16[528,256]{1,0:T(8,128)(2,1)S(1)} %collective-permute-done.12.refs_4_), channel_id=1, source_target_pairs={{0,4},{4,0},{8,12},{12,8},{16,20},{20,16},{24,28},{28,24},{1,5},{5... | collective-permute-start | bytes 811016 | tf_op jit(solution)/shard_map/ppermute | solution.py:268
  42.8 1.8 %collective-permute-start.16 = (bf16[528,256]{1,0:T(8,128)(2,1)S(1)}, bf16[528,256]{1,0:T(8,128)(2,1)S(1)}, u32[]{:S(2)}, u32[]{:S(2)}) collective-permute-start(bf16[528,256]{1,0:T(8,128)(2,1)S(1)} %collective-permute-done.13.refs_6_), channel_id=1, source_target_pairs={{0,4},{4,0},{8,12},{12,8},{16,20},{20,16},{24,28},{28,24},{1,5},{5... | collective-permute-start | bytes 811016 | tf_op jit(solution)/shard_map/ppermute | solution.py:268
  44.6 9.3 %copy-start = (bf16[1024,1024]{1,0:T(8,128)(2,1)S(1)}, bf16[1024,1024]{1,0:T(8,128)(2,1)}, u32[]{:S(2)}) copy-start(bf16[1024,1024]{1,0:T(8,128)(2,1)} %refs_3_) | copy-start | bytes 6291460
  44.6 9.3 %copy-start.1 = (bf16[1024,1024]{1,0:T(8,128)(2,1)S(1)}, bf16[1024,1024]{1,0:T(8,128)(2,1)}, u32[]{:S(2)}) copy-start(bf16[1024,1024]{1,0:T(8,128)(2,1)} %refs_4_) | copy-start | bytes 6291460
  44.6 9.3 %copy-start.2 = (bf16[1024,1024]{1,0:T(8,128)(2,1)S(1)}, bf16[1024,1024]{1,0:T(8,128)(2,1)}, u32[]{:S(2)}) copy-start(bf16[1024,1024]{1,0:T(8,128)(2,1)} %refs_5_) | copy-start | bytes 6291460
  44.7 9.3 %copy-start.4 = (bf16[128,1024]{1,0:T(8,128)(2,1)S(1)}, bf16[128,1024]{1,0:T(8,128)(2,1)}, u32[]{:S(2)}) copy-start(bf16[128,1024]{1,0:T(8,128)(2,1)} %refs_0_.3) | copy-start | bytes 786436
  44.7 9.3 %copy-start.12 = (bf16[1024]{0:T(1024)(128)(2,1)S(1)}, bf16[1024]{0:T(1024)(128)(2,1)}, u32[]{:S(2)}) copy-start(bf16[1024]{0:T(1024)(128)(2,1)} %refs_2_.3) | copy-start | bytes 6148
  49.4 5.1 %collective-permute-start.20 = (bf16[128,512]{1,0:T(8,128)(2,1)S(1)}, bf16[128,512]{1,0:T(8,128)(2,1)S(1)}, u32[]{:S(2)}, u32[]{:S(2)}) collective-permute-start(bf16[128,512]{1,0:T(8,128)(2,1)S(1)} %collective-permute-done.9.refs_9_), channel_id=1, source_target_pairs={{0,4},{4,0},{8,12},{12,8},{16,20},{20,16},{24,28},{28,24},{1,5},{5... | collective-permute-start | bytes 393224 | tf_op jit(solution)/shard_map/ppermute | solution.py:268
  49.5 8.3 %collective-permute-start.19 = (bf16[512,128]{1,0:T(8,128)(2,1)S(1)}, bf16[512,128]{1,0:T(8,128)(2,1)S(1)}, u32[]{:S(2)}, u32[]{:S(2)}) collective-permute-start(bf16[512,128]{1,0:T(8,128)(2,1)S(1)} %attend.1.refs_0_), channel_id=1, source_target_pairs={{0,3},{1,2},{2,1},{3,0},{4,7},{5,6},{6,5},{7,4},{8,11},{9,10},{10,... | collective-permute-start | bytes 393224 | tf_op jit(solution)/shard_map/ppermute | solution.py:57
  49.7 13.8 %collective-permute-start.18 = (bf16[512,128]{1,0:T(8,128)(2,1)S(1)}, bf16[512,128]{1,0:T(8,128)(2,1)S(1)}, u32[]{:S(2)}, u32[]{:S(2)}) collective-permute-start(bf16[512,128]{1,0:T(8,128)(2,1)S(1)} %attend.1.refs_0_), channel_id=1, source_target_pairs={{0,2},{1,3},{2,0},{3,1},{4,6},{5,7},{6,4},{7,5},{8,10},{9,11},{10,... | collective-permute-start | bytes 393224 | tf_op jit(solution)/shard_map/ppermute | solution.py:57
  51.3 12.3 %collective-permute-start.17 = (bf16[512,128]{1,0:T(8,128)(2,1)S(1)}, bf16[512,128]{1,0:T(8,128)(2,1)S(1)}, u32[]{:S(2)}, u32[]{:S(2)}) collective-permute-start(bf16[512,128]{1,0:T(8,128)(2,1)S(1)} %attend.1.refs_0_), channel_id=1, source_target_pairs={{0,1},{1,0},{2,3},{3,2},{4,5},{5,4},{6,7},{7,6},{8,9},{9,8},{10,11... | collective-permute-start | bytes 393224 | tf_op jit(solution)/shard_map/ppermute | solution.py:57
  67.4 6.5 %collective-permute-start.22 = (bf16[256,256]{1,0:T(8,128)(2,1)S(1)}, bf16[256,256]{1,0:T(8,128)(2,1)S(1)}, u32[]{:S(2)}, u32[]{:S(2)}) collective-permute-start(bf16[256,256]{1,0:T(8,128)(2,1)S(1)} %get-tuple-element.113), channel_id=1, source_target_pairs={{0,1},{1,0},{2,3},{3,2},{4,5},{5,4},{6,7},{7,6},{8,9},{9,8},{10,11... | collective-permute-start | bytes 393224 | tf_op jit(solution)/shard_map/ppermute | solution.py:57
  67.5 13.0 %collective-permute-start.24 = (bf16[256,256]{1,0:T(8,128)(2,1)S(1)}, bf16[256,256]{1,0:T(8,128)(2,1)S(1)}, u32[]{:S(2)}, u32[]{:S(2)}) collective-permute-start(bf16[256,256]{1,0:T(8,128)(2,1)S(1)} %get-tuple-element.115), channel_id=1, source_target_pairs={{0,1},{1,0},{2,3},{3,2},{4,5},{5,4},{6,7},{7,6},{8,9},{9,8},{10,11... | collective-permute-start | bytes 393224 | tf_op jit(solution)/shard_map/ppermute | solution.py:57
  69.5 11.1 %copy-start.16 = (s32[72]{0:T(128)S(1)}, s32[72]{0:T(128)}, u32[]{:S(2)}) copy-start(s32[72]{0:T(128)} %page_table.1) | copy-start | bytes 868
  70.5 17.3 %collective-permute-start.21 = (bf16[512,256]{1,0:T(8,128)(2,1)S(1)}, bf16[512,256]{1,0:T(8,128)(2,1)S(1)}, u32[]{:S(2)}, u32[]{:S(2)}) collective-permute-start(bf16[512,256]{1,0:T(8,128)(2,1)S(1)} %get-tuple-element.111), channel_id=1, source_target_pairs={{0,1},{1,0},{2,3},{3,2},{4,5},{5,4},{6,7},{7,6},{8,9},{9,8},{10,11... | collective-permute-start | bytes 786440 | tf_op jit(solution)/shard_map/ppermute | solution.py:57
  73.9 11.4 %collective-permute-start.23 = (bf16[256,256]{1,0:T(8,128)(2,1)S(1)}, bf16[256,256]{1,0:T(8,128)(2,1)S(1)}, u32[]{:S(2)}, u32[]{:S(2)}) collective-permute-start(bf16[256,256]{1,0:T(8,128)(2,1)S(1)} %add_up.3), channel_id=1, source_target_pairs={{0,2},{1,3},{2,0},{3,1},{4,6},{5,7},{6,4},{7,5},{8,10},{9,11},{10,... | collective-permute-start | bytes 393224 | tf_op jit(solution)/shard_map/ppermute | solution.py:57
  80.5 7.3 %collective-permute-start.25 = (bf16[256,256]{1,0:T(8,128)(2,1)S(1)}, bf16[256,256]{1,0:T(8,128)(2,1)S(1)}, u32[]{:S(2)}, u32[]{:S(2)}) collective-permute-start(bf16[256,256]{1,0:T(8,128)(2,1)S(1)} %add_up.4), channel_id=1, source_target_pairs={{0,2},{1,3},{2,0},{3,1},{4,6},{5,7},{6,4},{7,5},{8,10},{9,11},{10,... | collective-permute-start | bytes 393224 | tf_op jit(solution)/shard_map/ppermute | solution.py:57
